TPU v7x, 32 devices: a whole 2x2x4 slice. The times are simulated.
32 devices in a mesh: batch: 4 (over x, core), blk: 8 (over z, y).
Axes of the slice: x: 2, y: 2, z: 4, core: 2. Of those that a mesh axis runs over, the one named last changes fastest.
Arguments:
- frames: bfloat16 [4096, 1024], P(('batch', 'blk')), may hold values from -6 to 6
- step_table: float32 [32, 1024], replicated, may hold values from -6 to 6
- clip_lengths: int32 [4, 4], P('batch'), may hold values from 1 to 866, as said below
- clip_steps: int32 [4, 4], P('batch'), may hold values from 0 to 31
- w_mod: bfloat16 [1024, 6144], replicated, may hold values from -0.1875 to 0.1875
- b_mod: float32 [6144], replicated, may hold values from -3 to 3
- w_qkv: bfloat16 [1024, 3072], replicated, may hold values from -0.1875 to 0.1875
- b_qkv: float32 [3072], replicated, may hold values from -3 to 3
- w_out: bfloat16 [1024, 1024], replicated, may hold values from -0.75 to 0.75
- b_out: float32 [1024], replicated, may hold values from -2 to 2
- w_up: bfloat16 [1024, 2048], replicated, may hold values from -0.1875 to 0.1875
- b_up: float32 [2048], replicated, may hold values from -3 to 3
- w_down: bfloat16 [2048, 1024], replicated, may hold values from -0.125 to 0.125
- b_down: float32 [1024], replicated, may hold values from -2 to 2
- cotangent: bfloat16 [4096, 1024], P(('batch', 'blk')), may hold values from -6 to 6
Outputs:
- frames_out: bfloat16 [4096, 1024], P(('batch', 'blk'))
- d_frames: bfloat16 [4096, 1024], P(('batch', 'blk'))
- d_table: float32 [32, 1024], replicated
- d_w_mod: float32 [1024, 6144], P('blk')
- d_b_mod: float32 [6144], replicated
- d_w_qkv: float32 [1024, 3072], P('blk')
- d_b_qkv: float32 [3072], replicated
- d_w_out: float32 [1024, 1024], P('blk')
- d_b_out: float32 [1024], replicated
- d_w_up: float32 [1024, 2048], P('blk')
- d_b_up: float32 [2048], replicated
- d_w_down: float32 [2048, 1024], P('blk')
- d_b_down: float32 [1024], replicated
Inputs may be any that keep to these rules, and one draw needn't show every extreme that they name: `clip_lengths`: each length is at least one frame, and each row's lengths sum to 1024. In each row one clip has exactly the largest length; it begins within the first 128 frames and ends within the last 128 frames.
All inputs are finite; a program needn't handle non-finite values.
Results may differ from a plain program's by a relative error of at most 0.018.
The roundings to bfloat16 on the way count: a program that leaves them out, or rounds other values in their place, can miss the bound.
Values may be sent and summed in bfloat16 or wider, within the bound.
No kernel may reach another device: no remote copies, remote signals or barrier semaphores. Data moves between devices by JAX's collectives and lax.ppermute only.
A program may use at most 256 MiB of HBM per device.

v0:
```python
import jax
import jax.numpy as jnp
from jax import lax
from jax.sharding import PartitionSpec as P

HEADS = 16


HIGH_PRECISION = lax.Precision.HIGHEST
NEGATIVE = -1e30


def passed_along(value, axis, by):
    size = lax.axis_size(axis)
    return lax.ppermute(value, axis, [(i, (i + by) % size) for i in range(size)])


def norm_rows(inputs):
    average = jnp.mean(inputs, axis=-1, keepdims=True)
    centred = inputs - average
    variance = jnp.mean(centred * centred, axis=-1, keepdims=True)
    return centred * lax.rsqrt(variance + 1e-06)


def modulated(inputs, shift_part, scale_part):
    return norm_rows(inputs) * (1.0 + scale_part) + shift_part


def rotate(vectors, cosine, sine_part):
    half_size = vectors.shape[-1] // 2
    first_half = vectors[..., :half_size]
    second_half = vectors[..., half_size:]
    return jnp.concatenate(
        [
            first_half * cosine - second_half * sine_part,
            second_half * cosine + first_half * sine_part,
        ],
        axis=-1,
    )


def exact_dot(left_side, right_side):
    return jnp.dot(left_side, right_side, precision=HIGH_PRECISION)


def clip_index(positions, clip_ends):
    return jnp.sum((clip_ends[None, :] <= positions[:, None]).astype(jnp.int32), axis=1)


def attend_block(queries, key_rows, value_rows, visible, carry_state, scale):
    running_max, denominator, numerator = carry_state
    scores = (
        jnp.einsum("qhd,khd->hqk", queries, key_rows, preferred_element_type=jnp.float32) * scale
    )
    scores = jnp.where(visible[None], scores, NEGATIVE)
    new_max = jnp.maximum(running_max, jnp.max(scores, axis=-1))
    factor = jnp.exp(running_max - new_max)
    probabilities = jnp.where(visible[None], jnp.exp(scores - new_max[..., None]), 0.0)
    denominator = factor * denominator + jnp.sum(probabilities, axis=-1)
    numerator = numerator * jnp.transpose(factor)[:, :, None] + jnp.einsum(
        "hqk,khd->qhd",
        probabilities.astype(jnp.bfloat16),
        value_rows,
        preferred_element_type=jnp.float32,
    )
    return (new_max, denominator, numerator)


def grad_block(queries, upstream, log_total, row_delta, key_rows, value_rows, visible, scale):
    scores = (
        jnp.einsum("qhd,khd->hqk", queries, key_rows, preferred_element_type=jnp.float32) * scale
    )
    probabilities = jnp.where(
        visible[None],
        jnp.exp(jnp.where(visible[None], scores, NEGATIVE) - log_total[..., None]),
        0.0,
    )
    d_probs = jnp.einsum("qhd,khd->hqk", upstream, value_rows, preferred_element_type=jnp.float32)
    d_scores = (probabilities * (d_probs - row_delta[..., None])).astype(jnp.bfloat16)
    d_query = scale * jnp.einsum(
        "hqk,khd->qhd", d_scores, key_rows, preferred_element_type=jnp.float32
    )
    d_key = scale * jnp.einsum(
        "hqk,qhd->khd", d_scores, queries, preferred_element_type=jnp.float32
    )
    d_value = jnp.einsum(
        "hqk,qhd->khd",
        probabilities.astype(jnp.bfloat16),
        upstream,
        preferred_element_type=jnp.float32,
    )
    return (d_query, d_key, d_value)


def pass_key_grads(gradients):
    return (
        passed_along(gradients[0].astype(jnp.bfloat16), "blk", 1).astype(jnp.float32),
        passed_along(gradients[1].astype(jnp.bfloat16), "blk", 1).astype(jnp.float32),
    )


def body(
    frames,
    step_table,
    clip_lengths,
    clip_steps,
    w_mod,
    b_mod,
    w_qkv,
    b_qkv,
    w_out,
    b_out,
    w_up,
    b_up,
    w_down,
    b_down,
    cotangent,
):
    frame_count, model_width = frames.shape
    ffn_width = w_up.shape[1]
    cycle_size = lax.axis_size("blk")
    cycle_place = lax.axis_index("blk")
    head_count = HEADS
    head_size = model_width // head_count
    scale = head_size ** (-0.5)
    lengths = clip_lengths[0]
    steps = clip_steps[0]
    clip_count = lengths.shape[0]
    clip_ends = jnp.cumsum(lengths)
    clip_starts = clip_ends - lengths
    local_rows = jnp.arange(frame_count, dtype=jnp.int32)
    places = cycle_place * frame_count + local_rows
    clip_own = clip_index(places, clip_ends)
    member = (clip_own[:, None] == jnp.arange(clip_count, dtype=jnp.int32)[None, :]).astype(
        jnp.float32
    )
    offsets = jnp.sum(member * clip_starts[None, :].astype(jnp.float32), axis=1)
    freqs = 10000.0 ** (-2.0 * jnp.arange(head_size // 2, dtype=jnp.float32) / head_size)
    angles = (places.astype(jnp.float32) - offsets)[:, None] * freqs[None, :]
    cosine = jnp.cos(angles)[:, None, :]
    sine_part = jnp.sin(angles)[:, None, :]

    def clip_of(turn_index):
        source = (cycle_place - turn_index) % cycle_size
        return clip_index(source * frame_count + local_rows, clip_ends)

    step_pick = (
        steps[:, None] == jnp.arange(step_table.shape[0], dtype=jnp.int32)[None, :]
    ).astype(jnp.float32)
    condition = exact_dot(step_pick, step_table)
    silu_low = jax.nn.silu(condition).astype(jnp.bfloat16)
    modulation = jnp.dot(silu_low, w_mod, preferred_element_type=jnp.float32) + b_mod
    frame_mod = exact_dot(member, modulation)
    shift_one, scale_one, gate_one, shift_two, scale_two, gate_two = jnp.split(frame_mod, 6, axis=1)
    inputs = frames.astype(jnp.float32)
    first, first_back = jax.vjp(modulated, inputs, shift_one, scale_one)
    first_low = first.astype(jnp.bfloat16)
    projected = jnp.dot(first_low, w_qkv, preferred_element_type=jnp.float32) + b_qkv
    query_part, key_part, value_part = jnp.split(projected, 3, axis=1)

    def spin(query_lin, key_lin):
        return (
            rotate(query_lin.reshape(frame_count, head_count, head_size), cosine, sine_part),
            rotate(key_lin.reshape(frame_count, head_count, head_size), cosine, sine_part),
        )

    (query_rot, key_rot), spin_back = jax.vjp(spin, query_part, key_part)
    queries = query_rot.astype(jnp.bfloat16)
    key_rows = key_rot.astype(jnp.bfloat16)
    value_rows = value_part.reshape(frame_count, head_count, head_size).astype(jnp.bfloat16)

    def forward_step(turn_index, key_value, carry_state):
        visible = clip_own[:, None] == clip_of(turn_index)[None, :]
        return attend_block(queries, key_value[0], key_value[1], visible, carry_state, scale)

    def forward_turn(turn_index, carry):
        key_value, carry_state = carry
        carry_state = forward_step(turn_index, key_value, carry_state)
        key_value = passed_along((key_value[0], key_value[1]), "blk", 1)
        return (key_value, carry_state)

    initial = (
        jnp.full((head_count, frame_count), NEGATIVE, jnp.float32),
        jnp.zeros((head_count, frame_count), jnp.float32),
        jnp.zeros((frame_count, head_count, head_size), jnp.float32),
    )
    key_value, carry_state = lax.fori_loop(
        0, cycle_size - 1, forward_turn, ((key_rows, value_rows), initial)
    )
    running_max, denominator, numerator = forward_step(cycle_size - 1, key_value, carry_state)
    attended = numerator / jnp.transpose(denominator)[:, :, None]
    log_total = running_max + jnp.log(denominator)
    attended_low = attended.reshape(frame_count, model_width).astype(jnp.bfloat16)
    attn_out = jnp.dot(attended_low, w_out, preferred_element_type=jnp.float32) + b_out
    middle = inputs + gate_one * attn_out
    second, second_back = jax.vjp(modulated, middle, shift_two, scale_two)
    second_low = second.astype(jnp.bfloat16)
    hidden = jnp.dot(second_low, w_up, preferred_element_type=jnp.float32) + b_up
    activated, gelu_back = jax.vjp(
        lambda values_in: jax.nn.gelu(values_in, approximate=True), hidden
    )
    activated_low = activated.astype(jnp.bfloat16)
    ffn_out = jnp.dot(activated_low, w_down, preferred_element_type=jnp.float32) + b_down
    result = middle + gate_two * ffn_out
    upstream_y = cotangent.astype(jnp.float32)
    d_ffn = (gate_two * upstream_y).astype(jnp.bfloat16)
    d_gate_two = upstream_y * ffn_out
    d_act = jnp.dot(d_ffn, w_down.T, preferred_element_type=jnp.float32)
    d_hidden = gelu_back(d_act)[0].astype(jnp.bfloat16)
    d_second = jnp.dot(d_hidden, w_up.T, preferred_element_type=jnp.float32)
    d_middle_norm, d_shift_two, d_scale_two = second_back(d_second)
    d_middle = upstream_y + d_middle_norm
    d_attn = (gate_one * d_middle).astype(jnp.bfloat16)
    d_gate_one = d_middle * attn_out
    d_attended = jnp.dot(d_attn, w_out.T, preferred_element_type=jnp.float32).astype(jnp.bfloat16)
    d_attended = d_attended.reshape(frame_count, head_count, head_size)
    row_delta = jnp.transpose(jnp.sum(d_attended.astype(jnp.float32) * attended, axis=-1))
    zeros_three = jnp.zeros((frame_count, head_count, head_size), jnp.float32)

    def key_step(turn_index, key_value, owed):
        visible = clip_own[:, None] == clip_of(turn_index)[None, :]
        d_query, d_key, d_value = grad_block(
            queries, d_attended, log_total, row_delta, key_value[0], key_value[1], visible, scale
        )
        return (owed[0] + d_query, (owed[1][0] + d_key, owed[1][1] + d_value))

    def key_turn(turn_index, carry):
        key_value, owed = carry
        d_query_sum, gradients = key_step(turn_index, key_value, owed)
        key_value = passed_along((key_value[0], key_value[1]), "blk", 1)
        gradients = pass_key_grads(gradients)
        return (key_value, (d_query_sum, gradients))

    key_value, owed = lax.fori_loop(
        0,
        cycle_size - 1,
        key_turn,
        ((key_rows, value_rows), (zeros_three, (zeros_three, zeros_three))),
    )
    d_query_rot, gradients = key_step(cycle_size - 1, key_value, owed)
    d_key_rot, d_value_all = pass_key_grads(gradients)
    d_query_lin, d_key_lin = spin_back((d_query_rot, d_key_rot))
    d_projected = jnp.concatenate(
        [d_query_lin, d_key_lin, d_value_all.reshape(frame_count, model_width)], axis=1
    ).astype(jnp.bfloat16)
    d_first = jnp.dot(d_projected, w_qkv.T, preferred_element_type=jnp.float32)
    d_input_norm, d_shift_one, d_scale_one = first_back(d_first)
    d_inputs = d_middle + d_input_norm
    d_frame_mod = jnp.concatenate(
        [d_shift_one, d_scale_one, d_gate_one, d_shift_two, d_scale_two, d_gate_two], axis=1
    )
    d_modulation = exact_dot(member.T, d_frame_mod)
    d_silu = jnp.dot(d_modulation, w_mod.T, precision=HIGH_PRECISION)
    d_condition = jax.vjp(jax.nn.silu, condition)[1](d_silu)[0]
    d_table_local = exact_dot(step_pick.T, d_condition)
    small = lax.psum(
        (
            jnp.sum(d_modulation, axis=0),
            jnp.sum(d_projected.astype(jnp.float32), axis=0),
            jnp.sum(d_attn.astype(jnp.float32), axis=0),
            jnp.sum(d_hidden.astype(jnp.float32), axis=0),
            jnp.sum(d_ffn.astype(jnp.float32), axis=0),
            d_table_local,
        ),
        ("batch", "blk"),
    )
    d_b_mod, d_b_qkv, d_b_out, d_b_up, d_b_down, d_table = small
    blocks_list = [
        jnp.dot(first_low.T, d_projected, preferred_element_type=jnp.float32),
        jnp.dot(attended_low.T, d_attn, preferred_element_type=jnp.float32),
        jnp.dot(second_low.T, d_hidden, preferred_element_type=jnp.float32),
    ]
    blocks_list.append(exact_dot(silu_low.T.astype(jnp.float32), d_modulation))
    wide_rows = lax.psum_scatter(
        jnp.concatenate(blocks_list, axis=1), "blk", scatter_dimension=0, tiled=True
    )
    down_part = lax.psum_scatter(
        jnp.dot(activated_low.T, d_ffn, preferred_element_type=jnp.float32),
        "blk",
        scatter_dimension=0,
        tiled=True,
    )
    wide_rows, down_part = (
        lax.psum(wide_rows.astype(jnp.bfloat16), "batch").astype(jnp.float32),
        lax.psum(down_part.astype(jnp.bfloat16), "batch").astype(jnp.float32),
    )
    qkv_end = 3 * model_width
    out_end = qkv_end + model_width
    up_end = out_end + ffn_width
    return (
        result.astype(jnp.bfloat16),
        d_inputs.astype(jnp.bfloat16),
        d_table,
        wide_rows[:, up_end:],
        d_b_mod,
        wide_rows[:, :qkv_end],
        d_b_qkv,
        wide_rows[:, qkv_end:out_end],
        d_b_out,
        wide_rows[:, out_end:up_end],
        d_b_up,
        down_part,
        d_b_down,
    )


def solution(mesh):
    placed = (
        P(("batch", "blk"), None),
        P(),
        P("batch", None),
        P("batch", None),
        P(),
        P(),
        P(),
        P(),
        P(),
        P(),
        P(),
        P(),
        P(),
        P(),
        P(("batch", "blk"), None),
    )
    return jax.shard_map(
        body,
        mesh=mesh,
        in_specs=placed,
        out_specs=(
            P(("batch", "blk"), None),
            P(("batch", "blk"), None),
            P(),
            P("blk", None),
            P(),
            P("blk", None),
            P(),
            P("blk", None),
            P(),
            P("blk", None),
            P(),
            P("blk", None),
            P(),
        ),
        check_vma=False,
    )
```

profile of v0, /device:TPU:0, one launch (start us, length us, event | category | flops | bytes accessed | tf_op | source)
XLA Modules:
  0.0 1501.4 jit_solution(12611839306116647929)
XLA Ops:
  12.5 6.5 convolution_add_fusion
  31.3 106.8 %while.48 = (s32[]{:T(128)}, bf16[128,16,64]{0,2,1:T(8,128)(2,1)}, bf16[128,16,64]{0,2,1:T(8,128)(2,1)S(1)}, f32[16,128]{1,0:T(8,128)S(1)}, f32[16,128]{1,0:T(8,...) while((s32[]{:T(128)}, bf16[128,16,64]{0,2,1:T(8,128)(2,1)}, ...), condition=%wide.region_9.10_spmd.clone, body=%wide.region_5.9_spmd.clone.sunk | while | flops 69891600 | bytes 12520378 | solution.py:187
  32.5 3.0 collective-permute-start
  39.5 6.2 collective-permute-done
  45.7 4.7 collective-permute-done.1
  55.0 8.4 collective-permute-done
  63.4 3.8 collective-permute-done.1
  70.7 9.5 collective-permute-done
  80.2 2.8 collective-permute-done.1
  86.5 8.7 collective-permute-done
  95.2 2.7 collective-permute-done.1
  101.5 7.9 collective-permute-done
  109.3 2.7 collective-permute-done.1
  115.6 7.0 collective-permute-done
  128.8 6.6 collective-permute-done
  148.1 3.0 convert_reduce_fusion.3
  152.1 4.6 fusion.100
  156.8 4.4 multiply_reduce_fusion.1
  161.7 3.2 fusion.104
  169.8 237.2 %while.49 = (s32[]{:T(128)}, bf16[128,16,64]{0,2,1:T(8,128)(2,1)S(1)}, bf16[128,16,64]{0,2,1:T(8,128)(2,1)}, f32[128,16,64]{0,2,1:T(8,128)}, f32[128,16,64]{0,2,...) while((s32[]{:T(128)}, ...), condition=%wide.region_20.21_spmd.clone, body=%wide.region_18.20_spmd.clone.sunk | while | flops 171460112 | bytes 18140164 | solution.py:234
  177.0 34.1 %collective-permute-done.4 = bf16[128,16,64]{0,2,1:T(8,128)(2,1)} collective-permute-done((bf16[128,16,64]{0,2,1:T(8,128)(2,1)}, bf16[128,16,64]{0,2,1:T(8,128)(2,1)}, u32[]{:S(2)}, u32[]{:S(2)}) %collective-permute-start.4) | collective-permute-done | bytes 262176 | tf_op jit(solution)/shard_map/while/body/eval_jaxpr/ppermute | solution.py:15
  212.8 7.1 collective-permute-done.5
  228.2 3.6 collective-permute-start.5
  234.1 26.9 %collective-permute-done.4 = bf16[128,16,64]{0,2,1:T(8,128)(2,1)} collective-permute-done((bf16[128,16,64]{0,2,1:T(8,128)(2,1)}, bf16[128,16,64]{0,2,1:T(8,128)(2,1)}, u32[]{:S(2)}, u32[]{:S(2)}) %collective-permute-start.4) | collective-permute-done | bytes 262176 | tf_op jit(solution)/shard_map/while/body/eval_jaxpr/ppermute | solution.py:15
  262.8 7.1 collective-permute-done.5
  278.4 3.3 collective-permute-start.5
  283.9 13.7 collective-permute-done.4
  306.3 3.3 collective-permute-start.5
  312.0 11.8 collective-permute-done.4
  332.2 2.9 collective-permute-start.5
  337.4 17.8 %collective-permute-done.4 = bf16[128,16,64]{0,2,1:T(8,128)(2,1)} collective-permute-done((bf16[128,16,64]{0,2,1:T(8,128)(2,1)}, bf16[128,16,64]{0,2,1:T(8,128)(2,1)}, u32[]{:S(2)}, u32[]{:S(2)}) %collective-permute-start.4) | collective-permute-done | bytes 262176 | tf_op jit(solution)/shard_map/while/body/eval_jaxpr/ppermute | solution.py:15
  356.9 2.8 collective-permute-done.5
  370.1 8.9 collective-permute-done.4
  395.6 8.5 collective-permute-done.4
  411.7 2.8 fusion.113
  414.5 4.5 fusion.114
  419.3 4.1 collective-permute-done.6
  423.7 5.1 collective-permute-done.7
  428.8 3.5 constant_dynamic-update-slice_fusion.1
  436.4 6.4 fusion.98
  442.8 13.6 fusion.97
  456.3 33.5 %pad_maximum_fusion = f32[1024,12288]{1,0:T(8,128)} fusion(f32[1024,6144]{1,0:T(8,128)} %fusion.97, f32[1024,2048]{1,0:T(8,128)} %fusion.114, f32[1024,1024]{1,0:T(8,128)} %fusion.113, f32[1024,3072]{1,0:T(8,128)} %fusion.98), kind=kLoop, calls=%fused_computation.44 | loop fusion | flops 37748736 | bytes 100663296 | tf_op jit(solution)/shard_map/concatenate | solution.py:275
  492.1 790.1 %reduce-scatter.3.cloned.1.call-done = f32[128,12288]{1,0:T(8,128)} async-done(((f32[1024,12288]{1,0:T(8,128)}), f32[128,12288]{1,0:T(8,128)}) %reduce-scatter.3.cloned.1.call-update) | async-done | bytes 6291472 | tf_op jit(solution)/shard_map/reduce_scatter | solution.py:274
  1282.2 4.8 convert_element_type.233
  1287.1 12.7 fusion.112
  1301.2 41.8 %all-reduce.4 = (f32[6144]{0:T(1024)}, f32[3072]{0:T(1024)}, f32[1024]{0:T(1024)}, f32[2048]{0:T(1024)}, f32[1024]{0:T(1024)}) all-reduce(f32[6144]{0:T(1024)S(1)} %get-tuple-element.837, f32[3072]{0:T(1024)S(1)} %convert_reduce_fusion.2, f32[1024]{0:T(1024)S(1)} %copy-done.50, ...), channel_id=1, replica_groups=mesh['batch'=4,'blk'=8] {'batch','blk'}, use_global_device_ids=true, to_apply=%region_27.28 | all-reduce | flops 13312 | bytes 106496 | tf_op jit(solution)/shard_map/psum | solution.py:256
  1343.0 21.8 %all-reduce.11.cloned.1.call-done = (bf16[128,12288]{1,0:T(8,128)(2,1)}, bf16[256,1024]{1,0:T(8,128)(2,1)}) async-done(((bf16[128,12288]{1,0:T(8,128)(2,1)}, bf16[256,1024]{1,0:T(8,128)(2,1)}), (bf16[128,12288]{1,0:T(8,128)(2,1)}, bf16[256,1024]{1,0:T(8,128)(2,1)})) %all-reduce.11.cloned.1.call-update) | async-done | bytes 3670032 | tf_op jit(solution)/shard_map/psum | solution.py:284
  1373.2 120.1 %all-reduce.9.cloned.1.call-done = f32[32,1024]{1,0:T(8,128)} async-done(((f32[32,1024]{1,0:T(8,128)}), f32[32,1024]{1,0:T(8,128)}) %all-reduce.9.cloned.1.call-update) | async-done | bytes 131088 | tf_op jit(solution)/shard_map/psum | solution.py:256
  (495 shorter events, 172.6 us)
Async XLA Ops:
  7.2 482.8 %reduce-scatter.5.cloned.1.call-start = ((), (), s32[]{:S(2)}) async-start(), calls=%async_computation.4 | async-start | bytes 9437184 | tf_op jit(solution)/shard_map/reduce_scatter | solution.py:277
  32.5 13.2 collective-permute-start
  35.5 14.9 collective-permute-start.1
  51.4 12.0 collective-permute-start
  51.4 15.8 %collective-permute-start.1 = (bf16[128,16,64]{0,2,1:T(8,128)(2,1)S(1)}, bf16[128,16,64]{0,2,1:T(8,128)(2,1)S(1)}, u32[]{:S(2)}, u32[]{:S(2)}) collective-permute-start(bf16[128,16,64]{0,2,1:T(8,128)(2,1)S(1)} %copy.83), channel_id=1, source_target_pairs={{0,1},{1,2},{2,3},{3,4},{4,5},{5,6},{6,7},{7,0},{8,9},{9,10},{10,1... | collective-permute-start | bytes 786440 | tf_op jit(solution)/shard_map/while/body/eval_jaxpr/ppermute | solution.py:15
  68.1 12.0 collective-permute-start
  68.1 14.9 collective-permute-start.1
  84.0 11.3 collective-permute-start
  84.0 13.9 collective-permute-start.1
  98.9 10.4 collective-permute-start
  98.9 13.1 collective-permute-start.1
  113.0 9.6 collective-permute-start
  113.0 12.3 collective-permute-start.1
  126.3 9.2 collective-permute-start
  126.3 11.9 collective-permute-start.1
  156.7 1125.5 %reduce-scatter.3.cloned.1.call-start = ((), (), s32[]{:S(2)}) async-start(), calls=%async_computation.3 | async-start | bytes 56623104 | tf_op jit(solution)/shard_map/reduce_scatter | solution.py:274
  171.0 49.0 %collective-permute-start.3 = (bf16[128,16,64]{0,2,1:T(8,128)(2,1)S(1)}, bf16[128,16,64]{0,2,1:T(8,128)(2,1)}, u32[]{:S(2)}, u32[]{:S(2)}) collective-permute-start(bf16[128,16,64]{0,2,1:T(8,128)(2,1)S(1)} %copy.101), channel_id=1, source_target_pairs={{0,1},{1,2},{2,3},{3,4},{4,5},{5,6},{6,7},{7,0},{8,9},{9,10},{10,1... | collective-permute-start | bytes 786440 | tf_op jit(solution)/shard_map/while/body/eval_jaxpr/ppermute | solution.py:15
  171.0 49.0 %collective-permute-start.2 = (bf16[128,16,64]{0,2,1:T(8,128)(2,1)S(1)}, bf16[128,16,64]{0,2,1:T(8,128)(2,1)S(1)}, u32[]{:S(2)}, u32[]{:S(2)}) collective-permute-start(bf16[128,16,64]{0,2,1:T(8,128)(2,1)S(1)} %copy.100), channel_id=1, source_target_pairs={{0,1},{1,2},{2,3},{3,4},{4,5},{5,6},{6,7},{7,0},{8,9},{9,10},{10,1... | collective-permute-start | bytes 786440 | tf_op jit(solution)/shard_map/while/body/eval_jaxpr/ppermute | solution.py:15
  174.7 36.3 %collective-permute-start.4 = (bf16[128,16,64]{0,2,1:T(8,128)(2,1)}, bf16[128,16,64]{0,2,1:T(8,128)(2,1)}, u32[]{:S(2)}, u32[]{:S(2)}) collective-permute-start(bf16[128,16,64]{0,2,1:T(8,128)(2,1)} %fusion.209), channel_id=1, source_target_pairs={{0,1},{1,2},{2,3},{3,4},{4,5},{5,6},{6,7},{7,0},{8,9},{9,10},{10,1... | collective-permute-start | bytes 786440 | tf_op jit(solution)/shard_map/while/body/eval_jaxpr/ppermute | solution.py:15
  175.7 44.2 %collective-permute-start.5 = (bf16[128,16,64]{0,2,1:T(8,128)(2,1)}, bf16[128,16,64]{0,2,1:T(8,128)(2,1)S(1)}, u32[]{:S(2)}, u32[]{:S(2)}) collective-permute-start(bf16[128,16,64]{0,2,1:T(8,128)(2,1)} %fusion.210), channel_id=1, source_target_pairs={{0,1},{1,2},{2,3},{3,4},{4,5},{5,6},{6,7},{7,0},{8,9},{9,10},{10,1... | collective-permute-start | bytes 786440 | tf_op jit(solution)/shard_map/while/body/eval_jaxpr/ppermute | solution.py:15
  221.0 49.0 %collective-permute-start.3 = (bf16[128,16,64]{0,2,1:T(8,128)(2,1)S(1)}, bf16[128,16,64]{0,2,1:T(8,128)(2,1)}, u32[]{:S(2)}, u32[]{:S(2)}) collective-permute-start(bf16[128,16,64]{0,2,1:T(8,128)(2,1)S(1)} %copy.101), channel_id=1, source_target_pairs={{0,1},{1,2},{2,3},{3,4},{4,5},{5,6},{6,7},{7,0},{8,9},{9,10},{10,1... | collective-permute-start | bytes 786440 | tf_op jit(solution)/shard_map/while/body/eval_jaxpr/ppermute | solution.py:15
  221.0 49.0 %collective-permute-start.2 = (bf16[128,16,64]{0,2,1:T(8,128)(2,1)S(1)}, bf16[128,16,64]{0,2,1:T(8,128)(2,1)S(1)}, u32[]{:S(2)}, u32[]{:S(2)}) collective-permute-start(bf16[128,16,64]{0,2,1:T(8,128)(2,1)S(1)} %copy.100), channel_id=1, source_target_pairs={{0,1},{1,2},{2,3},{3,4},{4,5},{5,6},{6,7},{7,0},{8,9},{9,10},{10,1... | collective-permute-start | bytes 786440 | tf_op jit(solution)/shard_map/while/body/eval_jaxpr/ppermute | solution.py:15
  224.7 36.3 %collective-permute-start.4 = (bf16[128,16,64]{0,2,1:T(8,128)(2,1)}, bf16[128,16,64]{0,2,1:T(8,128)(2,1)}, u32[]{:S(2)}, u32[]{:S(2)}) collective-permute-start(bf16[128,16,64]{0,2,1:T(8,128)(2,1)} %fusion.209), channel_id=1, source_target_pairs={{0,1},{1,2},{2,3},{3,4},{4,5},{5,6},{6,7},{7,0},{8,9},{9,10},{10,1... | collective-permute-start | bytes 786440 | tf_op jit(solution)/shard_map/while/body/eval_jaxpr/ppermute | solution.py:15
  228.2 41.8 %collective-permute-start.5 = (bf16[128,16,64]{0,2,1:T(8,128)(2,1)}, bf16[128,16,64]{0,2,1:T(8,128)(2,1)S(1)}, u32[]{:S(2)}, u32[]{:S(2)}) collective-permute-start(bf16[128,16,64]{0,2,1:T(8,128)(2,1)} %fusion.210), channel_id=1, source_target_pairs={{0,1},{1,2},{2,3},{3,4},{4,5},{5,6},{6,7},{7,0},{8,9},{9,10},{10,1... | collective-permute-start | bytes 786440 | tf_op jit(solution)/shard_map/while/body/eval_jaxpr/ppermute | solution.py:15
  271.0 29.4 %collective-permute-start.3 = (bf16[128,16,64]{0,2,1:T(8,128)(2,1)S(1)}, bf16[128,16,64]{0,2,1:T(8,128)(2,1)}, u32[]{:S(2)}, u32[]{:S(2)}) collective-permute-start(bf16[128,16,64]{0,2,1:T(8,128)(2,1)S(1)} %copy.101), channel_id=1, source_target_pairs={{0,1},{1,2},{2,3},{3,4},{4,5},{5,6},{6,7},{7,0},{8,9},{9,10},{10,1... | collective-permute-start | bytes 786440 | tf_op jit(solution)/shard_map/while/body/eval_jaxpr/ppermute | solution.py:15
  271.0 29.4 %collective-permute-start.2 = (bf16[128,16,64]{0,2,1:T(8,128)(2,1)S(1)}, bf16[128,16,64]{0,2,1:T(8,128)(2,1)S(1)}, u32[]{:S(2)}, u32[]{:S(2)}) collective-permute-start(bf16[128,16,64]{0,2,1:T(8,128)(2,1)S(1)} %copy.100), channel_id=1, source_target_pairs={{0,1},{1,2},{2,3},{3,4},{4,5},{5,6},{6,7},{7,0},{8,9},{9,10},{10,1... | collective-permute-start | bytes 786440 | tf_op jit(solution)/shard_map/while/body/eval_jaxpr/ppermute | solution.py:15
  274.7 22.9 %collective-permute-start.4 = (bf16[128,16,64]{0,2,1:T(8,128)(2,1)}, bf16[128,16,64]{0,2,1:T(8,128)(2,1)}, u32[]{:S(2)}, u32[]{:S(2)}) collective-permute-start(bf16[128,16,64]{0,2,1:T(8,128)(2,1)} %fusion.209), channel_id=1, source_target_pairs={{0,1},{1,2},{2,3},{3,4},{4,5},{5,6},{6,7},{7,0},{8,9},{9,10},{10,1... | collective-permute-start | bytes 786440 | tf_op jit(solution)/shard_map/while/body/eval_jaxpr/ppermute | solution.py:15
  278.4 22.0 %collective-permute-start.5 = (bf16[128,16,64]{0,2,1:T(8,128)(2,1)}, bf16[128,16,64]{0,2,1:T(8,128)(2,1)S(1)}, u32[]{:S(2)}, u32[]{:S(2)}) collective-permute-start(bf16[128,16,64]{0,2,1:T(8,128)(2,1)} %fusion.210), channel_id=1, source_target_pairs={{0,1},{1,2},{2,3},{3,4},{4,5},{5,6},{6,7},{7,0},{8,9},{9,10},{10,1... | collective-permute-start | bytes 786440 | tf_op jit(solution)/shard_map/while/body/eval_jaxpr/ppermute | solution.py:15
  301.4 25.1 %collective-permute-start.3 = (bf16[128,16,64]{0,2,1:T(8,128)(2,1)S(1)}, bf16[128,16,64]{0,2,1:T(8,128)(2,1)}, u32[]{:S(2)}, u32[]{:S(2)}) collective-permute-start(bf16[128,16,64]{0,2,1:T(8,128)(2,1)S(1)} %copy.101), channel_id=1, source_target_pairs={{0,1},{1,2},{2,3},{3,4},{4,5},{5,6},{6,7},{7,0},{8,9},{9,10},{10,1... | collective-permute-start | bytes 786440 | tf_op jit(solution)/shard_map/while/body/eval_jaxpr/ppermute | solution.py:15
  301.4 25.1 %collective-permute-start.2 = (bf16[128,16,64]{0,2,1:T(8,128)(2,1)S(1)}, bf16[128,16,64]{0,2,1:T(8,128)(2,1)S(1)}, u32[]{:S(2)}, u32[]{:S(2)}) collective-permute-start(bf16[128,16,64]{0,2,1:T(8,128)(2,1)S(1)} %copy.100), channel_id=1, source_target_pairs={{0,1},{1,2},{2,3},{3,4},{4,5},{5,6},{6,7},{7,0},{8,9},{9,10},{10,1... | collective-permute-start | bytes 786440 | tf_op jit(solution)/shard_map/while/body/eval_jaxpr/ppermute | solution.py:15
  305.2 18.6 %collective-permute-start.4 = (bf16[128,16,64]{0,2,1:T(8,128)(2,1)}, bf16[128,16,64]{0,2,1:T(8,128)(2,1)}, u32[]{:S(2)}, u32[]{:S(2)}) collective-permute-start(bf16[128,16,64]{0,2,1:T(8,128)(2,1)} %fusion.209), channel_id=1, source_target_pairs={{0,1},{1,2},{2,3},{3,4},{4,5},{5,6},{6,7},{7,0},{8,9},{9,10},{10,1... | collective-permute-start | bytes 786440 | tf_op jit(solution)/shard_map/while/body/eval_jaxpr/ppermute | solution.py:15
  306.3 20.1 %collective-permute-start.5 = (bf16[128,16,64]{0,2,1:T(8,128)(2,1)}, bf16[128,16,64]{0,2,1:T(8,128)(2,1)S(1)}, u32[]{:S(2)}, u32[]{:S(2)}) collective-permute-start(bf16[128,16,64]{0,2,1:T(8,128)(2,1)} %fusion.210), channel_id=1, source_target_pairs={{0,1},{1,2},{2,3},{3,4},{4,5},{5,6},{6,7},{7,0},{8,9},{9,10},{10,1... | collective-permute-start | bytes 786440 | tf_op jit(solution)/shard_map/while/body/eval_jaxpr/ppermute | solution.py:15
  327.5 32.3 %collective-permute-start.3 = (bf16[128,16,64]{0,2,1:T(8,128)(2,1)S(1)}, bf16[128,16,64]{0,2,1:T(8,128)(2,1)}, u32[]{:S(2)}, u32[]{:S(2)}) collective-permute-start(bf16[128,16,64]{0,2,1:T(8,128)(2,1)S(1)} %copy.101), channel_id=1, source_target_pairs={{0,1},{1,2},{2,3},{3,4},{4,5},{5,6},{6,7},{7,0},{8,9},{9,10},{10,1... | collective-permute-start | bytes 786440 | tf_op jit(solution)/shard_map/while/body/eval_jaxpr/ppermute | solution.py:15
  327.5 32.3 %collective-permute-start.2 = (bf16[128,16,64]{0,2,1:T(8,128)(2,1)S(1)}, bf16[128,16,64]{0,2,1:T(8,128)(2,1)S(1)}, u32[]{:S(2)}, u32[]{:S(2)}) collective-permute-start(bf16[128,16,64]{0,2,1:T(8,128)(2,1)S(1)} %copy.100), channel_id=1, source_target_pairs={{0,1},{1,2},{2,3},{3,4},{4,5},{5,6},{6,7},{7,0},{8,9},{9,10},{10,1... | collective-permute-start | bytes 786440 | tf_op jit(solution)/shard_map/while/body/eval_jaxpr/ppermute | solution.py:15
  331.2 23.9 %collective-permute-start.4 = (bf16[128,16,64]{0,2,1:T(8,128)(2,1)}, bf16[128,16,64]{0,2,1:T(8,128)(2,1)}, u32[]{:S(2)}, u32[]{:S(2)}) collective-permute-start(bf16[128,16,64]{0,2,1:T(8,128)(2,1)} %fusion.209), channel_id=1, source_target_pairs={{0,1},{1,2},{2,3},{3,4},{4,5},{5,6},{6,7},{7,0},{8,9},{9,10},{10,1... | collective-permute-start | bytes 786440 | tf_op jit(solution)/shard_map/while/body/eval_jaxpr/ppermute | solution.py:15
  332.2 27.5 %collective-permute-start.5 = (bf16[128,16,64]{0,2,1:T(8,128)(2,1)}, bf16[128,16,64]{0,2,1:T(8,128)(2,1)S(1)}, u32[]{:S(2)}, u32[]{:S(2)}) collective-permute-start(bf16[128,16,64]{0,2,1:T(8,128)(2,1)} %fusion.210), channel_id=1, source_target_pairs={{0,1},{1,2},{2,3},{3,4},{4,5},{5,6},{6,7},{7,0},{8,9},{9,10},{10,1... | collective-permute-start | bytes 786440 | tf_op jit(solution)/shard_map/while/body/eval_jaxpr/ppermute | solution.py:15
  360.7 22.3 %collective-permute-start.3 = (bf16[128,16,64]{0,2,1:T(8,128)(2,1)S(1)}, bf16[128,16,64]{0,2,1:T(8,128)(2,1)}, u32[]{:S(2)}, u32[]{:S(2)}) collective-permute-start(bf16[128,16,64]{0,2,1:T(8,128)(2,1)S(1)} %copy.101), channel_id=1, source_target_pairs={{0,1},{1,2},{2,3},{3,4},{4,5},{5,6},{6,7},{7,0},{8,9},{9,10},{10,1... | collective-permute-start | bytes 786440 | tf_op jit(solution)/shard_map/while/body/eval_jaxpr/ppermute | solution.py:15
  363.1 20.0 %collective-permute-start.2 = (bf16[128,16,64]{0,2,1:T(8,128)(2,1)S(1)}, bf16[128,16,64]{0,2,1:T(8,128)(2,1)S(1)}, u32[]{:S(2)}, u32[]{:S(2)}) collective-permute-start(bf16[128,16,64]{0,2,1:T(8,128)(2,1)S(1)} %copy.100), channel_id=1, source_target_pairs={{0,1},{1,2},{2,3},{3,4},{4,5},{5,6},{6,7},{7,0},{8,9},{9,10},{10,1... | collective-permute-start | bytes 786440 | tf_op jit(solution)/shard_map/while/body/eval_jaxpr/ppermute | solution.py:15
  366.8 12.2 collective-permute-start.4
  367.8 15.2 %collective-permute-start.5 = (bf16[128,16,64]{0,2,1:T(8,128)(2,1)}, bf16[128,16,64]{0,2,1:T(8,128)(2,1)S(1)}, u32[]{:S(2)}, u32[]{:S(2)}) collective-permute-start(bf16[128,16,64]{0,2,1:T(8,128)(2,1)} %fusion.210), channel_id=1, source_target_pairs={{0,1},{1,2},{2,3},{3,4},{4,5},{5,6},{6,7},{7,0},{8,9},{9,10},{10,1... | collective-permute-start | bytes 786440 | tf_op jit(solution)/shard_map/while/body/eval_jaxpr/ppermute | solution.py:15
  384.1 22.9 %collective-permute-start.3 = (bf16[128,16,64]{0,2,1:T(8,128)(2,1)S(1)}, bf16[128,16,64]{0,2,1:T(8,128)(2,1)}, u32[]{:S(2)}, u32[]{:S(2)}) collective-permute-start(bf16[128,16,64]{0,2,1:T(8,128)(2,1)S(1)} %copy.101), channel_id=1, source_target_pairs={{0,1},{1,2},{2,3},{3,4},{4,5},{5,6},{6,7},{7,0},{8,9},{9,10},{10,1... | collective-permute-start | bytes 786440 | tf_op jit(solution)/shard_map/while/body/eval_jaxpr/ppermute | solution.py:15
  386.5 20.5 %collective-permute-start.2 = (bf16[128,16,64]{0,2,1:T(8,128)(2,1)S(1)}, bf16[128,16,64]{0,2,1:T(8,128)(2,1)S(1)}, u32[]{:S(2)}, u32[]{:S(2)}) collective-permute-start(bf16[128,16,64]{0,2,1:T(8,128)(2,1)S(1)} %copy.100), channel_id=1, source_target_pairs={{0,1},{1,2},{2,3},{3,4},{4,5},{5,6},{6,7},{7,0},{8,9},{9,10},{10,1... | collective-permute-start | bytes 786440 | tf_op jit(solution)/shard_map/while/body/eval_jaxpr/ppermute | solution.py:15
  390.2 14.0 collective-permute-start.4
  391.1 15.7 %collective-permute-start.5 = (bf16[128,16,64]{0,2,1:T(8,128)(2,1)}, bf16[128,16,64]{0,2,1:T(8,128)(2,1)S(1)}, u32[]{:S(2)}, u32[]{:S(2)}) collective-permute-start(bf16[128,16,64]{0,2,1:T(8,128)(2,1)} %fusion.210), channel_id=1, source_target_pairs={{0,1},{1,2},{2,3},{3,4},{4,5},{5,6},{6,7},{7,0},{8,9},{9,10},{10,1... | collective-permute-start | bytes 786440 | tf_op jit(solution)/shard_map/while/body/eval_jaxpr/ppermute | solution.py:15
  410.3 13.1 collective-permute-start.6
  410.8 17.9 %collective-permute-start.7 = (bf16[128,16,64]{0,2,1:T(8,128)(2,1)S(1)}, bf16[128,16,64]{0,2,1:T(8,128)(2,1)S(1)}, u32[]{:S(2)}, u32[]{:S(2)}) collective-permute-start(bf16[128,16,64]{0,2,1:T(8,128)(2,1)S(1)} %fusion.44), channel_id=1, source_target_pairs={{0,1},{1,2},{2,3},{3,4},{4,5},{5,6},{6,7},{7,0},{8,9},{9,10},{10,1... | collective-permute-start | bytes 786440 | tf_op jit(solution)/shard_map/ppermute | solution.py:15
  489.9 874.9 %all-reduce.11.cloned.1.call-start = ((), (), s32[]{:S(2)}) async-start(), calls=%async_computation.5 | async-start | bytes 7340032 | tf_op jit(solution)/shard_map/psum | solution.py:284
  1287.1 206.2 %all-reduce.9.cloned.1.call-start = ((), (), s32[]{:S(2)}) async-start(), calls=%async_computation.2 | async-start | bytes 262144 | tf_op jit(solution)/shard_map/psum | solution.py:256
  (94 other events, 744.6 us)
Sparse Core Ops, SparseCore 0:
  156.8 301.3 reduce-scatter.4
  490.0 792.1 reduce-scatter.2
  1287.2 77.5 all-reduce.10
  1370.8 122.5 all-reduce.8
where the time goes:
time: 1500 us
  waiting for transfers between devices  1160 us (77%)
  matrix products  128 us (9%)
  other arithmetic  87 us (6%)
  blocking collectives  41.8 us (3%)
  local copies, waits for them, and re-layouts  33.9 us (2%)
  starting transfers between devices  33.1 us (2%)
    reduce_scatter x1, waiting for transfers between devices, body(): lax.psum_scatter(jnp.concatenate(blocks_list, axis=1), 'blk', scatter_dim...  790 us
    ppermute x44, waiting for transfers between devices, passed_along(): lax.ppermute(value, axis, [(i, (i + by) % size) for i in range(size)])  229 us
    psum x1, waiting for transfers between devices, body(): lax.psum((jnp.sum(d_modulation, axis=0), jnp.sum(d_projected.astype(jnp.f...  120 us
    psum x1, blocking collectives, body(): lax.psum((jnp.sum(d_modulation, axis=0), jnp.sum(d_projected.astype(jnp.f...  41.8 us
    concatenate x1, other arithmetic, body(): jnp.concatenate(blocks_list, axis=1)  33.5 us
    ppermute x44, starting transfers between devices, passed_along(): lax.ppermute(value, axis, [(i, (i + by) % size) for i in range(size)])  32.9 us
  transfers between devices with their start and end apart: 48, of which 33 were waited for; matrix products, arithmetic and copies ran while one was open for 13% of the time, Pallas kernels for 0%

commit v1 on v0

--- a/solution.py
+++ b/solution.py
@@ -1,6 +1,8 @@
 import jax
 import jax.numpy as jnp
 from jax import lax
+from jax.experimental import pallas as pl
+from jax.experimental.pallas import tpu as pltpu
 from jax.sharding import PartitionSpec as P
 
 HEADS = 16
@@ -99,7 +101,7 @@
     )
 
 
-def body(
+def ring_body(
     frames,
     step_table,
     clip_lengths,
@@ -304,7 +306,1132 @@
     )
 
 
+BF = jnp.bfloat16
+F32 = jnp.float32
+LANES = 128
+MIB = 1024 * 1024
+
+
+def swapped_with(value, axis, offset):
+    size = lax.axis_size(axis)
+    return lax.ppermute(value, axis, [(i, i ^ offset) for i in range(size)])
+
+
+def even_blocks(value, count):
+    return [value] + [swapped_with(value, "blk", k) for k in range(2, count, 2)]
+
+
+def gathered_blocks(value, count):
+    evens = even_blocks(value, count)
+    return evens, [swapped_with(e, "blk", 1) for e in evens]
+
+
+def offset_of(index, count):
+    return (2 * index) % count + (2 * index) // count
+
+
+def after(value, *others):
+    return lax.optimization_barrier((value,) + others)[0]
+
+
+def half_swap(value, lane):
+    return jnp.where((lane % 64) < 32, pltpu.roll(value, 96, 1), pltpu.roll(value, 32, 1))
+
+
+def by_clip(clip, table, first, count):
+    chosen = table[first : first + 1, :]
+    for c in range(1, count):
+        chosen = jnp.where(clip == c, table[first + c : first + c + 1, :], chosen)
+    return chosen
+
+
+def full(shape):
+    return pl.BlockSpec(shape, lambda *_: (0,) * len(shape))
+
+
+ANYWHERE = pl.BlockSpec(memory_space=pl.ANY)
+SCALARS = pl.BlockSpec(memory_space=pltpu.SMEM)
+
+
+KEPT = pl.BlockSpec(memory_space=pltpu.VMEM)
+
+
+def in_hbm(value):
+    return pltpu.with_memory_space_constraint(value, pltpu.HBM)
+
+
+def all_in_hbm(values):
+    return [in_hbm(v) for v in values]
+
+
+def shape_of(shape, dtype=BF):
+    return pltpu.HBM(shape, dtype)
+
+
+def params(mib=24):
+    return pltpu.CompilerParams(vmem_limit_bytes=mib * MIB)
+
+
+def cost(flops, moved):
+    return pl.CostEstimate(flops=flops, bytes_accessed=moved, transcendentals=0)
+
+
+def prepare_kernel(
+    count, me_ref, lengths_ref, steps_ref, table_ref, freq_ref, w_ref, b_ref, later_ref, *refs
+):
+    silu, sems = refs[-2:]
+    kept = (len(refs) - 10) // 2
+    sources, targets = refs[:kept], refs[-2 - kept : -2]
+    out_ref, silu_ref, clip_ref, cliprow_ref, cos_ref, sin_ref, marks_ref, passed_ref = refs[
+        kept : kept + 8
+    ]
+    clips = lengths_ref.shape[1]
+    rows = cos_ref.shape[0] // count
+    i = pl.program_id(0)
+
+    def copies():
+        return [
+            pltpu.make_async_copy(
+                source.at[:, pl.ds(0, target.shape[1])], target, sems.at[j]
+            )
+            for j, (source, target) in enumerate(zip(sources, targets))
+        ]
+
+    @pl.when(i == 0)
+    def _():
+        for copy in copies():
+            copy.start()
+        passed_ref[...] = later_ref[...]
+        for c in range(clips):
+            row = table_ref[pl.ds(steps_ref[0, c], 1), :]
+            silu[c : c + 1, :] = row / (1.0 + jnp.exp(-row))
+        silu_ref[...] = silu[:clips, :].astype(BF)
+
+    out_ref[...] = dot_low(silu[...].astype(BF), w_ref[...])[:clips] + b_ref[...]
+
+    @pl.when(i == 0)
+    def _():
+        def clip_and_start(places):
+            clip, start, end = jnp.zeros_like(places), jnp.zeros_like(places), 0
+            for c in range(clips):
+                end = end + lengths_ref[0, c]
+                clip = jnp.where(places >= end, c + 1, clip)
+                start = jnp.where(places >= end, end, start)
+            return clip, start
+
+        for j in range(count):
+            first = (me_ref[0] ^ offset_of(j, count)) * rows
+            here = slice(j * rows, (j + 1) * rows)
+            places = first + lax.broadcasted_iota(jnp.int32, (rows, LANES), 0)
+            lane = lax.broadcasted_iota(jnp.int32, (rows, LANES), 1)
+            clip, start = clip_and_start(places)
+            angles = (places - start).astype(F32) * freq_ref[...]
+            cos_ref[here, :] = jnp.cos(angles)
+            sine = jnp.sin(angles)
+            sin_ref[here, :] = jnp.where((lane % 64) < 32, -sine, sine)
+            clip_ref[here, :] = clip[:, :1]
+            places = first + lax.broadcasted_iota(jnp.int32, (1, rows), 1)
+            cliprow_ref[:, here] = clip_and_start(places)[0]
+            other = jnp.where((clip != lane) & (lane < clips), NEGATIVE, 0.0)
+            marks_ref[here, :LANES] = other.astype(BF)
+            marks_ref[here, LANES:] = jnp.where(clip == lane, 1.0, 0.0).astype(BF)
+
+    @pl.when(i == pl.num_programs(0) - 1)
+    def _():
+        for copy in copies():
+            copy.wait()
+
+
+def prepare(me, lengths, steps, step_table, freqs, w_mod, b_mod, later, weights, own_rows, count):
+    width = w_mod.shape[0]
+    clips = lengths.shape[1]
+    tile = width
+    rows = own_rows * count
+    shapes = [
+        shape_of((clips, 2 * width), F32),
+        shape_of((clips, width)),
+        shape_of((rows, 1), jnp.int32),
+        shape_of((1, rows), jnp.int32),
+        shape_of((rows, LANES), F32),
+        shape_of((rows, LANES), F32),
+        shape_of((rows, 2 * LANES)),
+        shape_of(later.shape, later.dtype),
+    ]
+    return pl.pallas_call(
+        lambda *refs: prepare_kernel(count, *refs),
+        grid=(2,),
+        in_specs=[SCALARS] * 3
+        + [
+            full(step_table.shape),
+            full(freqs.shape),
+            pl.BlockSpec((width, tile), lambda i: (0, i)),
+            pl.BlockSpec((1, tile), lambda i: (0, i)),
+            full(later.shape),
+        ]
+        + [ANYWHERE] * len(weights),
+        out_specs=[pl.BlockSpec((clips, tile), lambda i: (0, i))]
+        + [full(v.shape) for v in shapes[1:]]
+        + [KEPT] * len(weights),
+        out_shape=shapes + [pltpu.VMEM(w.shape, w.dtype) for w in weights],
+        scratch_shapes=[pltpu.VMEM((8, width), F32), pltpu.SemaphoreType.DMA((len(weights),))],
+        compiler_params=params(),
+        cost_estimate=cost(4 * clips * width * width, 5 * width * width),
+    )(me, lengths, steps, *all_in_hbm([step_table, freqs, w_mod, b_mod, later, *weights]))
+
+
+def modulate_kernel(silu_ref, w_ref, b_ref, out_ref):
+    out_ref[...] = dot_low(silu_ref[...], w_ref[...]) + b_ref[...]
+
+
+def modulate(silu, w_mod, b_mod):
+    clips, width = silu.shape
+    return pl.pallas_call(
+        modulate_kernel,
+        grid=(4,),
+        in_specs=[
+            full(silu.shape),
+            pl.BlockSpec((width, width), lambda i: (0, 2 + i)),
+            pl.BlockSpec((1, width), lambda i: (0, 2 + i)),
+        ],
+        out_specs=pl.BlockSpec((clips, width), lambda i: (0, i)),
+        out_shape=shape_of((clips, 4 * width), F32),
+        compiler_params=params(),
+        cost_estimate=cost(8 * clips * width * width, 8 * width * width),
+    )(*all_in_hbm([silu, w_mod, b_mod]))
+
+
+def project_kernel(clips, with_own, me_ref, clip_ref, mod_ref, b_ref, cos_ref, sin_ref, w, *refs):
+    blocks = refs[: len(refs) - (4 if with_own else 3)]
+    h_ref, kv_ref, q_ref = refs[len(blocks) : len(blocks) + 3]
+    rows, width = blocks[0].shape
+    column = pl.multiple_of(me_ref[0] * LANES, LANES)
+    if with_own:
+        own_ref = refs[-1]
+
+    mod = mod_ref[...]
+    for pair in range(len(blocks) // 2):
+        here = slice(2 * pair * rows, 2 * (pair + 1) * rows)
+        x = jnp.concatenate([blocks[2 * pair][...], blocks[2 * pair + 1][...]], axis=0).astype(F32)
+        normed, _ = norm_parts(x)
+        clip = clip_ref[here, :]
+        scale = by_clip(clip, mod[:, width:], 0, clips)
+        h_ref[here, :] = (normed * (1.0 + scale) + by_clip(clip, mod[:, :width], 0, clips)).astype(BF)
+
+    h = h_ref[...]
+    cosine, sine = cos_ref[...], sin_ref[...]
+    lane = lax.broadcasted_iota(jnp.int32, cosine.shape, 1)
+
+    def turned(piece, some):
+        return piece * cosine[:some] + half_swap(piece, lane[:some]) * sine[:some]
+
+    part = dot_low(h, w[:, pl.ds(column, LANES)]) + b_ref[:, pl.ds(column, LANES)]
+    q_ref[...] = (turned(part, h.shape[0]) * 0.125).astype(BF)
+    step = 2 * LANES
+    for start in range(0 if with_own else width, 3 * width, step):
+        some = rows if start < width else h.shape[0]
+        part = dot_low(h[:some], w[:, start : start + step]) + b_ref[:, start : start + step]
+        for inner in range(0, step, LANES):
+            piece = part[:, inner : inner + LANES]
+            at = start + inner
+            if start < 2 * width:
+                piece = turned(piece, some)
+            if start < width:
+                own_ref[:, at : at + LANES] = (piece * 0.125).astype(BF)
+            else:
+                kv_ref[(at - width) // LANES] = piece.astype(BF)
+
+
+def project(half, blocks, me, clip_col, modulation, w_qkv, b_qkv, cosine, sine, with_own):
+    own_rows, width = blocks[0].shape
+    rows = own_rows * len(blocks)
+    clips = modulation.shape[0]
+    out_shape = [
+        shape_of((rows, width)),
+        pltpu.VMEM((2 * width // LANES, rows, LANES), BF),
+        shape_of((rows, LANES)),
+    ]
+    if with_own:
+        out_shape.append(shape_of((own_rows, width)))
+    return pl.pallas_call(
+        lambda *refs: project_kernel(clips, with_own, *refs),
+        grid=(1,),
+        in_specs=[
+            SCALARS,
+            pl.BlockSpec((rows, 1), lambda *_: (half, 0)),
+            pl.BlockSpec((clips, 2 * width), lambda *_: (0, 0)),
+            full(b_qkv.shape),
+            pl.BlockSpec((rows, LANES), lambda *_: (half, 0)),
+            pl.BlockSpec((rows, LANES), lambda *_: (half, 0)),
+            KEPT,
+        ]
+        + [full(v.shape) for v in blocks],
+        out_specs=[full(out_shape[0].shape), KEPT] + [full(o.shape) for o in out_shape[2:]],
+        out_shape=out_shape,
+        compiler_params=params(),
+        cost_estimate=cost(4 * rows * width * width, 6 * MIB),
+    )(me, *all_in_hbm([clip_col, modulation, b_qkv, cosine, sine]), w_qkv, *all_in_hbm(blocks))
+
+
+def contract_last(left, right):
+    return lax.dot_general(left, right, (((1,), (1,)), ((), ())), preferred_element_type=F32)
+
+
+def head_rows(value):
+    lane = lax.broadcasted_iota(jnp.int32, value.shape, 1)
+    zero = jnp.zeros_like(value)
+    return jnp.concatenate(
+        [jnp.where(lane < 64, value, zero), jnp.where(lane < 64, zero, value)], axis=0
+    )
+
+
+def head_diagonal(value):
+    rows = value.shape[1] // 2
+    return jnp.concatenate([value[:64, :rows], value[64:, rows:]], axis=0).T
+
+
+def softmax_over_keys(keys, queries):
+    scores = contract_last(keys, queries)
+    expo = jnp.exp(scores - jnp.max(scores, axis=0, keepdims=True))
+    return expo, 1.0 / jnp.sum(expo, axis=0, keepdims=True)
+
+
+def attend_kernel(keymark_ref, rowmark_ref, q_ref, ka_ref, kb_ref, o_ref, keys, values, queries):
+    half = ka_ref.shape[1]
+    pair, pairs = pl.program_id(0), pl.num_programs(0)
+
+    @pl.when(pair == 0)
+    def _():
+        keys[:, LANES:] = keymark_ref[...]
+        marks = rowmark_ref[...]
+        queries[:, LANES:] = jnp.concatenate([marks, marks], axis=0)
+
+    keys[:half, :LANES] = ka_ref[pair]
+    keys[half:, :LANES] = kb_ref[pair]
+    values[:half] = ka_ref[pairs + pair]
+    values[half:] = kb_ref[pairs + pair]
+    queries[:, :LANES] = head_rows(q_ref[...])
+    expo, inverse = softmax_over_keys(keys[...], queries[...])
+    turned = jnp.dot(values[...].T, expo.astype(BF), preferred_element_type=F32) * inverse
+    o_ref[...] = head_diagonal(turned).astype(BF)
+
+
+def attend(q, kv_a, kv_b, marks):
+    own_rows, width = q.shape
+    rows = 2 * kv_a.shape[1]
+    return pl.pallas_call(
+        attend_kernel,
+        grid=(width // LANES,),
+        in_specs=[
+            pl.BlockSpec((rows, LANES), lambda p: (0, 0)),
+            pl.BlockSpec((own_rows, LANES), lambda p: (0, 1)),
+            pl.BlockSpec((own_rows, LANES), lambda p: (0, p)),
+            KEPT,
+            KEPT,
+        ],
+        out_specs=pl.BlockSpec((own_rows, LANES), lambda p: (0, p)),
+        out_shape=shape_of((own_rows, width)),
+        scratch_shapes=[
+            pltpu.VMEM((rows, 2 * LANES), BF),
+            pltpu.VMEM((rows, LANES), BF),
+            pltpu.VMEM((2 * own_rows, 2 * LANES), BF),
+        ],
+        compiler_params=params(),
+        cost_estimate=cost(4 * own_rows * rows * width, MIB),
+    )(*all_in_hbm([marks, marks, q]), kv_a, kv_b)
+
+
+def probs_kernel(me_ref, keyclip_ref, rowclip_ref, qa_ref, qb_ref, ka_ref, kb_ref, *refs):
+    out_ref, keys = refs[-2:]
+    i, blocks = pl.program_id(0), pl.num_programs(0)
+    half = ka_ref.shape[1]
+
+    @pl.when(i == 0)
+    def _():
+        keys[:half] = ka_ref[me_ref[0]]
+        keys[half:] = kb_ref[me_ref[0]]
+
+    query = jnp.where(i < blocks // 2, qa_ref[...], qb_ref[...])
+    visible = keyclip_ref[...] == rowclip_ref[...]
+    visible = jnp.concatenate([visible, visible], axis=1)
+    scores = jnp.where(visible, contract_last(keys[...], head_rows(query)), NEGATIVE)
+    expo = jnp.exp(scores - jnp.max(scores, axis=0, keepdims=True))
+    out_ref[...] = expo * (1.0 / jnp.sum(expo, axis=0, keepdims=True))
+
+
+def heads_probs(me, q_a, q_b, kv_a, kv_b, clip_col, clip_row, blocks, earlier):
+    half = kv_a.shape[1]
+    rows = 2 * half
+    own_rows = rows // blocks
+    halfway = blocks // 2
+    grid_spec = pltpu.PrefetchScalarGridSpec(
+        num_scalar_prefetch=1,
+        grid=(blocks,),
+        in_specs=[
+            pl.BlockSpec((rows, 1), lambda i, m: (0, 0)),
+            pl.BlockSpec((1, own_rows), lambda i, m: (0, i)),
+            pl.BlockSpec((own_rows, LANES), lambda i, m: (jnp.minimum(i, halfway - 1), 0)),
+            pl.BlockSpec((own_rows, LANES), lambda i, m: (jnp.maximum(i - halfway, 0), 0)),
+            KEPT,
+            KEPT,
+        ]
+        + [ANYWHERE] * len(earlier),
+        out_specs=pl.BlockSpec((rows, 2 * own_rows), lambda i, m: (0, i)),
+        scratch_shapes=[pltpu.VMEM((rows, LANES), BF)],
+    )
+    return pl.pallas_call(
+        probs_kernel,
+        grid_spec=grid_spec,
+        out_shape=shape_of((rows, 2 * rows), F32),
+        compiler_params=params(),
+        cost_estimate=cost(4 * rows * rows * LANES, 9 * MIB),
+    )(me, *all_in_hbm([clip_col, clip_row, q_a, q_b]), kv_a, kv_b, *all_in_hbm(earlier))
+
+
+def attend_back_kernel(
+    me_ref, p_ref, qa_ref, qb_ref, ka_ref, kb_ref, do_ref, cos_ref, sin_ref, *refs
+):
+    out_ref, sent_ref = refs[-9:-7]
+    dk_ref, dv_ref, values, keys_turned, d_probs = refs[-5:]
+    i, blocks = pl.program_id(0), pl.num_programs(0)
+    rows = do_ref.shape[1]
+    half = ka_ref.shape[1]
+    me = me_ref[0]
+
+    @pl.when(i == 0)
+    def _():
+        dk_ref[...] = jnp.zeros_like(dk_ref)
+        dv_ref[...] = jnp.zeros_like(dv_ref)
+        for at, ref in ((0, ka_ref), (half, kb_ref)):
+            values[at : at + half] = ref[ref.shape[0] // 2 + me]
+            keys_turned[:, at : at + half] = ref[me].T
+
+    query = jnp.where(i < blocks // 2, qa_ref[...], qb_ref[...])
+    q_two, up_two = head_rows(query), head_rows(do_ref[0])
+    delta = jnp.zeros((1, 2 * rows), F32)
+    step = 256
+    for start in range(0, 2 * half, step):
+        part = slice(start, start + step)
+        probs_low = p_ref[part, :].astype(BF)
+        dv_ref[part, :] += dot_low(probs_low, up_two)
+        products = contract_last(values[part, :], up_two)
+        d_probs[part, :] = products
+        delta += jnp.sum(probs_low.astype(F32) * products, axis=0, keepdims=True)
+    d_query = jnp.zeros((LANES, 2 * rows), F32)
+    for start in range(0, 2 * half, step):
+        part = slice(start, start + step)
+        ds = (p_ref[part, :] * (d_probs[part, :] - delta)).astype(BF)
+        dk_ref[part, :] += dot_low(ds, q_two)
+        d_query += dot_low(keys_turned[:, part], ds)
+    lane = lax.broadcasted_iota(jnp.int32, (rows, LANES), 1)
+
+    def turned_back(value, where):
+        return (value * cos_ref[where, :] - half_swap(value, lane) * sin_ref[where, :]).astype(BF)
+
+    here = pl.ds(pl.multiple_of(i * rows, rows), rows)
+    dq = turned_back(head_diagonal(d_query) * 0.125, here)
+    out_ref[here, 0:LANES] = dq
+    sent_ref[me ^ offset_of(i, blocks), :, 0:LANES] = dq
+
+    @pl.when(i == blocks - 1)
+    def _():
+        @pl.loop(0, blocks)
+        def _(j):
+            there = pl.ds(pl.multiple_of(j * rows, rows), rows)
+            dk = turned_back(dk_ref[there, :], there)
+            dv = dv_ref[there, :].astype(BF)
+            out_ref[there, LANES : 2 * LANES] = dk
+            out_ref[there, 2 * LANES : 3 * LANES] = dv
+            owner = me ^ offset_of(j, blocks)
+            sent_ref[owner, :, LANES : 2 * LANES] = dk
+            sent_ref[owner, :, 2 * LANES : 3 * LANES] = dv
+
+
+def attend_back(me, probs, q_a, q_b, kv_a, kv_b, d_o, cosine, sine, passed, earlier):
+    half = kv_a.shape[1]
+    rows = 2 * half
+    blocks, own_rows, _ = d_o.shape
+    halfway = blocks // 2
+    grid_spec = pltpu.PrefetchScalarGridSpec(
+        num_scalar_prefetch=1,
+        grid=(blocks,),
+        in_specs=[
+            pl.BlockSpec((rows, 2 * own_rows), lambda i, m: (0, i)),
+            pl.BlockSpec((own_rows, LANES), lambda i, m: (jnp.minimum(i, halfway - 1), 0)),
+            pl.BlockSpec((own_rows, LANES), lambda i, m: (jnp.maximum(i - halfway, 0), 0)),
+            KEPT,
+            KEPT,
+            pl.BlockSpec((1, own_rows, LANES), lambda i, m: (m[0] ^ offset_of(i, blocks), 0, 0)),
+            pl.BlockSpec((rows, LANES), lambda i, m: (0, 0)),
+            pl.BlockSpec((rows, LANES), lambda i, m: (0, 0)),
+            ANYWHERE,
+            ANYWHERE,
+        ]
+        + [ANYWHERE] * len(earlier),
+        out_specs=[
+            pl.BlockSpec((rows, 3 * LANES), lambda i, m: (0, 0)),
+            pl.BlockSpec((blocks, own_rows, 3 * LANES), lambda i, m: (0, 0, 0)),
+            ANYWHERE,
+            ANYWHERE,
+        ],
+        scratch_shapes=[
+            pltpu.VMEM((rows, LANES), F32),
+            pltpu.VMEM((rows, LANES), F32),
+            pltpu.VMEM((rows, LANES), BF),
+            pltpu.VMEM((LANES, rows), BF),
+            pltpu.VMEM((rows, 2 * own_rows), F32),
+        ],
+    )
+    return pl.pallas_call(
+        attend_back_kernel,
+        grid_spec=grid_spec,
+        out_shape=[
+            shape_of((rows, 3 * LANES)),
+            shape_of((blocks, own_rows, 3 * LANES)),
+            shape_of(passed[0].shape, passed[0].dtype),
+            shape_of(passed[1].shape, passed[1].dtype),
+        ],
+        input_output_aliases={9: 2, 10: 3},
+        compiler_params=params(),
+        cost_estimate=cost(8 * rows * rows * LANES, 12 * MIB),
+    )(
+        me,
+        *all_in_hbm([probs, q_a, q_b]),
+        kv_a,
+        kv_b,
+        *all_in_hbm([d_o, cosine, sine, *passed, *earlier]),
+    )
+
+
+def norm_parts(inputs):
+    centred = inputs - jnp.mean(inputs, axis=-1, keepdims=True)
+    rstd = lax.rsqrt(jnp.mean(centred * centred, axis=-1, keepdims=True) + 1e-06)
+    return centred * rstd, rstd
+
+
+def norm_back(normed, rstd, gradient):
+    return rstd * (
+        gradient
+        - jnp.mean(gradient, axis=-1, keepdims=True)
+        - normed * jnp.mean(gradient * normed, axis=-1, keepdims=True)
+    )
+
+
+def dot_low(left, right):
+    return jnp.dot(left, right, preferred_element_type=F32)
+
+
+def dot_rows(left, right):
+    return lax.dot_general(left, right, (((0,), (0,)), ((), ())), preferred_element_type=F32)
+
+
+def gelu_parts(hidden):
+    square = hidden * hidden
+    tanh = jnp.tanh(0.7978845608028654 * hidden * (1.0 + 0.044715 * square))
+    upper = 0.5 * (1.0 + tanh)
+    slope = upper + 0.5 * hidden * (1.0 - tanh * tanh) * (
+        0.7978845608028654 * (1.0 + 3.0 * 0.044715 * square)
+    )
+    return hidden * upper, slope
+
+
+def high_low(value):
+    high = value.astype(BF)
+    return high, (value - high.astype(F32)).astype(BF)
+
+
+class RowSums:
+    def __init__(self, clip_row, clips):
+        self.place = lax.broadcasted_iota(jnp.int32, (8, clip_row.shape[1]), 0)
+        self.member = ((self.place == clip_row) & (self.place < clips)).astype(F32).astype(BF)
+
+    def by_clip(self, value):
+        high, low = high_low(value)
+        return dot_low(
+            jnp.concatenate([self.member, self.member], axis=1),
+            jnp.concatenate([high, low], axis=0),
+        )
+
+    def whole(self, value, row):
+        return dot_low((self.place == row).astype(F32).astype(BF), value)
+
+
+def middle_kernel(
+    clips, steps_ref, clipc_ref, clipr_ref, x_ref, dy_ref, o_ref, mod_ref, bo_ref, bu_ref, bd_ref,
+    wo_hbm, wu_hbm, wd_hbm, *refs,
+):
+    out_ref, h2_ref, dx_ref, da_ref, do_ref, sums_ref, wo, wu, wd, sems = refs[-10:]
+    copies = [
+        pltpu.make_async_copy(source, target, sems.at[i])
+        for i, (source, target) in enumerate([(wo_hbm, wo), (wu_hbm, wu), (wd_hbm, wd)])
+    ]
+    for copy in copies:
+        copy.start()
+    width = x_ref.shape[1]
+    ffn = wu.shape[1]
+    clip = clipc_ref[...]
+
+    def frame_rows(index):
+        return by_clip(clip, mod_ref[:, (index - 2) * width : (index - 1) * width], 0, clips)
+
+    gate_one, scale_two, gate_two = frame_rows(2), 1.0 + frame_rows(4), frame_rows(5)
+    upstream = dy_ref[...].astype(F32)
+    d_ffn = (gate_two * upstream).astype(BF)
+    copies[0].wait()
+    attn_out = dot_low(o_ref[...], wo[...]) + bo_ref[...]
+    middle = x_ref[...].astype(F32) + gate_one * attn_out
+    normed, rstd = norm_parts(middle)
+    second = (normed * scale_two + frame_rows(3)).astype(BF)
+    h2_ref[...] = second
+    copies[1].wait()
+    copies[2].wait()
+    sums = RowSums(clipr_ref[...], clips)
+    ffn_out = jnp.zeros(x_ref.shape, F32)
+    d_second = jnp.zeros(x_ref.shape, F32)
+    step = 512
+    up_sums = []
+    for start in range(0, ffn, step):
+        here = slice(start, start + step)
+        activated, slope = gelu_parts(dot_low(second, wu[:, here]) + bu_ref[:, here])
+        ffn_out += dot_low(activated.astype(BF), wd[here, :])
+        d_hidden = (contract_last(d_ffn, wd[here, :]) * slope).astype(BF)
+        d_second += contract_last(d_hidden, wu[:, here])
+        up_sums.append(sums.whole(d_hidden, clips))
+    ffn_out += bd_ref[...]
+    out_ref[...] = (middle + gate_two * ffn_out).astype(BF)
+    d_middle = upstream + norm_back(normed, rstd, d_second * scale_two)
+    dx_ref[...] = d_middle
+    d_attn = (gate_one * d_middle).astype(BF)
+    da_ref[...] = d_attn
+    d_o = contract_last(d_attn, wo[...]).astype(BF)
+    for k in range(width // LANES):
+        do_ref[k] = d_o[:, k * LANES : (k + 1) * LANES]
+    up_sums = jnp.concatenate(up_sums, axis=1)
+    place = lax.broadcasted_iota(jnp.int32, (8, width), 0)
+    lane = lax.broadcasted_iota(jnp.int32, (8, width), 1)
+    steps = jnp.zeros((8, width), F32)
+    for c in range(clips):
+        here = (place == clips + 1) & (lane == c)
+        steps = jnp.where(here, steps_ref[0, c].astype(F32), steps)
+    sums_ref[:, :width] = (
+        sums.by_clip(d_middle * attn_out) + sums.whole(d_attn, clips) + steps
+    )
+    sums_ref[:, width : 2 * width] = sums.by_clip(d_second) + up_sums[:, :width]
+    sums_ref[:, 2 * width : 3 * width] = sums.by_clip(d_second * normed) + up_sums[:, width:]
+    sums_ref[:, 3 * width :] = sums.by_clip(upstream * ffn_out) + sums.whole(d_ffn, clips)
+
+
+def middle_part(
+    steps, clip_col, clip_row, frames, cotangent, attended, modulation, b_out, b_up, b_down,
+    w_out, w_up, w_down, earlier,
+):
+    rows, width = frames.shape
+    clips = modulation.shape[0]
+    small = [
+        clip_col, clip_row, frames, cotangent, attended, modulation, b_out, b_up, b_down
+    ]
+    out_shape = [
+        shape_of((rows, width)),
+        shape_of((rows, width)),
+        shape_of((rows, width), F32),
+        shape_of((rows, width)),
+        shape_of((width // LANES, rows, LANES)),
+        shape_of((8, 4 * width), F32),
+    ]
+    return pl.pallas_call(
+        lambda *refs: middle_kernel(clips, *refs),
+        grid=(1,),
+        in_specs=[SCALARS, full((rows, 1)), full((1, rows))]
+        + [full(v.shape) for v in small[2:]]
+        + [ANYWHERE] * 3
+        + [ANYWHERE] * len(earlier),
+        out_specs=[full(o.shape) for o in out_shape],
+        out_shape=out_shape,
+        scratch_shapes=[
+            pltpu.VMEM(w_out.shape, BF),
+            pltpu.VMEM(w_up.shape, BF),
+            pltpu.VMEM(w_down.shape, BF),
+            pltpu.SemaphoreType.DMA((3,)),
+        ],
+        compiler_params=params(32),
+        cost_estimate=cost(20 * rows * width * width, 3 * MIB),
+    )(steps, *all_in_hbm([*small, w_out, w_up, w_down, *earlier]))
+
+
+def last_kernel(clips, clipc_ref, clipr_ref, x_ref, mod_ref, dx_ref, d_ref, w_hbm, *refs):
+    out_ref, sums_ref, d_all, w, sems = refs[-5:]
+    width = x_ref.shape[1]
+    parts = 3
+    copies = [
+        pltpu.make_async_copy(
+            w_hbm.at[:, pl.ds(i * width, width)], w.at[:, pl.ds(i * width, width)], sems.at[i]
+        )
+        for i in range(parts)
+    ]
+    for copy in copies:
+        copy.start()
+    for k in range(d_ref.shape[0]):
+        for i in range(3):
+            at = i * width + k * LANES
+            d_all[:, at : at + LANES] = d_ref[k, :, i * LANES : (i + 1) * LANES]
+    normed, rstd = norm_parts(x_ref[...].astype(F32))
+    scale = 1.0 + by_clip(clipc_ref[...], mod_ref[...], 0, clips)
+    d_first = jnp.zeros(x_ref.shape, F32)
+    for i in range(parts):
+        copies[i].wait()
+        here = slice(i * width, (i + 1) * width)
+        d_first += contract_last(d_all[:, here], w[:, here])
+    out_ref[...] = (dx_ref[...] + norm_back(normed, rstd, d_first * scale)).astype(BF)
+    sums = RowSums(clipr_ref[...], clips)
+    sums_ref[:, :width] = (
+        sums.by_clip(d_first)
+        + sums.whole(d_all[:, :width], clips)
+        + sums.whole(d_all[:, width : 2 * width], clips + 1)
+    )
+    sums_ref[:, width:] = sums.by_clip(d_first * normed) + sums.whole(d_all[:, 2 * width :], clips)
+
+
+def last_part(clip_col, clip_row, frames, modulation, d_middle, d_own, w_qkv, earlier):
+    rows, width = frames.shape
+    clips = modulation.shape[0]
+    return pl.pallas_call(
+        lambda *refs: last_kernel(clips, *refs),
+        grid=(1,),
+        in_specs=[
+            full((rows, 1)),
+            full((1, rows)),
+            full(frames.shape),
+            pl.BlockSpec((clips, width), lambda *_: (0, 1)),
+            full(d_middle.shape),
+            full(d_own.shape),
+        ]
+        + [ANYWHERE] * (1 + len(earlier)),
+        out_specs=[full((rows, width)), full((8, 2 * width))],
+        out_shape=[shape_of((rows, width)), shape_of((8, 2 * width), F32)],
+        scratch_shapes=[
+            pltpu.VMEM((rows, 3 * width), BF),
+            pltpu.VMEM(w_qkv.shape, BF),
+            pltpu.SemaphoreType.DMA((3,)),
+        ],
+        compiler_params=params(),
+        cost_estimate=cost(6 * rows * width * width, 2 * MIB),
+    )(
+        *all_in_hbm([clip_col, clip_row, frames, modulation, d_middle, d_own, w_qkv, *earlier]),
+    )
+
+
+def half_rows(core, value, kept_ref, sent_ref, at, columns):
+    half = value.shape[0] // 2
+    low, high = value[:half], value[half:]
+    here = slice(at, at + half)
+    kept_ref[here, columns] = jnp.where(core == 0, low, high)
+    sent_ref[here, columns] = jnp.where(core == 0, high, low).astype(BF)
+
+
+def weights_kernel(clips, count, who_ref, clip_ref, gate_ref, bu_ref, wu_hbm, wd_hbm, *refs):
+    kept_ref, sent_ref, up_sum, down_sum, wu, wd, sems = refs[-7:]
+    ha_ref, hb_ref, d_ref = refs[:3]
+    blocks = refs[3 : 3 + count]
+    seconds, upstreams = blocks[: len(blocks) // 2], blocks[len(blocks) // 2 :]
+    me, core = who_ref[0], who_ref[1]
+    rows, width = seconds[0].shape
+    part = up_sum.shape[1]
+    columns = d_ref.shape[1]
+    half = ha_ref.shape[0]
+    own = pl.ds(pl.multiple_of((me // 2) * part, part), part)
+    copies = [
+        pltpu.make_async_copy(wu_hbm.at[:, own], wu, sems.at[0]),
+        pltpu.make_async_copy(wd_hbm.at[own, :], wd, sems.at[1]),
+    ]
+    for copy in copies:
+        copy.start()
+    shard = part // 2
+
+    step = 2 * LANES
+    for start in range(0, width, step):
+        here = slice(start, start + step)
+        value = dot_rows(ha_ref[:, here], d_ref[:half, :])
+        value += dot_rows(hb_ref[:, here], d_ref[half:, :])
+        for inner in range(0, step, LANES):
+            half_rows(
+                core, value[inner : inner + LANES], kept_ref, sent_ref, (start + inner) // 2,
+                slice(0, columns),
+            )
+
+    for copy in copies:
+        copy.wait()
+    up_weights, down_weights = wu[...], wd[...]
+    for pair in range(len(seconds) // 2):
+        here = slice(2 * pair * rows, 2 * (pair + 1) * rows)
+        second = jnp.concatenate([r[...] for r in seconds[2 * pair : 2 * pair + 2]], axis=0)
+        upstream = jnp.concatenate([r[...] for r in upstreams[2 * pair : 2 * pair + 2]], axis=0)
+        gate = by_clip(clip_ref[here, :], gate_ref[...], 0, clips)
+        d_ffn = (gate * upstream.astype(F32)).astype(BF)
+        activated, slope = gelu_parts(dot_low(second, up_weights) + bu_ref[:, own])
+        d_hidden = (contract_last(d_ffn, down_weights) * slope).astype(BF)
+        up, down = dot_rows(second, d_hidden), dot_rows(activated.astype(BF), d_ffn)
+        if pair == 0:
+            up_sum[...] = up
+            down_sum[...] = down
+        else:
+            up_sum[...] += up
+            down_sum[...] += down
+    for y in range(2):
+        mine = slice(y * shard, (y + 1) * shard)
+        at = columns + 2 * y * shard
+        for k in range(width // LANES):
+            half_rows(
+                core, up_sum[k * LANES : (k + 1) * LANES, mine], kept_ref, sent_ref,
+                k * LANES // 2, slice(at, at + shard),
+            )
+        for c in range(width // shard):
+            half_rows(
+                core, down_sum[mine, c * shard : (c + 1) * shard], kept_ref, sent_ref,
+                c * shard // 2, slice(at + shard, at + 2 * shard),
+            )
+
+
+def weights_part(who, clip_col, modulation, b_up, w_up, w_down, h1_a, h1_b, d_qkv, seconds, upstreams):
+    width, ffn = w_up.shape
+    count = 2 * len(seconds)
+    part = 2 * ffn // count
+    clips = modulation.shape[0]
+    shape = (width // 2, d_qkv.shape[1] + 2 * part)
+    rows = d_qkv.shape[0]
+    arrays = [h1_a, h1_b, d_qkv, *seconds, *upstreams]
+    return pl.pallas_call(
+        lambda *refs: weights_kernel(clips, count, *refs),
+        grid=(1,),
+        in_specs=[
+            SCALARS,
+            pl.BlockSpec((rows // 2, 1), lambda *_: (0, 0)),
+            pl.BlockSpec((clips, width), lambda *_: (0, 3)),
+            full(b_up.shape),
+            ANYWHERE,
+            ANYWHERE,
+        ]
+        + [full(v.shape) for v in arrays],
+        out_specs=[full(shape)] * 2,
+        out_shape=[shape_of(shape, F32), shape_of(shape)],
+        scratch_shapes=[
+            pltpu.VMEM((width, part), F32),
+            pltpu.VMEM((part, width), F32),
+            pltpu.VMEM((width, part), BF),
+            pltpu.VMEM((part, width), BF),
+            pltpu.SemaphoreType.DMA((2,)),
+        ],
+        compiler_params=params(36),
+        cost_estimate=cost(7 * rows * width * part, 10 * MIB),
+    )(who, *all_in_hbm([clip_col, modulation, b_up, w_up, w_down, *arrays]))
+
+
+def table_kernel(first, clips, place_ref, *refs):
+    parts, refs = refs[:4], refs[4:]
+    if first:
+        silu_ref, w_ref = refs[:2]
+        dw_ref, db_ref, out_ref, total, sums = refs[-5:]
+    else:
+        silu_ref, w_ref, cond_ref, pick_ref, earlier_ref, _, _ = refs[:7]
+        dw_ref, db_ref, out_ref, total, sums = refs[7:]
+    i = pl.program_id(0)
+
+    @pl.when(i == 0)
+    def _():
+        total[...] = jnp.zeros_like(total) if first else earlier_ref[...]
+
+    for j, part in enumerate(parts):
+        value = part[...]
+        valid = lax.broadcasted_iota(jnp.int32, value.shape, 0) < clips
+        sums[pl.ds(pl.multiple_of((place_ref[0] ^ j) * 8, 8), 8), :] = jnp.where(valid, value, 0.0)
+    high, low = high_low(sums[...])
+    total[...] += contract_last(w_ref[...], jnp.concatenate([high, low], axis=0))
+    silu = silu_ref[...]
+    dw_ref[...] = dot_rows(
+        jnp.concatenate([silu, silu], axis=0), jnp.concatenate([high, low], axis=0)
+    )
+    db_ref[...] = jnp.sum(sums[...], axis=0, keepdims=True)
+
+    @pl.when(i == pl.num_programs(0) - 1)
+    def _():
+        if first:
+            out_ref[...] = total[...]
+        else:
+            rows = high.shape[0]
+            d_silu = total[:, :rows] + total[:, rows:]
+            cond = cond_ref[...]
+            gate = 1.0 / (1.0 + jnp.exp(-cond))
+            d_cond = d_silu.T * (gate * (1.0 + cond * (1.0 - gate)))
+            d_high, d_low = high_low(d_cond)
+            lowest = (d_cond - d_high.astype(F32) - d_low.astype(F32)).astype(BF)
+            pick = pick_ref[...].astype(BF)
+            out_ref[...] = dot_rows(pick, d_high) + dot_rows(pick, d_low) + dot_rows(pick, lowest)
+
+
+def table_part(place, sums, silu, w_mod, column, clips, rest=None, earlier=()):
+    columns = sums[0].shape[1]
+    width = w_mod.shape[0]
+    all_columns = 6 * width
+    rows, own = silu.shape
+    tile = 1024
+    skip = column // tile
+    first = rest is None
+    shapes = [
+        shape_of((own, all_columns), F32),
+        shape_of((1, all_columns), F32),
+        shape_of((width, 2 * rows), F32),
+    ]
+    in_specs = [SCALARS] + [pl.BlockSpec((8, tile), lambda i: (0, i))] * 4 + [
+        pl.BlockSpec((rows, own), lambda i: (0, 0)),
+        pl.BlockSpec((width, tile), lambda i: (0, skip + i)),
+    ]
+    args = [place, *all_in_hbm([*sums, silu, w_mod])]
+    aliases = {}
+    if first:
+        in_specs += [ANYWHERE] * len(earlier)
+        args += all_in_hbm(earlier)
+    else:
+        condition, pick, earlier, d_w, d_b = rest
+        in_specs += [
+            pl.BlockSpec((rows, width), lambda i: (0, 0)),
+            pl.BlockSpec(pick.shape, lambda i: (0, 0)),
+            pl.BlockSpec((width, 2 * rows), lambda i: (0, 0)),
+            ANYWHERE,
+            ANYWHERE,
+        ]
+        args += all_in_hbm([condition, pick, earlier, d_w, d_b])
+        aliases = {10: 0, 11: 1}
+        shapes[2] = shape_of((pick.shape[1], width), F32)
+    return pl.pallas_call(
+        lambda *refs: table_kernel(first, clips, *refs),
+        grid=(columns // tile,),
+        in_specs=in_specs,
+        out_specs=[
+            pl.BlockSpec((own, tile), lambda i: (0, skip + i)),
+            pl.BlockSpec((1, tile), lambda i: (0, skip + i)),
+            pl.BlockSpec(shapes[2].shape, lambda i: (0, 0)),
+        ],
+        out_shape=shapes,
+        scratch_shapes=[pltpu.VMEM((width, 2 * rows), F32), pltpu.VMEM((rows, tile), F32)],
+        input_output_aliases=aliases,
+        compiler_params=params(),
+        cost_estimate=pl.CostEstimate(
+            flops=4 * rows * width * columns, bytes_accessed=3 * width * columns, transcendentals=0
+        ),
+    )(*args)
+
+
+def in_order(bit, mine, other):
+    return jnp.stack([jnp.where(bit == 0, mine, other), jnp.where(bit == 0, other, mine)])
+
+
+def everyone(sums, count):
+    pairs = sums + swapped_with(sums, "blk", 1)
+    others = [swapped_with(pairs, "blk", k) for k in range(2, count, 2)]
+    level = [pairs] + others
+    while len(level) > 1:
+        level = [level[i] + level[i + 1] for i in range(0, len(level), 2)]
+    sums = level[0]
+    far = swapped_with(sums, "batch", 2)
+    both = swapped_with(jnp.concatenate([sums, far], axis=0), "batch", 1)
+    return [sums, both[:8], far, both[8:]]
+
+
+def assemble_kernel(ffn, who_ref, *refs):
+    qkv_ref, out_ref, up_ref, down_ref = refs[-4:]
+    width = out_ref.shape[1]
+    rows = qkv_ref.shape[0] // 4
+    for j, ref in enumerate(refs[:4]):
+        owner = who_ref[2] ^ j
+        core, far = owner % 2, owner // 2
+        at = pl.multiple_of(core * 2 * rows + far * rows, rows)
+        piece = 0
+        for target, count in ((qkv_ref, 3), (up_ref, ffn // width)):
+            for i in range(count):
+                here = slice(piece * rows, (piece + 1) * rows)
+                target[pl.ds(at, rows), i * width : (i + 1) * width] = ref[here, :].astype(F32)
+                piece += 1
+        for g in range(2):
+            here = slice(piece * rows, (piece + 1) * rows)
+            there = pl.multiple_of(core * 4 * rows + g * 2 * rows + far * rows, rows)
+            down_ref[pl.ds(there, rows), :] = ref[here, :].astype(F32)
+            piece += 1
+        part = width // 4
+        for g in range(4):
+            column = pl.multiple_of(owner * part, part)
+            out_ref[g * rows : (g + 1) * rows, pl.ds(column, part)] = ref[
+                piece * rows : (piece + 1) * rows, g * part : (g + 1) * part
+            ].astype(F32)
+
+
+def assemble(who, parts, own_rows, ffn):
+    width = parts[0].shape[1]
+    shapes = [
+        shape_of((own_rows, 3 * width), F32),
+        shape_of((own_rows, width), F32),
+        shape_of((own_rows, ffn), F32),
+        shape_of((2 * own_rows, width), F32),
+    ]
+    return pl.pallas_call(
+        lambda *refs: assemble_kernel(ffn, *refs),
+        grid=(1,),
+        in_specs=[SCALARS] + [full(v.shape) for v in parts],
+        out_specs=[full(o.shape) for o in shapes],
+        out_shape=shapes,
+        compiler_params=params(),
+        cost_estimate=cost(0, 6 * MIB),
+    )(who, *all_in_hbm(parts))
+
+
+def heads_body(
+    frames, step_table, clip_lengths, clip_steps, w_mod, b_mod, w_qkv, b_qkv, w_out, b_out,
+    w_up, b_up, w_down, b_down, cotangent,
+):
+    own_rows, width = frames.shape
+    ffn = w_up.shape[1]
+    count = lax.axis_size("blk")
+    me = lax.axis_index("blk")
+    place = lax.axis_index("batch")
+    core, far = place % 2, place // 2
+    who = jnp.stack([me, core, place])
+    clips = clip_lengths.shape[1]
+    rows = own_rows * count
+
+    evens, odds = gathered_blocks(frames, count)
+    head_size = width // HEADS
+    half = head_size // 2
+    lane = jnp.arange(LANES, dtype=jnp.int32)
+    freqs = 10000.0 ** (-2.0 * (lane % half).astype(F32) / head_size)
+    rows_of_table = jnp.arange(step_table.shape[0], dtype=jnp.int32)
+    (
+        modulation, silu_own, clip_col, clip_row, cosine, sine, marks, later, kept_qkv,
+    ) = prepare(
+        me[None], clip_lengths, clip_steps, step_table, freqs[None, :], w_mod, b_mod[None, :],
+        cotangent, [w_qkv], own_rows, count,
+    )
+    modulation_two = modulate(silu_own, w_mod, b_mod[None, :])
+
+    shared = (me[None], clip_col, modulation, kept_qkv, b_qkv[None, :], cosine, sine)
+    h1_a, kv_a, q_a, q_own = project(0, evens, *shared, True)
+    upstreams = even_blocks(later, count)
+    h1_b, kv_b, q_b = project(1, odds, *shared, False)
+    attended = attend(q_own, kv_a, kv_b, marks)
+    result, second, d_middle, d_attn, d_o, sums_two = middle_part(
+        clip_steps, clip_col, clip_row, frames, cotangent, attended, modulation_two,
+        b_out[None, :], b_up[None, :], b_down[None, :], w_out, w_up, w_down,
+        upstreams,
+    )
+    d_o = lax.all_to_all(d_o, "blk", 0, 0, tiled=True)
+    seconds = even_blocks(second, count)
+    probs = heads_probs(
+        me[None], q_a, q_b, kv_a, kv_b, clip_col, clip_row, count, [d_middle]
+    )
+    d_qkv, d_qkv_sent, sums_two, d_attn = attend_back(
+        me[None], probs, q_a, q_b, kv_a, kv_b, d_o, cosine, sine, (sums_two, d_attn), seconds[:-1]
+    )
+    d_own = lax.all_to_all(d_qkv_sent, "blk", 0, 0, tiled=True)
+
+    kept, sent = weights_part(
+        who, clip_col, modulation_two, b_up[None, :], w_up, w_down, h1_a, h1_b, d_qkv,
+        seconds, upstreams,
+    )
+
+    d_inputs, sums_one = last_part(
+        clip_col, clip_row, frames, modulation, d_middle, d_own, w_qkv, []
+    )
+    sums_two = everyone(sums_two, count)
+    steps_all = jnp.stack([v[clips + 1, :clips] for v in sums_two]) * (1.0 / count)
+    steps_all = steps_all[place ^ jnp.arange(4, dtype=jnp.int32)].astype(jnp.int32)
+    pick_all = (steps_all[:, :, None] == rows_of_table[None, None, :]).astype(F32)
+    pick_all = jnp.pad(pick_all, ((0, 0), (0, 8 - clips), (0, 0))).reshape(32, -1)
+    condition_all = exact_dot(pick_all, step_table)
+    silu_all = jax.nn.silu(condition_all).astype(BF)
+    silu_cols = lax.dynamic_slice_in_dim(silu_all, me * own_rows, own_rows, 1)
+    d_w_mod, d_b_mod, d_silu = table_part(
+        place[None], sums_two, silu_cols, w_mod, 2 * width, clips, earlier=[sums_one]
+    )
+    sums_one = everyone(sums_one, count)
+    d_w_mod, d_b_mod, d_table = table_part(
+        place[None], sums_one, silu_cols, w_mod, 0, clips,
+        (condition_all, pick_all, d_silu, d_w_mod, d_b_mod),
+    )
+
+    def batch_total(parts):
+        return (parts[0] + parts[1]) + (parts[2] + parts[3])
+
+    bias_two = batch_total([v[clips] for v in sums_two])
+    bias_one = batch_total([v[clips : clips + 2] for v in sums_one])
+    d_b_qkv = jnp.concatenate(
+        [bias_one[0, :width], bias_one[1, :width], bias_one[0, width:]], axis=0
+    )
+    d_b_out, d_b_up, d_b_down = jnp.split(bias_two, [width, width + ffn])
+
+    quarter = own_rows // 4
+    part = ffn // count
+    mine = kept + swapped_with(sent, "batch", 1).astype(F32)
+    first, even, odd = jnp.split(mine, [3 * LANES, 3 * LANES + 2 * part], axis=1)
+    sent = jnp.where(me % 2 == 0, odd, even).astype(BF)
+    both = jnp.where(me % 2 == 0, even, odd) + swapped_with(sent, "blk", 1).astype(F32)
+    columns = 3 * LANES + 2 * part
+    mine = jnp.concatenate([first, both], axis=1).reshape(count, 2, quarter, columns)
+    low, high = mine[:, 0], mine[:, 1]
+    sent = jnp.where(far == 0, high, low).astype(BF)
+    mine = jnp.where(far == 0, low, high) + swapped_with(sent, "batch", 2).astype(F32)
+    mine = mine.astype(BF)
+    rows_mine = lax.all_to_all(mine[:, :, : columns - part], "blk", 0, 0, tiled=True)
+    qkv_rows = [
+        jnp.transpose(rows_mine[:, :, i * LANES : (i + 1) * LANES], (1, 0, 2)).reshape(quarter, width)
+        for i in range(3)
+    ]
+    up_rows = jnp.transpose(rows_mine[:, :, 3 * LANES :], (1, 0, 2)).reshape(quarter, ffn)
+    down_rows = mine[:, :, columns - part :].reshape(width // part, 2, quarter, part)
+    down_rows = jnp.transpose(down_rows, (1, 2, 0, 3)).reshape(2 * quarter, width)
+
+    wide = width // 2
+    da_low, da_high = d_attn[:, :wide], d_attn[:, wide:]
+    sent = jnp.concatenate([attended, jnp.where(far == 0, da_high, da_low)], axis=1)
+    kept = jnp.concatenate([attended, jnp.where(far == 0, da_low, da_high)], axis=1)
+    pair = jnp.concatenate([kept, swapped_with(sent, "batch", 2)], axis=0)
+    left, low, high = pair[:, :width], pair[:, width : width + wide // 2], pair[:, width + wide // 2 :]
+    sent = jnp.concatenate([left, jnp.where(core == 0, high, low)], axis=1)
+    kept = jnp.concatenate([left, jnp.where(core == 0, low, high)], axis=1)
+    pair = jnp.concatenate([kept, swapped_with(sent, "batch", 1)], axis=0)
+    out_sums = dot_rows(pair[:, :width], pair[:, width:]).astype(BF).reshape(count, own_rows, -1)
+    out_sums = lax.all_to_all(out_sums, "blk", 0, 0, tiled=True)
+    out_sums = jnp.sum(out_sums.astype(F32), axis=0).astype(BF)
+    out_rows = jnp.concatenate(
+        [out_sums[g * quarter : (g + 1) * quarter] for g in range(4)], axis=1
+    )
+
+    pieces = qkv_rows + [up_rows[:, i * width : (i + 1) * width] for i in range(ffn // width)]
+    mine = jnp.concatenate(pieces + [down_rows, out_rows], axis=0)
+    other = swapped_with(mine, "batch", 2)
+    d_w_qkv, d_w_out, d_w_up, d_w_down = assemble(
+        who,
+        [mine, swapped_with(mine, "batch", 1), other, swapped_with(other, "batch", 1)],
+        own_rows,
+        ffn,
+    )
+
+    return (
+        result,
+        d_inputs,
+        d_table,
+        d_w_mod,
+        d_b_mod[0],
+        d_w_qkv,
+        d_b_qkv,
+        d_w_out,
+        d_b_out,
+        d_w_up,
+        d_b_up,
+        d_w_down,
+        d_b_down,
+    )
+
+
 def solution(mesh):
+    blk = mesh.shape["blk"]
+    heads_fit = HEADS % (2 * blk) == 0 and mesh.shape["batch"] == 4
+    chosen = heads_body if heads_fit else ring_body
     placed = (
         P(("batch", "blk"), None),
         P(),
@@ -323,7 +1450,7 @@
         P(("batch", "blk"), None),
     )
     return jax.shard_map(
-        body,
+        chosen,
         mesh=mesh,
         in_specs=placed,
         out_specs=(

time: 1500 us -> 253 us (0.17)
  waiting for transfers between devices: 1160 us -> 70.7 us
  matrix products: 128 us -> 1.48 us
  Pallas kernels: 0 us -> 99.2 us
  other arithmetic: 87 us -> 7.11 us
  blocking collectives: 41.8 us -> 0 us
  starting transfers between devices: 33.1 us -> 59.3 us
  local copies, waits for them, and re-layouts: 33.9 us -> 12.9 us
    reduce_scatter x2 -> x0, waiting for transfers between devices: 790 us -> none  [the longest x1 790 us: body(): lax.psum_scatter(jnp.concatenate(blocks_list, axis=1), 'blk', scatter_dim...]
    ppermute x44 -> x33, waiting for transfers between devices: 229 us -> 66.8 us  [swapped_with(): return lax.ppermute(value, axis, [(i, i ^ offset) for i in range(size)])]
    psum x2 -> x0, waiting for transfers between devices: 142 us -> none  [the longest x1 120 us: body(): lax.psum((jnp.sum(d_modulation, axis=0), jnp.sum(d_projected.astype(jnp.f...]
    dot_general x70 -> x1, matrix products: 109 us -> 1.28 us  [dot_rows(): lax.dot_general(left, right, (((0,), (0,)), ((), ())), preferred_element_...]
    pallas_call x0 -> x13, Pallas kernels: none -> 99.2 us  [the longest x1 12.9 us: attend_back(): pl.pallas_call(attend_back_kernel, grid_spec=grid_spec, out_shape=[shape_...]
    psum x1 -> x0, blocking collectives: 41.8 us -> none  [body(): lax.psum((jnp.sum(d_modulation, axis=0), jnp.sum(d_projected.astype(jnp.f...]
    concatenate x4 -> x9, other arithmetic: 33.6 us -> 0.97 us  [the longest x1 0.6 us: heads_body(): jnp.concatenate([bias_one[0, :width], bias_one[1, :width], bias_one[0, wi...]
    reduce_sum x32 -> x1, other arithmetic: 20.5 us -> 0.08 us  [heads_body(): out_sums = jnp.sum(out_sums.astype(F32), axis=0).astype(BF)]
  transfers between devices with their start and end apart: 48 -> 37, of which waited for: 33 -> 12; matrix products, arithmetic and copies ran while one was open for 13% -> 5% of each run, Pallas kernels for 0% -> 33%
where the time goes in v1:
time: 253 us; the launch traced here: 252 us
  Pallas kernels  99.2 us (39%)
  waiting for transfers between devices  70.7 us (28%)
  starting transfers between devices  59.3 us (23%)
  local copies, waits for them, and re-layouts  12.9 us (5%)
  other arithmetic  7.11 us (3%)
    ppermute x33, waiting for transfers between devices, swapped_with(): return lax.ppermute(value, axis, [(i, i ^ offset) for i in range(size)])  66.8 us
    ppermute x33, starting transfers between devices, swapped_with(): return lax.ppermute(value, axis, [(i, i ^ offset) for i in range(size)])  40.7 us
    pallas_call x1, Pallas kernels, attend_back(): pl.pallas_call(attend_back_kernel, grid_spec=grid_spec, out_shape=[shape_...  12.9 us
    pallas_call x1, Pallas kernels, middle_part(): pl.pallas_call(lambda *refs: middle_kernel(clips, *refs), grid=(1,), in_s...  12.2 us
    pallas_call x2, Pallas kernels, table_part(): pl.pallas_call(lambda *refs: table_kernel(first, clips, *refs), grid=(col...  12.1 us
    pallas_call x2, Pallas kernels, project(): pl.pallas_call(lambda *refs: project_kernel(clips, with_own, *refs), grid...  11.9 us
    pallas_call x1, Pallas kernels, attend(): pl.pallas_call(attend_kernel, grid=(width // LANES,), in_specs=[pl.BlockS...  9.41 us
    pallas_call x1, Pallas kernels, weights_part(): pl.pallas_call(lambda *refs: weights_kernel(clips, count, *refs), grid=(1...  9.21 us
  transfers between devices with their start and end apart: 37, of which 12 were waited for; matrix products, arithmetic and copies ran while one was open for 5% of the time, Pallas kernels for 33%

profile of v1, /device:TPU:0, one launch (start us, length us, event | category | flops | bytes accessed | tf_op | source)
XLA Modules:
  0.0 252.0 jit_solution(11836179999268800994)
XLA Ops:
  0.6 3.1 %collective-permute-start = (bf16[128,1024]{1,0:T(8,128)(2,1)}, bf16[128,1024]{1,0:T(8,128)(2,1)S(1)}, u32[]{:S(2)}, u32[]{:S(2)}) collective-permute-start(bf16[128,1024]{1,0:T(8,128)(2,1)} %refs_2_.3), channel_id=1, source_target_pairs={{0,2},{1,3},{2,0},{3,1},{4,6},{5,7},{6,4},{7,5},{8,10},{9,11},{10,... | collective-permute-start | bytes 786440 | tf_op jit(solution)/shard_map/ppermute | solution.py:317
  3.7 2.6 %collective-permute-start.1 = (bf16[128,1024]{1,0:T(8,128)(2,1)}, bf16[128,1024]{1,0:T(8,128)(2,1)S(1)}, u32[]{:S(2)}, u32[]{:S(2)}) collective-permute-start(bf16[128,1024]{1,0:T(8,128)(2,1)} %refs_2_.3), channel_id=1, source_target_pairs={{0,4},{1,5},{2,6},{3,7},{4,0},{5,1},{6,2},{7,3},{8,12},{9,13},{10,... | collective-permute-start | bytes 786440 | tf_op jit(solution)/shard_map/ppermute | solution.py:317
  6.3 1.7 collective-permute-start.3
  8.1 7.0 %collective-permute-done.refs_8_ = bf16[128,1024]{1,0:T(8,128)(2,1)S(1)} collective-permute-done((bf16[128,1024]{1,0:T(8,128)(2,1)}, bf16[128,1024]{1,0:T(8,128)(2,1)S(1)}, u32[]{:S(2)}, u32[]{:S(2)}) %collective-permute-start) | collective-permute-done | bytes 262176 | tf_op jit(solution)/shard_map/ppermute | solution.py:317
  15.1 1.7 collective-permute-start.4
  16.8 8.5 %collective-permute-done.1.refs_9_ = bf16[128,1024]{1,0:T(8,128)(2,1)S(1)} collective-permute-done((bf16[128,1024]{1,0:T(8,128)(2,1)}, bf16[128,1024]{1,0:T(8,128)(2,1)S(1)}, u32[]{:S(2)}, u32[]{:S(2)}) %collective-permute-start.1) | collective-permute-done | bytes 262176 | tf_op jit(solution)/shard_map/ppermute | solution.py:317
  25.3 1.5 collective-permute-start.5
  29.2 6.3 %shard_map.246 = (f32[4,2048]{1,0:T(4,128)}, bf16[4,1024]{1,0:T(4,128)(2,1)}, s32[1024,1]{1,0:T(8,128)}, s32[1,1024]{1,0:T(1,128)}, f32[1024,128]{1,0:T(8,128)},...) custom-call(s32[1]{0:T(128)} %bitcast.refs_0_.me_ref, ...), custom_call_target="tpu_custom_call" | custom-call | flops 16777216 | bytes 5242880 | tf_op jit(solution)/shard_map/pallas_call | solution.py:460
  35.6 4.3 %collective-permute-start.7 = (bf16[128,1024]{1,0:T(8,128)(2,1)}, bf16[128,1024]{1,0:T(8,128)(2,1)S(1)}, u32[]{:S(2)}, u32[]{:S(2)}) collective-permute-start(bf16[128,1024]{1,0:T(8,128)(2,1)} %get-tuple-element.64.refs_13_), channel_id=1, source_target_pairs={{0,2},{1,3},{2,0},{3,1},{4,6},{5,7},{6,4},{7,5},{8,10},{9,11},{10,... | collective-permute-start | bytes 786440 | tf_op jit(solution)/shard_map/ppermute | solution.py:317
  39.9 5.4 %shard_map.250.refs_6_.refs_2_ = f32[4,4096]{1,0:T(4,128)} custom-call(bf16[4,1024]{1,0:T(4,128)(2,1)} %get-tuple-element.63.silu_ref, bf16[1024,6144]{1,0:T(8,128)(2,1)} %refs_6_.5, f32[1,6144]{1,0:T(1,128)} %bitcast.80), custom_call_target="tpu_custom_call" | custom-call | flops 33554432 | bytes 8388608 | tf_op jit(solution)/shard_map/pallas_call | solution.py:488
  46.4 1.5 collective-permute-start.9
  48.0 6.2 %shard_map.247 = (bf16[512,1024]{1,0:T(8,128)(2,1)}, bf16[16,512,128]{2,1,0:T(8,128)(2,1)S(1)}, bf16[512,128]{1,0:T(8,128)(2,1)}, bf16[128,1024]{1,0:T(8,128)(2,1)}) custom-call(s32[1]{0:T(128)} %bitcast.refs_0_.me_ref, s32[1024,1]{1,0:T(8,128)} %get-tuple-element.53.refs_1_.keyclip_ref.refs_0_, f32[4,2048]{1,0:T(4,128)} %get-tuple-element.56.refs_2_.refs_3_, ...), custom_call_target="tpu_custom_call" | custom-call | flops 2147483648 | bytes 6291456 | tf_op jit(solution)/shard_map/pallas_call | solution.py:555
  54.2 5.7 %shard_map.248 = (bf16[512,1024]{1,0:T(8,128)(2,1)}, bf16[16,512,128]{2,1,0:T(8,128)(2,1)S(1)}, bf16[512,128]{1,0:T(8,128)(2,1)}) custom-call(s32[1]{0:T(128)} %bitcast.refs_0_.me_ref, s32[1024,1]{1,0:T(8,128)} %get-tuple-element.53.refs_1_.keyclip_ref.refs_0_, f32[4,2048]{1,0:T(4,128)} %get-tuple-element.56.refs_2_.refs_3_, f32[1,3072]{1,0:T(1,128)} %bitcast.82, ...), custom_call_target="tpu_custom_call" | custom-call | flops 2147483648 | bytes 6291456 | tf_op jit(solution)/shard_map/pallas_call | solution.py:555
  59.9 9.4 %shard_map.249.refs_5_ = bf16[128,1024]{1,0:T(8,128)(2,1)} custom-call(bf16[1024,256]{1,0:T(8,128)(2,1)} %get-tuple-element.55.keymark_ref.rowmark_ref, bf16[1024,256]{1,0:T(8,128)(2,1)} %get-tuple-element.55.keymark_ref.rowmark_ref, bf16[128,1024]{1,0:T(8,128)(2,1)} %get-tuple-element.60.q_ref, bf16[16,512,128]{2,1,0:T(8,128)(2,1)S(1)} %get-tuple-element.61.ka_ref, ...), custom_call_target="tpu_custom_call" | custom-call | flops 536870912 | bytes 1048576 | tf_op jit(solution)/shard_map/pallas_call | solution.py:621
  70.3 12.2 %shard_map.251 = (bf16[128,1024]{1,0:T(8,128)(2,1)}, bf16[128,1024]{1,0:T(8,128)(2,1)}, f32[128,1024]{1,0:T(8,128)}, bf16[128,1024]{1,0:T(8,128)(2,1)}, bf16[8,128,128]{2,1,0:T(8,128)(2,1)}, /*index=5*/f32[8,4096]{1,0:T(8,128)}) custom-call(s32[1,4]{1,0:T(1,128)S(1)} %copy-done.4, s32[1024,1]{1,0:T(8,128)} %get-tuple-element.53.refs_1_.keyclip_ref.refs_0_, ...), custom_call_target="tpu_custom_call" | custom-call | flops 2684354560 | bytes 3145728 | tf_op jit(solution)/shard_map/pallas_call | solution.py:940
  82.4 3.6 %all-to-all-start = ((bf16[8,128,128]{2,1,0:T(8,128)(2,1)}), bf16[8,128,128]{2,1,0:T(8,128)(2,1)S(1)}, u32[]{:S(2)}, u32[]{:S(2)}) async-start(bf16[8,128,128]{2,1,0:T(8,128)(2,1)} %get-tuple-element.69), calls=%async_computation | async-start | bytes 524288 | tf_op jit(solution)/shard_map/all_to_all | solution.py:1322
  86.1 2.1 collective-permute-start.10
  88.2 2.4 collective-permute-start.11
  90.7 1.6 copy-done.1
  92.3 8.7 %shard_map.252.p_ref = f32[1024,2048]{1,0:T(8,128)} custom-call(s32[1]{0:T(128)} %bitcast.refs_0_.me_ref, s32[1024,1]{1,0:T(8,128)} %get-tuple-element.53.refs_1_.keyclip_ref.refs_0_, s32[1,1024]{1,0:T(1,128)} %get-tuple-element.54.refs_2_.rowclip_ref.refs_1_, bf16[512,128]{1,0:T(8,128)(2,1)} %get-tuple-element.67.qa_ref, ...), custom_call_target="tpu_custom_call" | custom-call | flops 536870912 | bytes 9437184 | tf_op jit(solution)/shard_map/pallas_call | solution.py:681
  102.1 10.6 %collective-permute-done.11.refs_4_.refs_11_ = bf16[128,1024]{1,0:T(8,128)(2,1)S(1)} collective-permute-done((bf16[128,1024]{1,0:T(8,128)(2,1)}, bf16[128,1024]{1,0:T(8,128)(2,1)S(1)}, u32[]{:S(2)}, u32[]{:S(2)}) %collective-permute-start.11) | collective-permute-done | bytes 262176 | tf_op jit(solution)/shard_map/ppermute | solution.py:317
  113.5 1.6 copy-done.2
  115.1 12.9 %shard_map.253 = (bf16[1024,384]{1,0:T(8,128)(2,1)}, bf16[8,128,384]{2,1,0:T(8,128)(2,1)}, f32[8,4096]{1,0:T(8,128)}, bf16[128,1024]{1,0:T(8,128)(2,1)}) custom-call(s32[1]{0:T(128)} %bitcast.refs_0_.me_ref, f32[1024,2048]{1,0:T(8,128)} %shard_map.252.p_ref, ...), custom_call_target="tpu_custom_call", output_to_operand_aliasing={{2}: (9, {}), {3}: (10, {})} | custom-call | flops 1073741824 | bytes 12582912 | tf_op jit(solution)/shard_map/pallas_call | solution.py:784
  128.0 3.8 %all-to-all-start.1 = ((bf16[8,128,384]{2,1,0:T(8,128)(2,1)}), bf16[8,128,384]{2,1,0:T(8,128)(2,1)S(1)}, u32[]{:S(2)}, u32[]{:S(2)}) async-start(bf16[8,128,384]{2,1,0:T(8,128)(2,1)} %get-tuple-element.73), calls=%async_computation.1 | async-start | bytes 1572864 | tf_op jit(solution)/shard_map/all_to_all | solution.py:1330
  131.8 1.7 collective-permute-start.18
  134.2 9.2 %shard_map.257 = (f32[512,1408]{1,0:T(8,128)}, bf16[512,1408]{1,0:T(8,128)(2,1)}) custom-call(s32[3]{0:T(128)S(1)} %pad_add_fusion.refs_0_, s32[1024,1]{1,0:T(8,128)} %get-tuple-element.53.refs_1_.keyclip_ref.refs_0_, f32[4,4096]{1,0:T(4,128)} %shard_map.250.refs_6_.refs_2_, f32[1,2048]{1,0:T(1,128)} %bitcast.84, bf16[1024,2048]{1,0:T(8,128)(2,1)} %refs_4_.3, ...), custom_call_target="tpu_custom_call" | custom-call | flops 3758096384 | bytes 10485760 | tf_op jit(solution)/shard_map/pallas_call | solution.py:1101
  143.5 2.5 collective-permute-start.20
  146.0 1.4 collective-permute-start.21
  147.5 12.0 %collective-permute-done.20 = f32[8,4096]{1,0:T(8,128)S(1)} collective-permute-done((f32[8,4096]{1,0:T(8,128)S(1)}, f32[8,4096]{1,0:T(8,128)S(1)}, u32[]{:S(2)}, u32[]{:S(2)}) %collective-permute-start.20) | collective-permute-done | bytes 131104 | tf_op jit(solution)/shard_map/ppermute | solution.py:317
  159.6 1.6 collective-permute-start.22
  161.8 4.3 %collective-permute-done.22.refs_3_ = f32[8,4096]{1,0:T(8,128)S(1)} collective-permute-done((f32[8,4096]{1,0:T(8,128)S(1)}, f32[8,4096]{1,0:T(8,128)S(1)}, u32[]{:S(2)}, u32[]{:S(2)}) %collective-permute-start.22) | collective-permute-done | bytes 131104 | tf_op jit(solution)/shard_map/ppermute | solution.py:317
  166.2 4.5 %collective-permute-done.28 = bf16[128,1536]{1,0:T(8,128)(2,1)S(1)} collective-permute-done((bf16[128,1536]{1,0:T(8,128)(2,1)S(1)}, bf16[128,1536]{1,0:T(8,128)(2,1)S(1)}, u32[]{:S(2)}, u32[]{:S(2)}) %collective-permute-start.28) | collective-permute-done | bytes 393248 | tf_op jit(solution)/shard_map/ppermute | solution.py:317
  172.5 2.5 convert_add_fusion
  177.2 12.2 %collective-permute-done.26 = bf16[512,512]{1,0:T(8,128)(2,1)S(1)} collective-permute-done((bf16[512,512]{1,0:T(8,128)(2,1)S(1)}, bf16[512,512]{1,0:T(8,128)(2,1)S(1)}, u32[]{:S(2)}, u32[]{:S(2)}) %collective-permute-start.26) | collective-permute-done | bytes 524320 | tf_op jit(solution)/shard_map/ppermute | solution.py:317
  189.8 6.1 %all-to-all-start.3 = ((bf16[8,128,256]{2,1,0:T(8,128)(2,1)}), bf16[8,128,256]{2,1,0:T(8,128)(2,1)S(1)}, u32[]{:S(2)}, u32[]{:S(2)}) async-start(bf16[8,128,256]{2,1,0:T(8,128)(2,1)} %bitcast.73), calls=%async_computation.3 | async-start | bytes 1048576 | tf_op jit(solution)/shard_map/all_to_all | solution.py:1398
  196.0 1.6 collective-permute-start.27
  197.8 7.3 %shard_map.254 = (bf16[128,1024]{1,0:T(8,128)(2,1)}, f32[8,2048]{1,0:T(8,128)}) custom-call(s32[1024,1]{1,0:T(8,128)} %get-tuple-element.53.refs_1_.keyclip_ref.refs_0_, s32[1,1024]{1,0:T(1,128)} %get-tuple-element.54.refs_2_.rowclip_ref.refs_1_, bf16[128,1024]{1,0:T(8,128)(2,1)} %refs_2_.3, f32[4,2048]{1,0:T(4,128)} %get-tuple-element.56.refs_2_.refs_3_, ...), custom_call_target="tpu_custom_call" | custom-call | flops 805306368 | bytes 2097152 | tf_op jit(solution)/shard_map/pallas_call | solution.py:996
  205.2 2.1 collective-permute-start.12
  207.9 1.9 collective-permute-done.12
  210.6 3.0 %collective-permute-start.14 = (f32[8,2048]{1,0:T(8,128)S(1)}, f32[8,2048]{1,0:T(8,128)S(1)}, u32[]{:S(2)}, u32[]{:S(2)}) collective-permute-start(f32[8,2048]{1,0:T(8,128)S(1)} %add.94), channel_id=1, source_target_pairs={{0,4},{1,5},{2,6},{3,7},{4,0},{5,1},{6,2},{7,3},{8,12},{9,13},{10,... | collective-permute-start | bytes 196616 | tf_op jit(solution)/shard_map/ppermute | solution.py:317
  213.5 1.5 collective-permute-start.15
  216.0 5.1 %all-to-all-start.2 = ((bf16[8,32,640]{2,1,0:T(8,128)(2,1)}), bf16[8,32,640]{2,1,0:T(8,128)(2,1)S(1)}, u32[]{:S(2)}, u32[]{:S(2)}) async-start(bf16[8,32,640]{2,1,0:T(8,128)(2,1)} %slice.181), calls=%async_computation.2 | async-start | bytes 655360 | tf_op jit(solution)/shard_map/all_to_all | solution.py:1379
  222.3 3.1 %collective-permute-done.16.refs_3_ = f32[8,2048]{1,0:T(8,128)S(1)} collective-permute-done((f32[8,2048]{1,0:T(8,128)S(1)}, f32[8,2048]{1,0:T(8,128)S(1)}, u32[]{:S(2)}, u32[]{:S(2)}) %collective-permute-start.16) | collective-permute-done | bytes 65568 | tf_op jit(solution)/shard_map/ppermute | solution.py:317
  225.8 3.9 %all-to-all-done.2 = bf16[8,32,640]{2,1,0:T(8,128)(2,1)S(1)} async-done(((bf16[8,32,640]{2,1,0:T(8,128)(2,1)}), bf16[8,32,640]{2,1,0:T(8,128)(2,1)S(1)}, u32[]{:S(2)}, u32[]{:S(2)}) %all-to-all-start.2) | async-done | bytes 327712 | tf_op jit(solution)/shard_map/all_to_all | solution.py:1379
  231.7 7.1 %shard_map.255 = (f32[128,6144]{1,0:T(8,128)}, f32[1,6144]{1,0:T(1,128)}, f32[1024,64]{1,0:T(8,128)}) custom-call(s32[1]{0:T(128)} %bitcast.6.refs_0_, f32[8,4096]{1,0:T(8,128)} %copy-done.8, f32[8,4096]{1,0:T(8,128)} %get-tuple-element.102.refs_2_, f32[8,4096]{1,0:T(8,128)} %copy-done.20, f32[8,4096]{1,0:T(8,128)} %get-tuple-element.101.refs_4_, ...), custom_call_target="tpu_custom_call" | custom-call | flops 536870912 | bytes 12582912 | tf_op jit(solution)/shard_map/pallas_call | solution.py:1203
  239.0 1.4 collective-permute-done.31.refs_3_
  241.1 4.9 %shard_map.256 = (f32[128,6144]{1,0:T(8,128)}, f32[1,6144]{1,0:T(1,128)}, f32[32,1024]{1,0:T(8,128)}) custom-call(s32[1]{0:T(128)} %bitcast.6.refs_0_, f32[8,2048]{1,0:T(8,128)} %copy-done.17, f32[8,2048]{1,0:T(8,128)} %get-tuple-element.106.refs_2_, f32[8,2048]{1,0:T(8,128)} %copy-done.26, ...), custom_call_target="tpu_custom_call", output_to_operand_aliasing={{0}: (10, {}), {1}: (11, {})} | custom-call | flops 268435456 | bytes 6291456 | tf_op jit(solution)/shard_map/pallas_call | solution.py:1203
  248.2 3.8 %shard_map.258 = (f32[128,3072]{1,0:T(8,128)}, f32[128,1024]{1,0:T(8,128)}, f32[128,2048]{1,0:T(8,128)}, f32[256,1024]{1,0:T(8,128)}) custom-call(s32[3]{0:T(128)S(1)} %pad_add_fusion.refs_0_, bf16[256,1024]{1,0:T(8,128)(2,1)} %copy-done.18, bf16[256,1024]{1,0:T(8,128)(2,1)} %copy-done.24, bf16[256,1024]{1,0:T(8,128)(2,1)} %copy-done.23, ...), custom_call_target="tpu_custom_call" | custom-call | bytes 6291456 | tf_op jit(solution)/shard_map/pallas_call | solution.py:1273
  (165 shorter events, 21.5 us)
Async XLA Ops:
  0.6 14.5 %collective-permute-start = (bf16[128,1024]{1,0:T(8,128)(2,1)}, bf16[128,1024]{1,0:T(8,128)(2,1)S(1)}, u32[]{:S(2)}, u32[]{:S(2)}) collective-permute-start(bf16[128,1024]{1,0:T(8,128)(2,1)} %refs_2_.3), channel_id=1, source_target_pairs={{0,2},{1,3},{2,0},{3,1},{4,6},{5,7},{6,4},{7,5},{8,10},{9,11},{10,... | collective-permute-start | bytes 786440 | tf_op jit(solution)/shard_map/ppermute | solution.py:317
  3.7 21.6 %collective-permute-start.1 = (bf16[128,1024]{1,0:T(8,128)(2,1)}, bf16[128,1024]{1,0:T(8,128)(2,1)S(1)}, u32[]{:S(2)}, u32[]{:S(2)}) collective-permute-start(bf16[128,1024]{1,0:T(8,128)(2,1)} %refs_2_.3), channel_id=1, source_target_pairs={{0,4},{1,5},{2,6},{3,7},{4,0},{5,1},{6,2},{7,3},{8,12},{9,13},{10,... | collective-permute-start | bytes 786440 | tf_op jit(solution)/shard_map/ppermute | solution.py:317
  6.3 20.5 %collective-permute-start.2 = (bf16[128,1024]{1,0:T(8,128)(2,1)}, bf16[128,1024]{1,0:T(8,128)(2,1)S(1)}, u32[]{:S(2)}, u32[]{:S(2)}) collective-permute-start(bf16[128,1024]{1,0:T(8,128)(2,1)} %refs_2_.3), channel_id=1, source_target_pairs={{0,6},{1,7},{2,4},{3,5},{4,2},{5,3},{6,0},{7,1},{8,14},{9,15},{10,... | collective-permute-start | bytes 786440 | tf_op jit(solution)/shard_map/ppermute | solution.py:317
  6.3 39.0 %collective-permute-start.3 = (bf16[128,1024]{1,0:T(8,128)(2,1)}, bf16[128,1024]{1,0:T(8,128)(2,1)S(1)}, u32[]{:S(2)}, u32[]{:S(2)}) collective-permute-start(bf16[128,1024]{1,0:T(8,128)(2,1)} %refs_2_.3), channel_id=1, source_target_pairs={{0,1},{1,0},{2,3},{3,2},{4,5},{5,4},{6,7},{7,6},{8,9},{9,8},{10,11... | collective-permute-start | bytes 786440 | tf_op jit(solution)/shard_map/ppermute | solution.py:317
  15.1 20.4 %copy-start.28 = (bf16[128,1024]{1,0:T(8,128)(2,1)}, bf16[128,1024]{1,0:T(8,128)(2,1)S(1)}, u32[]{:S(2)}) copy-start(bf16[128,1024]{1,0:T(8,128)(2,1)S(1)} %collective-permute-done.refs_8_) | copy-start | bytes 786436
  15.1 31.3 %collective-permute-start.4 = (bf16[128,1024]{1,0:T(8,128)(2,1)S(1)}, bf16[128,1024]{1,0:T(8,128)(2,1)S(1)}, u32[]{:S(2)}, u32[]{:S(2)}) collective-permute-start(bf16[128,1024]{1,0:T(8,128)(2,1)S(1)} %collective-permute-done.refs_8_), channel_id=1, source_target_pairs={{0,1},{1,0},{2,3},{3,2},{4,5},{5,4},{6,7},{7,6},{8,9},{9,8},{10,11... | collective-permute-start | bytes 786440 | tf_op jit(solution)/shard_map/ppermute | solution.py:317
  25.3 10.2 %copy-start.29 = (bf16[128,1024]{1,0:T(8,128)(2,1)}, bf16[128,1024]{1,0:T(8,128)(2,1)S(1)}, u32[]{:S(2)}) copy-start(bf16[128,1024]{1,0:T(8,128)(2,1)S(1)} %collective-permute-done.1.refs_9_) | copy-start | bytes 786436
  25.3 28.8 %collective-permute-start.5 = (bf16[128,1024]{1,0:T(8,128)(2,1)S(1)}, bf16[128,1024]{1,0:T(8,128)(2,1)}, u32[]{:S(2)}, u32[]{:S(2)}) collective-permute-start(bf16[128,1024]{1,0:T(8,128)(2,1)S(1)} %collective-permute-done.1.refs_9_), channel_id=1, source_target_pairs={{0,1},{1,0},{2,3},{3,2},{4,5},{5,4},{6,7},{7,6},{8,9},{9,8},{10,11... | collective-permute-start | bytes 786440 | tf_op jit(solution)/shard_map/ppermute | solution.py:317
  26.8 27.3 %collective-permute-start.6 = (bf16[128,1024]{1,0:T(8,128)(2,1)S(1)}, bf16[128,1024]{1,0:T(8,128)(2,1)}, u32[]{:S(2)}, u32[]{:S(2)}) collective-permute-start(bf16[128,1024]{1,0:T(8,128)(2,1)S(1)} %collective-permute-done.2.refs_10_), channel_id=1, source_target_pairs={{0,1},{1,0},{2,3},{3,2},{4,5},{5,4},{6,7},{7,6},{8,9},{9,8},{10,11... | collective-permute-start | bytes 786440 | tf_op jit(solution)/shard_map/ppermute | solution.py:317
  35.6 33.8 %collective-permute-start.7 = (bf16[128,1024]{1,0:T(8,128)(2,1)}, bf16[128,1024]{1,0:T(8,128)(2,1)S(1)}, u32[]{:S(2)}, u32[]{:S(2)}) collective-permute-start(bf16[128,1024]{1,0:T(8,128)(2,1)} %get-tuple-element.64.refs_13_), channel_id=1, source_target_pairs={{0,2},{1,3},{2,0},{3,1},{4,6},{5,7},{6,4},{7,5},{8,10},{9,11},{10,... | collective-permute-start | bytes 786440 | tf_op jit(solution)/shard_map/ppermute | solution.py:317
  45.3 24.0 %collective-permute-start.8 = (bf16[128,1024]{1,0:T(8,128)(2,1)S(1)}, bf16[128,1024]{1,0:T(8,128)(2,1)S(1)}, u32[]{:S(2)}, u32[]{:S(2)}) collective-permute-start(bf16[128,1024]{1,0:T(8,128)(2,1)S(1)} %copy-done.13), channel_id=1, source_target_pairs={{0,4},{1,5},{2,6},{3,7},{4,0},{5,1},{6,2},{7,3},{8,12},{9,13},{10,... | collective-permute-start | bytes 786440 | tf_op jit(solution)/shard_map/ppermute | solution.py:317
  46.4 22.9 %collective-permute-start.9 = (bf16[128,1024]{1,0:T(8,128)(2,1)S(1)}, bf16[128,1024]{1,0:T(8,128)(2,1)S(1)}, u32[]{:S(2)}, u32[]{:S(2)}) collective-permute-start(bf16[128,1024]{1,0:T(8,128)(2,1)S(1)} %copy-done.13), channel_id=1, source_target_pairs={{0,6},{1,7},{2,4},{3,5},{4,2},{5,3},{6,0},{7,1},{8,14},{9,15},{10,... | collective-permute-start | bytes 786440 | tf_op jit(solution)/shard_map/ppermute | solution.py:317
  59.9 9.4 %copy-start = (bf16[16,512,128]{2,1,0:T(8,128)(2,1)}, bf16[16,512,128]{2,1,0:T(8,128)(2,1)S(1)}, u32[]{:S(2)}) copy-start(bf16[16,512,128]{2,1,0:T(8,128)(2,1)S(1)} %get-tuple-element.62.kb_ref) | copy-start | bytes 6291460
  59.9 10.4 %copy-start.4 = (s32[1,4]{1,0:T(1,128)S(1)}, s32[1,4]{1,0:T(1,128)}, u32[]{:S(2)}) copy-start(s32[1,4]{1,0:T(1,128)} %refs_0_.1) | copy-start | bytes 52
  82.4 30.2 %all-to-all-start = ((bf16[8,128,128]{2,1,0:T(8,128)(2,1)}), bf16[8,128,128]{2,1,0:T(8,128)(2,1)S(1)}, u32[]{:S(2)}, u32[]{:S(2)}) async-start(bf16[8,128,128]{2,1,0:T(8,128)(2,1)} %get-tuple-element.69), calls=%async_computation | async-start | bytes 524288 | tf_op jit(solution)/shard_map/all_to_all | solution.py:1322
  86.1 16.0 %collective-permute-start.10 = (bf16[128,1024]{1,0:T(8,128)(2,1)}, bf16[128,1024]{1,0:T(8,128)(2,1)S(1)}, u32[]{:S(2)}, u32[]{:S(2)}) collective-permute-start(bf16[128,1024]{1,0:T(8,128)(2,1)} %get-tuple-element.72.refs_2_.refs_9_), channel_id=1, source_target_pairs={{0,2},{1,3},{2,0},{3,1},{4,6},{5,7},{6,4},{7,5},{8,10},{9,11},{10,... | collective-permute-start | bytes 786440 | tf_op jit(solution)/shard_map/ppermute | solution.py:317
  88.2 24.5 %collective-permute-start.11 = (bf16[128,1024]{1,0:T(8,128)(2,1)}, bf16[128,1024]{1,0:T(8,128)(2,1)S(1)}, u32[]{:S(2)}, u32[]{:S(2)}) collective-permute-start(bf16[128,1024]{1,0:T(8,128)(2,1)} %get-tuple-element.72.refs_2_.refs_9_), channel_id=1, source_target_pairs={{0,4},{1,5},{2,6},{3,7},{4,0},{5,1},{6,2},{7,3},{8,12},{9,13},{10,... | collective-permute-start | bytes 786440 | tf_op jit(solution)/shard_map/ppermute | solution.py:317
  90.5 43.0 %collective-permute-start.24 = (bf16[128,1024]{1,0:T(8,128)(2,1)}, bf16[128,1024]{1,0:T(8,128)(2,1)S(1)}, u32[]{:S(2)}, u32[]{:S(2)}) collective-permute-start(bf16[128,1024]{1,0:T(8,128)(2,1)} %get-tuple-element.72.refs_2_.refs_9_), channel_id=1, source_target_pairs={{0,6},{1,7},{2,4},{3,5},{4,2},{5,3},{6,0},{7,1},{8,14},{9,15},{10,... | collective-permute-start | bytes 786440 | tf_op jit(solution)/shard_map/ppermute | solution.py:317
  102.1 10.6 %copy-start.9 = (bf16[128,1024]{1,0:T(8,128)(2,1)}, bf16[128,1024]{1,0:T(8,128)(2,1)S(1)}, u32[]{:S(2)}) copy-start(bf16[128,1024]{1,0:T(8,128)(2,1)S(1)} %collective-permute-done.10.refs_3_.refs_10_) | copy-start | bytes 786436
  128.0 61.8 %all-to-all-start.1 = ((bf16[8,128,384]{2,1,0:T(8,128)(2,1)}), bf16[8,128,384]{2,1,0:T(8,128)(2,1)S(1)}, u32[]{:S(2)}, u32[]{:S(2)}) async-start(bf16[8,128,384]{2,1,0:T(8,128)(2,1)} %get-tuple-element.73), calls=%async_computation.1 | async-start | bytes 1572864 | tf_op jit(solution)/shard_map/all_to_all | solution.py:1330
  131.8 11.7 %collective-permute-start.18 = (f32[8,4096]{1,0:T(8,128)}, f32[8,4096]{1,0:T(8,128)S(1)}, u32[]{:S(2)}, u32[]{:S(2)}) collective-permute-start(f32[8,4096]{1,0:T(8,128)} %get-tuple-element.76), channel_id=1, source_target_pairs={{0,1},{1,0},{2,3},{3,2},{4,5},{5,4},{6,7},{7,6},{8,9},{9,8},{10,11... | collective-permute-start | bytes 393224 | tf_op jit(solution)/shard_map/ppermute | solution.py:317
  134.2 13.3 %copy-start.11 = (bf16[128,1024]{1,0:T(8,128)(2,1)S(1)}, bf16[128,1024]{1,0:T(8,128)(2,1)}, u32[]{:S(2)}) copy-start(bf16[128,1024]{1,0:T(8,128)(2,1)} %get-tuple-element.88) | copy-start | bytes 786436
  134.2 27.0 %copy-start.6 = (bf16[128,1024]{1,0:T(8,128)(2,1)S(1)}, bf16[128,1024]{1,0:T(8,128)(2,1)}, u32[]{:S(2)}) copy-start(bf16[128,1024]{1,0:T(8,128)(2,1)} %shard_map.249.refs_5_) | copy-start | bytes 786436
  143.4 29.1 %collective-permute-start.25 = (bf16[512,1408]{1,0:T(8,128)(2,1)}, bf16[512,1408]{1,0:T(8,128)(2,1)}, u32[]{:S(2)}, u32[]{:S(2)}) collective-permute-start(bf16[512,1408]{1,0:T(8,128)(2,1)} %get-tuple-element.87), channel_id=1, source_target_pairs={{0,8},{8,0},{16,24},{24,16},{1,9},{9,1},{17,25},{25,17},{2,10},{10... | collective-permute-start | bytes 4325384 | tf_op jit(solution)/shard_map/ppermute | solution.py:317
  143.5 16.0 %collective-permute-start.20 = (f32[8,4096]{1,0:T(8,128)S(1)}, f32[8,4096]{1,0:T(8,128)S(1)}, u32[]{:S(2)}, u32[]{:S(2)}) collective-permute-start(f32[8,4096]{1,0:T(8,128)S(1)} %add.98), channel_id=1, source_target_pairs={{0,4},{1,5},{2,6},{3,7},{4,0},{5,1},{6,2},{7,3},{8,12},{9,13},{10,... | collective-permute-start | bytes 393224 | tf_op jit(solution)/shard_map/ppermute | solution.py:317
  146.0 13.5 %collective-permute-start.21 = (f32[8,4096]{1,0:T(8,128)S(1)}, f32[8,4096]{1,0:T(8,128)S(1)}, u32[]{:S(2)}, u32[]{:S(2)}) collective-permute-start(f32[8,4096]{1,0:T(8,128)S(1)} %add.98), channel_id=1, source_target_pairs={{0,6},{1,7},{2,4},{3,5},{4,2},{5,3},{6,0},{7,1},{8,14},{9,15},{10,... | collective-permute-start | bytes 393224 | tf_op jit(solution)/shard_map/ppermute | solution.py:317
  147.4 12.1 %collective-permute-start.19 = (f32[8,4096]{1,0:T(8,128)S(1)}, f32[8,4096]{1,0:T(8,128)S(1)}, u32[]{:S(2)}, u32[]{:S(2)}) collective-permute-start(f32[8,4096]{1,0:T(8,128)S(1)} %add.98), channel_id=1, source_target_pairs={{0,2},{1,3},{2,0},{3,1},{4,6},{5,7},{6,4},{7,5},{8,10},{9,11},{10,... | collective-permute-start | bytes 393224 | tf_op jit(solution)/shard_map/ppermute | solution.py:317
  159.6 12.9 %copy-start.8 = (f32[8,4096]{1,0:T(8,128)}, f32[8,4096]{1,0:T(8,128)S(1)}, u32[]{:S(2)}) copy-start(f32[8,4096]{1,0:T(8,128)S(1)} %add_add_fusion.refs_1_) | copy-start | bytes 393220
  159.6 6.5 %collective-permute-start.22 = (f32[8,4096]{1,0:T(8,128)S(1)}, f32[8,4096]{1,0:T(8,128)S(1)}, u32[]{:S(2)}, u32[]{:S(2)}) collective-permute-start(f32[8,4096]{1,0:T(8,128)S(1)} %add_add_fusion.refs_1_), channel_id=1, source_target_pairs={{0,16},{8,24},{16,0},{24,8},{1,17},{9,25},{17,1},{25,9},{2,18},{10... | collective-permute-start | bytes 393224 | tf_op jit(solution)/shard_map/ppermute | solution.py:317
  161.2 9.5 %collective-permute-start.28 = (bf16[128,1536]{1,0:T(8,128)(2,1)S(1)}, bf16[128,1536]{1,0:T(8,128)(2,1)S(1)}, u32[]{:S(2)}, u32[]{:S(2)}) collective-permute-start(bf16[128,1536]{1,0:T(8,128)(2,1)S(1)} %pad_maximum_fusion.4), channel_id=1, source_target_pairs={{0,16},{8,24},{16,0},{24,8},{1,17},{9,25},{17,1},{25,9},{2,18},{10... | collective-permute-start | bytes 1179656 | tf_op jit(solution)/shard_map/ppermute | solution.py:317
  166.1 4.9 %collective-permute-start.23 = (f32[16,4096]{1,0:T(8,128)S(1)}, f32[16,4096]{1,0:T(8,128)S(1)}, u32[]{:S(2)}, u32[]{:S(2)}) collective-permute-start(f32[16,4096]{1,0:T(8,128)S(1)} %pad_maximum_fusion.5), channel_id=1, source_target_pairs={{0,8},{8,0},{16,24},{24,16},{1,9},{9,1},{17,25},{25,17},{2,10},{10... | collective-permute-start | bytes 786440 | tf_op jit(solution)/shard_map/ppermute | solution.py:317
  170.9 4.8 %collective-permute-start.29 = (bf16[256,1280]{1,0:T(8,128)(2,1)S(1)}, bf16[256,1280]{1,0:T(8,128)(2,1)S(1)}, u32[]{:S(2)}, u32[]{:S(2)}) collective-permute-start(bf16[256,1280]{1,0:T(8,128)(2,1)S(1)} %pad_maximum_fusion.3), channel_id=1, source_target_pairs={{0,8},{8,0},{16,24},{24,16},{1,9},{9,1},{17,25},{25,17},{2,10},{10... | collective-permute-start | bytes 1966088 | tf_op jit(solution)/shard_map/ppermute | solution.py:317
  175.1 14.4 %collective-permute-start.26 = (bf16[512,512]{1,0:T(8,128)(2,1)S(1)}, bf16[512,512]{1,0:T(8,128)(2,1)S(1)}, u32[]{:S(2)}, u32[]{:S(2)}) collective-permute-start(bf16[512,512]{1,0:T(8,128)(2,1)S(1)} %select_convert_fusion), channel_id=1, source_target_pairs={{0,1},{1,0},{2,3},{3,2},{4,5},{5,4},{6,7},{7,6},{8,9},{9,8},{10,11... | collective-permute-start | bytes 1572872 | tf_op jit(solution)/shard_map/ppermute | solution.py:317
  189.8 26.2 %all-to-all-start.3 = ((bf16[8,128,256]{2,1,0:T(8,128)(2,1)}), bf16[8,128,256]{2,1,0:T(8,128)(2,1)S(1)}, u32[]{:S(2)}, u32[]{:S(2)}) async-start(bf16[8,128,256]{2,1,0:T(8,128)(2,1)} %bitcast.73), calls=%async_computation.3 | async-start | bytes 1048576 | tf_op jit(solution)/shard_map/all_to_all | solution.py:1398
  196.0 19.0 %collective-permute-start.27 = (bf16[8,32,896]{2,1,0:T(8,128)(2,1)S(1)}, bf16[8,32,896]{2,1,0:T(8,128)(2,1)S(1)}, u32[]{:S(2)}, u32[]{:S(2)}) collective-permute-start(bf16[8,32,896]{2,1,0:T(8,128)(2,1)S(1)} %fusion.2), channel_id=1, source_target_pairs={{0,16},{8,24},{16,0},{24,8},{1,17},{9,25},{17,1},{25,9},{2,18},{10... | collective-permute-start | bytes 1376264 | tf_op jit(solution)/shard_map/ppermute | solution.py:317
  197.8 32.7 %copy-start.19 = (f32[32,1024]{1,0:T(8,128)}, f32[32,1024]{1,0:T(8,128)S(1)}, u32[]{:S(2)}) copy-start(f32[32,1024]{1,0:T(8,128)S(1)} %fusion.10.refs_7_) | copy-start | bytes 393220
  205.2 4.5 %collective-permute-start.12 = (f32[8,2048]{1,0:T(8,128)}, f32[8,2048]{1,0:T(8,128)S(1)}, u32[]{:S(2)}, u32[]{:S(2)}) collective-permute-start(f32[8,2048]{1,0:T(8,128)} %get-tuple-element.75.refs_7_), channel_id=1, source_target_pairs={{0,1},{1,0},{2,3},{3,2},{4,5},{5,4},{6,7},{7,6},{8,9},{9,8},{10,11... | collective-permute-start | bytes 196616 | tf_op jit(solution)/shard_map/ppermute | solution.py:317
  210.6 10.5 %collective-permute-start.14 = (f32[8,2048]{1,0:T(8,128)S(1)}, f32[8,2048]{1,0:T(8,128)S(1)}, u32[]{:S(2)}, u32[]{:S(2)}) collective-permute-start(f32[8,2048]{1,0:T(8,128)S(1)} %add.94), channel_id=1, source_target_pairs={{0,4},{1,5},{2,6},{3,7},{4,0},{5,1},{6,2},{7,3},{8,12},{9,13},{10,... | collective-permute-start | bytes 196616 | tf_op jit(solution)/shard_map/ppermute | solution.py:317
  213.5 7.5 %collective-permute-start.15 = (f32[8,2048]{1,0:T(8,128)S(1)}, f32[8,2048]{1,0:T(8,128)S(1)}, u32[]{:S(2)}, u32[]{:S(2)}) collective-permute-start(f32[8,2048]{1,0:T(8,128)S(1)} %add.94), channel_id=1, source_target_pairs={{0,6},{1,7},{2,4},{3,5},{4,2},{5,3},{6,0},{7,1},{8,14},{9,15},{10,... | collective-permute-start | bytes 196616 | tf_op jit(solution)/shard_map/ppermute | solution.py:317
  215.0 6.1 %collective-permute-start.13 = (f32[8,2048]{1,0:T(8,128)S(1)}, f32[8,2048]{1,0:T(8,128)S(1)}, u32[]{:S(2)}, u32[]{:S(2)}) collective-permute-start(f32[8,2048]{1,0:T(8,128)S(1)} %add.94), channel_id=1, source_target_pairs={{0,2},{1,3},{2,0},{3,1},{4,6},{5,7},{6,4},{7,5},{8,10},{9,11},{10,... | collective-permute-start | bytes 196616 | tf_op jit(solution)/shard_map/ppermute | solution.py:317
  216.0 13.8 %all-to-all-start.2 = ((bf16[8,32,640]{2,1,0:T(8,128)(2,1)}), bf16[8,32,640]{2,1,0:T(8,128)(2,1)S(1)}, u32[]{:S(2)}, u32[]{:S(2)}) async-start(bf16[8,32,640]{2,1,0:T(8,128)(2,1)} %slice.181), calls=%async_computation.2 | async-start | bytes 655360 | tf_op jit(solution)/shard_map/all_to_all | solution.py:1379
  221.1 17.8 %copy-start.17 = (f32[8,2048]{1,0:T(8,128)}, f32[8,2048]{1,0:T(8,128)S(1)}, u32[]{:S(2)}) copy-start(f32[8,2048]{1,0:T(8,128)S(1)} %add_add_fusion.1.refs_1_) | copy-start | bytes 196612
  221.1 4.3 %collective-permute-start.16 = (f32[8,2048]{1,0:T(8,128)S(1)}, f32[8,2048]{1,0:T(8,128)S(1)}, u32[]{:S(2)}, u32[]{:S(2)}) collective-permute-start(f32[8,2048]{1,0:T(8,128)S(1)} %add_add_fusion.1.refs_1_), channel_id=1, source_target_pairs={{0,16},{8,24},{16,0},{24,8},{1,17},{9,25},{17,1},{25,9},{2,18},{10... | collective-permute-start | bytes 196616 | tf_op jit(solution)/shard_map/ppermute | solution.py:317
  225.5 13.4 %copy-start.26 = (f32[8,2048]{1,0:T(8,128)}, f32[8,2048]{1,0:T(8,128)S(1)}, u32[]{:S(2)}) copy-start(f32[8,2048]{1,0:T(8,128)S(1)} %collective-permute-done.16.refs_3_) | copy-start | bytes 196612
  225.5 13.4 %collective-permute-start.17 = (f32[16,2048]{1,0:T(8,128)S(1)}, f32[16,2048]{1,0:T(8,128)S(1)}, u32[]{:S(2)}, u32[]{:S(2)}) collective-permute-start(f32[16,2048]{1,0:T(8,128)S(1)} %pad_maximum_fusion.8), channel_id=1, source_target_pairs={{0,8},{8,0},{16,24},{24,16},{1,9},{9,1},{17,25},{25,17},{2,10},{10... | collective-permute-start | bytes 393224 | tf_op jit(solution)/shard_map/ppermute | solution.py:317
  229.9 10.5 %collective-permute-start.31 = (bf16[256,1024]{1,0:T(8,128)(2,1)S(1)}, bf16[256,1024]{1,0:T(8,128)(2,1)S(1)}, u32[]{:S(2)}, u32[]{:S(2)}) collective-permute-start(bf16[256,1024]{1,0:T(8,128)(2,1)S(1)} %maximum_dynamic-update-slice_fusion.refs_1_), channel_id=1, source_target_pairs={{0,16},{8,24},{16,0},{24,8},{1,17},{9,25},{17,1},{25,9},{2,18},{10... | collective-permute-start | bytes 1572872 | tf_op jit(solution)/shard_map/ppermute | solution.py:317
  239.0 7.7 %collective-permute-start.30 = (bf16[256,1024]{1,0:T(8,128)(2,1)S(1)}, bf16[256,1024]{1,0:T(8,128)(2,1)S(1)}, u32[]{:S(2)}, u32[]{:S(2)}) collective-permute-start(bf16[256,1024]{1,0:T(8,128)(2,1)S(1)} %maximum_dynamic-update-slice_fusion.refs_1_), channel_id=1, source_target_pairs={{0,8},{8,0},{16,24},{24,16},{1,9},{9,1},{17,25},{25,17},{2,10},{10... | collective-permute-start | bytes 1572872 | tf_op jit(solution)/shard_map/ppermute | solution.py:317
  240.4 6.2 %collective-permute-start.32 = (bf16[256,1024]{1,0:T(8,128)(2,1)S(1)}, bf16[256,1024]{1,0:T(8,128)(2,1)S(1)}, u32[]{:S(2)}, u32[]{:S(2)}) collective-permute-start(bf16[256,1024]{1,0:T(8,128)(2,1)S(1)} %collective-permute-done.31.refs_3_), channel_id=1, source_target_pairs={{0,8},{8,0},{16,24},{24,16},{1,9},{9,1},{17,25},{25,17},{2,10},{10... | collective-permute-start | bytes 1572872 | tf_op jit(solution)/shard_map/ppermute | solution.py:317
  (22 other events, 87.5 us)

commit v2 on v1

--- a/solution.py
+++ b/solution.py
@@ -321,9 +321,11 @@
     return [value] + [swapped_with(value, "blk", k) for k in range(2, count, 2)]
 
 
-def gathered_blocks(value, count):
+def gathered_blocks(value, count, zero):
     evens = even_blocks(value, count)
-    return evens, [swapped_with(e, "blk", 1) for e in evens]
+    return evens, [swapped_with(e, "blk", 1) for e in evens[:1]] + [
+        swapped_with(e + zero, "blk", 1) for e in evens[1:]
+    ]
 
 
 def offset_of(index, count):
@@ -377,14 +379,12 @@
 
 
 def prepare_kernel(
-    count, me_ref, lengths_ref, steps_ref, table_ref, freq_ref, w_ref, b_ref, later_ref, *refs
+    count, me_ref, lengths_ref, steps_ref, table_ref, freq_ref, w_ref, b_ref, *refs
 ):
     silu, sems = refs[-2:]
-    kept = (len(refs) - 10) // 2
+    kept = (len(refs) - 9) // 2
     sources, targets = refs[:kept], refs[-2 - kept : -2]
-    out_ref, silu_ref, clip_ref, cliprow_ref, cos_ref, sin_ref, marks_ref, passed_ref = refs[
-        kept : kept + 8
-    ]
+    out_ref, silu_ref, clip_ref, cliprow_ref, cos_ref, sin_ref, marks_ref = refs[kept : kept + 7]
     clips = lengths_ref.shape[1]
     rows = cos_ref.shape[0] // count
     i = pl.program_id(0)
@@ -401,7 +401,6 @@
     def _():
         for copy in copies():
             copy.start()
-        passed_ref[...] = later_ref[...]
         for c in range(clips):
             row = table_ref[pl.ds(steps_ref[0, c], 1), :]
             silu[c : c + 1, :] = row / (1.0 + jnp.exp(-row))
@@ -442,7 +441,7 @@
             copy.wait()
 
 
-def prepare(me, lengths, steps, step_table, freqs, w_mod, b_mod, later, weights, own_rows, count):
+def prepare(me, lengths, steps, step_table, freqs, w_mod, b_mod, weights, own_rows, count):
     width = w_mod.shape[0]
     clips = lengths.shape[1]
     tile = width
@@ -455,7 +454,6 @@
         shape_of((rows, LANES), F32),
         shape_of((rows, LANES), F32),
         shape_of((rows, 2 * LANES)),
-        shape_of(later.shape, later.dtype),
     ]
     return pl.pallas_call(
         lambda *refs: prepare_kernel(count, *refs),
@@ -466,7 +464,6 @@
             full(freqs.shape),
             pl.BlockSpec((width, tile), lambda i: (0, i)),
             pl.BlockSpec((1, tile), lambda i: (0, i)),
-            full(later.shape),
         ]
         + [ANYWHERE] * len(weights),
         out_specs=[pl.BlockSpec((clips, tile), lambda i: (0, i))]
@@ -476,7 +473,7 @@
         scratch_shapes=[pltpu.VMEM((8, width), F32), pltpu.SemaphoreType.DMA((len(weights),))],
         compiler_params=params(),
         cost_estimate=cost(4 * clips * width * width, 5 * width * width),
-    )(me, lengths, steps, *all_in_hbm([step_table, freqs, w_mod, b_mod, later, *weights]))
+    )(me, lengths, steps, *all_in_hbm([step_table, freqs, w_mod, b_mod, *weights]))
 
 
 def modulate_kernel(silu_ref, w_ref, b_ref, out_ref):
@@ -501,12 +498,14 @@
 
 
 def project_kernel(clips, with_own, me_ref, clip_ref, mod_ref, b_ref, cos_ref, sin_ref, w, *refs):
-    blocks = refs[: len(refs) - (4 if with_own else 3)]
+    blocks = refs[: len(refs) - (5 if with_own else 3)]
     h_ref, kv_ref, q_ref = refs[len(blocks) : len(blocks) + 3]
     rows, width = blocks[0].shape
     column = pl.multiple_of(me_ref[0] * LANES, LANES)
     if with_own:
-        own_ref = refs[-1]
+        own_ref, passed_ref = refs[-2:]
+        passed_ref[...] = blocks[-1][...]
+        blocks = blocks[:-1]
 
     mod = mod_ref[...]
     for pair in range(len(blocks) // 2):
@@ -541,7 +540,8 @@
                 kv_ref[(at - width) // LANES] = piece.astype(BF)
 
 
-def project(half, blocks, me, clip_col, modulation, w_qkv, b_qkv, cosine, sine, with_own):
+def project(half, blocks, me, clip_col, modulation, w_qkv, b_qkv, cosine, sine, passed=None):
+    with_own = passed is not None
     own_rows, width = blocks[0].shape
     rows = own_rows * len(blocks)
     clips = modulation.shape[0]
@@ -551,7 +551,8 @@
         shape_of((rows, LANES)),
     ]
     if with_own:
-        out_shape.append(shape_of((own_rows, width)))
+        out_shape += [shape_of((own_rows, width)), shape_of(passed.shape)]
+        blocks = blocks + [passed]
     return pl.pallas_call(
         lambda *refs: project_kernel(clips, with_own, *refs),
         grid=(1,),
@@ -595,9 +596,27 @@
     return expo, 1.0 / jnp.sum(expo, axis=0, keepdims=True)
 
 
-def attend_kernel(keymark_ref, rowmark_ref, q_ref, ka_ref, kb_ref, o_ref, keys, values, queries):
+def attend_kernel(keymark_ref, rowmark_ref, q_ref, ka_ref, kb_ref, *refs):
+    sources, o_ref, targets = refs[:3], refs[3], refs[4:7]
+    keys, values, queries, sems = refs[7:]
     half = ka_ref.shape[1]
     pair, pairs = pl.program_id(0), pl.num_programs(0)
+
+    def copies():
+        return [
+            pltpu.make_async_copy(source, target, sems.at[j])
+            for j, (source, target) in enumerate(zip(sources, targets))
+        ]
+
+    @pl.when(pair == 0)
+    def _():
+        for copy in copies():
+            copy.start()
+
+    @pl.when(pair == pairs - 1)
+    def _():
+        for copy in copies():
+            copy.wait()
 
     @pl.when(pair == 0)
     def _():
@@ -615,7 +634,7 @@
     o_ref[...] = head_diagonal(turned).astype(BF)
 
 
-def attend(q, kv_a, kv_b, marks):
+def attend(q, kv_a, kv_b, marks, weights):
     own_rows, width = q.shape
     rows = 2 * kv_a.shape[1]
     return pl.pallas_call(
@@ -627,17 +646,19 @@
             pl.BlockSpec((own_rows, LANES), lambda p: (0, p)),
             KEPT,
             KEPT,
-        ],
-        out_specs=pl.BlockSpec((own_rows, LANES), lambda p: (0, p)),
-        out_shape=shape_of((own_rows, width)),
+        ]
+        + [ANYWHERE] * 3,
+        out_specs=[pl.BlockSpec((own_rows, LANES), lambda p: (0, p))] + [KEPT] * 3,
+        out_shape=[shape_of((own_rows, width))] + [pltpu.VMEM(w.shape, BF) for w in weights],
         scratch_shapes=[
             pltpu.VMEM((rows, 2 * LANES), BF),
             pltpu.VMEM((rows, LANES), BF),
             pltpu.VMEM((2 * own_rows, 2 * LANES), BF),
+            pltpu.SemaphoreType.DMA((3,)),
         ],
         compiler_params=params(),
         cost_estimate=cost(4 * own_rows * rows * width, MIB),
-    )(*all_in_hbm([marks, marks, q]), kv_a, kv_b)
+    )(*all_in_hbm([marks, marks, q]), kv_a, kv_b, *all_in_hbm(weights))
 
 
 def probs_kernel(me_ref, keyclip_ref, rowclip_ref, qa_ref, qb_ref, ka_ref, kb_ref, *refs):
@@ -798,7 +819,8 @@
         *all_in_hbm([probs, q_a, q_b]),
         kv_a,
         kv_b,
-        *all_in_hbm([d_o, cosine, sine, *passed, *earlier]),
+        d_o,
+        *all_in_hbm([cosine, sine, *passed, *earlier]),
     )
 
 
@@ -857,15 +879,9 @@
 
 def middle_kernel(
     clips, steps_ref, clipc_ref, clipr_ref, x_ref, dy_ref, o_ref, mod_ref, bo_ref, bu_ref, bd_ref,
-    wo_hbm, wu_hbm, wd_hbm, *refs,
+    wo, wu, wd, *refs,
 ):
-    out_ref, h2_ref, dx_ref, da_ref, do_ref, sums_ref, wo, wu, wd, sems = refs[-10:]
-    copies = [
-        pltpu.make_async_copy(source, target, sems.at[i])
-        for i, (source, target) in enumerate([(wo_hbm, wo), (wu_hbm, wu), (wd_hbm, wd)])
-    ]
-    for copy in copies:
-        copy.start()
+    out_ref, h2_ref, dx_ref, da_ref, do_ref, sums_ref = refs[-6:]
     width = x_ref.shape[1]
     ffn = wu.shape[1]
     clip = clipc_ref[...]
@@ -876,14 +892,11 @@
     gate_one, scale_two, gate_two = frame_rows(2), 1.0 + frame_rows(4), frame_rows(5)
     upstream = dy_ref[...].astype(F32)
     d_ffn = (gate_two * upstream).astype(BF)
-    copies[0].wait()
     attn_out = dot_low(o_ref[...], wo[...]) + bo_ref[...]
     middle = x_ref[...].astype(F32) + gate_one * attn_out
     normed, rstd = norm_parts(middle)
     second = (normed * scale_two + frame_rows(3)).astype(BF)
     h2_ref[...] = second
-    copies[1].wait()
-    copies[2].wait()
     sums = RowSums(clipr_ref[...], clips)
     ffn_out = jnp.zeros(x_ref.shape, F32)
     d_second = jnp.zeros(x_ref.shape, F32)
@@ -942,23 +955,19 @@
         grid=(1,),
         in_specs=[SCALARS, full((rows, 1)), full((1, rows))]
         + [full(v.shape) for v in small[2:]]
-        + [ANYWHERE] * 3
+        + [KEPT] * 3
         + [ANYWHERE] * len(earlier),
         out_specs=[full(o.shape) for o in out_shape],
         out_shape=out_shape,
-        scratch_shapes=[
-            pltpu.VMEM(w_out.shape, BF),
-            pltpu.VMEM(w_up.shape, BF),
-            pltpu.VMEM(w_down.shape, BF),
-            pltpu.SemaphoreType.DMA((3,)),
-        ],
-        compiler_params=params(32),
+        compiler_params=params(),
         cost_estimate=cost(20 * rows * width * width, 3 * MIB),
-    )(steps, *all_in_hbm([*small, w_out, w_up, w_down, *earlier]))
+    )(steps, *all_in_hbm(small), w_out, w_up, w_down, *all_in_hbm(earlier))
 
 
 def last_kernel(clips, clipc_ref, clipr_ref, x_ref, mod_ref, dx_ref, d_ref, w_hbm, *refs):
-    out_ref, sums_ref, d_all, w, sems = refs[-5:]
+    passed = (len(refs) - 5) // 2
+    out_ref, sums_ref = refs[passed : passed + 2]
+    d_all, w, sems = refs[-3:]
     width = x_ref.shape[1]
     parts = 3
     copies = [
@@ -990,7 +999,7 @@
     sums_ref[:, width:] = sums.by_clip(d_first * normed) + sums.whole(d_all[:, 2 * width :], clips)
 
 
-def last_part(clip_col, clip_row, frames, modulation, d_middle, d_own, w_qkv, earlier):
+def last_part(clip_col, clip_row, frames, modulation, d_middle, d_own, w_qkv, passed):
     rows, width = frames.shape
     clips = modulation.shape[0]
     return pl.pallas_call(
@@ -1004,9 +1013,11 @@
             full(d_middle.shape),
             full(d_own.shape),
         ]
-        + [ANYWHERE] * (1 + len(earlier)),
-        out_specs=[full((rows, width)), full((8, 2 * width))],
-        out_shape=[shape_of((rows, width)), shape_of((8, 2 * width), F32)],
+        + [ANYWHERE] * (1 + len(passed)),
+        out_specs=[full((rows, width)), full((8, 2 * width))] + [ANYWHERE] * len(passed),
+        out_shape=[shape_of((rows, width)), shape_of((8, 2 * width), F32)]
+        + [shape_of(v.shape, v.dtype) for v in passed],
+        input_output_aliases={7 + i: 2 + i for i in range(len(passed))},
         scratch_shapes=[
             pltpu.VMEM((rows, 3 * width), BF),
             pltpu.VMEM(w_qkv.shape, BF),
@@ -1015,22 +1026,31 @@
         compiler_params=params(),
         cost_estimate=cost(6 * rows * width * width, 2 * MIB),
     )(
-        *all_in_hbm([clip_col, clip_row, frames, modulation, d_middle, d_own, w_qkv, *earlier]),
-    )
-
-
-def half_rows(core, value, kept_ref, sent_ref, at, columns):
+        *all_in_hbm([clip_col, clip_row, frames, modulation, d_middle]),
+        d_own,
+        *all_in_hbm([w_qkv, *passed]),
+    )
+
+
+def half_rows(core, value, kept_ref, sent_refs, at, columns):
     half = value.shape[0] // 2
     low, high = value[:half], value[half:]
     here = slice(at, at + half)
     kept_ref[here, columns] = jnp.where(core == 0, low, high)
-    sent_ref[here, columns] = jnp.where(core == 0, high, low).astype(BF)
+    sent = jnp.where(core == 0, high, low).astype(BF)
+    wide = sent_refs[0].shape[1]
+    for i, ref in enumerate(sent_refs):
+        start, stop = max(columns.start, i * wide), min(columns.stop, (i + 1) * wide)
+        if start < stop:
+            ref[here, start - i * wide : stop - i * wide] = sent[
+                :, start - columns.start : stop - columns.start
+            ]
 
 
 def weights_kernel(clips, count, who_ref, clip_ref, gate_ref, bu_ref, wu_hbm, wd_hbm, *refs):
-    kept_ref, sent_ref, up_sum, down_sum, wu, wd, sems = refs[-7:]
-    ha_ref, hb_ref, d_ref = refs[:3]
-    blocks = refs[3 : 3 + count]
+    kept_ref, sent_ref, (up_sum, down_sum, wu, wd, sems) = refs[-9], refs[-8:-5], refs[-5:]
+    ha_ref, hb_ref, d_ref, mine_ref, theirs_ref = refs[:5]
+    blocks = refs[5 : 5 + count]
     seconds, upstreams = blocks[: len(blocks) // 2], blocks[len(blocks) // 2 :]
     me, core = who_ref[0], who_ref[1]
     rows, width = seconds[0].shape
@@ -1055,6 +1075,17 @@
             half_rows(
                 core, value[inner : inner + LANES], kept_ref, sent_ref, (start + inner) // 2,
                 slice(0, columns),
+            )
+
+    left = jnp.concatenate([mine_ref[:, :width], theirs_ref[:, :width]], axis=0)
+    right = jnp.concatenate([mine_ref[:, width:], theirs_ref[:, width:]], axis=0)
+    at = columns + 2 * part
+    for start in range(0, width, step):
+        value = dot_rows(left[:, start : start + step], right)
+        for inner in range(0, step, LANES):
+            half_rows(
+                core, value[inner : inner + LANES], kept_ref, sent_ref, (start + inner) // 2,
+                slice(at, at + width // 2),
             )
 
     for copy in copies:
@@ -1090,14 +1121,14 @@
             )
 
 
-def weights_part(who, clip_col, modulation, b_up, w_up, w_down, h1_a, h1_b, d_qkv, seconds, upstreams):
+def weights_part(who, clip_col, modulation, b_up, w_up, w_down, h1_a, h1_b, d_qkv, outs, seconds, upstreams):
     width, ffn = w_up.shape
     count = 2 * len(seconds)
     part = 2 * ffn // count
     clips = modulation.shape[0]
-    shape = (width // 2, d_qkv.shape[1] + 2 * part)
+    shape = (width // 2, d_qkv.shape[1] + 2 * part + width // 2)
     rows = d_qkv.shape[0]
-    arrays = [h1_a, h1_b, d_qkv, *seconds, *upstreams]
+    arrays = [h1_a, h1_b, d_qkv, *outs, *seconds, *upstreams]
     return pl.pallas_call(
         lambda *refs: weights_kernel(clips, count, *refs),
         grid=(1,),
@@ -1110,8 +1141,8 @@
             ANYWHERE,
         ]
         + [full(v.shape) for v in arrays],
-        out_specs=[full(shape)] * 2,
-        out_shape=[shape_of(shape, F32), shape_of(shape)],
+        out_specs=[full(shape)] + [full((shape[0], shape[1] // 3))] * 3,
+        out_shape=[shape_of(shape, F32)] + [shape_of((shape[0], shape[1] // 3))] * 3,
         scratch_shapes=[
             pltpu.VMEM((width, part), F32),
             pltpu.VMEM((part, width), F32),
@@ -1183,7 +1214,7 @@
         pl.BlockSpec((rows, own), lambda i: (0, 0)),
         pl.BlockSpec((width, tile), lambda i: (0, skip + i)),
     ]
-    args = [place, *all_in_hbm([*sums, silu, w_mod])]
+    args = [place, *all_in_hbm([*sums, silu]), in_hbm(w_mod)]
     aliases = {}
     if first:
         in_specs += [ANYWHERE] * len(earlier)
@@ -1210,12 +1241,13 @@
             pl.BlockSpec(shapes[2].shape, lambda i: (0, 0)),
         ],
         out_shape=shapes,
-        scratch_shapes=[pltpu.VMEM((width, 2 * rows), F32), pltpu.VMEM((rows, tile), F32)],
+        scratch_shapes=[
+            pltpu.VMEM((width, 2 * rows), F32),
+            pltpu.VMEM((rows, tile), F32),
+        ],
         input_output_aliases=aliases,
         compiler_params=params(),
-        cost_estimate=pl.CostEstimate(
-            flops=4 * rows * width * columns, bytes_accessed=3 * width * columns, transcendentals=0
-        ),
+        cost_estimate=cost(rows * width, width),
     )(*args)
 
 
@@ -1223,16 +1255,128 @@
     return jnp.stack([jnp.where(bit == 0, mine, other), jnp.where(bit == 0, other, mine)])
 
 
-def everyone(sums, count):
-    pairs = sums + swapped_with(sums, "blk", 1)
-    others = [swapped_with(pairs, "blk", k) for k in range(2, count, 2)]
-    level = [pairs] + others
-    while len(level) > 1:
-        level = [level[i] + level[i + 1] for i in range(0, len(level), 2)]
-    sums = level[0]
-    far = swapped_with(sums, "batch", 2)
-    both = swapped_with(jnp.concatenate([sums, far], axis=0), "batch", 1)
-    return [sums, both[:8], far, both[8:]]
+def batch_parts(sums):
+    return [sums] + [swapped_with(sums, "batch", k) for k in range(1, 4)]
+
+
+def share_kernel(columns, part, who_ref, kept_ref, *refs):
+    others = refs[:3]
+    own_ref, x_ref, y_ref, both_ref, out_ref = refs[-5:]
+    far, odd = who_ref[2] // 2 == 1, who_ref[0] % 2 == 1
+    rows = own_ref.shape[1]
+    first, second = slice(columns, columns + part), slice(columns + part, columns + 2 * part)
+    for k in range(own_ref.shape[0]):
+        here = slice(2 * k * rows, 2 * (k + 1) * rows)
+        other = jnp.concatenate([ref[here, :] for ref in others], axis=1)
+        value = kept_ref[here, :] + other.astype(F32)
+        low, high = value[:rows], value[rows:]
+        near, away = jnp.where(far, high, low), jnp.where(far, low, high)
+        own_ref[k, :, :columns] = near[:, :columns]
+        own_ref[k, :, columns:] = jnp.where(odd, near[:, second], near[:, first])
+        y_ref[k] = jnp.where(odd, near[:, first], near[:, second]).astype(BF)
+        x_ref[k, :, :columns] = away[:, :columns].astype(BF)
+        x_ref[k, :, columns:] = jnp.where(odd, away[:, second], away[:, first]).astype(BF)
+        both_ref[k] = jnp.where(odd, away[:, first], away[:, second]).astype(BF)
+        out_ref[k] = jnp.concatenate(
+            [low[:, columns + 2 * part :], high[:, columns + 2 * part :]], axis=1
+        ).astype(BF)
+
+
+def share(who, kept, others, count, columns, part):
+    rows = kept.shape[0] // count // 2
+    width = 2 * (kept.shape[1] - columns - 2 * part)
+    shapes = [
+        shape_of((count, rows, columns + part), F32),
+        shape_of((count, rows, columns + part)),
+        shape_of((count, rows, part)),
+        shape_of((count, rows, part)),
+        shape_of((count, rows, width)),
+    ]
+    return pl.pallas_call(
+        lambda *refs: share_kernel(columns, part, *refs),
+        grid=(1,),
+        in_specs=[SCALARS, full(kept.shape)] + [full(v.shape) for v in others],
+        out_specs=[full(v.shape) for v in shapes],
+        out_shape=shapes,
+        compiler_params=params(),
+        cost_estimate=cost(0, 8 * MIB),
+    )(who, in_hbm(kept), *others)
+
+
+def gather_sums_kernel(columns, own_ref, x_ref, y_ref, both_ref, out_ref, *refs):
+    sent_ref, down_ref = refs[-2:]
+    count, rows, _ = own_ref.shape
+    shard = y_ref.shape[2] // 2
+    ready = columns + shard
+    for k in range(count):
+        from_x = x_ref[k].astype(F32)
+        sent_ref[k, :, :columns] = (own_ref[k, :, :columns] + from_x[:, :columns]).astype(BF)
+        value = (own_ref[k, :, columns:] + from_x[:, columns:]) + (
+            y_ref[k].astype(F32) + both_ref[k].astype(F32)
+        )
+        sent_ref[k, :, columns:ready] = value[:, :shard].astype(BF)
+        group, at = k % 2, k // 2 * shard
+        down_ref[group * rows : (group + 1) * rows, at : at + shard] = value[:, shard:].astype(BF)
+        sent_ref[k, :, ready:] = out_ref[k]
+
+
+def gather_sums(own, from_x, from_y, from_both, out_parts, columns, passed):
+    count, rows, _ = own.shape
+    width = out_parts.shape[2]
+    args = [own, from_x, from_y, from_both, out_parts]
+    shapes = [
+        shape_of((count, rows, columns + from_y.shape[2] // 2 + width)),
+        shape_of((2 * rows, width)),
+    ]
+    return pl.pallas_call(
+        lambda *refs: gather_sums_kernel(columns, *refs),
+        grid=(1,),
+        in_specs=[full(v.shape) for v in args] + [ANYWHERE] * len(passed),
+        out_specs=[ANYWHERE] * len(passed) + [full(v.shape) for v in shapes],
+        out_shape=[shape_of(v.shape, v.dtype) for v in passed] + shapes,
+        input_output_aliases={5 + i: i for i in range(len(passed))},
+        compiler_params=params(),
+        cost_estimate=cost(0, 4 * MIB),
+    )(in_hbm(own), from_x, from_y, from_both, *all_in_hbm([out_parts, *passed]))
+
+
+def rows_kernel(columns, rows_ref, down_ref, *refs):
+    out_ref = refs[-1]
+    count, rows, wide = rows_ref.shape
+    width = out_ref.shape[1]
+    shard = wide - width - columns
+    total = jnp.zeros((rows, width), F32)
+    for k in range(count):
+        for i in range(columns // LANES):
+            out_ref[i * rows : (i + 1) * rows, k * LANES : (k + 1) * LANES] = rows_ref[
+                k, :, i * LANES : (i + 1) * LANES
+            ]
+        piece = columns // LANES + k * shard // width
+        at = k * shard % width
+        out_ref[piece * rows : (piece + 1) * rows, at : at + shard] = rows_ref[
+            k, :, columns : columns + shard
+        ]
+        total += rows_ref[k, :, columns + shard :].astype(F32)
+    piece = columns // LANES + count * shard // width
+    out_ref[piece * rows : (piece + 2) * rows, :] = down_ref[...]
+    out_ref[(piece + 2) * rows :, :] = total.astype(BF)
+
+
+def gather_rows(rows_mine, down_rows, columns, passed, earlier):
+    count, rows, wide = rows_mine.shape
+    width = down_rows.shape[1]
+    shard = wide - width - columns
+    shape = ((columns // LANES + count * shard // width + 3) * rows, width)
+    return pl.pallas_call(
+        lambda *refs: rows_kernel(columns, *refs),
+        grid=(1,),
+        in_specs=[full(rows_mine.shape), full(down_rows.shape), ANYWHERE, ANYWHERE],
+        out_specs=[ANYWHERE, full(shape)],
+        out_shape=[shape_of(passed.shape, passed.dtype), shape_of(shape)],
+        input_output_aliases={2: 0},
+        compiler_params=params(),
+        cost_estimate=cost(0, 2 * MIB),
+    )(rows_mine, *all_in_hbm([down_rows, passed, earlier]))
 
 
 def assemble_kernel(ffn, who_ref, *refs):
@@ -1254,10 +1398,11 @@
             there = pl.multiple_of(core * 4 * rows + g * 2 * rows + far * rows, rows)
             down_ref[pl.ds(there, rows), :] = ref[here, :].astype(F32)
             piece += 1
-        part = width // 4
-        for g in range(4):
-            column = pl.multiple_of(owner * part, part)
-            out_ref[g * rows : (g + 1) * rows, pl.ds(column, part)] = ref[
+        part = width // 2
+        column = pl.multiple_of(far * part, part)
+        for g in range(2):
+            there = pl.multiple_of(core * 2 * rows + g * rows, rows)
+            out_ref[pl.ds(there, rows), pl.ds(column, part)] = ref[
                 piece * rows : (piece + 1) * rows, g * part : (g + 1) * part
             ].astype(F32)
 
@@ -1278,7 +1423,7 @@
         out_shape=shapes,
         compiler_params=params(),
         cost_estimate=cost(0, 6 * MIB),
-    )(who, *all_in_hbm(parts))
+    )(who, *parts)
 
 
 def heads_body(
@@ -1295,28 +1440,30 @@
     clips = clip_lengths.shape[1]
     rows = own_rows * count
 
-    evens, odds = gathered_blocks(frames, count)
     head_size = width // HEADS
     half = head_size // 2
     lane = jnp.arange(LANES, dtype=jnp.int32)
     freqs = 10000.0 ** (-2.0 * (lane % half).astype(F32) / head_size)
     rows_of_table = jnp.arange(step_table.shape[0], dtype=jnp.int32)
     (
-        modulation, silu_own, clip_col, clip_row, cosine, sine, marks, later, kept_qkv,
+        modulation, silu_own, clip_col, clip_row, cosine, sine, marks, kept_qkv,
     ) = prepare(
         me[None], clip_lengths, clip_steps, step_table, freqs[None, :], w_mod, b_mod[None, :],
-        cotangent, [w_qkv], own_rows, count,
+        [w_qkv], own_rows, count,
     )
     modulation_two = modulate(silu_own, w_mod, b_mod[None, :])
+    evens, odds = gathered_blocks(frames, count, (modulation_two[0, 0] * 0.0).astype(BF))
 
     shared = (me[None], clip_col, modulation, kept_qkv, b_qkv[None, :], cosine, sine)
-    h1_a, kv_a, q_a, q_own = project(0, evens, *shared, True)
+    h1_a, kv_a, q_a, q_own, later = project(0, evens, *shared, cotangent)
     upstreams = even_blocks(later, count)
-    h1_b, kv_b, q_b = project(1, odds, *shared, False)
-    attended = attend(q_own, kv_a, kv_b, marks)
+    h1_b, kv_b, q_b = project(1, odds, *shared)
+    attended, kept_out, kept_up, kept_down = attend(
+        q_own, kv_a, kv_b, marks, [w_out, w_up, w_down]
+    )
     result, second, d_middle, d_attn, d_o, sums_two = middle_part(
         clip_steps, clip_col, clip_row, frames, cotangent, attended, modulation_two,
-        b_out[None, :], b_up[None, :], b_down[None, :], w_out, w_up, w_down,
+        b_out[None, :], b_up[None, :], b_down[None, :], kept_out, kept_up, kept_down,
         upstreams,
     )
     d_o = lax.all_to_all(d_o, "blk", 0, 0, tiled=True)
@@ -1324,20 +1471,49 @@
     probs = heads_probs(
         me[None], q_a, q_b, kv_a, kv_b, clip_col, clip_row, count, [d_middle]
     )
-    d_qkv, d_qkv_sent, sums_two, d_attn = attend_back(
-        me[None], probs, q_a, q_b, kv_a, kv_b, d_o, cosine, sine, (sums_two, d_attn), seconds[:-1]
+    sums_two = sums_two + swapped_with(sums_two, "blk", 1)
+    sums_two = sums_two + swapped_with(sums_two, "blk", 2)
+
+    wide = width // 2
+    da_low, da_high = d_attn[:, :wide], d_attn[:, wide:]
+    out_sent = jnp.concatenate([attended, jnp.where(far == 0, da_high, da_low)], axis=1)
+    out_kept = jnp.concatenate([attended, jnp.where(far == 0, da_low, da_high)], axis=1)
+    out_sent = swapped_with(out_sent, "batch", 2)
+
+    d_qkv, d_qkv_sent, sums_two, out_sent = attend_back(
+        me[None], probs, q_a, q_b, kv_a, kv_b, d_o, cosine, sine, (sums_two, out_sent), seconds
     )
     d_own = lax.all_to_all(d_qkv_sent, "blk", 0, 0, tiled=True)
-
-    kept, sent = weights_part(
+    kept, *sent = weights_part(
         who, clip_col, modulation_two, b_up[None, :], w_up, w_down, h1_a, h1_b, d_qkv,
-        seconds, upstreams,
-    )
-
-    d_inputs, sums_one = last_part(
-        clip_col, clip_row, frames, modulation, d_middle, d_own, w_qkv, []
-    )
-    sums_two = everyone(sums_two, count)
+        [out_kept, out_sent], seconds, upstreams,
+    )
+    own_sums, for_x, for_y, for_both, out_parts = share(
+        who, kept, [swapped_with(v, "batch", 1) for v in sent], count, 3 * LANES, 2 * ffn // count
+    )
+
+    d_inputs, sums_one, own_sums, sums_two = last_part(
+        clip_col, clip_row, frames, modulation, d_middle, d_own, w_qkv,
+        [own_sums, sums_two],
+    )
+    sums_one = sums_one + swapped_with(sums_one, "blk", 1)
+    sums_two = sums_two + swapped_with(sums_two, "blk", 4)
+
+    pairs = [
+        (b * count + k, (b ^ 2) * count + (k ^ 1)) for b in range(4) for k in range(count)
+    ]
+    sums_one, sums_two, sent, down_rows = gather_sums(
+        own_sums,
+        swapped_with(for_x, "batch", 2),
+        swapped_with(for_y, "blk", 1),
+        lax.ppermute(for_both, ("batch", "blk"), pairs),
+        out_parts,
+        3 * LANES,
+        [sums_one, sums_two],
+    )
+    rows_mine = lax.all_to_all(sent, "blk", 0, 0, tiled=True)
+    sums_one = sums_one + swapped_with(sums_one, "blk", 2)
+    sums_two = batch_parts(sums_two)
     steps_all = jnp.stack([v[clips + 1, :clips] for v in sums_two]) * (1.0 / count)
     steps_all = steps_all[place ^ jnp.arange(4, dtype=jnp.int32)].astype(jnp.int32)
     pick_all = (steps_all[:, :, None] == rows_of_table[None, None, :]).astype(F32)
@@ -1346,9 +1522,10 @@
     silu_all = jax.nn.silu(condition_all).astype(BF)
     silu_cols = lax.dynamic_slice_in_dim(silu_all, me * own_rows, own_rows, 1)
     d_w_mod, d_b_mod, d_silu = table_part(
-        place[None], sums_two, silu_cols, w_mod, 2 * width, clips, earlier=[sums_one]
-    )
-    sums_one = everyone(sums_one, count)
+        place[None], sums_two, silu_cols, w_mod, 2 * width, clips
+    )
+    sums_one, mine = gather_rows(rows_mine, down_rows, 3 * LANES, sums_one, d_silu)
+    sums_one = batch_parts(sums_one + swapped_with(sums_one, "blk", 4))
     d_w_mod, d_b_mod, d_table = table_part(
         place[None], sums_one, silu_cols, w_mod, 0, clips,
         (condition_all, pick_all, d_silu, d_w_mod, d_b_mod),
@@ -1364,45 +1541,6 @@
     )
     d_b_out, d_b_up, d_b_down = jnp.split(bias_two, [width, width + ffn])
 
-    quarter = own_rows // 4
-    part = ffn // count
-    mine = kept + swapped_with(sent, "batch", 1).astype(F32)
-    first, even, odd = jnp.split(mine, [3 * LANES, 3 * LANES + 2 * part], axis=1)
-    sent = jnp.where(me % 2 == 0, odd, even).astype(BF)
-    both = jnp.where(me % 2 == 0, even, odd) + swapped_with(sent, "blk", 1).astype(F32)
-    columns = 3 * LANES + 2 * part
-    mine = jnp.concatenate([first, both], axis=1).reshape(count, 2, quarter, columns)
-    low, high = mine[:, 0], mine[:, 1]
-    sent = jnp.where(far == 0, high, low).astype(BF)
-    mine = jnp.where(far == 0, low, high) + swapped_with(sent, "batch", 2).astype(F32)
-    mine = mine.astype(BF)
-    rows_mine = lax.all_to_all(mine[:, :, : columns - part], "blk", 0, 0, tiled=True)
-    qkv_rows = [
-        jnp.transpose(rows_mine[:, :, i * LANES : (i + 1) * LANES], (1, 0, 2)).reshape(quarter, width)
-        for i in range(3)
-    ]
-    up_rows = jnp.transpose(rows_mine[:, :, 3 * LANES :], (1, 0, 2)).reshape(quarter, ffn)
-    down_rows = mine[:, :, columns - part :].reshape(width // part, 2, quarter, part)
-    down_rows = jnp.transpose(down_rows, (1, 2, 0, 3)).reshape(2 * quarter, width)
-
-    wide = width // 2
-    da_low, da_high = d_attn[:, :wide], d_attn[:, wide:]
-    sent = jnp.concatenate([attended, jnp.where(far == 0, da_high, da_low)], axis=1)
-    kept = jnp.concatenate([attended, jnp.where(far == 0, da_low, da_high)], axis=1)
-    pair = jnp.concatenate([kept, swapped_with(sent, "batch", 2)], axis=0)
-    left, low, high = pair[:, :width], pair[:, width : width + wide // 2], pair[:, width + wide // 2 :]
-    sent = jnp.concatenate([left, jnp.where(core == 0, high, low)], axis=1)
-    kept = jnp.concatenate([left, jnp.where(core == 0, low, high)], axis=1)
-    pair = jnp.concatenate([kept, swapped_with(sent, "batch", 1)], axis=0)
-    out_sums = dot_rows(pair[:, :width], pair[:, width:]).astype(BF).reshape(count, own_rows, -1)
-    out_sums = lax.all_to_all(out_sums, "blk", 0, 0, tiled=True)
-    out_sums = jnp.sum(out_sums.astype(F32), axis=0).astype(BF)
-    out_rows = jnp.concatenate(
-        [out_sums[g * quarter : (g + 1) * quarter] for g in range(4)], axis=1
-    )
-
-    pieces = qkv_rows + [up_rows[:, i * width : (i + 1) * width] for i in range(ffn // width)]
-    mine = jnp.concatenate(pieces + [down_rows, out_rows], axis=0)
     other = swapped_with(mine, "batch", 2)
     d_w_qkv, d_w_out, d_w_up, d_w_down = assemble(
         who,

time: 253 us -> 229 us (0.905)
  waiting for transfers between devices: 70.7 us -> 31 us
  Pallas kernels: 99.2 us -> 108 us
  other arithmetic: 7.11 us -> 14.1 us
    ppermute x33 -> x34, waiting for transfers between devices: 66.8 us -> 31 us  [swapped_with(): return lax.ppermute(value, axis, [(i, i ^ offset) for i in range(size)])]
    pallas_call x0 -> x3, Pallas kernels: none -> 8.11 us  [the longest x1 3.84 us: share(): pl.pallas_call(lambda *refs: share_kernel(columns, part, *refs), grid=(1,...]
    all_to_all x2 -> x1, starting transfers between devices: 11.2 us -> 4.26 us  [heads_body(): rows_mine = lax.all_to_all(sent, 'blk', 0, 0, tiled=True)]
    add x6 -> x9, other arithmetic: 3.58 us -> 8.57 us  [the longest x3 1.6 us: gathered_blocks(): e + zero]
    ppermute x33 -> x34, starting transfers between devices: 40.7 us -> 44.8 us  [swapped_with(): return lax.ppermute(value, axis, [(i, i ^ offset) for i in range(size)])]
    all_to_all x2 -> x1, waiting for transfers between devices: 3.92 us -> 0.01 us  [heads_body(): rows_mine = lax.all_to_all(sent, 'blk', 0, 0, tiled=True)]
    pallas_call x1, Pallas kernels: 12.2 us -> 8.93 us  [middle_part(): pl.pallas_call(lambda *refs: middle_kernel(clips, *refs), grid=(1,), in_s...]
    unnamed x75 -> x62, local copies, waits for them, and re-layouts: 8.68 us -> 9.7 us
  transfers between devices with their start and end apart: 37 -> 38, of which waited for: 12 -> 12; matrix products, arithmetic and copies ran while one was open for 5% -> 8% of each run, Pallas kernels for 33% -> 35%
where the time goes in v2:
time: 229 us; the launch traced here: 227 us
  Pallas kernels  108 us (47%)
  starting transfers between devices  59 us (26%)
  waiting for transfers between devices  31 us (14%)
  other arithmetic  14.1 us (6%)
  local copies, waits for them, and re-layouts  13.4 us (6%)
    ppermute x34, starting transfers between devices, swapped_with(): return lax.ppermute(value, axis, [(i, i ^ offset) for i in range(size)])  44.8 us
    ppermute x34, waiting for transfers between devices, swapped_with(): return lax.ppermute(value, axis, [(i, i ^ offset) for i in range(size)])  31 us
    pallas_call x1, Pallas kernels, attend_back(): pl.pallas_call(attend_back_kernel, grid_spec=grid_spec, out_shape=[shape_...  12.9 us
    pallas_call x2, Pallas kernels, project(): pl.pallas_call(lambda *refs: project_kernel(clips, with_own, *refs), grid...  12.2 us
    pallas_call x2, Pallas kernels, table_part(): pl.pallas_call(lambda *refs: table_kernel(first, clips, *refs), grid=(col...  12.1 us
    pallas_call x1, Pallas kernels, attend(): pl.pallas_call(attend_kernel, grid=(width // LANES,), in_specs=[pl.BlockS...  11.6 us
    unnamed x62, local copies, waits for them, and re-layouts  9.7 us
    pallas_call x1, Pallas kernels, weights_part(): pl.pallas_call(lambda *refs: weights_kernel(clips, count, *refs), grid=(1...  9.65 us
  transfers between devices with their start and end apart: 38, of which 12 were waited for; matrix products, arithmetic and copies ran while one was open for 8% of the time, Pallas kernels for 35%

profile of v2, /device:TPU:0, one launch (start us, length us, event | category | flops | bytes accessed | tf_op | source)
XLA Modules:
  0.0 227.2 jit_solution(13894634724279596162)
XLA Ops:
  0.6 3.1 %collective-permute-start = (bf16[128,1024]{1,0:T(8,128)(2,1)}, bf16[128,1024]{1,0:T(8,128)(2,1)S(1)}, u32[]{:S(2)}, u32[]{:S(2)}) collective-permute-start(bf16[128,1024]{1,0:T(8,128)(2,1)} %refs_2_.5), channel_id=1, source_target_pairs={{0,2},{1,3},{2,0},{3,1},{4,6},{5,7},{6,4},{7,5},{8,10},{9,11},{10,... | collective-permute-start | bytes 786440 | tf_op jit(solution)/shard_map/ppermute | solution.py:317
  3.7 2.6 %collective-permute-start.1 = (bf16[128,1024]{1,0:T(8,128)(2,1)}, bf16[128,1024]{1,0:T(8,128)(2,1)S(1)}, u32[]{:S(2)}, u32[]{:S(2)}) collective-permute-start(bf16[128,1024]{1,0:T(8,128)(2,1)} %refs_2_.5), channel_id=1, source_target_pairs={{0,4},{1,5},{2,6},{3,7},{4,0},{5,1},{6,2},{7,3},{8,12},{9,13},{10,... | collective-permute-start | bytes 786440 | tf_op jit(solution)/shard_map/ppermute | solution.py:317
  6.3 1.7 collective-permute-start.3
  9.9 6.2 %shard_map.246 = (f32[4,2048]{1,0:T(4,128)}, bf16[4,1024]{1,0:T(4,128)(2,1)}, s32[1024,1]{1,0:T(8,128)}, s32[1,1024]{1,0:T(1,128)}, f32[1024,128]{1,0:T(8,128)},...) custom-call(s32[1]{0:T(128)} %bitcast.refs_0_.me_ref, s32[1,4]{1,0:T(1,128)S(1)} %copy-done.8, ...), custom_call_target="tpu_custom_call" | custom-call | flops 16777216 | bytes 5242880 | tf_op jit(solution)/shard_map/pallas_call | solution.py:458
  16.1 7.6 %shard_map.248.refs_6_.refs_2_ = f32[4,4096]{1,0:T(4,128)} custom-call(bf16[4,1024]{1,0:T(4,128)(2,1)} %get-tuple-element.81.silu_ref, bf16[1024,6144]{1,0:T(8,128)(2,1)} %refs_6_.5, f32[1,6144]{1,0:T(1,128)} %bitcast.24), custom_call_target="tpu_custom_call" | custom-call | flops 33554432 | bytes 8388608 | tf_op jit(solution)/shard_map/pallas_call | solution.py:485
  26.8 1.7 collective-permute-start.5
  29.6 6.5 %shard_map.247 = (bf16[512,1024]{1,0:T(8,128)(2,1)}, bf16[16,512,128]{2,1,0:T(8,128)(2,1)S(1)}, bf16[512,128]{1,0:T(8,128)(2,1)}, bf16[128,1024]{1,0:T(8,128)(2,1)}, bf16[128,1024]{1,0:T(8,128)(2,1)}) custom-call(s32[1]{0:T(128)} %bitcast.refs_0_.me_ref, s32[1024,1]{1,0:T(8,128)} %get-tuple-element.72.refs_1_.keyclip_ref.refs_0_, ...), custom_call_target="tpu_custom_call" | custom-call | flops 2147483648 | bytes 6291456 | tf_op jit(solution)/shard_map/pallas_call | solution.py:556
  36.1 2.8 %collective-permute-start.7 = (bf16[128,1024]{1,0:T(8,128)(2,1)}, bf16[128,1024]{1,0:T(8,128)(2,1)S(1)}, u32[]{:S(2)}, u32[]{:S(2)}) collective-permute-start(bf16[128,1024]{1,0:T(8,128)(2,1)} %get-tuple-element.87.refs_13_.refs_15_), channel_id=1, source_target_pairs={{0,2},{1,3},{2,0},{3,1},{4,6},{5,7},{6,4},{7,5},{8,10},{9,11},{10,... | collective-permute-start | bytes 786440 | tf_op jit(solution)/shard_map/ppermute | solution.py:317
  38.9 1.6 collective-permute-start.8
  41.5 2.6 %collective-permute-done.6.refs_10_ = bf16[128,1024]{1,0:T(8,128)(2,1)} collective-permute-done((bf16[128,1024]{1,0:T(8,128)(2,1)}, bf16[128,1024]{1,0:T(8,128)(2,1)}, u32[]{:S(2)}, u32[]{:S(2)}) %collective-permute-start.6) | collective-permute-done | bytes 262176 | tf_op jit(solution)/shard_map/ppermute | solution.py:317
  44.0 2.8 %copy-done.1 = bf16[1024,3072]{1,0:T(8,128)(2,1)S(1)} copy-done((bf16[1024,3072]{1,0:T(8,128)(2,1)S(1)}, bf16[1024,3072]{1,0:T(8,128)(2,1)}, u32[]{:S(2)}) %copy-start.1) | copy-done | bytes 6291480
  46.8 5.7 %shard_map.249 = (bf16[512,1024]{1,0:T(8,128)(2,1)}, bf16[16,512,128]{2,1,0:T(8,128)(2,1)S(1)}, bf16[512,128]{1,0:T(8,128)(2,1)}) custom-call(s32[1]{0:T(128)} %bitcast.refs_0_.me_ref, s32[1024,1]{1,0:T(8,128)} %get-tuple-element.72.refs_1_.keyclip_ref.refs_0_, f32[4,2048]{1,0:T(4,128)} %get-tuple-element.75.refs_2_.refs_3_, f32[1,3072]{1,0:T(1,128)} %bitcast.26, ...), custom_call_target="tpu_custom_call" | custom-call | flops 2147483648 | bytes 6291456 | tf_op jit(solution)/shard_map/pallas_call | solution.py:556
  52.5 11.6 %shard_map.250 = (bf16[128,1024]{1,0:T(8,128)(2,1)}, bf16[1024,1024]{1,0:T(8,128)(2,1)S(1)}, bf16[1024,2048]{1,0:T(8,128)(2,1)S(1)}, bf16[2048,1024]{1,0:T(8,128)(2,1)S(1)}) custom-call(bf16[1024,256]{1,0:T(8,128)(2,1)} %get-tuple-element.74.keymark_ref.rowmark_ref, bf16[1024,256]{1,0:T(8,128)(2,1)} %get-tuple-element.74.keymark_ref.rowmark_ref, ...), custom_call_target="tpu_custom_call" | custom-call | flops 536870912 | bytes 1048576 | tf_op jit(solution)/shard_map/pallas_call | solution.py:640
  65.0 8.9 %shard_map.251 = (bf16[128,1024]{1,0:T(8,128)(2,1)}, bf16[128,1024]{1,0:T(8,128)(2,1)}, f32[128,1024]{1,0:T(8,128)}, bf16[128,1024]{1,0:T(8,128)(2,1)}, bf16[8,128,128]{2,1,0:T(8,128)(2,1)}, /*index=5*/f32[8,4096]{1,0:T(8,128)}) custom-call(s32[1,4]{1,0:T(1,128)S(1)} %copy-done.7, s32[1024,1]{1,0:T(8,128)} %get-tuple-element.72.refs_1_.keyclip_ref.refs_0_, ...), custom_call_target="tpu_custom_call" | custom-call | flops 2684354560 | bytes 3145728 | tf_op jit(solution)/shard_map/pallas_call | solution.py:953
  73.9 4.8 %all-to-all-start = ((bf16[8,128,128]{2,1,0:T(8,128)(2,1)}), bf16[8,128,128]{2,1,0:T(8,128)(2,1)S(1)}, u32[]{:S(2)}, u32[]{:S(2)}) async-start(bf16[8,128,128]{2,1,0:T(8,128)(2,1)} %get-tuple-element.92), calls=%async_computation | async-start | bytes 524288 | tf_op jit(solution)/shard_map/all_to_all | solution.py:1469
  80.6 1.5 collective-permute-start.12
  82.1 2.0 collective-permute-start.10
  85.6 2.4 %collective-permute-start.14 = (bf16[128,1024]{1,0:T(8,128)(2,1)}, bf16[128,1024]{1,0:T(8,128)(2,1)S(1)}, u32[]{:S(2)}, u32[]{:S(2)}) collective-permute-start(bf16[128,1024]{1,0:T(8,128)(2,1)} %get-tuple-element.95.refs_2_.refs_11_), channel_id=1, source_target_pairs={{0,4},{1,5},{2,6},{3,7},{4,0},{5,1},{6,2},{7,3},{8,12},{9,13},{10,... | collective-permute-start | bytes 786440 | tf_op jit(solution)/shard_map/ppermute | solution.py:317
  90.3 1.6 copy-done.3
  91.9 8.7 %shard_map.252.p_ref = f32[1024,2048]{1,0:T(8,128)} custom-call(s32[1]{0:T(128)} %bitcast.refs_0_.me_ref, s32[1024,1]{1,0:T(8,128)} %get-tuple-element.72.refs_1_.keyclip_ref.refs_0_, s32[1,1024]{1,0:T(1,128)} %get-tuple-element.73.refs_2_.rowclip_ref.refs_1_, bf16[512,128]{1,0:T(8,128)(2,1)} %get-tuple-element.90.qa_ref, ...), custom_call_target="tpu_custom_call" | custom-call | flops 536870912 | bytes 9437184 | tf_op jit(solution)/shard_map/pallas_call | solution.py:702
  100.6 1.6 collective-permute-done.11
  102.9 3.3 %collective-permute-done.14.refs_4_.refs_13_ = bf16[128,1024]{1,0:T(8,128)(2,1)S(1)} collective-permute-done((bf16[128,1024]{1,0:T(8,128)(2,1)}, bf16[128,1024]{1,0:T(8,128)(2,1)S(1)}, u32[]{:S(2)}, u32[]{:S(2)}) %collective-permute-start.14) | collective-permute-done | bytes 262176 | tf_op jit(solution)/shard_map/ppermute | solution.py:317
  107.2 1.6 copy-done.4
  108.8 12.9 %shard_map.253 = (bf16[1024,384]{1,0:T(8,128)(2,1)}, bf16[8,128,384]{2,1,0:T(8,128)(2,1)}, f32[8,4096]{1,0:T(8,128)}, bf16[128,1536]{1,0:T(8,128)(2,1)}) custom-call(s32[1]{0:T(128)} %bitcast.refs_0_.me_ref, f32[1024,2048]{1,0:T(8,128)} %shard_map.252.p_ref, ...), custom_call_target="tpu_custom_call", output_to_operand_aliasing={{2}: (9, {}), {3}: (10, {})} | custom-call | flops 1073741824 | bytes 12582912 | tf_op jit(solution)/shard_map/pallas_call | solution.py:805
  121.7 5.2 %all-to-all-start.1 = ((bf16[8,128,384]{2,1,0:T(8,128)(2,1)}), bf16[8,128,384]{2,1,0:T(8,128)(2,1)S(1)}, u32[]{:S(2)}, u32[]{:S(2)}) async-start(bf16[8,128,384]{2,1,0:T(8,128)(2,1)} %get-tuple-element.96), calls=%async_computation.1 | async-start | bytes 1572864 | tf_op jit(solution)/shard_map/all_to_all | solution.py:1486
  126.9 9.7 %shard_map.254 = (f32[512,1920]{1,0:T(8,128)}, bf16[512,640]{1,0:T(8,128)(2,1)}, bf16[512,640]{1,0:T(8,128)(2,1)}, bf16[512,640]{1,0:T(8,128)(2,1)}) custom-call(s32[3]{0:T(128)S(1)} %pad_add_fusion.refs_0_, s32[1024,1]{1,0:T(8,128)} %get-tuple-element.72.refs_1_.keyclip_ref.refs_0_, f32[4,4096]{1,0:T(4,128)} %shard_map.248.refs_6_.refs_2_, ...), custom_call_target="tpu_custom_call" | custom-call | flops 3758096384 | bytes 10485760 | tf_op jit(solution)/shard_map/pallas_call | solution.py:1132
  137.2 1.7 collective-permute-done.16.refs_2_
  140.8 3.8 %shard_map.255 = (f32[8,32,896]{2,1,0:T(8,128)}, bf16[8,32,896]{2,1,0:T(8,128)(2,1)}, bf16[8,32,512]{2,1,0:T(8,128)(2,1)}, bf16[8,32,512]{2,1,0:T(8,128)(2,1)}, bf16[8,32,1024]{2,1,0:T(8,128)(2,1)}) custom-call(s32[3]{0:T(128)S(1)} %pad_add_fusion.refs_0_, f32[512,1920]{1,0:T(8,128)} %get-tuple-element.101.refs_1_, ...), custom_call_target="tpu_custom_call" | custom-call | bytes 8388608 | tf_op jit(solution)/shard_map/pallas_call | solution.py:1295
  144.7 1.5 collective-permute-start.19
  146.2 2.0 collective-permute-start.20
  148.2 7.1 %shard_map.256 = (bf16[128,1024]{1,0:T(8,128)(2,1)}, f32[8,2048]{1,0:T(8,128)}, f32[8,32,896]{2,1,0:T(8,128)}, f32[8,4096]{1,0:T(8,128)}) custom-call(s32[1024,1]{1,0:T(8,128)} %get-tuple-element.72.refs_1_.keyclip_ref.refs_0_, s32[1,1024]{1,0:T(1,128)} %get-tuple-element.73.refs_2_.rowclip_ref.refs_1_, ...), custom_call_target="tpu_custom_call", output_to_operand_aliasing={{2}: (7, {}), {3}: (8, {})} | custom-call | flops 805306368 | bytes 2097152 | tf_op jit(solution)/shard_map/pallas_call | solution.py:1005
  155.3 2.9 %collective-permute-start.23 = (f32[8,4096]{1,0:T(8,128)}, f32[8,4096]{1,0:T(8,128)S(1)}, u32[]{:S(2)}, u32[]{:S(2)}) collective-permute-start(f32[8,4096]{1,0:T(8,128)} %get-tuple-element.114), channel_id=1, source_target_pairs={{0,4},{1,5},{2,6},{3,7},{4,0},{5,1},{6,2},{7,3},{8,12},{9,13},{10,... | collective-permute-start | bytes 393224 | tf_op jit(solution)/shard_map/ppermute | solution.py:317
  159.7 6.2 %collective-permute-done.22 = f32[8,2048]{1,0:T(8,128)S(1)} collective-permute-done((f32[8,2048]{1,0:T(8,128)}, f32[8,2048]{1,0:T(8,128)S(1)}, u32[]{:S(2)}, u32[]{:S(2)}) %collective-permute-start.22) | collective-permute-done | bytes 65568 | tf_op jit(solution)/shard_map/ppermute | solution.py:317
  167.4 1.6 add.97.refs_6_
  169.0 2.4 %shard_map.257 = (f32[8,2048]{1,0:T(8,128)}, f32[8,4096]{1,0:T(8,128)}, bf16[8,32,1664]{2,1,0:T(8,128)(2,1)}, bf16[64,1024]{1,0:T(8,128)(2,1)}) custom-call(f32[8,32,896]{2,1,0:T(8,128)} %get-tuple-element.108.refs_0_, bf16[8,32,896]{2,1,0:T(8,128)(2,1)S(1)} %collective-permute-done.19.refs_1_, ...), custom_call_target="tpu_custom_call", output_to_operand_aliasing={{0}: (5, {}), {1}: (6, {})} | custom-call | bytes 4194304 | tf_op jit(solution)/shard_map/pallas_call | solution.py:1331
  171.4 4.3 %all-to-all-start.2 = ((bf16[8,32,1664]{2,1,0:T(8,128)(2,1)}), bf16[8,32,1664]{2,1,0:T(8,128)(2,1)S(1)}, u32[]{:S(2)}, u32[]{:S(2)}) async-start(bf16[8,32,1664]{2,1,0:T(8,128)(2,1)} %get-tuple-element.115), calls=%async_computation.2 | async-start | bytes 1703936 | tf_op jit(solution)/shard_map/all_to_all | solution.py:1514
  175.7 1.6 collective-permute-start.26
  178.3 2.0 collective-permute-start.24
  180.3 3.9 %collective-permute-done.27.refs_4_ = f32[8,4096]{1,0:T(8,128)S(1)} collective-permute-done((f32[8,4096]{1,0:T(8,128)}, f32[8,4096]{1,0:T(8,128)S(1)}, u32[]{:S(2)}, u32[]{:S(2)}) %collective-permute-start.27) | collective-permute-done | bytes 131104 | tf_op jit(solution)/shard_map/ppermute | solution.py:317
  185.7 5.3 %collective-permute-done.24 = f32[8,2048]{1,0:T(8,128)S(1)} collective-permute-done((f32[8,2048]{1,0:T(8,128)}, f32[8,2048]{1,0:T(8,128)S(1)}, u32[]{:S(2)}, u32[]{:S(2)}) %collective-permute-start.24) | collective-permute-done | bytes 65568 | tf_op jit(solution)/shard_map/ppermute | solution.py:317
  192.5 7.2 %shard_map.258 = (f32[128,6144]{1,0:T(8,128)}, f32[1,6144]{1,0:T(1,128)}, f32[1024,64]{1,0:T(8,128)}) custom-call(s32[1]{0:T(128)} %bitcast.8.refs_0_, f32[8,4096]{1,0:T(8,128)} %get-tuple-element.118.refs_1_, f32[8,4096]{1,0:T(8,128)} %copy-done.25, f32[8,4096]{1,0:T(8,128)} %copy-done.26, f32[8,4096]{1,0:T(8,128)} %copy-done.27, ...), custom_call_target="tpu_custom_call" | custom-call | flops 32768 | bytes 1024 | tf_op jit(solution)/shard_map/pallas_call | solution.py:1234
  199.7 1.8 shard_map.259
  201.5 1.5 collective-permute-start.33
  204.2 4.5 %collective-permute-start.28 = (f32[8,2048]{1,0:T(8,128)}, f32[8,2048]{1,0:T(8,128)S(1)}, u32[]{:S(2)}, u32[]{:S(2)}) collective-permute-start(f32[8,2048]{1,0:T(8,128)} %get-tuple-element.120), channel_id=1, source_target_pairs={{0,4},{1,5},{2,6},{3,7},{4,0},{5,1},{6,2},{7,3},{8,12},{9,13},{10,... | collective-permute-start | bytes 196616 | tf_op jit(solution)/shard_map/ppermute | solution.py:317
  209.8 2.0 collective-permute-done.28
  215.7 2.0 collective-permute-done.30.refs_3_
  218.8 4.9 %shard_map.260 = (f32[128,6144]{1,0:T(8,128)}, f32[1,6144]{1,0:T(1,128)}, f32[32,1024]{1,0:T(8,128)}) custom-call(s32[1]{0:T(128)} %bitcast.8.refs_0_, f32[8,2048]{1,0:T(8,128)} %copy-done.22, f32[8,2048]{1,0:T(8,128)} %copy-done.28, f32[8,2048]{1,0:T(8,128)} %copy-done.29, f32[8,2048]{1,0:T(8,128)} %copy-done.30, ...), custom_call_target="tpu_custom_call", output_to_operand_aliasing={{0}: (10, {}), {1}: (11, {})} | custom-call | flops 32768 | bytes 1024 | tf_op jit(solution)/shard_map/pallas_call | solution.py:1234
  224.4 2.8 %shard_map.261 = (f32[128,3072]{1,0:T(8,128)}, f32[128,1024]{1,0:T(8,128)}, f32[128,2048]{1,0:T(8,128)}, f32[256,1024]{1,0:T(8,128)}) custom-call(s32[3]{0:T(128)S(1)} %pad_add_fusion.refs_0_, bf16[256,1024]{1,0:T(8,128)(2,1)S(1)} %copy-done.5, bf16[256,1024]{1,0:T(8,128)(2,1)S(1)} %collective-permute-done.32.refs_2_, ...), custom_call_target="tpu_custom_call" | custom-call | bytes 6291456 | tf_op jit(solution)/shard_map/pallas_call | solution.py:1418
  (139 shorter events, 31.9 us)
Async XLA Ops:
  0.6 24.9 %collective-permute-start = (bf16[128,1024]{1,0:T(8,128)(2,1)}, bf16[128,1024]{1,0:T(8,128)(2,1)S(1)}, u32[]{:S(2)}, u32[]{:S(2)}) collective-permute-start(bf16[128,1024]{1,0:T(8,128)(2,1)} %refs_2_.5), channel_id=1, source_target_pairs={{0,2},{1,3},{2,0},{3,1},{4,6},{5,7},{6,4},{7,5},{8,10},{9,11},{10,... | collective-permute-start | bytes 786440 | tf_op jit(solution)/shard_map/ppermute | solution.py:317
  3.7 22.2 %collective-permute-start.1 = (bf16[128,1024]{1,0:T(8,128)(2,1)}, bf16[128,1024]{1,0:T(8,128)(2,1)S(1)}, u32[]{:S(2)}, u32[]{:S(2)}) collective-permute-start(bf16[128,1024]{1,0:T(8,128)(2,1)} %refs_2_.5), channel_id=1, source_target_pairs={{0,4},{1,5},{2,6},{3,7},{4,0},{5,1},{6,2},{7,3},{8,12},{9,13},{10,... | collective-permute-start | bytes 786440 | tf_op jit(solution)/shard_map/ppermute | solution.py:317
  6.3 22.2 %collective-permute-start.2 = (bf16[128,1024]{1,0:T(8,128)(2,1)}, bf16[128,1024]{1,0:T(8,128)(2,1)S(1)}, u32[]{:S(2)}, u32[]{:S(2)}) collective-permute-start(bf16[128,1024]{1,0:T(8,128)(2,1)} %refs_2_.5), channel_id=1, source_target_pairs={{0,6},{1,7},{2,4},{3,5},{4,2},{5,3},{6,0},{7,1},{8,14},{9,15},{10,... | collective-permute-start | bytes 786440 | tf_op jit(solution)/shard_map/ppermute | solution.py:317
  6.3 32.6 %collective-permute-start.3 = (bf16[128,1024]{1,0:T(8,128)(2,1)}, bf16[128,1024]{1,0:T(8,128)(2,1)S(1)}, u32[]{:S(2)}, u32[]{:S(2)}) collective-permute-start(bf16[128,1024]{1,0:T(8,128)(2,1)} %refs_2_.5), channel_id=1, source_target_pairs={{0,1},{1,0},{2,3},{3,2},{4,5},{5,4},{6,7},{7,6},{8,9},{9,8},{10,11... | collective-permute-start | bytes 786440 | tf_op jit(solution)/shard_map/ppermute | solution.py:317
  16.1 13.5 %copy-start = (bf16[1024,3072]{1,0:T(8,128)(2,1)}, bf16[1024,3072]{1,0:T(8,128)(2,1)S(1)}, u32[]{:S(2)}) copy-start(bf16[1024,3072]{1,0:T(8,128)(2,1)S(1)} %get-tuple-element.78.refs_6_) | copy-start | bytes 18874372
  25.6 14.9 %collective-permute-start.4 = (bf16[128,1024]{1,0:T(8,128)(2,1)S(1)}, bf16[128,1024]{1,0:T(8,128)(2,1)S(1)}, u32[]{:S(2)}, u32[]{:S(2)}) collective-permute-start(bf16[128,1024]{1,0:T(8,128)(2,1)S(1)} %broadcast_add_fusion.2), channel_id=1, source_target_pairs={{0,1},{1,0},{2,3},{3,2},{4,5},{5,4},{6,7},{7,6},{8,9},{9,8},{10,11... | collective-permute-start | bytes 786440 | tf_op jit(solution)/shard_map/ppermute | solution.py:317
  26.8 14.7 %collective-permute-start.5 = (bf16[128,1024]{1,0:T(8,128)(2,1)}, bf16[128,1024]{1,0:T(8,128)(2,1)}, u32[]{:S(2)}, u32[]{:S(2)}) collective-permute-start(bf16[128,1024]{1,0:T(8,128)(2,1)} %broadcast_add_fusion.1), channel_id=1, source_target_pairs={{0,1},{1,0},{2,3},{3,2},{4,5},{5,4},{6,7},{7,6},{8,9},{9,8},{10,11... | collective-permute-start | bytes 786440 | tf_op jit(solution)/shard_map/ppermute | solution.py:317
  29.3 14.7 %collective-permute-start.6 = (bf16[128,1024]{1,0:T(8,128)(2,1)}, bf16[128,1024]{1,0:T(8,128)(2,1)}, u32[]{:S(2)}, u32[]{:S(2)}) collective-permute-start(bf16[128,1024]{1,0:T(8,128)(2,1)} %broadcast_add_fusion), channel_id=1, source_target_pairs={{0,1},{1,0},{2,3},{3,2},{4,5},{5,4},{6,7},{7,6},{8,9},{9,8},{10,11... | collective-permute-start | bytes 786440 | tf_op jit(solution)/shard_map/ppermute | solution.py:317
  36.1 28.0 %collective-permute-start.7 = (bf16[128,1024]{1,0:T(8,128)(2,1)}, bf16[128,1024]{1,0:T(8,128)(2,1)S(1)}, u32[]{:S(2)}, u32[]{:S(2)}) collective-permute-start(bf16[128,1024]{1,0:T(8,128)(2,1)} %get-tuple-element.87.refs_13_.refs_15_), channel_id=1, source_target_pairs={{0,2},{1,3},{2,0},{3,1},{4,6},{5,7},{6,4},{7,5},{8,10},{9,11},{10,... | collective-permute-start | bytes 786440 | tf_op jit(solution)/shard_map/ppermute | solution.py:317
  38.9 25.2 %collective-permute-start.8 = (bf16[128,1024]{1,0:T(8,128)(2,1)}, bf16[128,1024]{1,0:T(8,128)(2,1)S(1)}, u32[]{:S(2)}, u32[]{:S(2)}) collective-permute-start(bf16[128,1024]{1,0:T(8,128)(2,1)} %get-tuple-element.87.refs_13_.refs_15_), channel_id=1, source_target_pairs={{0,4},{1,5},{2,6},{3,7},{4,0},{5,1},{6,2},{7,3},{8,12},{9,13},{10,... | collective-permute-start | bytes 786440 | tf_op jit(solution)/shard_map/ppermute | solution.py:317
  40.5 23.6 %collective-permute-start.9 = (bf16[128,1024]{1,0:T(8,128)(2,1)}, bf16[128,1024]{1,0:T(8,128)(2,1)S(1)}, u32[]{:S(2)}, u32[]{:S(2)}) collective-permute-start(bf16[128,1024]{1,0:T(8,128)(2,1)} %get-tuple-element.87.refs_13_.refs_15_), channel_id=1, source_target_pairs={{0,6},{1,7},{2,4},{3,5},{4,2},{5,3},{6,0},{7,1},{8,14},{9,15},{10,... | collective-permute-start | bytes 786440 | tf_op jit(solution)/shard_map/ppermute | solution.py:317
  52.5 11.6 %copy-start.2 = (bf16[16,512,128]{2,1,0:T(8,128)(2,1)}, bf16[16,512,128]{2,1,0:T(8,128)(2,1)S(1)}, u32[]{:S(2)}) copy-start(bf16[16,512,128]{2,1,0:T(8,128)(2,1)S(1)} %get-tuple-element.82.kb_ref) | copy-start | bytes 6291460
  52.5 12.5 %copy-start.7 = (s32[1,4]{1,0:T(1,128)S(1)}, s32[1,4]{1,0:T(1,128)}, u32[]{:S(2)}) copy-start(s32[1,4]{1,0:T(1,128)} %refs_0_.3) | copy-start | bytes 52
  65.0 14.8 %copy-start.16 = (bf16[128,1024]{1,0:T(8,128)(2,1)S(1)}, bf16[128,1024]{1,0:T(8,128)(2,1)}, u32[]{:S(2)}) copy-start(bf16[128,1024]{1,0:T(8,128)(2,1)} %get-tuple-element.83.refs_5_) | copy-start | bytes 786436
  73.9 32.3 %all-to-all-start = ((bf16[8,128,128]{2,1,0:T(8,128)(2,1)}), bf16[8,128,128]{2,1,0:T(8,128)(2,1)S(1)}, u32[]{:S(2)}, u32[]{:S(2)}) async-start(bf16[8,128,128]{2,1,0:T(8,128)(2,1)} %get-tuple-element.92), calls=%async_computation | async-start | bytes 524288 | tf_op jit(solution)/shard_map/all_to_all | solution.py:1469
  80.6 25.7 %collective-permute-start.12 = (bf16[128,1536]{1,0:T(8,128)(2,1)S(1)}, bf16[128,1536]{1,0:T(8,128)(2,1)S(1)}, u32[]{:S(2)}, u32[]{:S(2)}) collective-permute-start(bf16[128,1536]{1,0:T(8,128)(2,1)S(1)} %get-tuple-element.132), channel_id=1, source_target_pairs={{0,16},{8,24},{16,0},{24,8},{1,17},{9,25},{17,1},{25,9},{2,18},{10... | collective-permute-start | bytes 1179656 | tf_op jit(solution)/shard_map/ppermute | solution.py:317
  82.1 6.4 %collective-permute-start.10 = (f32[8,4096]{1,0:T(8,128)}, f32[8,4096]{1,0:T(8,128)S(1)}, u32[]{:S(2)}, u32[]{:S(2)}) collective-permute-start(f32[8,4096]{1,0:T(8,128)} %get-tuple-element.93), channel_id=1, source_target_pairs={{0,1},{1,0},{2,3},{3,2},{4,5},{5,4},{6,7},{7,6},{8,9},{9,8},{10,11... | collective-permute-start | bytes 393224 | tf_op jit(solution)/shard_map/ppermute | solution.py:317
  84.1 18.8 %collective-permute-start.13 = (bf16[128,1024]{1,0:T(8,128)(2,1)}, bf16[128,1024]{1,0:T(8,128)(2,1)S(1)}, u32[]{:S(2)}, u32[]{:S(2)}) collective-permute-start(bf16[128,1024]{1,0:T(8,128)(2,1)} %get-tuple-element.95.refs_2_.refs_11_), channel_id=1, source_target_pairs={{0,2},{1,3},{2,0},{3,1},{4,6},{5,7},{6,4},{7,5},{8,10},{9,11},{10,... | collective-permute-start | bytes 786440 | tf_op jit(solution)/shard_map/ppermute | solution.py:317
  85.6 20.7 %collective-permute-start.14 = (bf16[128,1024]{1,0:T(8,128)(2,1)}, bf16[128,1024]{1,0:T(8,128)(2,1)S(1)}, u32[]{:S(2)}, u32[]{:S(2)}) collective-permute-start(bf16[128,1024]{1,0:T(8,128)(2,1)} %get-tuple-element.95.refs_2_.refs_11_), channel_id=1, source_target_pairs={{0,4},{1,5},{2,6},{3,7},{4,0},{5,1},{6,2},{7,3},{8,12},{9,13},{10,... | collective-permute-start | bytes 786440 | tf_op jit(solution)/shard_map/ppermute | solution.py:317
  87.9 18.3 %collective-permute-start.15 = (bf16[128,1024]{1,0:T(8,128)(2,1)}, bf16[128,1024]{1,0:T(8,128)(2,1)S(1)}, u32[]{:S(2)}, u32[]{:S(2)}) collective-permute-start(bf16[128,1024]{1,0:T(8,128)(2,1)} %get-tuple-element.95.refs_2_.refs_11_), channel_id=1, source_target_pairs={{0,6},{1,7},{2,4},{3,5},{4,2},{5,3},{6,0},{7,1},{8,14},{9,15},{10,... | collective-permute-start | bytes 786440 | tf_op jit(solution)/shard_map/ppermute | solution.py:317
  89.4 12.8 %collective-permute-start.11 = (f32[8,4096]{1,0:T(8,128)S(1)}, f32[8,4096]{1,0:T(8,128)S(1)}, u32[]{:S(2)}, u32[]{:S(2)}) collective-permute-start(f32[8,4096]{1,0:T(8,128)S(1)} %add.93), channel_id=1, source_target_pairs={{0,2},{1,3},{2,0},{3,1},{4,6},{5,7},{6,4},{7,5},{8,10},{9,11},{10,... | collective-permute-start | bytes 393224 | tf_op jit(solution)/shard_map/ppermute | solution.py:317
  121.7 26.5 %all-to-all-start.1 = ((bf16[8,128,384]{2,1,0:T(8,128)(2,1)}), bf16[8,128,384]{2,1,0:T(8,128)(2,1)S(1)}, u32[]{:S(2)}, u32[]{:S(2)}) async-start(bf16[8,128,384]{2,1,0:T(8,128)(2,1)} %get-tuple-element.96), calls=%async_computation.1 | async-start | bytes 1572864 | tf_op jit(solution)/shard_map/all_to_all | solution.py:1486
  136.6 2.4 %collective-permute-start.16 = (bf16[512,640]{1,0:T(8,128)(2,1)}, bf16[512,640]{1,0:T(8,128)(2,1)S(1)}, u32[]{:S(2)}, u32[]{:S(2)}) collective-permute-start(bf16[512,640]{1,0:T(8,128)(2,1)} %get-tuple-element.102), channel_id=1, source_target_pairs={{0,8},{8,0},{16,24},{24,16},{1,9},{9,1},{17,25},{25,17},{2,10},{10... | collective-permute-start | bytes 1966088 | tf_op jit(solution)/shard_map/ppermute | solution.py:317
  136.7 3.2 %collective-permute-start.17 = (bf16[512,640]{1,0:T(8,128)(2,1)}, bf16[512,640]{1,0:T(8,128)(2,1)S(1)}, u32[]{:S(2)}, u32[]{:S(2)}) collective-permute-start(bf16[512,640]{1,0:T(8,128)(2,1)} %get-tuple-element.103), channel_id=1, source_target_pairs={{0,8},{8,0},{16,24},{24,16},{1,9},{9,1},{17,25},{25,17},{2,10},{10... | collective-permute-start | bytes 1966088 | tf_op jit(solution)/shard_map/ppermute | solution.py:317
  137.2 3.7 %collective-permute-start.18 = (bf16[512,640]{1,0:T(8,128)(2,1)}, bf16[512,640]{1,0:T(8,128)(2,1)S(1)}, u32[]{:S(2)}, u32[]{:S(2)}) collective-permute-start(bf16[512,640]{1,0:T(8,128)(2,1)} %get-tuple-element.104), channel_id=1, source_target_pairs={{0,8},{8,0},{16,24},{24,16},{1,9},{9,1},{17,25},{25,17},{2,10},{10... | collective-permute-start | bytes 1966088 | tf_op jit(solution)/shard_map/ppermute | solution.py:317
  144.7 24.3 %collective-permute-start.19 = (bf16[8,32,896]{2,1,0:T(8,128)(2,1)}, bf16[8,32,896]{2,1,0:T(8,128)(2,1)S(1)}, u32[]{:S(2)}, u32[]{:S(2)}) collective-permute-start(bf16[8,32,896]{2,1,0:T(8,128)(2,1)} %get-tuple-element.109), channel_id=1, source_target_pairs={{0,16},{8,24},{16,0},{24,8},{1,17},{9,25},{17,1},{25,9},{2,18},{10... | collective-permute-start | bytes 1376264 | tf_op jit(solution)/shard_map/ppermute | solution.py:317
  146.2 22.8 %collective-permute-start.20 = (bf16[8,32,512]{2,1,0:T(8,128)(2,1)}, bf16[8,32,512]{2,1,0:T(8,128)(2,1)S(1)}, u32[]{:S(2)}, u32[]{:S(2)}) collective-permute-start(bf16[8,32,512]{2,1,0:T(8,128)(2,1)} %get-tuple-element.110), channel_id=1, source_target_pairs={{0,1},{1,0},{2,3},{3,2},{4,5},{5,4},{6,7},{7,6},{8,9},{9,8},{10,11... | collective-permute-start | bytes 786440 | tf_op jit(solution)/shard_map/ppermute | solution.py:317
  148.2 20.8 %collective-permute-start.21 = (bf16[8,32,512]{2,1,0:T(8,128)(2,1)}, bf16[8,32,512]{2,1,0:T(8,128)(2,1)S(1)}, u32[]{:S(2)}, u32[]{:S(2)}) collective-permute-start(bf16[8,32,512]{2,1,0:T(8,128)(2,1)} %get-tuple-element.111), channel_id=1, source_target_pairs={{0,17},{1,16},{2,19},{3,18},{4,21},{5,20},{6,23},{7,22},{8,25},{9,... | collective-permute-start | bytes 786440 | tf_op jit(solution)/shard_map/ppermute | solution.py:1509
  155.3 29.6 %copy-start.21 = (f32[32,1024]{1,0:T(8,128)S(1)}, f32[32,1024]{1,0:T(8,128)}, u32[]{:S(2)}) copy-start(f32[32,1024]{1,0:T(8,128)} %refs_3_.2) | copy-start | bytes 393220
  155.3 12.1 %collective-permute-start.23 = (f32[8,4096]{1,0:T(8,128)}, f32[8,4096]{1,0:T(8,128)S(1)}, u32[]{:S(2)}, u32[]{:S(2)}) collective-permute-start(f32[8,4096]{1,0:T(8,128)} %get-tuple-element.114), channel_id=1, source_target_pairs={{0,4},{1,5},{2,6},{3,7},{4,0},{5,1},{6,2},{7,3},{8,12},{9,13},{10,... | collective-permute-start | bytes 393224 | tf_op jit(solution)/shard_map/ppermute | solution.py:317
  158.2 7.7 %collective-permute-start.22 = (f32[8,2048]{1,0:T(8,128)}, f32[8,2048]{1,0:T(8,128)S(1)}, u32[]{:S(2)}, u32[]{:S(2)}) collective-permute-start(f32[8,2048]{1,0:T(8,128)} %get-tuple-element.113), channel_id=1, source_target_pairs={{0,1},{1,0},{2,3},{3,2},{4,5},{5,4},{6,7},{7,6},{8,9},{9,8},{10,11... | collective-permute-start | bytes 196616 | tf_op jit(solution)/shard_map/ppermute | solution.py:317
  171.4 28.3 %all-to-all-start.2 = ((bf16[8,32,1664]{2,1,0:T(8,128)(2,1)}), bf16[8,32,1664]{2,1,0:T(8,128)(2,1)S(1)}, u32[]{:S(2)}, u32[]{:S(2)}) async-start(bf16[8,32,1664]{2,1,0:T(8,128)(2,1)} %get-tuple-element.115), calls=%async_computation.2 | async-start | bytes 1703936 | tf_op jit(solution)/shard_map/all_to_all | solution.py:1514
  175.7 8.5 %collective-permute-start.25 = (f32[8,4096]{1,0:T(8,128)}, f32[8,4096]{1,0:T(8,128)S(1)}, u32[]{:S(2)}, u32[]{:S(2)}) collective-permute-start(f32[8,4096]{1,0:T(8,128)} %get-tuple-element.118.refs_1_), channel_id=1, source_target_pairs={{0,8},{8,0},{16,24},{24,16},{1,9},{9,1},{17,25},{25,17},{2,10},{10... | collective-permute-start | bytes 393224 | tf_op jit(solution)/shard_map/ppermute | solution.py:317
  175.7 8.5 %collective-permute-start.26 = (f32[8,4096]{1,0:T(8,128)}, f32[8,4096]{1,0:T(8,128)S(1)}, u32[]{:S(2)}, u32[]{:S(2)}) collective-permute-start(f32[8,4096]{1,0:T(8,128)} %get-tuple-element.118.refs_1_), channel_id=1, source_target_pairs={{0,16},{8,24},{16,0},{24,8},{1,17},{9,25},{17,1},{25,9},{2,18},{10... | collective-permute-start | bytes 393224 | tf_op jit(solution)/shard_map/ppermute | solution.py:317
  177.3 6.9 %collective-permute-start.27 = (f32[8,4096]{1,0:T(8,128)}, f32[8,4096]{1,0:T(8,128)S(1)}, u32[]{:S(2)}, u32[]{:S(2)}) collective-permute-start(f32[8,4096]{1,0:T(8,128)} %get-tuple-element.118.refs_1_), channel_id=1, source_target_pairs={{0,24},{8,16},{16,8},{24,0},{1,25},{9,17},{17,9},{25,1},{2,26},{10... | collective-permute-start | bytes 393224 | tf_op jit(solution)/shard_map/ppermute | solution.py:317
  178.3 12.7 %collective-permute-start.24 = (f32[8,2048]{1,0:T(8,128)}, f32[8,2048]{1,0:T(8,128)S(1)}, u32[]{:S(2)}, u32[]{:S(2)}) collective-permute-start(f32[8,2048]{1,0:T(8,128)} %get-tuple-element.117), channel_id=1, source_target_pairs={{0,2},{1,3},{2,0},{3,1},{4,6},{5,7},{6,4},{7,5},{8,10},{9,11},{10,... | collective-permute-start | bytes 196616 | tf_op jit(solution)/shard_map/ppermute | solution.py:317
  184.1 8.3 %copy-start.27 = (f32[8,4096]{1,0:T(8,128)}, f32[8,4096]{1,0:T(8,128)S(1)}, u32[]{:S(2)}) copy-start(f32[8,4096]{1,0:T(8,128)S(1)} %collective-permute-done.27.refs_4_) | copy-start | bytes 393220
  184.2 8.3 %copy-start.26 = (f32[8,4096]{1,0:T(8,128)}, f32[8,4096]{1,0:T(8,128)S(1)}, u32[]{:S(2)}) copy-start(f32[8,4096]{1,0:T(8,128)S(1)} %collective-permute-done.26.refs_3_) | copy-start | bytes 393220
  184.2 8.3 %copy-start.25 = (f32[8,4096]{1,0:T(8,128)}, f32[8,4096]{1,0:T(8,128)S(1)}, u32[]{:S(2)}) copy-start(f32[8,4096]{1,0:T(8,128)S(1)} %collective-permute-done.25.refs_2_) | copy-start | bytes 393220
  185.1 14.6 %copy-start.20 = (f32[32,1024]{1,0:T(8,128)}, f32[32,1024]{1,0:T(8,128)S(1)}, u32[]{:S(2)}) copy-start(f32[32,1024]{1,0:T(8,128)S(1)} %fusion.2.refs_7_) | copy-start | bytes 393220
  201.5 14.0 %collective-permute-start.33 = (bf16[256,1024]{1,0:T(8,128)(2,1)}, bf16[256,1024]{1,0:T(8,128)(2,1)S(1)}, u32[]{:S(2)}, u32[]{:S(2)}) collective-permute-start(bf16[256,1024]{1,0:T(8,128)(2,1)} %get-tuple-element.126.refs_1_), channel_id=1, source_target_pairs={{0,16},{8,24},{16,0},{24,8},{1,17},{9,25},{17,1},{25,9},{2,18},{10... | collective-permute-start | bytes 1572872 | tf_op jit(solution)/shard_map/ppermute | solution.py:317
  204.2 7.6 %collective-permute-start.28 = (f32[8,2048]{1,0:T(8,128)}, f32[8,2048]{1,0:T(8,128)S(1)}, u32[]{:S(2)}, u32[]{:S(2)}) collective-permute-start(f32[8,2048]{1,0:T(8,128)} %get-tuple-element.120), channel_id=1, source_target_pairs={{0,4},{1,5},{2,6},{3,7},{4,0},{5,1},{6,2},{7,3},{8,12},{9,13},{10,... | collective-permute-start | bytes 196616 | tf_op jit(solution)/shard_map/ppermute | solution.py:317
  212.6 5.6 %copy-start.22 = (f32[8,2048]{1,0:T(8,128)}, f32[8,2048]{1,0:T(8,128)S(1)}, u32[]{:S(2)}) copy-start(f32[8,2048]{1,0:T(8,128)S(1)} %add.102.refs_1_) | copy-start | bytes 196612
  212.6 3.1 %collective-permute-start.29 = (f32[8,2048]{1,0:T(8,128)S(1)}, f32[8,2048]{1,0:T(8,128)S(1)}, u32[]{:S(2)}, u32[]{:S(2)}) collective-permute-start(f32[8,2048]{1,0:T(8,128)S(1)} %add.102.refs_1_), channel_id=1, source_target_pairs={{0,8},{8,0},{16,24},{24,16},{1,9},{9,1},{17,25},{25,17},{2,10},{10... | collective-permute-start | bytes 196616 | tf_op jit(solution)/shard_map/ppermute | solution.py:317
  212.7 5.0 %collective-permute-start.30 = (f32[8,2048]{1,0:T(8,128)S(1)}, f32[8,2048]{1,0:T(8,128)S(1)}, u32[]{:S(2)}, u32[]{:S(2)}) collective-permute-start(f32[8,2048]{1,0:T(8,128)S(1)} %add.102.refs_1_), channel_id=1, source_target_pairs={{0,16},{8,24},{16,0},{24,8},{1,17},{9,25},{17,1},{25,9},{2,18},{10... | collective-permute-start | bytes 196616 | tf_op jit(solution)/shard_map/ppermute | solution.py:317
  213.3 4.9 %collective-permute-start.31 = (f32[8,2048]{1,0:T(8,128)S(1)}, f32[8,2048]{1,0:T(8,128)S(1)}, u32[]{:S(2)}, u32[]{:S(2)}) collective-permute-start(f32[8,2048]{1,0:T(8,128)S(1)} %add.102.refs_1_), channel_id=1, source_target_pairs={{0,24},{8,16},{16,8},{24,0},{1,25},{9,17},{17,9},{25,1},{2,26},{10... | collective-permute-start | bytes 196616 | tf_op jit(solution)/shard_map/ppermute | solution.py:317
  215.2 9.2 %collective-permute-start.32 = (bf16[256,1024]{1,0:T(8,128)(2,1)}, bf16[256,1024]{1,0:T(8,128)(2,1)S(1)}, u32[]{:S(2)}, u32[]{:S(2)}) collective-permute-start(bf16[256,1024]{1,0:T(8,128)(2,1)} %get-tuple-element.126.refs_1_), channel_id=1, source_target_pairs={{0,8},{8,0},{16,24},{24,16},{1,9},{9,1},{17,25},{25,17},{2,10},{10... | collective-permute-start | bytes 1572872 | tf_op jit(solution)/shard_map/ppermute | solution.py:317
  215.5 8.8 %collective-permute-start.34 = (bf16[256,1024]{1,0:T(8,128)(2,1)S(1)}, bf16[256,1024]{1,0:T(8,128)(2,1)S(1)}, u32[]{:S(2)}, u32[]{:S(2)}) collective-permute-start(bf16[256,1024]{1,0:T(8,128)(2,1)S(1)} %collective-permute-done.33.refs_3_), channel_id=1, source_target_pairs={{0,8},{8,0},{16,24},{24,16},{1,9},{9,1},{17,25},{25,17},{2,10},{10... | collective-permute-start | bytes 1572872 | tf_op jit(solution)/shard_map/ppermute | solution.py:317
  (21 other events, 42.1 us)

commit v3 on v2

--- a/solution.py
+++ b/solution.py
@@ -359,6 +359,8 @@
 
 
 def in_hbm(value):
+    if value.size * value.dtype.itemsize < 140000:
+        return value
     return pltpu.with_memory_space_constraint(value, pltpu.HBM)
 
 
@@ -367,7 +369,10 @@
 
 
 def shape_of(shape, dtype=BF):
-    return pltpu.HBM(shape, dtype)
+    size = jnp.dtype(dtype).itemsize
+    for n in shape:
+        size *= n
+    return jax.ShapeDtypeStruct(shape, dtype) if size < 140000 else pltpu.HBM(shape, dtype)
 
 
 def params(mib=24):
@@ -498,6 +503,19 @@
 
 
 def project_kernel(clips, with_own, me_ref, clip_ref, mod_ref, b_ref, cos_ref, sin_ref, w, *refs):
+    copies = []
+    if not with_own:
+        source, (w, sems), refs = w, refs[-2:], refs[:-2]
+        width, step = source.shape[0], 512
+        column = pl.ds(pl.multiple_of(me_ref[0] * LANES, LANES), LANES)
+        copies = [pltpu.make_async_copy(source.at[:, column], w.at[:, pl.ds(0, LANES)], sems.at[0])]
+        for i, start in enumerate(range(width, 3 * width, step)):
+            here = pl.ds(start, step)
+            copies.append(
+                pltpu.make_async_copy(source.at[:, here], w.at[:, here], sems.at[1 + i])
+            )
+        for copy in copies:
+            copy.start()
     blocks = refs[: len(refs) - (5 if with_own else 3)]
     h_ref, kv_ref, q_ref = refs[len(blocks) : len(blocks) + 3]
     rows, width = blocks[0].shape
@@ -523,11 +541,18 @@
     def turned(piece, some):
         return piece * cosine[:some] + half_swap(piece, lane[:some]) * sine[:some]
 
-    part = dot_low(h, w[:, pl.ds(column, LANES)]) + b_ref[:, pl.ds(column, LANES)]
+    if with_own:
+        heads = w[:, pl.ds(column, LANES)]
+    else:
+        copies[0].wait()
+        heads = w[:, :LANES]
+    part = dot_low(h, heads) + b_ref[:, pl.ds(column, LANES)]
     q_ref[...] = (turned(part, h.shape[0]) * 0.125).astype(BF)
     step = 2 * LANES
     for start in range(0 if with_own else width, 3 * width, step):
         some = rows if start < width else h.shape[0]
+        if copies and (start - width) % 512 == 0:
+            copies[1 + (start - width) // 512].wait()
         part = dot_low(h[:some], w[:, start : start + step]) + b_ref[:, start : start + step]
         for inner in range(0, step, LANES):
             piece = part[:, inner : inner + LANES]
@@ -563,14 +588,17 @@
             full(b_qkv.shape),
             pl.BlockSpec((rows, LANES), lambda *_: (half, 0)),
             pl.BlockSpec((rows, LANES), lambda *_: (half, 0)),
-            KEPT,
+            KEPT if with_own else ANYWHERE,
         ]
         + [full(v.shape) for v in blocks],
         out_specs=[full(out_shape[0].shape), KEPT] + [full(o.shape) for o in out_shape[2:]],
         out_shape=out_shape,
+        scratch_shapes=[]
+        if with_own
+        else [pltpu.VMEM(w_qkv.shape, BF), pltpu.SemaphoreType.DMA((1 + 4 * width // 1024,))],
         compiler_params=params(),
         cost_estimate=cost(4 * rows * width * width, 6 * MIB),
-    )(me, *all_in_hbm([clip_col, modulation, b_qkv, cosine, sine]), w_qkv, *all_in_hbm(blocks))
+    )(me, *all_in_hbm([clip_col, modulation, b_qkv, cosine, sine]), w_qkv if with_own else in_hbm(w_qkv), *all_in_hbm(blocks))
 
 
 def contract_last(left, right):
@@ -668,8 +696,8 @@
 
     @pl.when(i == 0)
     def _():
-        keys[:half] = ka_ref[me_ref[0]]
-        keys[half:] = kb_ref[me_ref[0]]
+        keys[:half] = ka_ref[0]
+        keys[half:] = kb_ref[0]
 
     query = jnp.where(i < blocks // 2, qa_ref[...], qb_ref[...])
     visible = keyclip_ref[...] == rowclip_ref[...]
@@ -692,8 +720,8 @@
             pl.BlockSpec((1, own_rows), lambda i, m: (0, i)),
             pl.BlockSpec((own_rows, LANES), lambda i, m: (jnp.minimum(i, halfway - 1), 0)),
             pl.BlockSpec((own_rows, LANES), lambda i, m: (jnp.maximum(i - halfway, 0), 0)),
-            KEPT,
-            KEPT,
+            pl.BlockSpec((1, half, LANES), lambda i, m: (m[0], 0, 0)),
+            pl.BlockSpec((1, half, LANES), lambda i, m: (m[0], 0, 0)),
         ]
         + [ANYWHERE] * len(earlier),
         out_specs=pl.BlockSpec((rows, 2 * own_rows), lambda i, m: (0, i)),
@@ -705,11 +733,11 @@
         out_shape=shape_of((rows, 2 * rows), F32),
         compiler_params=params(),
         cost_estimate=cost(4 * rows * rows * LANES, 9 * MIB),
-    )(me, *all_in_hbm([clip_col, clip_row, q_a, q_b]), kv_a, kv_b, *all_in_hbm(earlier))
+    )(me, *all_in_hbm([clip_col, clip_row, q_a, q_b]), *all_in_hbm([kv_a, kv_b, *earlier]))
 
 
 def attend_back_kernel(
-    me_ref, p_ref, qa_ref, qb_ref, ka_ref, kb_ref, do_ref, cos_ref, sin_ref, *refs
+    me_ref, p_ref, qa_ref, qb_ref, ka_ref, kb_ref, va_ref, vb_ref, do_ref, cos_ref, sin_ref, *refs
 ):
     out_ref, sent_ref = refs[-9:-7]
     dk_ref, dv_ref, values, keys_turned, d_probs = refs[-5:]
@@ -722,9 +750,9 @@
     def _():
         dk_ref[...] = jnp.zeros_like(dk_ref)
         dv_ref[...] = jnp.zeros_like(dv_ref)
-        for at, ref in ((0, ka_ref), (half, kb_ref)):
-            values[at : at + half] = ref[ref.shape[0] // 2 + me]
-            keys_turned[:, at : at + half] = ref[me].T
+        for at, key_ref, value_ref in ((0, ka_ref, va_ref), (half, kb_ref, vb_ref)):
+            values[at : at + half] = value_ref[0]
+            keys_turned[:, at : at + half] = key_ref[0].T
 
     query = jnp.where(i < blocks // 2, qa_ref[...], qb_ref[...])
     q_two, up_two = head_rows(query), head_rows(do_ref[0])
@@ -770,6 +798,7 @@
 def attend_back(me, probs, q_a, q_b, kv_a, kv_b, d_o, cosine, sine, passed, earlier):
     half = kv_a.shape[1]
     rows = 2 * half
+    pairs = kv_a.shape[0] // 2
     blocks, own_rows, _ = d_o.shape
     halfway = blocks // 2
     grid_spec = pltpu.PrefetchScalarGridSpec(
@@ -779,8 +808,10 @@
             pl.BlockSpec((rows, 2 * own_rows), lambda i, m: (0, i)),
             pl.BlockSpec((own_rows, LANES), lambda i, m: (jnp.minimum(i, halfway - 1), 0)),
             pl.BlockSpec((own_rows, LANES), lambda i, m: (jnp.maximum(i - halfway, 0), 0)),
-            KEPT,
-            KEPT,
+            pl.BlockSpec((1, half, LANES), lambda i, m: (m[0], 0, 0)),
+            pl.BlockSpec((1, half, LANES), lambda i, m: (m[0], 0, 0)),
+            pl.BlockSpec((1, half, LANES), lambda i, m: (pairs + m[0], 0, 0)),
+            pl.BlockSpec((1, half, LANES), lambda i, m: (pairs + m[0], 0, 0)),
             pl.BlockSpec((1, own_rows, LANES), lambda i, m: (m[0] ^ offset_of(i, blocks), 0, 0)),
             pl.BlockSpec((rows, LANES), lambda i, m: (0, 0)),
             pl.BlockSpec((rows, LANES), lambda i, m: (0, 0)),
@@ -811,14 +842,13 @@
             shape_of(passed[0].shape, passed[0].dtype),
             shape_of(passed[1].shape, passed[1].dtype),
         ],
-        input_output_aliases={9: 2, 10: 3},
+        input_output_aliases={11: 2, 12: 3},
         compiler_params=params(),
         cost_estimate=cost(8 * rows * rows * LANES, 12 * MIB),
     )(
         me,
         *all_in_hbm([probs, q_a, q_b]),
-        kv_a,
-        kv_b,
+        *all_in_hbm([kv_a, kv_b, kv_a, kv_b]),
         d_o,
         *all_in_hbm([cosine, sine, *passed, *earlier]),
     )
@@ -1454,10 +1484,11 @@
     modulation_two = modulate(silu_own, w_mod, b_mod[None, :])
     evens, odds = gathered_blocks(frames, count, (modulation_two[0, 0] * 0.0).astype(BF))
 
-    shared = (me[None], clip_col, modulation, kept_qkv, b_qkv[None, :], cosine, sine)
-    h1_a, kv_a, q_a, q_own, later = project(0, evens, *shared, cotangent)
+    shared = (b_qkv[None, :], cosine, sine)
+    first = (me[None], clip_col, modulation)
+    h1_a, kv_a, q_a, q_own, later = project(0, evens, *first, kept_qkv, *shared, cotangent)
     upstreams = even_blocks(later, count)
-    h1_b, kv_b, q_b = project(1, odds, *shared)
+    h1_b, kv_b, q_b = project(1, odds, *first, w_qkv, *shared)
     attended, kept_out, kept_up, kept_down = attend(
         q_own, kv_a, kv_b, marks, [w_out, w_up, w_down]
     )

time: 229 us -> 215 us (0.939)
  other arithmetic: 14.1 us -> 4.33 us
  local copies, waits for them, and re-layouts: 13.4 us -> 7.02 us
  waiting for transfers between devices: 31 us -> 37.2 us
  Pallas kernels: 108 us -> 105 us
    ppermute x34, waiting for transfers between devices: 31 us -> 37.2 us  [swapped_with(): return lax.ppermute(value, axis, [(i, i ^ offset) for i in range(size)])]
    unnamed x62 -> x46, local copies, waits for them, and re-layouts: 9.7 us -> 4.73 us
    pallas_call x1, Pallas kernels: 7.63 us -> 4.83 us  [modulate(): pl.pallas_call(modulate_kernel, grid=(4,), in_specs=[full(silu.shape), pl...]
  transfers between devices with their start and end apart: 38 -> 38, of which waited for: 12 -> 13; matrix products, arithmetic and copies ran while one was open for 8% -> 3% of each run, Pallas kernels for 35% -> 36%
where the time goes in v3:
time: 215 us; the launch traced here: 214 us
  Pallas kernels  105 us (49%)
  starting transfers between devices  59 us (27%)
  waiting for transfers between devices  37.2 us (17%)
  local copies, waits for them, and re-layouts  7.02 us (3%)
  other arithmetic  4.33 us (2%)
    ppermute x34, starting transfers between devices, swapped_with(): return lax.ppermute(value, axis, [(i, i ^ offset) for i in range(size)])  45 us
    ppermute x34, waiting for transfers between devices, swapped_with(): return lax.ppermute(value, axis, [(i, i ^ offset) for i in range(size)])  37.2 us
    pallas_call x2, Pallas kernels, project(): pl.pallas_call(lambda *refs: project_kernel(clips, with_own, *refs), grid...  14 us
    pallas_call x1, Pallas kernels, attend_back(): pl.pallas_call(attend_back_kernel, grid_spec=grid_spec, out_shape=[shape_...  13 us
    pallas_call x2, Pallas kernels, table_part(): pl.pallas_call(lambda *refs: table_kernel(first, clips, *refs), grid=(col...  11.8 us
    pallas_call x1, Pallas kernels, attend(): pl.pallas_call(attend_kernel, grid=(width // LANES,), in_specs=[pl.BlockS...  11.5 us
    pallas_call x1, Pallas kernels, weights_part(): pl.pallas_call(lambda *refs: weights_kernel(clips, count, *refs), grid=(1...  9.74 us
    pallas_call x1, Pallas kernels, middle_part(): pl.pallas_call(lambda *refs: middle_kernel(clips, *refs), grid=(1,), in_s...  8.59 us
  transfers between devices with their start and end apart: 38, of which 13 were waited for; matrix products, arithmetic and copies ran while one was open for 3% of the time, Pallas kernels for 36%

profile of v3, /device:TPU:0, one launch (start us, length us, event | category | flops | bytes accessed | tf_op | source)
XLA Modules:
  0.0 214.2 jit_solution(8231069335278968927)
XLA Ops:
  0.6 3.1 %collective-permute-start = (bf16[128,1024]{1,0:T(8,128)(2,1)}, bf16[128,1024]{1,0:T(8,128)(2,1)S(1)}, u32[]{:S(2)}, u32[]{:S(2)}) collective-permute-start(bf16[128,1024]{1,0:T(8,128)(2,1)} %refs_2_.5), channel_id=1, source_target_pairs={{0,2},{1,3},{2,0},{3,1},{4,6},{5,7},{6,4},{7,5},{8,10},{9,11},{10,... | collective-permute-start | bytes 786440 | tf_op jit(solution)/shard_map/ppermute | solution.py:317
  3.7 2.6 %collective-permute-start.1 = (bf16[128,1024]{1,0:T(8,128)(2,1)}, bf16[128,1024]{1,0:T(8,128)(2,1)S(1)}, u32[]{:S(2)}, u32[]{:S(2)}) collective-permute-start(bf16[128,1024]{1,0:T(8,128)(2,1)} %refs_2_.5), channel_id=1, source_target_pairs={{0,4},{1,5},{2,6},{3,7},{4,0},{5,1},{6,2},{7,3},{8,12},{9,13},{10,... | collective-permute-start | bytes 786440 | tf_op jit(solution)/shard_map/ppermute | solution.py:317
  6.3 1.7 collective-permute-start.3
  11.0 5.9 %shard_map.246 = (f32[4,2048]{1,0:T(4,128)S(1)}, bf16[4,1024]{1,0:T(4,128)(2,1)S(1)}, s32[1024,1]{1,0:T(8,128)S(1)}, s32[1,1024]{1,0:T(1,128)S(1)}, f32[1024,128...) custom-call(s32[1]{0:T(128)} %bitcast.refs_0_.me_ref, ...), custom_call_target="tpu_custom_call" | custom-call | flops 16777216 | bytes 5242880 | tf_op jit(solution)/shard_map/pallas_call | solution.py:463
  17.0 4.8 %shard_map.248.refs_6_.refs_2_ = f32[4,4096]{1,0:T(4,128)S(1)} custom-call(bf16[4,1024]{1,0:T(4,128)(2,1)S(1)} %get-tuple-element.81.silu_ref, bf16[1024,6144]{1,0:T(8,128)(2,1)} %refs_6_.7, f32[1,6144]{1,0:T(1,128)S(1)} %bitcast.24), custom_call_target="tpu_custom_call" | custom-call | flops 33554432 | bytes 8388608 | tf_op jit(solution)/shard_map/pallas_call | solution.py:490
  23.4 1.9 collective-permute-done.1.refs_9_
  26.1 1.5 collective-permute-start.5
  28.9 6.4 %shard_map.247 = (bf16[512,1024]{1,0:T(8,128)(2,1)}, bf16[16,512,128]{2,1,0:T(8,128)(2,1)S(1)}, bf16[512,128]{1,0:T(8,128)(2,1)S(1)}, bf16[128,1024]{1,0:T(8,128)(2,1)}, bf16[128,1024]{1,0:T(8,128)(2,1)}) custom-call(s32[1]{0:T(128)} %bitcast.refs_0_.me_ref, s32[1024,1]{1,0:T(8,128)S(1)} %get-tuple-element.72.refs_1_.keyclip_ref.refs_0_, ...), custom_call_target="tpu_custom_call" | custom-call | flops 2147483648 | bytes 6291456 | tf_op jit(solution)/shard_map/pallas_call | solution.py:581
  35.3 3.5 %collective-permute-start.7 = (bf16[128,1024]{1,0:T(8,128)(2,1)}, bf16[128,1024]{1,0:T(8,128)(2,1)S(1)}, u32[]{:S(2)}, u32[]{:S(2)}) collective-permute-start(bf16[128,1024]{1,0:T(8,128)(2,1)} %get-tuple-element.87.refs_13_.refs_15_), channel_id=1, source_target_pairs={{0,2},{1,3},{2,0},{3,1},{4,6},{5,7},{6,4},{7,5},{8,10},{9,11},{10,... | collective-permute-start | bytes 786440 | tf_op jit(solution)/shard_map/ppermute | solution.py:317
  38.8 1.1 collective-permute-start.8
  39.9 1.5 collective-permute-start.9
  41.5 7.6 %shard_map.249 = (bf16[512,1024]{1,0:T(8,128)(2,1)}, bf16[16,512,128]{2,1,0:T(8,128)(2,1)S(1)}, bf16[512,128]{1,0:T(8,128)(2,1)S(1)}) custom-call(s32[1]{0:T(128)} %bitcast.refs_0_.me_ref, s32[1024,1]{1,0:T(8,128)S(1)} %get-tuple-element.72.refs_1_.keyclip_ref.refs_0_, f32[4,2048]{1,0:T(4,128)S(1)} %get-tuple-element.75.refs_2_.refs_3_, ...), custom_call_target="tpu_custom_call" | custom-call | flops 2147483648 | bytes 6291456 | tf_op jit(solution)/shard_map/pallas_call | solution.py:581
  49.2 11.5 %shard_map.250 = (bf16[128,1024]{1,0:T(8,128)(2,1)}, bf16[1024,1024]{1,0:T(8,128)(2,1)S(1)}, bf16[1024,2048]{1,0:T(8,128)(2,1)S(1)}, bf16[2048,1024]{1,0:T(8,128)(2,1)S(1)}) custom-call(bf16[1024,256]{1,0:T(8,128)(2,1)} %get-tuple-element.74.keymark_ref.rowmark_ref, bf16[1024,256]{1,0:T(8,128)(2,1)} %get-tuple-element.74.keymark_ref.rowmark_ref, ...), custom_call_target="tpu_custom_call" | custom-call | flops 536870912 | bytes 1048576 | tf_op jit(solution)/shard_map/pallas_call | solution.py:668
  61.6 8.6 %shard_map.251 = (bf16[128,1024]{1,0:T(8,128)(2,1)}, bf16[128,1024]{1,0:T(8,128)(2,1)}, f32[128,1024]{1,0:T(8,128)}, bf16[128,1024]{1,0:T(8,128)(2,1)}, bf16[8,1...) custom-call(s32[1,4]{1,0:T(1,128)S(1)} %copy-done.11, s32[1024,1]{1,0:T(8,128)S(1)} %get-tuple-element.72.refs_1_.keyclip_ref.refs_0_, ...), custom_call_target="tpu_custom_call" | custom-call | flops 2684354560 | bytes 3145728 | tf_op jit(solution)/shard_map/pallas_call | solution.py:983
  70.2 4.8 %all-to-all-start = ((bf16[8,128,128]{2,1,0:T(8,128)(2,1)}), bf16[8,128,128]{2,1,0:T(8,128)(2,1)S(1)}, u32[]{:S(2)}, u32[]{:S(2)}) async-start(bf16[8,128,128]{2,1,0:T(8,128)(2,1)} %get-tuple-element.92), calls=%async_computation | async-start | bytes 524288 | tf_op jit(solution)/shard_map/all_to_all | solution.py:1500
  75.0 1.0 broadcast_select_fusion
  76.8 1.5 collective-permute-start.12
  78.3 2.0 collective-permute-start.10
  80.3 1.5 collective-permute-start.13
  81.8 2.4 %collective-permute-start.14 = (bf16[128,1024]{1,0:T(8,128)(2,1)}, bf16[128,1024]{1,0:T(8,128)(2,1)S(1)}, u32[]{:S(2)}, u32[]{:S(2)}) collective-permute-start(bf16[128,1024]{1,0:T(8,128)(2,1)} %get-tuple-element.95.refs_2_.refs_11_), channel_id=1, source_target_pairs={{0,4},{1,5},{2,6},{3,7},{4,0},{5,1},{6,2},{7,3},{8,12},{9,13},{10,... | collective-permute-start | bytes 786440 | tf_op jit(solution)/shard_map/ppermute | solution.py:317
  85.3 8.4 %shard_map.252.p_ref = f32[1024,2048]{1,0:T(8,128)} custom-call(s32[1]{0:T(128)} %bitcast.refs_0_.me_ref, s32[1024,1]{1,0:T(8,128)S(1)} %get-tuple-element.72.refs_1_.keyclip_ref.refs_0_, s32[1,1024]{1,0:T(1,128)S(1)} %get-tuple-element.73.refs_2_.rowclip_ref.refs_1_, bf16[512,128]{1,0:T(8,128)(2,1)S(1)} %get-tuple-element.90.qa_ref, ...), custom_call_target="tpu_custom_call" | custom-call | flops 536870912 | bytes 9437184 | tf_op jit(solution)/shard_map/pallas_call | solution.py:730
  93.7 4.7 %collective-permute-done.11 = f32[8,4096]{1,0:T(8,128)S(1)} collective-permute-done((f32[8,4096]{1,0:T(8,128)S(1)}, f32[8,4096]{1,0:T(8,128)S(1)}, u32[]{:S(2)}, u32[]{:S(2)}) %collective-permute-start.11) | collective-permute-done | bytes 131104 | tf_op jit(solution)/shard_map/ppermute | solution.py:317
  98.5 4.0 %collective-permute-done.14.refs_4_.refs_13_ = bf16[128,1024]{1,0:T(8,128)(2,1)S(1)} collective-permute-done((bf16[128,1024]{1,0:T(8,128)(2,1)}, bf16[128,1024]{1,0:T(8,128)(2,1)S(1)}, u32[]{:S(2)}, u32[]{:S(2)}) %collective-permute-start.14) | collective-permute-done | bytes 262176 | tf_op jit(solution)/shard_map/ppermute | solution.py:317
  103.4 13.0 %shard_map.253 = (bf16[1024,384]{1,0:T(8,128)(2,1)}, bf16[8,128,384]{2,1,0:T(8,128)(2,1)}, f32[8,4096]{1,0:T(8,128)S(1)}, bf16[128,1536]{1,0:T(8,128)(2,1)}) custom-call(s32[1]{0:T(128)} %bitcast.refs_0_.me_ref, f32[1024,2048]{1,0:T(8,128)} %shard_map.252.p_ref, ...), custom_call_target="tpu_custom_call", output_to_operand_aliasing={{2}: (11, {}), {3}: (12, {})} | custom-call | flops 1073741824 | bytes 12582912 | tf_op jit(solution)/shard_map/pallas_call | solution.py:836
  116.4 5.2 %all-to-all-start.1 = ((bf16[8,128,384]{2,1,0:T(8,128)(2,1)}), bf16[8,128,384]{2,1,0:T(8,128)(2,1)S(1)}, u32[]{:S(2)}, u32[]{:S(2)}) async-start(bf16[8,128,384]{2,1,0:T(8,128)(2,1)} %get-tuple-element.96), calls=%async_computation.1 | async-start | bytes 1572864 | tf_op jit(solution)/shard_map/all_to_all | solution.py:1517
  121.7 9.7 %shard_map.254 = (f32[512,1920]{1,0:T(8,128)}, bf16[512,640]{1,0:T(8,128)(2,1)}, bf16[512,640]{1,0:T(8,128)(2,1)}, bf16[512,640]{1,0:T(8,128)(2,1)}) custom-call(s32[3]{0:T(128)S(1)} %pad_add_fusion.refs_0_, s32[1024,1]{1,0:T(8,128)S(1)} %get-tuple-element.72.refs_1_.keyclip_ref.refs_0_, f32[4,4096]{1,0:T(4,128)S(1)} %shard_map.248.refs_6_.refs_2_, ...), custom_call_target="tpu_custom_call" | custom-call | flops 3758096384 | bytes 10485760 | tf_op jit(solution)/shard_map/pallas_call | solution.py:1162
  132.1 1.7 collective-permute-done.16.refs_2_
  135.7 3.9 %shard_map.255 = (f32[8,32,896]{2,1,0:T(8,128)}, bf16[8,32,896]{2,1,0:T(8,128)(2,1)}, bf16[8,32,512]{2,1,0:T(8,128)(2,1)}, bf16[8,32,512]{2,1,0:T(8,128)(2,1)}, bf16[8,32,1024]{2,1,0:T(8,128)(2,1)}) custom-call(s32[3]{0:T(128)S(1)} %pad_add_fusion.refs_0_, f32[512,1920]{1,0:T(8,128)} %get-tuple-element.101.refs_1_, ...), custom_call_target="tpu_custom_call" | custom-call | bytes 8388608 | tf_op jit(solution)/shard_map/pallas_call | solution.py:1325
  139.6 1.5 collective-permute-start.19
  141.0 2.0 collective-permute-start.20
  143.0 6.9 %shard_map.256 = (bf16[128,1024]{1,0:T(8,128)(2,1)}, f32[8,2048]{1,0:T(8,128)S(1)}, f32[8,32,896]{2,1,0:T(8,128)}, f32[8,4096]{1,0:T(8,128)S(1)}) custom-call(s32[1024,1]{1,0:T(8,128)S(1)} %get-tuple-element.72.refs_1_.keyclip_ref.refs_0_, s32[1,1024]{1,0:T(1,128)S(1)} %get-tuple-element.73.refs_2_.rowclip_ref.refs_1_, ...), custom_call_target="tpu_custom_call", output_to_operand_aliasing={{2}: (7, {}), {3}: (8, {})} | custom-call | flops 805306368 | bytes 2097152 | tf_op jit(solution)/shard_map/pallas_call | solution.py:1035
  149.9 3.0 %collective-permute-start.23 = (f32[8,4096]{1,0:T(8,128)S(1)}, f32[8,4096]{1,0:T(8,128)S(1)}, u32[]{:S(2)}, u32[]{:S(2)}) collective-permute-start(f32[8,4096]{1,0:T(8,128)S(1)} %get-tuple-element.114), channel_id=1, source_target_pairs={{0,4},{1,5},{2,6},{3,7},{4,0},{5,1},{6,2},{7,3},{8,12},{9,13},{10,... | collective-permute-start | bytes 393224 | tf_op jit(solution)/shard_map/ppermute | solution.py:317
  152.9 1.5 collective-permute-start.22
  154.4 6.4 %collective-permute-done.22 = f32[8,2048]{1,0:T(8,128)S(1)} collective-permute-done((f32[8,2048]{1,0:T(8,128)S(1)}, f32[8,2048]{1,0:T(8,128)S(1)}, u32[]{:S(2)}, u32[]{:S(2)}) %collective-permute-start.22) | collective-permute-done | bytes 65568 | tf_op jit(solution)/shard_map/ppermute | solution.py:317
  160.8 2.3 %shard_map.257 = (f32[8,2048]{1,0:T(8,128)S(1)}, f32[8,4096]{1,0:T(8,128)S(1)}, bf16[8,32,1664]{2,1,0:T(8,128)(2,1)}, bf16[64,1024]{1,0:T(8,128)(2,1)S(1)}) custom-call(f32[8,32,896]{2,1,0:T(8,128)} %get-tuple-element.108.refs_0_, bf16[8,32,896]{2,1,0:T(8,128)(2,1)S(1)} %collective-permute-done.19.refs_1_, ...), custom_call_target="tpu_custom_call", output_to_operand_aliasing={{0}: (5, {}), {1}: (6, {})} | custom-call | bytes 4194304 | tf_op jit(solution)/shard_map/pallas_call | solution.py:1361
  163.2 4.1 %all-to-all-start.2 = ((bf16[8,32,1664]{2,1,0:T(8,128)(2,1)}), bf16[8,32,1664]{2,1,0:T(8,128)(2,1)S(1)}, u32[]{:S(2)}, u32[]{:S(2)}) async-start(bf16[8,32,1664]{2,1,0:T(8,128)(2,1)} %get-tuple-element.115), calls=%async_computation.2 | async-start | bytes 1703936 | tf_op jit(solution)/shard_map/all_to_all | solution.py:1545
  167.3 1.5 collective-permute-start.26
  169.2 2.1 collective-permute-start.24
  171.2 4.3 %collective-permute-done.27.refs_4_ = f32[8,4096]{1,0:T(8,128)S(1)} collective-permute-done((f32[8,4096]{1,0:T(8,128)S(1)}, f32[8,4096]{1,0:T(8,128)S(1)}, u32[]{:S(2)}, u32[]{:S(2)}) %collective-permute-start.27) | collective-permute-done | bytes 131104 | tf_op jit(solution)/shard_map/ppermute | solution.py:317
  176.5 6.2 %collective-permute-done.24 = f32[8,2048]{1,0:T(8,128)S(1)} collective-permute-done((f32[8,2048]{1,0:T(8,128)S(1)}, f32[8,2048]{1,0:T(8,128)S(1)}, u32[]{:S(2)}, u32[]{:S(2)}) %collective-permute-start.24) | collective-permute-done | bytes 65568 | tf_op jit(solution)/shard_map/ppermute | solution.py:317
  182.7 7.0 %shard_map.258 = (f32[128,6144]{1,0:T(8,128)}, f32[1,6144]{1,0:T(1,128)}, f32[1024,64]{1,0:T(8,128)}) custom-call(s32[1]{0:T(128)} %bitcast.8.refs_0_, f32[8,4096]{1,0:T(8,128)S(1)} %get-tuple-element.118.refs_1_, f32[8,4096]{1,0:T(8,128)S(1)} %collective-permute-done.25.refs_2_, f32[8,4096]{1,0:T(8,128)S(1)} %collective-permute-done.26.refs_3_, ...), custom_call_target="tpu_custom_call" | custom-call | flops 32768 | bytes 1024 | tf_op jit(solution)/shard_map/pallas_call | solution.py:1264
  190.6 1.5 collective-permute-start.33
  192.2 4.3 %collective-permute-start.28 = (f32[8,2048]{1,0:T(8,128)S(1)}, f32[8,2048]{1,0:T(8,128)S(1)}, u32[]{:S(2)}, u32[]{:S(2)}) collective-permute-start(f32[8,2048]{1,0:T(8,128)S(1)} %get-tuple-element.120), channel_id=1, source_target_pairs={{0,4},{1,5},{2,6},{3,7},{4,0},{5,1},{6,2},{7,3},{8,12},{9,13},{10,... | collective-permute-start | bytes 196616 | tf_op jit(solution)/shard_map/ppermute | solution.py:317
  197.7 1.7 collective-permute-done.28
  200.1 1.3 collective-permute-start.31
  201.7 3.2 %collective-permute-done.33.refs_3_ = bf16[256,1024]{1,0:T(8,128)(2,1)S(1)} collective-permute-done((bf16[256,1024]{1,0:T(8,128)(2,1)}, bf16[256,1024]{1,0:T(8,128)(2,1)S(1)}, u32[]{:S(2)}, u32[]{:S(2)}) %collective-permute-start.33) | collective-permute-done | bytes 524320 | tf_op jit(solution)/shard_map/ppermute | solution.py:317
  206.0 4.8 %shard_map.260 = (f32[128,6144]{1,0:T(8,128)}, f32[1,6144]{1,0:T(1,128)}, f32[32,1024]{1,0:T(8,128)}) custom-call(s32[1]{0:T(128)} %bitcast.8.refs_0_, f32[8,2048]{1,0:T(8,128)S(1)} %add.102.refs_1_, f32[8,2048]{1,0:T(8,128)S(1)} %collective-permute-done.29.refs_2_, ...), custom_call_target="tpu_custom_call", output_to_operand_aliasing={{0}: (10, {}), {1}: (11, {})} | custom-call | flops 32768 | bytes 1024 | tf_op jit(solution)/shard_map/pallas_call | solution.py:1264
  211.4 2.8 %shard_map.261 = (f32[128,3072]{1,0:T(8,128)}, f32[128,1024]{1,0:T(8,128)}, f32[128,2048]{1,0:T(8,128)}, f32[256,1024]{1,0:T(8,128)}) custom-call(s32[3]{0:T(128)S(1)} %pad_add_fusion.refs_0_, bf16[256,1024]{1,0:T(8,128)(2,1)S(1)} %copy-done.4, bf16[256,1024]{1,0:T(8,128)(2,1)S(1)} %collective-permute-done.32.refs_2_, ...), custom_call_target="tpu_custom_call" | custom-call | bytes 6291456 | tf_op jit(solution)/shard_map/pallas_call | solution.py:1448
  (123 shorter events, 18.6 us)
Async XLA Ops:
  0.6 22.4 %collective-permute-start = (bf16[128,1024]{1,0:T(8,128)(2,1)}, bf16[128,1024]{1,0:T(8,128)(2,1)S(1)}, u32[]{:S(2)}, u32[]{:S(2)}) collective-permute-start(bf16[128,1024]{1,0:T(8,128)(2,1)} %refs_2_.5), channel_id=1, source_target_pairs={{0,2},{1,3},{2,0},{3,1},{4,6},{5,7},{6,4},{7,5},{8,10},{9,11},{10,... | collective-permute-start | bytes 786440 | tf_op jit(solution)/shard_map/ppermute | solution.py:317
  3.7 21.6 %collective-permute-start.1 = (bf16[128,1024]{1,0:T(8,128)(2,1)}, bf16[128,1024]{1,0:T(8,128)(2,1)S(1)}, u32[]{:S(2)}, u32[]{:S(2)}) collective-permute-start(bf16[128,1024]{1,0:T(8,128)(2,1)} %refs_2_.5), channel_id=1, source_target_pairs={{0,4},{1,5},{2,6},{3,7},{4,0},{5,1},{6,2},{7,3},{8,12},{9,13},{10,... | collective-permute-start | bytes 786440 | tf_op jit(solution)/shard_map/ppermute | solution.py:317
  6.3 21.3 %collective-permute-start.2 = (bf16[128,1024]{1,0:T(8,128)(2,1)}, bf16[128,1024]{1,0:T(8,128)(2,1)S(1)}, u32[]{:S(2)}, u32[]{:S(2)}) collective-permute-start(bf16[128,1024]{1,0:T(8,128)(2,1)} %refs_2_.5), channel_id=1, source_target_pairs={{0,6},{1,7},{2,4},{3,5},{4,2},{5,3},{6,0},{7,1},{8,14},{9,15},{10,... | collective-permute-start | bytes 786440 | tf_op jit(solution)/shard_map/ppermute | solution.py:317
  6.3 32.5 %collective-permute-start.3 = (bf16[128,1024]{1,0:T(8,128)(2,1)}, bf16[128,1024]{1,0:T(8,128)(2,1)}, u32[]{:S(2)}, u32[]{:S(2)}) collective-permute-start(bf16[128,1024]{1,0:T(8,128)(2,1)} %refs_2_.5), channel_id=1, source_target_pairs={{0,1},{1,0},{2,3},{3,2},{4,5},{5,4},{6,7},{7,6},{8,9},{9,8},{10,11... | collective-permute-start | bytes 786440 | tf_op jit(solution)/shard_map/ppermute | solution.py:317
  17.0 11.9 %copy-start.6 = (f32[3072]{0:T(1024)S(1)}, f32[3072]{0:T(1024)}, u32[]{:S(2)}) copy-start(f32[3072]{0:T(1024)} %param.22) | copy-start | bytes 36868
  23.0 5.9 %copy-start.20 = (bf16[128,1024]{1,0:T(8,128)(2,1)}, bf16[128,1024]{1,0:T(8,128)(2,1)S(1)}, u32[]{:S(2)}) copy-start(bf16[128,1024]{1,0:T(8,128)(2,1)S(1)} %collective-permute-done.refs_8_) | copy-start | bytes 786436
  23.1 16.8 %collective-permute-start.4 = (bf16[128,1024]{1,0:T(8,128)(2,1)S(1)}, bf16[128,1024]{1,0:T(8,128)(2,1)}, u32[]{:S(2)}, u32[]{:S(2)}) collective-permute-start(bf16[128,1024]{1,0:T(8,128)(2,1)S(1)} %broadcast_add_fusion.2), channel_id=1, source_target_pairs={{0,1},{1,0},{2,3},{3,2},{4,5},{5,4},{6,7},{7,6},{8,9},{9,8},{10,11... | collective-permute-start | bytes 786440 | tf_op jit(solution)/shard_map/ppermute | solution.py:317
  26.1 15.3 %collective-permute-start.5 = (bf16[128,1024]{1,0:T(8,128)(2,1)}, bf16[128,1024]{1,0:T(8,128)(2,1)}, u32[]{:S(2)}, u32[]{:S(2)}) collective-permute-start(bf16[128,1024]{1,0:T(8,128)(2,1)} %broadcast_add_fusion.1), channel_id=1, source_target_pairs={{0,1},{1,0},{2,3},{3,2},{4,5},{5,4},{6,7},{7,6},{8,9},{9,8},{10,11... | collective-permute-start | bytes 786440 | tf_op jit(solution)/shard_map/ppermute | solution.py:317
  28.4 13.1 %collective-permute-start.6 = (bf16[128,1024]{1,0:T(8,128)(2,1)}, bf16[128,1024]{1,0:T(8,128)(2,1)}, u32[]{:S(2)}, u32[]{:S(2)}) collective-permute-start(bf16[128,1024]{1,0:T(8,128)(2,1)} %broadcast_add_fusion), channel_id=1, source_target_pairs={{0,1},{1,0},{2,3},{3,2},{4,5},{5,4},{6,7},{7,6},{8,9},{9,8},{10,11... | collective-permute-start | bytes 786440 | tf_op jit(solution)/shard_map/ppermute | solution.py:317
  35.3 13.8 %copy-start = (bf16[16,512,128]{2,1,0:T(8,128)(2,1)}, bf16[16,512,128]{2,1,0:T(8,128)(2,1)S(1)}, u32[]{:S(2)}) copy-start(bf16[16,512,128]{2,1,0:T(8,128)(2,1)S(1)} %get-tuple-element.80.ka_ref.va_ref) | copy-start | bytes 6291460
  35.3 25.5 %collective-permute-start.7 = (bf16[128,1024]{1,0:T(8,128)(2,1)}, bf16[128,1024]{1,0:T(8,128)(2,1)S(1)}, u32[]{:S(2)}, u32[]{:S(2)}) collective-permute-start(bf16[128,1024]{1,0:T(8,128)(2,1)} %get-tuple-element.87.refs_13_.refs_15_), channel_id=1, source_target_pairs={{0,2},{1,3},{2,0},{3,1},{4,6},{5,7},{6,4},{7,5},{8,10},{9,11},{10,... | collective-permute-start | bytes 786440 | tf_op jit(solution)/shard_map/ppermute | solution.py:317
  38.8 21.9 %collective-permute-start.8 = (bf16[128,1024]{1,0:T(8,128)(2,1)}, bf16[128,1024]{1,0:T(8,128)(2,1)S(1)}, u32[]{:S(2)}, u32[]{:S(2)}) collective-permute-start(bf16[128,1024]{1,0:T(8,128)(2,1)} %get-tuple-element.87.refs_13_.refs_15_), channel_id=1, source_target_pairs={{0,4},{1,5},{2,6},{3,7},{4,0},{5,1},{6,2},{7,3},{8,12},{9,13},{10,... | collective-permute-start | bytes 786440 | tf_op jit(solution)/shard_map/ppermute | solution.py:317
  39.9 20.9 %collective-permute-start.9 = (bf16[128,1024]{1,0:T(8,128)(2,1)}, bf16[128,1024]{1,0:T(8,128)(2,1)}, u32[]{:S(2)}, u32[]{:S(2)}) collective-permute-start(bf16[128,1024]{1,0:T(8,128)(2,1)} %get-tuple-element.87.refs_13_.refs_15_), channel_id=1, source_target_pairs={{0,6},{1,7},{2,4},{3,5},{4,2},{5,3},{6,0},{7,1},{8,14},{9,15},{10,... | collective-permute-start | bytes 786440 | tf_op jit(solution)/shard_map/ppermute | solution.py:317
  49.1 11.6 %copy-start.1 = (bf16[16,512,128]{2,1,0:T(8,128)(2,1)}, bf16[16,512,128]{2,1,0:T(8,128)(2,1)S(1)}, u32[]{:S(2)}) copy-start(bf16[16,512,128]{2,1,0:T(8,128)(2,1)S(1)} %get-tuple-element.82.kb_ref.vb_ref) | copy-start | bytes 6291460
  49.1 12.4 %copy-start.7 = (f32[2048]{0:T(1024)S(1)}, f32[2048]{0:T(1024)}, u32[]{:S(2)}) copy-start(f32[2048]{0:T(1024)} %param.26) | copy-start | bytes 24580
  49.1 12.4 %copy-start.8 = (f32[1024]{0:T(1024)S(1)}, f32[1024]{0:T(1024)}, u32[]{:S(2)}) copy-start(f32[1024]{0:T(1024)} %param.24) | copy-start | bytes 12292
  49.1 12.4 %copy-start.9 = (f32[1024]{0:T(1024)S(1)}, f32[1024]{0:T(1024)}, u32[]{:S(2)}) copy-start(f32[1024]{0:T(1024)} %param.28) | copy-start | bytes 12292
  49.2 12.4 %copy-start.11 = (s32[1,4]{1,0:T(1,128)S(1)}, s32[1,4]{1,0:T(1,128)}, u32[]{:S(2)}) copy-start(s32[1,4]{1,0:T(1,128)} %refs_0_.3) | copy-start | bytes 52
  61.6 14.4 %copy-start.19 = (bf16[128,1024]{1,0:T(8,128)(2,1)S(1)}, bf16[128,1024]{1,0:T(8,128)(2,1)}, u32[]{:S(2)}) copy-start(bf16[128,1024]{1,0:T(8,128)(2,1)} %get-tuple-element.83.refs_5_) | copy-start | bytes 786436
  70.2 32.3 %all-to-all-start = ((bf16[8,128,128]{2,1,0:T(8,128)(2,1)}), bf16[8,128,128]{2,1,0:T(8,128)(2,1)S(1)}, u32[]{:S(2)}, u32[]{:S(2)}) async-start(bf16[8,128,128]{2,1,0:T(8,128)(2,1)} %get-tuple-element.92), calls=%async_computation | async-start | bytes 524288 | tf_op jit(solution)/shard_map/all_to_all | solution.py:1500
  76.8 25.7 %collective-permute-start.12 = (bf16[128,1536]{1,0:T(8,128)(2,1)S(1)}, bf16[128,1536]{1,0:T(8,128)(2,1)S(1)}, u32[]{:S(2)}, u32[]{:S(2)}) collective-permute-start(bf16[128,1536]{1,0:T(8,128)(2,1)S(1)} %get-tuple-element.132), channel_id=1, source_target_pairs={{0,16},{8,24},{16,0},{24,8},{1,17},{9,25},{17,1},{25,9},{2,18},{10... | collective-permute-start | bytes 1179656 | tf_op jit(solution)/shard_map/ppermute | solution.py:317
  78.3 6.4 %collective-permute-start.10 = (f32[8,4096]{1,0:T(8,128)S(1)}, f32[8,4096]{1,0:T(8,128)S(1)}, u32[]{:S(2)}, u32[]{:S(2)}) collective-permute-start(f32[8,4096]{1,0:T(8,128)S(1)} %get-tuple-element.93), channel_id=1, source_target_pairs={{0,1},{1,0},{2,3},{3,2},{4,5},{5,4},{6,7},{7,6},{8,9},{9,8},{10,11... | collective-permute-start | bytes 393224 | tf_op jit(solution)/shard_map/ppermute | solution.py:317
  80.3 18.2 %collective-permute-start.13 = (bf16[128,1024]{1,0:T(8,128)(2,1)}, bf16[128,1024]{1,0:T(8,128)(2,1)S(1)}, u32[]{:S(2)}, u32[]{:S(2)}) collective-permute-start(bf16[128,1024]{1,0:T(8,128)(2,1)} %get-tuple-element.95.refs_2_.refs_11_), channel_id=1, source_target_pairs={{0,2},{1,3},{2,0},{3,1},{4,6},{5,7},{6,4},{7,5},{8,10},{9,11},{10,... | collective-permute-start | bytes 786440 | tf_op jit(solution)/shard_map/ppermute | solution.py:317
  81.8 20.7 %collective-permute-start.14 = (bf16[128,1024]{1,0:T(8,128)(2,1)}, bf16[128,1024]{1,0:T(8,128)(2,1)S(1)}, u32[]{:S(2)}, u32[]{:S(2)}) collective-permute-start(bf16[128,1024]{1,0:T(8,128)(2,1)} %get-tuple-element.95.refs_2_.refs_11_), channel_id=1, source_target_pairs={{0,4},{1,5},{2,6},{3,7},{4,0},{5,1},{6,2},{7,3},{8,12},{9,13},{10,... | collective-permute-start | bytes 786440 | tf_op jit(solution)/shard_map/ppermute | solution.py:317
  84.1 18.4 %collective-permute-start.15 = (bf16[128,1024]{1,0:T(8,128)(2,1)}, bf16[128,1024]{1,0:T(8,128)(2,1)S(1)}, u32[]{:S(2)}, u32[]{:S(2)}) collective-permute-start(bf16[128,1024]{1,0:T(8,128)(2,1)} %get-tuple-element.95.refs_2_.refs_11_), channel_id=1, source_target_pairs={{0,6},{1,7},{2,4},{3,5},{4,2},{5,3},{6,0},{7,1},{8,14},{9,15},{10,... | collective-permute-start | bytes 786440 | tf_op jit(solution)/shard_map/ppermute | solution.py:317
  84.7 13.8 %collective-permute-start.11 = (f32[8,4096]{1,0:T(8,128)S(1)}, f32[8,4096]{1,0:T(8,128)S(1)}, u32[]{:S(2)}, u32[]{:S(2)}) collective-permute-start(f32[8,4096]{1,0:T(8,128)S(1)} %add.93), channel_id=1, source_target_pairs={{0,2},{1,3},{2,0},{3,1},{4,6},{5,7},{6,4},{7,5},{8,10},{9,11},{10,... | collective-permute-start | bytes 393224 | tf_op jit(solution)/shard_map/ppermute | solution.py:317
  116.4 26.6 %all-to-all-start.1 = ((bf16[8,128,384]{2,1,0:T(8,128)(2,1)}), bf16[8,128,384]{2,1,0:T(8,128)(2,1)S(1)}, u32[]{:S(2)}, u32[]{:S(2)}) async-start(bf16[8,128,384]{2,1,0:T(8,128)(2,1)} %get-tuple-element.96), calls=%async_computation.1 | async-start | bytes 1572864 | tf_op jit(solution)/shard_map/all_to_all | solution.py:1517
  131.4 2.4 %collective-permute-start.16 = (bf16[512,640]{1,0:T(8,128)(2,1)}, bf16[512,640]{1,0:T(8,128)(2,1)S(1)}, u32[]{:S(2)}, u32[]{:S(2)}) collective-permute-start(bf16[512,640]{1,0:T(8,128)(2,1)} %get-tuple-element.102), channel_id=1, source_target_pairs={{0,8},{8,0},{16,24},{24,16},{1,9},{9,1},{17,25},{25,17},{2,10},{10... | collective-permute-start | bytes 1966088 | tf_op jit(solution)/shard_map/ppermute | solution.py:317
  131.5 3.2 %collective-permute-start.17 = (bf16[512,640]{1,0:T(8,128)(2,1)}, bf16[512,640]{1,0:T(8,128)(2,1)S(1)}, u32[]{:S(2)}, u32[]{:S(2)}) collective-permute-start(bf16[512,640]{1,0:T(8,128)(2,1)} %get-tuple-element.103), channel_id=1, source_target_pairs={{0,8},{8,0},{16,24},{24,16},{1,9},{9,1},{17,25},{25,17},{2,10},{10... | collective-permute-start | bytes 1966088 | tf_op jit(solution)/shard_map/ppermute | solution.py:317
  132.0 3.7 %collective-permute-start.18 = (bf16[512,640]{1,0:T(8,128)(2,1)}, bf16[512,640]{1,0:T(8,128)(2,1)S(1)}, u32[]{:S(2)}, u32[]{:S(2)}) collective-permute-start(bf16[512,640]{1,0:T(8,128)(2,1)} %get-tuple-element.104), channel_id=1, source_target_pairs={{0,8},{8,0},{16,24},{24,16},{1,9},{9,1},{17,25},{25,17},{2,10},{10... | collective-permute-start | bytes 1966088 | tf_op jit(solution)/shard_map/ppermute | solution.py:317
  139.6 21.3 %collective-permute-start.19 = (bf16[8,32,896]{2,1,0:T(8,128)(2,1)}, bf16[8,32,896]{2,1,0:T(8,128)(2,1)S(1)}, u32[]{:S(2)}, u32[]{:S(2)}) collective-permute-start(bf16[8,32,896]{2,1,0:T(8,128)(2,1)} %get-tuple-element.109), channel_id=1, source_target_pairs={{0,16},{8,24},{16,0},{24,8},{1,17},{9,25},{17,1},{25,9},{2,18},{10... | collective-permute-start | bytes 1376264 | tf_op jit(solution)/shard_map/ppermute | solution.py:317
  141.0 19.8 %collective-permute-start.20 = (bf16[8,32,512]{2,1,0:T(8,128)(2,1)}, bf16[8,32,512]{2,1,0:T(8,128)(2,1)S(1)}, u32[]{:S(2)}, u32[]{:S(2)}) collective-permute-start(bf16[8,32,512]{2,1,0:T(8,128)(2,1)} %get-tuple-element.110), channel_id=1, source_target_pairs={{0,1},{1,0},{2,3},{3,2},{4,5},{5,4},{6,7},{7,6},{8,9},{9,8},{10,11... | collective-permute-start | bytes 786440 | tf_op jit(solution)/shard_map/ppermute | solution.py:317
  143.0 17.8 %collective-permute-start.21 = (bf16[8,32,512]{2,1,0:T(8,128)(2,1)}, bf16[8,32,512]{2,1,0:T(8,128)(2,1)S(1)}, u32[]{:S(2)}, u32[]{:S(2)}) collective-permute-start(bf16[8,32,512]{2,1,0:T(8,128)(2,1)} %get-tuple-element.111), channel_id=1, source_target_pairs={{0,17},{1,16},{2,19},{3,18},{4,21},{5,20},{6,23},{7,22},{8,25},{9,... | collective-permute-start | bytes 786440 | tf_op jit(solution)/shard_map/ppermute | solution.py:1540
  149.9 26.3 %copy-start.3 = (f32[32,1024]{1,0:T(8,128)S(1)}, f32[32,1024]{1,0:T(8,128)}, u32[]{:S(2)}) copy-start(f32[32,1024]{1,0:T(8,128)} %refs_3_.2) | copy-start | bytes 393220
  149.9 10.9 %collective-permute-start.23 = (f32[8,4096]{1,0:T(8,128)S(1)}, f32[8,4096]{1,0:T(8,128)S(1)}, u32[]{:S(2)}, u32[]{:S(2)}) collective-permute-start(f32[8,4096]{1,0:T(8,128)S(1)} %get-tuple-element.114), channel_id=1, source_target_pairs={{0,4},{1,5},{2,6},{3,7},{4,0},{5,1},{6,2},{7,3},{8,12},{9,13},{10,... | collective-permute-start | bytes 393224 | tf_op jit(solution)/shard_map/ppermute | solution.py:317
  152.9 7.9 %collective-permute-start.22 = (f32[8,2048]{1,0:T(8,128)S(1)}, f32[8,2048]{1,0:T(8,128)S(1)}, u32[]{:S(2)}, u32[]{:S(2)}) collective-permute-start(f32[8,2048]{1,0:T(8,128)S(1)} %get-tuple-element.113), channel_id=1, source_target_pairs={{0,1},{1,0},{2,3},{3,2},{4,5},{5,4},{6,7},{7,6},{8,9},{9,8},{10,11... | collective-permute-start | bytes 196616 | tf_op jit(solution)/shard_map/ppermute | solution.py:317
  163.2 26.5 %all-to-all-start.2 = ((bf16[8,32,1664]{2,1,0:T(8,128)(2,1)}), bf16[8,32,1664]{2,1,0:T(8,128)(2,1)S(1)}, u32[]{:S(2)}, u32[]{:S(2)}) async-start(bf16[8,32,1664]{2,1,0:T(8,128)(2,1)} %get-tuple-element.115), calls=%async_computation.2 | async-start | bytes 1703936 | tf_op jit(solution)/shard_map/all_to_all | solution.py:1545
  167.3 8.3 %collective-permute-start.25 = (f32[8,4096]{1,0:T(8,128)S(1)}, f32[8,4096]{1,0:T(8,128)S(1)}, u32[]{:S(2)}, u32[]{:S(2)}) collective-permute-start(f32[8,4096]{1,0:T(8,128)S(1)} %get-tuple-element.118.refs_1_), channel_id=1, source_target_pairs={{0,8},{8,0},{16,24},{24,16},{1,9},{9,1},{17,25},{25,17},{2,10},{10... | collective-permute-start | bytes 393224 | tf_op jit(solution)/shard_map/ppermute | solution.py:317
  167.3 8.3 %collective-permute-start.26 = (f32[8,4096]{1,0:T(8,128)S(1)}, f32[8,4096]{1,0:T(8,128)S(1)}, u32[]{:S(2)}, u32[]{:S(2)}) collective-permute-start(f32[8,4096]{1,0:T(8,128)S(1)} %get-tuple-element.118.refs_1_), channel_id=1, source_target_pairs={{0,16},{8,24},{16,0},{24,8},{1,17},{9,25},{17,1},{25,9},{2,18},{10... | collective-permute-start | bytes 393224 | tf_op jit(solution)/shard_map/ppermute | solution.py:317
  168.8 6.7 %collective-permute-start.27 = (f32[8,4096]{1,0:T(8,128)S(1)}, f32[8,4096]{1,0:T(8,128)S(1)}, u32[]{:S(2)}, u32[]{:S(2)}) collective-permute-start(f32[8,4096]{1,0:T(8,128)S(1)} %get-tuple-element.118.refs_1_), channel_id=1, source_target_pairs={{0,24},{8,16},{16,8},{24,0},{1,25},{9,17},{17,9},{25,1},{2,26},{10... | collective-permute-start | bytes 393224 | tf_op jit(solution)/shard_map/ppermute | solution.py:317
  169.2 13.6 %collective-permute-start.24 = (f32[8,2048]{1,0:T(8,128)S(1)}, f32[8,2048]{1,0:T(8,128)S(1)}, u32[]{:S(2)}, u32[]{:S(2)}) collective-permute-start(f32[8,2048]{1,0:T(8,128)S(1)} %get-tuple-element.117), channel_id=1, source_target_pairs={{0,2},{1,3},{2,0},{3,1},{4,6},{5,7},{6,4},{7,5},{8,10},{9,11},{10,... | collective-permute-start | bytes 196616 | tf_op jit(solution)/shard_map/ppermute | solution.py:317
  190.6 14.3 %collective-permute-start.33 = (bf16[256,1024]{1,0:T(8,128)(2,1)}, bf16[256,1024]{1,0:T(8,128)(2,1)S(1)}, u32[]{:S(2)}, u32[]{:S(2)}) collective-permute-start(bf16[256,1024]{1,0:T(8,128)(2,1)} %get-tuple-element.126.refs_1_), channel_id=1, source_target_pairs={{0,16},{8,24},{16,0},{24,8},{1,17},{9,25},{17,1},{25,9},{2,18},{10... | collective-permute-start | bytes 1572872 | tf_op jit(solution)/shard_map/ppermute | solution.py:317
  192.2 7.3 %collective-permute-start.28 = (f32[8,2048]{1,0:T(8,128)S(1)}, f32[8,2048]{1,0:T(8,128)S(1)}, u32[]{:S(2)}, u32[]{:S(2)}) collective-permute-start(f32[8,2048]{1,0:T(8,128)S(1)} %get-tuple-element.120), channel_id=1, source_target_pairs={{0,4},{1,5},{2,6},{3,7},{4,0},{5,1},{6,2},{7,3},{8,12},{9,13},{10,... | collective-permute-start | bytes 196616 | tf_op jit(solution)/shard_map/ppermute | solution.py:317
  199.5 5.5 %collective-permute-start.29 = (f32[8,2048]{1,0:T(8,128)S(1)}, f32[8,2048]{1,0:T(8,128)S(1)}, u32[]{:S(2)}, u32[]{:S(2)}) collective-permute-start(f32[8,2048]{1,0:T(8,128)S(1)} %add.102.refs_1_), channel_id=1, source_target_pairs={{0,8},{8,0},{16,24},{24,16},{1,9},{9,1},{17,25},{25,17},{2,10},{10... | collective-permute-start | bytes 196616 | tf_op jit(solution)/shard_map/ppermute | solution.py:317
  199.5 6.4 %collective-permute-start.30 = (f32[8,2048]{1,0:T(8,128)S(1)}, f32[8,2048]{1,0:T(8,128)S(1)}, u32[]{:S(2)}, u32[]{:S(2)}) collective-permute-start(f32[8,2048]{1,0:T(8,128)S(1)} %add.102.refs_1_), channel_id=1, source_target_pairs={{0,16},{8,24},{16,0},{24,8},{1,17},{9,25},{17,1},{25,9},{2,18},{10... | collective-permute-start | bytes 196616 | tf_op jit(solution)/shard_map/ppermute | solution.py:317
  200.1 5.8 %collective-permute-start.31 = (f32[8,2048]{1,0:T(8,128)S(1)}, f32[8,2048]{1,0:T(8,128)S(1)}, u32[]{:S(2)}, u32[]{:S(2)}) collective-permute-start(f32[8,2048]{1,0:T(8,128)S(1)} %add.102.refs_1_), channel_id=1, source_target_pairs={{0,24},{8,16},{16,8},{24,0},{1,25},{9,17},{17,9},{25,1},{2,26},{10... | collective-permute-start | bytes 196616 | tf_op jit(solution)/shard_map/ppermute | solution.py:317
  201.4 10.0 %collective-permute-start.32 = (bf16[256,1024]{1,0:T(8,128)(2,1)}, bf16[256,1024]{1,0:T(8,128)(2,1)S(1)}, u32[]{:S(2)}, u32[]{:S(2)}) collective-permute-start(bf16[256,1024]{1,0:T(8,128)(2,1)} %get-tuple-element.126.refs_1_), channel_id=1, source_target_pairs={{0,8},{8,0},{16,24},{24,16},{1,9},{9,1},{17,25},{25,17},{2,10},{10... | collective-permute-start | bytes 1572872 | tf_op jit(solution)/shard_map/ppermute | solution.py:317
  205.0 6.4 %collective-permute-start.34 = (bf16[256,1024]{1,0:T(8,128)(2,1)S(1)}, bf16[256,1024]{1,0:T(8,128)(2,1)S(1)}, u32[]{:S(2)}, u32[]{:S(2)}) collective-permute-start(bf16[256,1024]{1,0:T(8,128)(2,1)S(1)} %collective-permute-done.33.refs_3_), channel_id=1, source_target_pairs={{0,8},{8,0},{16,24},{24,16},{1,9},{9,1},{17,25},{25,17},{2,10},{10... | collective-permute-start | bytes 1572872 | tf_op jit(solution)/shard_map/ppermute | solution.py:317
  (13 other events, 21.2 us)

commit v4 on v3

--- a/solution.py
+++ b/solution.py
@@ -690,7 +690,7 @@
 
 
 def probs_kernel(me_ref, keyclip_ref, rowclip_ref, qa_ref, qb_ref, ka_ref, kb_ref, *refs):
-    out_ref, keys = refs[-2:]
+    out_ref, keys = refs[-3], refs[-1]
     i, blocks = pl.program_id(0), pl.num_programs(0)
     half = ka_ref.shape[1]
 
@@ -707,7 +707,7 @@
     out_ref[...] = expo * (1.0 / jnp.sum(expo, axis=0, keepdims=True))
 
 
-def heads_probs(me, q_a, q_b, kv_a, kv_b, clip_col, clip_row, blocks, earlier):
+def heads_probs(me, q_a, q_b, kv_a, kv_b, clip_col, clip_row, blocks, earlier, passed):
     half = kv_a.shape[1]
     rows = 2 * half
     own_rows = rows // blocks
@@ -723,23 +723,24 @@
             pl.BlockSpec((1, half, LANES), lambda i, m: (m[0], 0, 0)),
             pl.BlockSpec((1, half, LANES), lambda i, m: (m[0], 0, 0)),
         ]
-        + [ANYWHERE] * len(earlier),
-        out_specs=pl.BlockSpec((rows, 2 * own_rows), lambda i, m: (0, i)),
+        + [ANYWHERE] * 2,
+        out_specs=[pl.BlockSpec((rows, 2 * own_rows), lambda i, m: (0, i)), ANYWHERE],
         scratch_shapes=[pltpu.VMEM((rows, LANES), BF)],
     )
     return pl.pallas_call(
         probs_kernel,
         grid_spec=grid_spec,
-        out_shape=shape_of((rows, 2 * rows), F32),
+        out_shape=[shape_of((rows, 2 * rows), F32), shape_of(passed.shape, passed.dtype)],
+        input_output_aliases={8: 1},
         compiler_params=params(),
         cost_estimate=cost(4 * rows * rows * LANES, 9 * MIB),
-    )(me, *all_in_hbm([clip_col, clip_row, q_a, q_b]), *all_in_hbm([kv_a, kv_b, *earlier]))
+    )(me, *all_in_hbm([clip_col, clip_row, q_a, q_b]), *all_in_hbm([kv_a, kv_b, earlier, passed]))
 
 
 def attend_back_kernel(
     me_ref, p_ref, qa_ref, qb_ref, ka_ref, kb_ref, va_ref, vb_ref, do_ref, cos_ref, sin_ref, *refs
 ):
-    out_ref, sent_ref = refs[-9:-7]
+    out_ref, sent_ref = refs[-8:-6]
     dk_ref, dv_ref, values, keys_turned, d_probs = refs[-5:]
     i, blocks = pl.program_id(0), pl.num_programs(0)
     rows = do_ref.shape[1]
@@ -816,13 +817,11 @@
             pl.BlockSpec((rows, LANES), lambda i, m: (0, 0)),
             pl.BlockSpec((rows, LANES), lambda i, m: (0, 0)),
             ANYWHERE,
-            ANYWHERE,
         ]
         + [ANYWHERE] * len(earlier),
         out_specs=[
             pl.BlockSpec((rows, 3 * LANES), lambda i, m: (0, 0)),
             pl.BlockSpec((blocks, own_rows, 3 * LANES), lambda i, m: (0, 0, 0)),
-            ANYWHERE,
             ANYWHERE,
         ],
         scratch_shapes=[
@@ -839,10 +838,9 @@
         out_shape=[
             shape_of((rows, 3 * LANES)),
             shape_of((blocks, own_rows, 3 * LANES)),
-            shape_of(passed[0].shape, passed[0].dtype),
-            shape_of(passed[1].shape, passed[1].dtype),
+            shape_of(passed.shape, passed.dtype),
         ],
-        input_output_aliases={11: 2, 12: 3},
+        input_output_aliases={11: 2},
         compiler_params=params(),
         cost_estimate=cost(8 * rows * rows * LANES, 12 * MIB),
     )(
@@ -850,7 +848,7 @@
         *all_in_hbm([probs, q_a, q_b]),
         *all_in_hbm([kv_a, kv_b, kv_a, kv_b]),
         d_o,
-        *all_in_hbm([cosine, sine, *passed, *earlier]),
+        *all_in_hbm([cosine, sine, passed, *earlier]),
     )
 
 
@@ -1370,7 +1368,7 @@
     )(in_hbm(own), from_x, from_y, from_both, *all_in_hbm([out_parts, *passed]))
 
 
-def rows_kernel(columns, rows_ref, down_ref, *refs):
+def rows_kernel(columns, rows_ref, *refs):
     out_ref = refs[-1]
     count, rows, wide = rows_ref.shape
     width = out_ref.shape[1]
@@ -1388,32 +1386,30 @@
         ]
         total += rows_ref[k, :, columns + shard :].astype(F32)
     piece = columns // LANES + count * shard // width
-    out_ref[piece * rows : (piece + 2) * rows, :] = down_ref[...]
-    out_ref[(piece + 2) * rows :, :] = total.astype(BF)
-
-
-def gather_rows(rows_mine, down_rows, columns, passed, earlier):
+    out_ref[piece * rows :, :] = total.astype(BF)
+
+
+def gather_rows(rows_mine, width, columns, passed, earlier):
     count, rows, wide = rows_mine.shape
-    width = down_rows.shape[1]
     shard = wide - width - columns
-    shape = ((columns // LANES + count * shard // width + 3) * rows, width)
+    shape = ((columns // LANES + count * shard // width + 1) * rows, width)
     return pl.pallas_call(
         lambda *refs: rows_kernel(columns, *refs),
         grid=(1,),
-        in_specs=[full(rows_mine.shape), full(down_rows.shape), ANYWHERE, ANYWHERE],
+        in_specs=[full(rows_mine.shape), ANYWHERE, ANYWHERE],
         out_specs=[ANYWHERE, full(shape)],
         out_shape=[shape_of(passed.shape, passed.dtype), shape_of(shape)],
-        input_output_aliases={2: 0},
+        input_output_aliases={1: 0},
         compiler_params=params(),
         cost_estimate=cost(0, 2 * MIB),
-    )(rows_mine, *all_in_hbm([down_rows, passed, earlier]))
+    )(rows_mine, *all_in_hbm([passed, earlier]))
 
 
 def assemble_kernel(ffn, who_ref, *refs):
     qkv_ref, out_ref, up_ref, down_ref = refs[-4:]
     width = out_ref.shape[1]
     rows = qkv_ref.shape[0] // 4
-    for j, ref in enumerate(refs[:4]):
+    for j, (ref, own_down) in enumerate(zip(refs[:4], refs[4:8])):
         owner = who_ref[2] ^ j
         core, far = owner % 2, owner // 2
         at = pl.multiple_of(core * 2 * rows + far * rows, rows)
@@ -1424,10 +1420,9 @@
                 target[pl.ds(at, rows), i * width : (i + 1) * width] = ref[here, :].astype(F32)
                 piece += 1
         for g in range(2):
-            here = slice(piece * rows, (piece + 1) * rows)
+            here = slice(g * rows, (g + 1) * rows)
             there = pl.multiple_of(core * 4 * rows + g * 2 * rows + far * rows, rows)
-            down_ref[pl.ds(there, rows), :] = ref[here, :].astype(F32)
-            piece += 1
+            down_ref[pl.ds(there, rows), :] = own_down[here, :].astype(F32)
         part = width // 2
         column = pl.multiple_of(far * part, part)
         for g in range(2):
@@ -1499,8 +1494,8 @@
     )
     d_o = lax.all_to_all(d_o, "blk", 0, 0, tiled=True)
     seconds = even_blocks(second, count)
-    probs = heads_probs(
-        me[None], q_a, q_b, kv_a, kv_b, clip_col, clip_row, count, [d_middle]
+    probs, d_attn = heads_probs(
+        me[None], q_a, q_b, kv_a, kv_b, clip_col, clip_row, count, d_middle, d_attn
     )
     sums_two = sums_two + swapped_with(sums_two, "blk", 1)
     sums_two = sums_two + swapped_with(sums_two, "blk", 2)
@@ -1511,8 +1506,8 @@
     out_kept = jnp.concatenate([attended, jnp.where(far == 0, da_low, da_high)], axis=1)
     out_sent = swapped_with(out_sent, "batch", 2)
 
-    d_qkv, d_qkv_sent, sums_two, out_sent = attend_back(
-        me[None], probs, q_a, q_b, kv_a, kv_b, d_o, cosine, sine, (sums_two, out_sent), seconds
+    d_qkv, d_qkv_sent, sums_two = attend_back(
+        me[None], probs, q_a, q_b, kv_a, kv_b, d_o, cosine, sine, sums_two, seconds
     )
     d_own = lax.all_to_all(d_qkv_sent, "blk", 0, 0, tiled=True)
     kept, *sent = weights_part(
@@ -1527,7 +1522,7 @@
         clip_col, clip_row, frames, modulation, d_middle, d_own, w_qkv,
         [own_sums, sums_two],
     )
-    sums_one = sums_one + swapped_with(sums_one, "blk", 1)
+    sums_one = sums_one + swapped_with(sums_one, "blk", 2)
     sums_two = sums_two + swapped_with(sums_two, "blk", 4)
 
     pairs = [
@@ -1543,7 +1538,7 @@
         [sums_one, sums_two],
     )
     rows_mine = lax.all_to_all(sent, "blk", 0, 0, tiled=True)
-    sums_one = sums_one + swapped_with(sums_one, "blk", 2)
+    sums_one = sums_one + swapped_with(sums_one, "blk", 1)
     sums_two = batch_parts(sums_two)
     steps_all = jnp.stack([v[clips + 1, :clips] for v in sums_two]) * (1.0 / count)
     steps_all = steps_all[place ^ jnp.arange(4, dtype=jnp.int32)].astype(jnp.int32)
@@ -1555,7 +1550,7 @@
     d_w_mod, d_b_mod, d_silu = table_part(
         place[None], sums_two, silu_cols, w_mod, 2 * width, clips
     )
-    sums_one, mine = gather_rows(rows_mine, down_rows, 3 * LANES, sums_one, d_silu)
+    sums_one, mine = gather_rows(rows_mine, width, 3 * LANES, sums_one, d_silu)
     sums_one = batch_parts(sums_one + swapped_with(sums_one, "blk", 4))
     d_w_mod, d_b_mod, d_table = table_part(
         place[None], sums_one, silu_cols, w_mod, 0, clips,
@@ -1572,12 +1567,12 @@
     )
     d_b_out, d_b_up, d_b_down = jnp.split(bias_two, [width, width + ffn])
 
-    other = swapped_with(mine, "batch", 2)
+    def everyone(value):
+        other = swapped_with(value, "batch", 2)
+        return [value, swapped_with(value, "batch", 1), other, swapped_with(other, "batch", 1)]
+
     d_w_qkv, d_w_out, d_w_up, d_w_down = assemble(
-        who,
-        [mine, swapped_with(mine, "batch", 1), other, swapped_with(other, "batch", 1)],
-        own_rows,
-        ffn,
+        who, everyone(mine) + everyone(down_rows), own_rows, ffn
     )
 
     return (

time: 215 us -> 209 us (0.972)
  waiting for transfers between devices: 37.2 us -> 32.4 us
    ppermute x34 -> x37, waiting for transfers between devices: 37.2 us -> 24.3 us  [swapped_with(): return lax.ppermute(value, axis, [(i, i ^ offset) for i in range(size)])]
    all_to_all x1, waiting for transfers between devices: 0.01 us -> 4.84 us  [heads_body(): rows_mine = lax.all_to_all(sent, 'blk', 0, 0, tiled=True)]
    all_to_all x1, waiting for transfers between devices: 0.01 us -> 2.61 us  [heads_body(): d_o = lax.all_to_all(d_o, 'blk', 0, 0, tiled=True)]
    ppermute x34 -> x37, starting transfers between devices: 45 us -> 44.4 us  [swapped_with(): return lax.ppermute(value, axis, [(i, i ^ offset) for i in range(size)])]
  transfers between devices with their start and end apart: 38 -> 41, of which waited for: 13 -> 15; matrix products, arithmetic and copies ran while one was open for 3% -> 3% of each run, Pallas kernels for 36% -> 44%
where the time goes in v4:
time: 209 us
  Pallas kernels  105 us (50%)
  starting transfers between devices  58.5 us (28%)
  waiting for transfers between devices  32.4 us (16%)
  local copies, waits for them, and re-layouts  6.86 us (3%)
  other arithmetic  4.33 us (2%)
    ppermute x37, starting transfers between devices, swapped_with(): return lax.ppermute(value, axis, [(i, i ^ offset) for i in range(size)])  44.4 us
    ppermute x37, waiting for transfers between devices, swapped_with(): return lax.ppermute(value, axis, [(i, i ^ offset) for i in range(size)])  24.3 us
    pallas_call x2, Pallas kernels, project(): pl.pallas_call(lambda *refs: project_kernel(clips, with_own, *refs), grid...  14 us
    pallas_call x1, Pallas kernels, attend_back(): pl.pallas_call(attend_back_kernel, grid_spec=grid_spec, out_shape=[shape_...  13 us
    pallas_call x2, Pallas kernels, table_part(): pl.pallas_call(lambda *refs: table_kernel(first, clips, *refs), grid=(col...  11.7 us
    pallas_call x1, Pallas kernels, attend(): pl.pallas_call(attend_kernel, grid=(width // LANES,), in_specs=[pl.BlockS...  11.5 us
    pallas_call x1, Pallas kernels, weights_part(): pl.pallas_call(lambda *refs: weights_kernel(clips, count, *refs), grid=(1...  9.72 us
    pallas_call x1, Pallas kernels, middle_part(): pl.pallas_call(lambda *refs: middle_kernel(clips, *refs), grid=(1,), in_s...  8.55 us
  transfers between devices with their start and end apart: 41, of which 15 were waited for; matrix products, arithmetic and copies ran while one was open for 3% of the time, Pallas kernels for 44%

profile of v4, /device:TPU:0, one launch (start us, length us, event | category | flops | bytes accessed | tf_op | source)
XLA Modules:
  0.0 208.5 jit_solution(5251460192726639794)
XLA Ops:
  0.6 3.1 %collective-permute-start = (bf16[128,1024]{1,0:T(8,128)(2,1)}, bf16[128,1024]{1,0:T(8,128)(2,1)S(1)}, u32[]{:S(2)}, u32[]{:S(2)}) collective-permute-start(bf16[128,1024]{1,0:T(8,128)(2,1)} %refs_2_.5), channel_id=1, source_target_pairs={{0,2},{1,3},{2,0},{3,1},{4,6},{5,7},{6,4},{7,5},{8,10},{9,11},{10,... | collective-permute-start | bytes 786440 | tf_op jit(solution)/shard_map/ppermute | solution.py:317
  3.7 2.6 %collective-permute-start.1 = (bf16[128,1024]{1,0:T(8,128)(2,1)}, bf16[128,1024]{1,0:T(8,128)(2,1)S(1)}, u32[]{:S(2)}, u32[]{:S(2)}) collective-permute-start(bf16[128,1024]{1,0:T(8,128)(2,1)} %refs_2_.5), channel_id=1, source_target_pairs={{0,4},{1,5},{2,6},{3,7},{4,0},{5,1},{6,2},{7,3},{8,12},{9,13},{10,... | collective-permute-start | bytes 786440 | tf_op jit(solution)/shard_map/ppermute | solution.py:317
  6.3 1.7 collective-permute-start.3
  11.0 5.9 %shard_map.246 = (f32[4,2048]{1,0:T(4,128)S(1)}, bf16[4,1024]{1,0:T(4,128)(2,1)S(1)}, s32[1024,1]{1,0:T(8,128)S(1)}, s32[1,1024]{1,0:T(1,128)S(1)}, f32[1024,128...) custom-call(s32[1]{0:T(128)} %bitcast.refs_0_.me_ref, ...), custom_call_target="tpu_custom_call" | custom-call | flops 16777216 | bytes 5242880 | tf_op jit(solution)/shard_map/pallas_call | solution.py:463
  17.0 4.8 %shard_map.248.refs_6_.refs_2_ = f32[4,4096]{1,0:T(4,128)S(1)} custom-call(bf16[4,1024]{1,0:T(4,128)(2,1)S(1)} %get-tuple-element.82.silu_ref, bf16[1024,6144]{1,0:T(8,128)(2,1)} %refs_6_.7, f32[1,6144]{1,0:T(1,128)S(1)} %bitcast.24), custom_call_target="tpu_custom_call" | custom-call | flops 33554432 | bytes 8388608 | tf_op jit(solution)/shard_map/pallas_call | solution.py:490
  23.4 1.9 collective-permute-done.1.refs_9_
  26.1 1.5 collective-permute-start.5
  28.9 6.4 %shard_map.247 = (bf16[512,1024]{1,0:T(8,128)(2,1)}, bf16[16,512,128]{2,1,0:T(8,128)(2,1)S(1)}, bf16[512,128]{1,0:T(8,128)(2,1)S(1)}, bf16[128,1024]{1,0:T(8,128)(2,1)}, bf16[128,1024]{1,0:T(8,128)(2,1)}) custom-call(s32[1]{0:T(128)} %bitcast.refs_0_.me_ref, s32[1024,1]{1,0:T(8,128)S(1)} %get-tuple-element.73.refs_1_.keyclip_ref.refs_0_, ...), custom_call_target="tpu_custom_call" | custom-call | flops 2147483648 | bytes 6291456 | tf_op jit(solution)/shard_map/pallas_call | solution.py:581
  35.3 3.5 %collective-permute-start.7 = (bf16[128,1024]{1,0:T(8,128)(2,1)}, bf16[128,1024]{1,0:T(8,128)(2,1)S(1)}, u32[]{:S(2)}, u32[]{:S(2)}) collective-permute-start(bf16[128,1024]{1,0:T(8,128)(2,1)} %get-tuple-element.88.refs_13_.refs_15_), channel_id=1, source_target_pairs={{0,2},{1,3},{2,0},{3,1},{4,6},{5,7},{6,4},{7,5},{8,10},{9,11},{10,... | collective-permute-start | bytes 786440 | tf_op jit(solution)/shard_map/ppermute | solution.py:317
  39.9 1.5 collective-permute-start.9
  41.5 7.6 %shard_map.249 = (bf16[512,1024]{1,0:T(8,128)(2,1)}, bf16[16,512,128]{2,1,0:T(8,128)(2,1)S(1)}, bf16[512,128]{1,0:T(8,128)(2,1)S(1)}) custom-call(s32[1]{0:T(128)} %bitcast.refs_0_.me_ref, s32[1024,1]{1,0:T(8,128)S(1)} %get-tuple-element.73.refs_1_.keyclip_ref.refs_0_, f32[4,2048]{1,0:T(4,128)S(1)} %get-tuple-element.76.refs_2_.refs_3_, ...), custom_call_target="tpu_custom_call" | custom-call | flops 2147483648 | bytes 6291456 | tf_op jit(solution)/shard_map/pallas_call | solution.py:581
  49.2 11.5 %shard_map.250 = (bf16[128,1024]{1,0:T(8,128)(2,1)}, bf16[1024,1024]{1,0:T(8,128)(2,1)S(1)}, bf16[1024,2048]{1,0:T(8,128)(2,1)S(1)}, bf16[2048,1024]{1,0:T(8,128)(2,1)S(1)}) custom-call(bf16[1024,256]{1,0:T(8,128)(2,1)} %get-tuple-element.75.keymark_ref.rowmark_ref, bf16[1024,256]{1,0:T(8,128)(2,1)} %get-tuple-element.75.keymark_ref.rowmark_ref, ...), custom_call_target="tpu_custom_call" | custom-call | flops 536870912 | bytes 1048576 | tf_op jit(solution)/shard_map/pallas_call | solution.py:668
  61.6 8.6 %shard_map.251 = (bf16[128,1024]{1,0:T(8,128)(2,1)}, bf16[128,1024]{1,0:T(8,128)(2,1)}, f32[128,1024]{1,0:T(8,128)}, bf16[128,1024]{1,0:T(8,128)(2,1)}, bf16[8,1...) custom-call(s32[1,4]{1,0:T(1,128)S(1)} %copy-done.11, s32[1024,1]{1,0:T(8,128)S(1)} %get-tuple-element.73.refs_1_.keyclip_ref.refs_0_, ...), custom_call_target="tpu_custom_call" | custom-call | flops 2684354560 | bytes 3145728 | tf_op jit(solution)/shard_map/pallas_call | solution.py:981
  70.1 2.4 %collective-permute-start.12 = (bf16[128,1024]{1,0:T(8,128)(2,1)}, bf16[128,1024]{1,0:T(8,128)(2,1)S(1)}, u32[]{:S(2)}, u32[]{:S(2)}) collective-permute-start(bf16[128,1024]{1,0:T(8,128)(2,1)} %get-tuple-element.97.refs_1_.refs_11_), channel_id=1, source_target_pairs={{0,2},{1,3},{2,0},{3,1},{4,6},{5,7},{6,4},{7,5},{8,10},{9,11},{10,... | collective-permute-start | bytes 786440 | tf_op jit(solution)/shard_map/ppermute | solution.py:317
  72.5 1.7 collective-permute-start.13
  75.0 4.4 %all-to-all-start = ((bf16[8,128,128]{2,1,0:T(8,128)(2,1)}), bf16[8,128,128]{2,1,0:T(8,128)(2,1)S(1)}, u32[]{:S(2)}, u32[]{:S(2)}) async-start(bf16[8,128,128]{2,1,0:T(8,128)(2,1)} %get-tuple-element.95), calls=%async_computation | async-start | bytes 524288 | tf_op jit(solution)/shard_map/all_to_all | solution.py:1495
  79.3 2.0 collective-permute-start.10
  81.4 8.4 %shard_map.252 = (f32[1024,2048]{1,0:T(8,128)}, bf16[128,1024]{1,0:T(8,128)(2,1)}) custom-call(s32[1]{0:T(128)} %bitcast.refs_0_.me_ref, s32[1024,1]{1,0:T(8,128)S(1)} %get-tuple-element.73.refs_1_.keyclip_ref.refs_0_, s32[1,1024]{1,0:T(1,128)S(1)} %get-tuple-element.74.refs_2_.rowclip_ref.refs_1_, ...), custom_call_target="tpu_custom_call", output_to_operand_aliasing={{1}: (8, {})} | custom-call | flops 536870912 | bytes 9437184 | tf_op jit(solution)/shard_map/pallas_call | solution.py:730
  91.5 1.5 collective-permute-start.15
  93.0 1.5 collective-permute-start.11
  94.6 4.2 %collective-permute-done.11 = f32[8,4096]{1,0:T(8,128)S(1)} collective-permute-done((f32[8,4096]{1,0:T(8,128)S(1)}, f32[8,4096]{1,0:T(8,128)S(1)}, u32[]{:S(2)}, u32[]{:S(2)}) %collective-permute-start.11) | collective-permute-done | bytes 131104 | tf_op jit(solution)/shard_map/ppermute | solution.py:317
  98.9 2.6 %all-to-all-done.do_ref = bf16[8,128,128]{2,1,0:T(8,128)(2,1)S(1)} async-done(((bf16[8,128,128]{2,1,0:T(8,128)(2,1)}), bf16[8,128,128]{2,1,0:T(8,128)(2,1)S(1)}, u32[]{:S(2)}, u32[]{:S(2)}) %all-to-all-start) | async-done | bytes 262176 | tf_op jit(solution)/shard_map/all_to_all | solution.py:1495
  101.5 13.0 %shard_map.253 = (bf16[1024,384]{1,0:T(8,128)(2,1)}, bf16[8,128,384]{2,1,0:T(8,128)(2,1)}, f32[8,4096]{1,0:T(8,128)S(1)}) custom-call(s32[1]{0:T(128)} %bitcast.refs_0_.me_ref, f32[1024,2048]{1,0:T(8,128)} %get-tuple-element.94.p_ref, bf16[512,128]{1,0:T(8,128)(2,1)S(1)} %get-tuple-element.91.qa_ref, ...), custom_call_target="tpu_custom_call", output_to_operand_aliasing={{2}: (11, {})} | custom-call | flops 1073741824 | bytes 12582912 | tf_op jit(solution)/shard_map/pallas_call | solution.py:835
  114.5 4.7 %all-to-all-start.1 = ((bf16[8,128,384]{2,1,0:T(8,128)(2,1)}), bf16[8,128,384]{2,1,0:T(8,128)(2,1)S(1)}, u32[]{:S(2)}, u32[]{:S(2)}) async-start(bf16[8,128,384]{2,1,0:T(8,128)(2,1)} %get-tuple-element.98), calls=%async_computation.1 | async-start | bytes 1572864 | tf_op jit(solution)/shard_map/all_to_all | solution.py:1512
  120.1 9.7 %shard_map.254 = (f32[512,1920]{1,0:T(8,128)}, bf16[512,640]{1,0:T(8,128)(2,1)}, bf16[512,640]{1,0:T(8,128)(2,1)}, bf16[512,640]{1,0:T(8,128)(2,1)}) custom-call(s32[3]{0:T(128)S(1)} %pad_add_fusion.refs_0_, s32[1024,1]{1,0:T(8,128)S(1)} %get-tuple-element.73.refs_1_.keyclip_ref.refs_0_, f32[4,4096]{1,0:T(4,128)S(1)} %shard_map.248.refs_6_.refs_2_, ...), custom_call_target="tpu_custom_call" | custom-call | flops 3758096384 | bytes 10485760 | tf_op jit(solution)/shard_map/pallas_call | solution.py:1160
  130.5 1.7 collective-permute-done.16.refs_2_
  134.1 3.9 %shard_map.255 = (f32[8,32,896]{2,1,0:T(8,128)}, bf16[8,32,896]{2,1,0:T(8,128)(2,1)}, bf16[8,32,512]{2,1,0:T(8,128)(2,1)}, bf16[8,32,512]{2,1,0:T(8,128)(2,1)}, bf16[8,32,1024]{2,1,0:T(8,128)(2,1)}) custom-call(s32[3]{0:T(128)S(1)} %pad_add_fusion.refs_0_, f32[512,1920]{1,0:T(8,128)} %get-tuple-element.103.refs_1_, ...), custom_call_target="tpu_custom_call" | custom-call | bytes 8388608 | tf_op jit(solution)/shard_map/pallas_call | solution.py:1323
  137.9 1.5 collective-permute-start.19
  139.4 2.0 collective-permute-start.20
  141.5 6.9 %shard_map.256 = (bf16[128,1024]{1,0:T(8,128)(2,1)}, f32[8,2048]{1,0:T(8,128)S(1)}, f32[8,32,896]{2,1,0:T(8,128)}, f32[8,4096]{1,0:T(8,128)S(1)}) custom-call(s32[1024,1]{1,0:T(8,128)S(1)} %get-tuple-element.73.refs_1_.keyclip_ref.refs_0_, s32[1,1024]{1,0:T(1,128)S(1)} %get-tuple-element.74.refs_2_.rowclip_ref.refs_1_, ...), custom_call_target="tpu_custom_call", output_to_operand_aliasing={{2}: (7, {}), {3}: (8, {})} | custom-call | flops 805306368 | bytes 2097152 | tf_op jit(solution)/shard_map/pallas_call | solution.py:1033
  148.4 3.0 %collective-permute-start.23 = (f32[8,4096]{1,0:T(8,128)S(1)}, f32[8,4096]{1,0:T(8,128)S(1)}, u32[]{:S(2)}, u32[]{:S(2)}) collective-permute-start(f32[8,4096]{1,0:T(8,128)S(1)} %get-tuple-element.116), channel_id=1, source_target_pairs={{0,4},{1,5},{2,6},{3,7},{4,0},{5,1},{6,2},{7,3},{8,12},{9,13},{10,... | collective-permute-start | bytes 393224 | tf_op jit(solution)/shard_map/ppermute | solution.py:317
  151.3 1.5 collective-permute-start.22
  152.8 3.0 %collective-permute-done.22 = f32[8,2048]{1,0:T(8,128)S(1)} collective-permute-done((f32[8,2048]{1,0:T(8,128)S(1)}, f32[8,2048]{1,0:T(8,128)S(1)}, u32[]{:S(2)}, u32[]{:S(2)}) %collective-permute-start.22) | collective-permute-done | bytes 65568 | tf_op jit(solution)/shard_map/ppermute | solution.py:317
  155.7 1.4 collective-permute-done.23
  157.8 2.3 %shard_map.257 = (f32[8,2048]{1,0:T(8,128)S(1)}, f32[8,4096]{1,0:T(8,128)S(1)}, bf16[8,32,1664]{2,1,0:T(8,128)(2,1)}, bf16[64,1024]{1,0:T(8,128)(2,1)S(1)}) custom-call(f32[8,32,896]{2,1,0:T(8,128)} %get-tuple-element.110.refs_0_, bf16[8,32,896]{2,1,0:T(8,128)(2,1)S(1)} %collective-permute-done.19.refs_1_, ...), custom_call_target="tpu_custom_call", output_to_operand_aliasing={{0}: (5, {}), {1}: (6, {})} | custom-call | bytes 4194304 | tf_op jit(solution)/shard_map/pallas_call | solution.py:1359
  160.1 5.0 %all-to-all-start.2 = ((bf16[8,32,1664]{2,1,0:T(8,128)(2,1)}), bf16[8,32,1664]{2,1,0:T(8,128)(2,1)S(1)}, u32[]{:S(2)}, u32[]{:S(2)}) async-start(bf16[8,32,1664]{2,1,0:T(8,128)(2,1)} %get-tuple-element.117), calls=%async_computation.2 | async-start | bytes 1703936 | tf_op jit(solution)/shard_map/all_to_all | solution.py:1540
  165.2 1.6 collective-permute-start.26
  167.0 2.1 %collective-permute-start.24 = (f32[8,2048]{1,0:T(8,128)S(1)}, f32[8,2048]{1,0:T(8,128)S(1)}, u32[]{:S(2)}, u32[]{:S(2)}) collective-permute-start(f32[8,2048]{1,0:T(8,128)S(1)} %get-tuple-element.118), channel_id=1, source_target_pairs={{0,1},{1,0},{2,3},{3,2},{4,5},{5,4},{6,7},{7,6},{8,9},{9,8},{10,11... | collective-permute-start | bytes 196616 | tf_op jit(solution)/shard_map/ppermute | solution.py:317
  169.1 1.5 collective-permute-start.36
  170.6 2.8 %collective-permute-done.27.refs_4_ = f32[8,4096]{1,0:T(8,128)S(1)} collective-permute-done((f32[8,4096]{1,0:T(8,128)S(1)}, f32[8,4096]{1,0:T(8,128)S(1)}, u32[]{:S(2)}, u32[]{:S(2)}) %collective-permute-start.27) | collective-permute-done | bytes 131104 | tf_op jit(solution)/shard_map/ppermute | solution.py:317
  175.0 7.0 %shard_map.258 = (f32[128,6144]{1,0:T(8,128)}, f32[1,6144]{1,0:T(1,128)}, f32[1024,64]{1,0:T(8,128)}) custom-call(s32[1]{0:T(128)} %bitcast.8.refs_0_, f32[8,4096]{1,0:T(8,128)S(1)} %get-tuple-element.119.refs_1_, f32[8,4096]{1,0:T(8,128)S(1)} %collective-permute-done.25.refs_2_, f32[8,4096]{1,0:T(8,128)S(1)} %collective-permute-done.26.refs_3_, ...), custom_call_target="tpu_custom_call" | custom-call | flops 32768 | bytes 1024 | tf_op jit(solution)/shard_map/pallas_call | solution.py:1262
  181.9 4.8 %all-to-all-done.2.refs_0_ = bf16[8,32,1664]{2,1,0:T(8,128)(2,1)S(1)} async-done(((bf16[8,32,1664]{2,1,0:T(8,128)(2,1)}), bf16[8,32,1664]{2,1,0:T(8,128)(2,1)S(1)}, u32[]{:S(2)}, u32[]{:S(2)}) %all-to-all-start.2) | async-done | bytes 852000 | tf_op jit(solution)/shard_map/all_to_all | solution.py:1540
  187.6 1.5 collective-permute-start.33
  190.5 4.2 %collective-permute-done.28 = f32[8,2048]{1,0:T(8,128)S(1)} collective-permute-done((f32[8,2048]{1,0:T(8,128)S(1)}, f32[8,2048]{1,0:T(8,128)S(1)}, u32[]{:S(2)}, u32[]{:S(2)}) %collective-permute-start.28) | collective-permute-done | bytes 65568 | tf_op jit(solution)/shard_map/ppermute | solution.py:317
  195.4 1.3 collective-permute-start.31
  197.2 2.5 %collective-permute-done.30.refs_3_ = f32[8,2048]{1,0:T(8,128)S(1)} collective-permute-done((f32[8,2048]{1,0:T(8,128)S(1)}, f32[8,2048]{1,0:T(8,128)S(1)}, u32[]{:S(2)}, u32[]{:S(2)}) %collective-permute-start.30) | collective-permute-done | bytes 65568 | tf_op jit(solution)/shard_map/ppermute | solution.py:317
  200.3 4.8 %shard_map.260 = (f32[128,6144]{1,0:T(8,128)}, f32[1,6144]{1,0:T(1,128)}, f32[32,1024]{1,0:T(8,128)}) custom-call(s32[1]{0:T(128)} %bitcast.8.refs_0_, f32[8,2048]{1,0:T(8,128)S(1)} %add.102.refs_1_, f32[8,2048]{1,0:T(8,128)S(1)} %collective-permute-done.29.refs_2_, ...), custom_call_target="tpu_custom_call", output_to_operand_aliasing={{0}: (10, {}), {1}: (11, {})} | custom-call | flops 32768 | bytes 1024 | tf_op jit(solution)/shard_map/pallas_call | solution.py:1262
  205.7 2.8 %shard_map.261 = (f32[128,3072]{1,0:T(8,128)}, f32[128,1024]{1,0:T(8,128)}, f32[128,2048]{1,0:T(8,128)}, f32[256,1024]{1,0:T(8,128)}) custom-call(s32[3]{0:T(128)S(1)} %pad_add_fusion.refs_0_, bf16[192,1024]{1,0:T(8,128)(2,1)S(1)} %copy-done.4, bf16[192,1024]{1,0:T(8,128)(2,1)S(1)} %collective-permute-done.32.refs_2_, ...), custom_call_target="tpu_custom_call" | custom-call | bytes 6291456 | tf_op jit(solution)/shard_map/pallas_call | solution.py:1443
  (129 shorter events, 21.0 us)
Async XLA Ops:
  0.6 22.4 %collective-permute-start = (bf16[128,1024]{1,0:T(8,128)(2,1)}, bf16[128,1024]{1,0:T(8,128)(2,1)S(1)}, u32[]{:S(2)}, u32[]{:S(2)}) collective-permute-start(bf16[128,1024]{1,0:T(8,128)(2,1)} %refs_2_.5), channel_id=1, source_target_pairs={{0,2},{1,3},{2,0},{3,1},{4,6},{5,7},{6,4},{7,5},{8,10},{9,11},{10,... | collective-permute-start | bytes 786440 | tf_op jit(solution)/shard_map/ppermute | solution.py:317
  3.7 21.6 %collective-permute-start.1 = (bf16[128,1024]{1,0:T(8,128)(2,1)}, bf16[128,1024]{1,0:T(8,128)(2,1)S(1)}, u32[]{:S(2)}, u32[]{:S(2)}) collective-permute-start(bf16[128,1024]{1,0:T(8,128)(2,1)} %refs_2_.5), channel_id=1, source_target_pairs={{0,4},{1,5},{2,6},{3,7},{4,0},{5,1},{6,2},{7,3},{8,12},{9,13},{10,... | collective-permute-start | bytes 786440 | tf_op jit(solution)/shard_map/ppermute | solution.py:317
  6.3 21.3 %collective-permute-start.2 = (bf16[128,1024]{1,0:T(8,128)(2,1)}, bf16[128,1024]{1,0:T(8,128)(2,1)S(1)}, u32[]{:S(2)}, u32[]{:S(2)}) collective-permute-start(bf16[128,1024]{1,0:T(8,128)(2,1)} %refs_2_.5), channel_id=1, source_target_pairs={{0,6},{1,7},{2,4},{3,5},{4,2},{5,3},{6,0},{7,1},{8,14},{9,15},{10,... | collective-permute-start | bytes 786440 | tf_op jit(solution)/shard_map/ppermute | solution.py:317
  6.3 32.5 %collective-permute-start.3 = (bf16[128,1024]{1,0:T(8,128)(2,1)}, bf16[128,1024]{1,0:T(8,128)(2,1)}, u32[]{:S(2)}, u32[]{:S(2)}) collective-permute-start(bf16[128,1024]{1,0:T(8,128)(2,1)} %refs_2_.5), channel_id=1, source_target_pairs={{0,1},{1,0},{2,3},{3,2},{4,5},{5,4},{6,7},{7,6},{8,9},{9,8},{10,11... | collective-permute-start | bytes 786440 | tf_op jit(solution)/shard_map/ppermute | solution.py:317
  23.1 16.8 %collective-permute-start.4 = (bf16[128,1024]{1,0:T(8,128)(2,1)S(1)}, bf16[128,1024]{1,0:T(8,128)(2,1)}, u32[]{:S(2)}, u32[]{:S(2)}) collective-permute-start(bf16[128,1024]{1,0:T(8,128)(2,1)S(1)} %broadcast_add_fusion.2), channel_id=1, source_target_pairs={{0,1},{1,0},{2,3},{3,2},{4,5},{5,4},{6,7},{7,6},{8,9},{9,8},{10,11... | collective-permute-start | bytes 786440 | tf_op jit(solution)/shard_map/ppermute | solution.py:317
  26.1 15.3 %collective-permute-start.5 = (bf16[128,1024]{1,0:T(8,128)(2,1)}, bf16[128,1024]{1,0:T(8,128)(2,1)}, u32[]{:S(2)}, u32[]{:S(2)}) collective-permute-start(bf16[128,1024]{1,0:T(8,128)(2,1)} %broadcast_add_fusion.1), channel_id=1, source_target_pairs={{0,1},{1,0},{2,3},{3,2},{4,5},{5,4},{6,7},{7,6},{8,9},{9,8},{10,11... | collective-permute-start | bytes 786440 | tf_op jit(solution)/shard_map/ppermute | solution.py:317
  28.4 13.1 %collective-permute-start.6 = (bf16[128,1024]{1,0:T(8,128)(2,1)}, bf16[128,1024]{1,0:T(8,128)(2,1)}, u32[]{:S(2)}, u32[]{:S(2)}) collective-permute-start(bf16[128,1024]{1,0:T(8,128)(2,1)} %broadcast_add_fusion), channel_id=1, source_target_pairs={{0,1},{1,0},{2,3},{3,2},{4,5},{5,4},{6,7},{7,6},{8,9},{9,8},{10,11... | collective-permute-start | bytes 786440 | tf_op jit(solution)/shard_map/ppermute | solution.py:317
  35.3 13.8 %copy-start = (bf16[16,512,128]{2,1,0:T(8,128)(2,1)}, bf16[16,512,128]{2,1,0:T(8,128)(2,1)S(1)}, u32[]{:S(2)}) copy-start(bf16[16,512,128]{2,1,0:T(8,128)(2,1)S(1)} %get-tuple-element.81.ka_ref.va_ref) | copy-start | bytes 6291460
  35.3 25.4 %collective-permute-start.7 = (bf16[128,1024]{1,0:T(8,128)(2,1)}, bf16[128,1024]{1,0:T(8,128)(2,1)S(1)}, u32[]{:S(2)}, u32[]{:S(2)}) collective-permute-start(bf16[128,1024]{1,0:T(8,128)(2,1)} %get-tuple-element.88.refs_13_.refs_15_), channel_id=1, source_target_pairs={{0,2},{1,3},{2,0},{3,1},{4,6},{5,7},{6,4},{7,5},{8,10},{9,11},{10,... | collective-permute-start | bytes 786440 | tf_op jit(solution)/shard_map/ppermute | solution.py:317
  38.8 21.9 %collective-permute-start.8 = (bf16[128,1024]{1,0:T(8,128)(2,1)}, bf16[128,1024]{1,0:T(8,128)(2,1)S(1)}, u32[]{:S(2)}, u32[]{:S(2)}) collective-permute-start(bf16[128,1024]{1,0:T(8,128)(2,1)} %get-tuple-element.88.refs_13_.refs_15_), channel_id=1, source_target_pairs={{0,4},{1,5},{2,6},{3,7},{4,0},{5,1},{6,2},{7,3},{8,12},{9,13},{10,... | collective-permute-start | bytes 786440 | tf_op jit(solution)/shard_map/ppermute | solution.py:317
  39.9 20.9 %collective-permute-start.9 = (bf16[128,1024]{1,0:T(8,128)(2,1)}, bf16[128,1024]{1,0:T(8,128)(2,1)}, u32[]{:S(2)}, u32[]{:S(2)}) collective-permute-start(bf16[128,1024]{1,0:T(8,128)(2,1)} %get-tuple-element.88.refs_13_.refs_15_), channel_id=1, source_target_pairs={{0,6},{1,7},{2,4},{3,5},{4,2},{5,3},{6,0},{7,1},{8,14},{9,15},{10,... | collective-permute-start | bytes 786440 | tf_op jit(solution)/shard_map/ppermute | solution.py:317
  49.1 12.4 %copy-start.7 = (f32[2048]{0:T(1024)S(1)}, f32[2048]{0:T(1024)}, u32[]{:S(2)}) copy-start(f32[2048]{0:T(1024)} %param.26) | copy-start | bytes 24580
  49.1 12.4 %copy-start.8 = (f32[1024]{0:T(1024)S(1)}, f32[1024]{0:T(1024)}, u32[]{:S(2)}) copy-start(f32[1024]{0:T(1024)} %param.24) | copy-start | bytes 12292
  49.1 12.4 %copy-start.9 = (f32[1024]{0:T(1024)S(1)}, f32[1024]{0:T(1024)}, u32[]{:S(2)}) copy-start(f32[1024]{0:T(1024)} %param.28) | copy-start | bytes 12292
  49.2 12.4 %copy-start.11 = (s32[1,4]{1,0:T(1,128)S(1)}, s32[1,4]{1,0:T(1,128)}, u32[]{:S(2)}) copy-start(s32[1,4]{1,0:T(1,128)} %refs_0_.3) | copy-start | bytes 52
  70.1 20.6 %copy-start.18 = (bf16[128,1024]{1,0:T(8,128)(2,1)S(1)}, bf16[128,1024]{1,0:T(8,128)(2,1)}, u32[]{:S(2)}) copy-start(bf16[128,1024]{1,0:T(8,128)(2,1)} %get-tuple-element.84.refs_5_) | copy-start | bytes 786436
  70.1 28.7 %collective-permute-start.12 = (bf16[128,1024]{1,0:T(8,128)(2,1)}, bf16[128,1024]{1,0:T(8,128)(2,1)S(1)}, u32[]{:S(2)}, u32[]{:S(2)}) collective-permute-start(bf16[128,1024]{1,0:T(8,128)(2,1)} %get-tuple-element.97.refs_1_.refs_11_), channel_id=1, source_target_pairs={{0,2},{1,3},{2,0},{3,1},{4,6},{5,7},{6,4},{7,5},{8,10},{9,11},{10,... | collective-permute-start | bytes 786440 | tf_op jit(solution)/shard_map/ppermute | solution.py:317
  72.5 26.3 %collective-permute-start.13 = (bf16[128,1024]{1,0:T(8,128)(2,1)}, bf16[128,1024]{1,0:T(8,128)(2,1)S(1)}, u32[]{:S(2)}, u32[]{:S(2)}) collective-permute-start(bf16[128,1024]{1,0:T(8,128)(2,1)} %get-tuple-element.97.refs_1_.refs_11_), channel_id=1, source_target_pairs={{0,4},{1,5},{2,6},{3,7},{4,0},{5,1},{6,2},{7,3},{8,12},{9,13},{10,... | collective-permute-start | bytes 786440 | tf_op jit(solution)/shard_map/ppermute | solution.py:317
  74.2 24.6 %collective-permute-start.14 = (bf16[128,1024]{1,0:T(8,128)(2,1)}, bf16[128,1024]{1,0:T(8,128)(2,1)S(1)}, u32[]{:S(2)}, u32[]{:S(2)}) collective-permute-start(bf16[128,1024]{1,0:T(8,128)(2,1)} %get-tuple-element.97.refs_1_.refs_11_), channel_id=1, source_target_pairs={{0,6},{1,7},{2,4},{3,5},{4,2},{5,3},{6,0},{7,1},{8,14},{9,15},{10,... | collective-permute-start | bytes 786440 | tf_op jit(solution)/shard_map/ppermute | solution.py:317
  75.0 26.5 %all-to-all-start = ((bf16[8,128,128]{2,1,0:T(8,128)(2,1)}), bf16[8,128,128]{2,1,0:T(8,128)(2,1)S(1)}, u32[]{:S(2)}, u32[]{:S(2)}) async-start(bf16[8,128,128]{2,1,0:T(8,128)(2,1)} %get-tuple-element.95), calls=%async_computation | async-start | bytes 524288 | tf_op jit(solution)/shard_map/all_to_all | solution.py:1495
  79.3 13.7 %collective-permute-start.10 = (f32[8,4096]{1,0:T(8,128)S(1)}, f32[8,4096]{1,0:T(8,128)S(1)}, u32[]{:S(2)}, u32[]{:S(2)}) collective-permute-start(f32[8,4096]{1,0:T(8,128)S(1)} %get-tuple-element.96), channel_id=1, source_target_pairs={{0,1},{1,0},{2,3},{3,2},{4,5},{5,4},{6,7},{7,6},{8,9},{9,8},{10,11... | collective-permute-start | bytes 393224 | tf_op jit(solution)/shard_map/ppermute | solution.py:317
  91.5 27.8 %collective-permute-start.15 = (bf16[128,1536]{1,0:T(8,128)(2,1)S(1)}, bf16[128,1536]{1,0:T(8,128)(2,1)S(1)}, u32[]{:S(2)}, u32[]{:S(2)}) collective-permute-start(bf16[128,1536]{1,0:T(8,128)(2,1)S(1)} %get-tuple-element.133), channel_id=1, source_target_pairs={{0,16},{8,24},{16,0},{24,8},{1,17},{9,25},{17,1},{25,9},{2,18},{10... | collective-permute-start | bytes 1179656 | tf_op jit(solution)/shard_map/ppermute | solution.py:317
  93.0 5.7 %collective-permute-start.11 = (f32[8,4096]{1,0:T(8,128)S(1)}, f32[8,4096]{1,0:T(8,128)S(1)}, u32[]{:S(2)}, u32[]{:S(2)}) collective-permute-start(f32[8,4096]{1,0:T(8,128)S(1)} %add.93), channel_id=1, source_target_pairs={{0,2},{1,3},{2,0},{3,1},{4,6},{5,7},{6,4},{7,5},{8,10},{9,11},{10,... | collective-permute-start | bytes 393224 | tf_op jit(solution)/shard_map/ppermute | solution.py:317
  114.5 26.9 %all-to-all-start.1 = ((bf16[8,128,384]{2,1,0:T(8,128)(2,1)}), bf16[8,128,384]{2,1,0:T(8,128)(2,1)S(1)}, u32[]{:S(2)}, u32[]{:S(2)}) async-start(bf16[8,128,384]{2,1,0:T(8,128)(2,1)} %get-tuple-element.98), calls=%async_computation.1 | async-start | bytes 1572864 | tf_op jit(solution)/shard_map/all_to_all | solution.py:1512
  129.8 2.4 %collective-permute-start.16 = (bf16[512,640]{1,0:T(8,128)(2,1)}, bf16[512,640]{1,0:T(8,128)(2,1)S(1)}, u32[]{:S(2)}, u32[]{:S(2)}) collective-permute-start(bf16[512,640]{1,0:T(8,128)(2,1)} %get-tuple-element.104), channel_id=1, source_target_pairs={{0,8},{8,0},{16,24},{24,16},{1,9},{9,1},{17,25},{25,17},{2,10},{10... | collective-permute-start | bytes 1966088 | tf_op jit(solution)/shard_map/ppermute | solution.py:317
  129.9 3.2 %collective-permute-start.17 = (bf16[512,640]{1,0:T(8,128)(2,1)}, bf16[512,640]{1,0:T(8,128)(2,1)S(1)}, u32[]{:S(2)}, u32[]{:S(2)}) collective-permute-start(bf16[512,640]{1,0:T(8,128)(2,1)} %get-tuple-element.105), channel_id=1, source_target_pairs={{0,8},{8,0},{16,24},{24,16},{1,9},{9,1},{17,25},{25,17},{2,10},{10... | collective-permute-start | bytes 1966088 | tf_op jit(solution)/shard_map/ppermute | solution.py:317
  130.4 3.7 %collective-permute-start.18 = (bf16[512,640]{1,0:T(8,128)(2,1)}, bf16[512,640]{1,0:T(8,128)(2,1)S(1)}, u32[]{:S(2)}, u32[]{:S(2)}) collective-permute-start(bf16[512,640]{1,0:T(8,128)(2,1)} %get-tuple-element.106), channel_id=1, source_target_pairs={{0,8},{8,0},{16,24},{24,16},{1,9},{9,1},{17,25},{25,17},{2,10},{10... | collective-permute-start | bytes 1966088 | tf_op jit(solution)/shard_map/ppermute | solution.py:317
  137.9 19.9 %collective-permute-start.19 = (bf16[8,32,896]{2,1,0:T(8,128)(2,1)}, bf16[8,32,896]{2,1,0:T(8,128)(2,1)S(1)}, u32[]{:S(2)}, u32[]{:S(2)}) collective-permute-start(bf16[8,32,896]{2,1,0:T(8,128)(2,1)} %get-tuple-element.111), channel_id=1, source_target_pairs={{0,16},{8,24},{16,0},{24,8},{1,17},{9,25},{17,1},{25,9},{2,18},{10... | collective-permute-start | bytes 1376264 | tf_op jit(solution)/shard_map/ppermute | solution.py:317
  139.4 17.7 %collective-permute-start.20 = (bf16[8,32,512]{2,1,0:T(8,128)(2,1)}, bf16[8,32,512]{2,1,0:T(8,128)(2,1)S(1)}, u32[]{:S(2)}, u32[]{:S(2)}) collective-permute-start(bf16[8,32,512]{2,1,0:T(8,128)(2,1)} %get-tuple-element.112), channel_id=1, source_target_pairs={{0,1},{1,0},{2,3},{3,2},{4,5},{5,4},{6,7},{7,6},{8,9},{9,8},{10,11... | collective-permute-start | bytes 786440 | tf_op jit(solution)/shard_map/ppermute | solution.py:317
  141.5 16.3 %collective-permute-start.21 = (bf16[8,32,512]{2,1,0:T(8,128)(2,1)}, bf16[8,32,512]{2,1,0:T(8,128)(2,1)S(1)}, u32[]{:S(2)}, u32[]{:S(2)}) collective-permute-start(bf16[8,32,512]{2,1,0:T(8,128)(2,1)} %get-tuple-element.113), channel_id=1, source_target_pairs={{0,17},{1,16},{2,19},{3,18},{4,21},{5,20},{6,23},{7,22},{8,25},{9,... | collective-permute-start | bytes 786440 | tf_op jit(solution)/shard_map/ppermute | solution.py:1535
  148.3 25.8 %copy-start.3 = (f32[32,1024]{1,0:T(8,128)S(1)}, f32[32,1024]{1,0:T(8,128)}, u32[]{:S(2)}) copy-start(f32[32,1024]{1,0:T(8,128)} %refs_3_.2) | copy-start | bytes 393220
  148.4 8.8 %collective-permute-start.23 = (f32[8,4096]{1,0:T(8,128)S(1)}, f32[8,4096]{1,0:T(8,128)S(1)}, u32[]{:S(2)}, u32[]{:S(2)}) collective-permute-start(f32[8,4096]{1,0:T(8,128)S(1)} %get-tuple-element.116), channel_id=1, source_target_pairs={{0,4},{1,5},{2,6},{3,7},{4,0},{5,1},{6,2},{7,3},{8,12},{9,13},{10,... | collective-permute-start | bytes 393224 | tf_op jit(solution)/shard_map/ppermute | solution.py:317
  151.3 4.4 %collective-permute-start.22 = (f32[8,2048]{1,0:T(8,128)S(1)}, f32[8,2048]{1,0:T(8,128)S(1)}, u32[]{:S(2)}, u32[]{:S(2)}) collective-permute-start(f32[8,2048]{1,0:T(8,128)S(1)} %get-tuple-element.115), channel_id=1, source_target_pairs={{0,2},{1,3},{2,0},{3,1},{4,6},{5,7},{6,4},{7,5},{8,10},{9,11},{10,... | collective-permute-start | bytes 196616 | tf_op jit(solution)/shard_map/ppermute | solution.py:317
  160.1 26.7 %all-to-all-start.2 = ((bf16[8,32,1664]{2,1,0:T(8,128)(2,1)}), bf16[8,32,1664]{2,1,0:T(8,128)(2,1)S(1)}, u32[]{:S(2)}, u32[]{:S(2)}) async-start(bf16[8,32,1664]{2,1,0:T(8,128)(2,1)} %get-tuple-element.117), calls=%async_computation.2 | async-start | bytes 1703936 | tf_op jit(solution)/shard_map/all_to_all | solution.py:1540
  165.1 8.3 %collective-permute-start.25 = (f32[8,4096]{1,0:T(8,128)S(1)}, f32[8,4096]{1,0:T(8,128)S(1)}, u32[]{:S(2)}, u32[]{:S(2)}) collective-permute-start(f32[8,4096]{1,0:T(8,128)S(1)} %get-tuple-element.119.refs_1_), channel_id=1, source_target_pairs={{0,8},{8,0},{16,24},{24,16},{1,9},{9,1},{17,25},{25,17},{2,10},{10... | collective-permute-start | bytes 393224 | tf_op jit(solution)/shard_map/ppermute | solution.py:317
  165.2 8.2 %collective-permute-start.26 = (f32[8,4096]{1,0:T(8,128)S(1)}, f32[8,4096]{1,0:T(8,128)S(1)}, u32[]{:S(2)}, u32[]{:S(2)}) collective-permute-start(f32[8,4096]{1,0:T(8,128)S(1)} %get-tuple-element.119.refs_1_), channel_id=1, source_target_pairs={{0,16},{8,24},{16,0},{24,8},{1,17},{9,25},{17,1},{25,9},{2,18},{10... | collective-permute-start | bytes 393224 | tf_op jit(solution)/shard_map/ppermute | solution.py:317
  166.7 6.7 %collective-permute-start.27 = (f32[8,4096]{1,0:T(8,128)S(1)}, f32[8,4096]{1,0:T(8,128)S(1)}, u32[]{:S(2)}, u32[]{:S(2)}) collective-permute-start(f32[8,4096]{1,0:T(8,128)S(1)} %get-tuple-element.119.refs_1_), channel_id=1, source_target_pairs={{0,24},{8,16},{16,8},{24,0},{1,25},{9,17},{17,9},{25,1},{2,26},{10... | collective-permute-start | bytes 393224 | tf_op jit(solution)/shard_map/ppermute | solution.py:317
  167.0 7.9 %collective-permute-start.24 = (f32[8,2048]{1,0:T(8,128)S(1)}, f32[8,2048]{1,0:T(8,128)S(1)}, u32[]{:S(2)}, u32[]{:S(2)}) collective-permute-start(f32[8,2048]{1,0:T(8,128)S(1)} %get-tuple-element.118), channel_id=1, source_target_pairs={{0,1},{1,0},{2,3},{3,2},{4,5},{5,4},{6,7},{7,6},{8,9},{9,8},{10,11... | collective-permute-start | bytes 196616 | tf_op jit(solution)/shard_map/ppermute | solution.py:317
  169.1 27.5 %collective-permute-start.36 = (bf16[64,1024]{1,0:T(8,128)(2,1)S(1)}, bf16[64,1024]{1,0:T(8,128)(2,1)S(1)}, u32[]{:S(2)}, u32[]{:S(2)}) collective-permute-start(bf16[64,1024]{1,0:T(8,128)(2,1)S(1)} %get-tuple-element.128.refs_5_), channel_id=1, source_target_pairs={{0,16},{8,24},{16,0},{24,8},{1,17},{9,25},{17,1},{25,9},{2,18},{10... | collective-permute-start | bytes 393224 | tf_op jit(solution)/shard_map/ppermute | solution.py:317
  187.6 12.1 %collective-permute-start.33 = (bf16[192,1024]{1,0:T(8,128)(2,1)}, bf16[192,1024]{1,0:T(8,128)(2,1)S(1)}, u32[]{:S(2)}, u32[]{:S(2)}) collective-permute-start(bf16[192,1024]{1,0:T(8,128)(2,1)} %get-tuple-element.127.refs_1_), channel_id=1, source_target_pairs={{0,16},{8,24},{16,0},{24,8},{1,17},{9,25},{17,1},{25,9},{2,18},{10... | collective-permute-start | bytes 1179656 | tf_op jit(solution)/shard_map/ppermute | solution.py:317
  189.2 5.5 %collective-permute-start.28 = (f32[8,2048]{1,0:T(8,128)S(1)}, f32[8,2048]{1,0:T(8,128)S(1)}, u32[]{:S(2)}, u32[]{:S(2)}) collective-permute-start(f32[8,2048]{1,0:T(8,128)S(1)} %get-tuple-element.121), channel_id=1, source_target_pairs={{0,4},{1,5},{2,6},{3,7},{4,0},{5,1},{6,2},{7,3},{8,12},{9,13},{10,... | collective-permute-start | bytes 196616 | tf_op jit(solution)/shard_map/ppermute | solution.py:317
  194.7 2.4 %collective-permute-start.29 = (f32[8,2048]{1,0:T(8,128)S(1)}, f32[8,2048]{1,0:T(8,128)S(1)}, u32[]{:S(2)}, u32[]{:S(2)}) collective-permute-start(f32[8,2048]{1,0:T(8,128)S(1)} %add.102.refs_1_), channel_id=1, source_target_pairs={{0,8},{8,0},{16,24},{24,16},{1,9},{9,1},{17,25},{25,17},{2,10},{10... | collective-permute-start | bytes 196616 | tf_op jit(solution)/shard_map/ppermute | solution.py:317
  194.8 5.0 %collective-permute-start.30 = (f32[8,2048]{1,0:T(8,128)S(1)}, f32[8,2048]{1,0:T(8,128)S(1)}, u32[]{:S(2)}, u32[]{:S(2)}) collective-permute-start(f32[8,2048]{1,0:T(8,128)S(1)} %add.102.refs_1_), channel_id=1, source_target_pairs={{0,16},{8,24},{16,0},{24,8},{1,17},{9,25},{17,1},{25,9},{2,18},{10... | collective-permute-start | bytes 196616 | tf_op jit(solution)/shard_map/ppermute | solution.py:317
  195.4 4.9 %collective-permute-start.31 = (f32[8,2048]{1,0:T(8,128)S(1)}, f32[8,2048]{1,0:T(8,128)S(1)}, u32[]{:S(2)}, u32[]{:S(2)}) collective-permute-start(f32[8,2048]{1,0:T(8,128)S(1)} %add.102.refs_1_), channel_id=1, source_target_pairs={{0,24},{8,16},{16,8},{24,0},{1,25},{9,17},{17,9},{25,1},{2,26},{10... | collective-permute-start | bytes 196616 | tf_op jit(solution)/shard_map/ppermute | solution.py:317
  196.7 9.0 %collective-permute-start.35 = (bf16[64,1024]{1,0:T(8,128)(2,1)S(1)}, bf16[64,1024]{1,0:T(8,128)(2,1)S(1)}, u32[]{:S(2)}, u32[]{:S(2)}) collective-permute-start(bf16[64,1024]{1,0:T(8,128)(2,1)S(1)} %get-tuple-element.128.refs_5_), channel_id=1, source_target_pairs={{0,8},{8,0},{16,24},{24,16},{1,9},{9,1},{17,25},{25,17},{2,10},{10... | collective-permute-start | bytes 393224 | tf_op jit(solution)/shard_map/ppermute | solution.py:317
  197.1 8.6 %collective-permute-start.37 = (bf16[64,1024]{1,0:T(8,128)(2,1)S(1)}, bf16[64,1024]{1,0:T(8,128)(2,1)S(1)}, u32[]{:S(2)}, u32[]{:S(2)}) collective-permute-start(bf16[64,1024]{1,0:T(8,128)(2,1)S(1)} %collective-permute-done.36.refs_7_), channel_id=1, source_target_pairs={{0,8},{8,0},{16,24},{24,16},{1,9},{9,1},{17,25},{25,17},{2,10},{10... | collective-permute-start | bytes 393224 | tf_op jit(solution)/shard_map/ppermute | solution.py:317
  199.7 6.0 %collective-permute-start.32 = (bf16[192,1024]{1,0:T(8,128)(2,1)}, bf16[192,1024]{1,0:T(8,128)(2,1)S(1)}, u32[]{:S(2)}, u32[]{:S(2)}) collective-permute-start(bf16[192,1024]{1,0:T(8,128)(2,1)} %get-tuple-element.127.refs_1_), channel_id=1, source_target_pairs={{0,8},{8,0},{16,24},{24,16},{1,9},{9,1},{17,25},{25,17},{2,10},{10... | collective-permute-start | bytes 1179656 | tf_op jit(solution)/shard_map/ppermute | solution.py:317
  199.7 6.0 %collective-permute-start.34 = (bf16[192,1024]{1,0:T(8,128)(2,1)S(1)}, bf16[192,1024]{1,0:T(8,128)(2,1)S(1)}, u32[]{:S(2)}, u32[]{:S(2)}) collective-permute-start(bf16[192,1024]{1,0:T(8,128)(2,1)S(1)} %collective-permute-done.33.refs_3_), channel_id=1, source_target_pairs={{0,8},{8,0},{16,24},{24,16},{1,9},{9,1},{17,25},{25,17},{2,10},{10... | collective-permute-start | bytes 1179656 | tf_op jit(solution)/shard_map/ppermute | solution.py:317
  (16 other events, 52.8 us)

commit v5 on v4

--- a/solution.py
+++ b/solution.py
@@ -1507,7 +1507,7 @@
     out_sent = swapped_with(out_sent, "batch", 2)
 
     d_qkv, d_qkv_sent, sums_two = attend_back(
-        me[None], probs, q_a, q_b, kv_a, kv_b, d_o, cosine, sine, sums_two, seconds
+        me[None], probs, q_a, q_b, kv_a, kv_b, d_o, cosine, sine, sums_two, seconds[:3]
     )
     d_own = lax.all_to_all(d_qkv_sent, "blk", 0, 0, tiled=True)
     kept, *sent = weights_part(
@@ -1594,7 +1594,7 @@
 
 def solution(mesh):
     blk = mesh.shape["blk"]
-    heads_fit = HEADS % (2 * blk) == 0 and mesh.shape["batch"] == 4
+    heads_fit = HEADS == 2 * blk and mesh.shape["batch"] == 4
     chosen = heads_body if heads_fit else ring_body
     placed = (
         P(("batch", "blk"), None),

time: 209 us -> 205 us (0.981)
  waiting for transfers between devices: 32.4 us -> 29.7 us
  starting transfers between devices: 58.5 us -> 56 us
    all_to_all x1, waiting for transfers between devices: 2.61 us -> 0.01 us  [heads_body(): d_o = lax.all_to_all(d_o, 'blk', 0, 0, tiled=True)]
where the time goes in v5:
time: 205 us; the launch traced here: 204 us
  Pallas kernels  104 us (51%)
  starting transfers between devices  56 us (27%)
  waiting for transfers between devices  29.7 us (14%)
  local copies, waits for them, and re-layouts  7.6 us (4%)
  other arithmetic  4.33 us (2%)
    ppermute x37, starting transfers between devices, swapped_with(): return lax.ppermute(value, axis, [(i, i ^ offset) for i in range(size)])  42.3 us
    ppermute x37, waiting for transfers between devices, swapped_with(): return lax.ppermute(value, axis, [(i, i ^ offset) for i in range(size)])  24.2 us
    pallas_call x2, Pallas kernels, project(): pl.pallas_call(lambda *refs: project_kernel(clips, with_own, *refs), grid...  14 us
    pallas_call x1, Pallas kernels, attend_back(): pl.pallas_call(attend_back_kernel, grid_spec=grid_spec, out_shape=[shape_...  13 us
    pallas_call x2, Pallas kernels, table_part(): pl.pallas_call(lambda *refs: table_kernel(first, clips, *refs), grid=(col...  11.7 us
    pallas_call x1, Pallas kernels, attend(): pl.pallas_call(attend_kernel, grid=(width // LANES,), in_specs=[pl.BlockS...  11.5 us
    pallas_call x1, Pallas kernels, weights_part(): pl.pallas_call(lambda *refs: weights_kernel(clips, count, *refs), grid=(1...  9.74 us
    pallas_call x1, Pallas kernels, middle_part(): pl.pallas_call(lambda *refs: middle_kernel(clips, *refs), grid=(1,), in_s...  8.55 us
  transfers between devices with their start and end apart: 41, of which 15 were waited for; matrix products, arithmetic and copies ran while one was open for 3% of the time, Pallas kernels for 44%

profile of v5, /device:TPU:0, one launch (start us, length us, event | category | flops | bytes accessed | tf_op | source)
XLA Modules:
  0.0 204.1 jit_solution(9315239395951262804)
XLA Ops:
  0.6 3.1 %collective-permute-start = (bf16[128,1024]{1,0:T(8,128)(2,1)}, bf16[128,1024]{1,0:T(8,128)(2,1)S(1)}, u32[]{:S(2)}, u32[]{:S(2)}) collective-permute-start(bf16[128,1024]{1,0:T(8,128)(2,1)} %refs_2_.5), channel_id=1, source_target_pairs={{0,2},{1,3},{2,0},{3,1},{4,6},{5,7},{6,4},{7,5},{8,10},{9,11},{10,... | collective-permute-start | bytes 786440 | tf_op jit(solution)/shard_map/ppermute | solution.py:317
  3.7 2.6 %collective-permute-start.1 = (bf16[128,1024]{1,0:T(8,128)(2,1)}, bf16[128,1024]{1,0:T(8,128)(2,1)S(1)}, u32[]{:S(2)}, u32[]{:S(2)}) collective-permute-start(bf16[128,1024]{1,0:T(8,128)(2,1)} %refs_2_.5), channel_id=1, source_target_pairs={{0,4},{1,5},{2,6},{3,7},{4,0},{5,1},{6,2},{7,3},{8,12},{9,13},{10,... | collective-permute-start | bytes 786440 | tf_op jit(solution)/shard_map/ppermute | solution.py:317
  6.3 1.7 collective-permute-start.3
  11.0 5.9 %shard_map.246 = (f32[4,2048]{1,0:T(4,128)S(1)}, bf16[4,1024]{1,0:T(4,128)(2,1)S(1)}, s32[1024,1]{1,0:T(8,128)S(1)}, s32[1,1024]{1,0:T(1,128)S(1)}, f32[1024,128...) custom-call(s32[1]{0:T(128)} %bitcast.refs_0_.me_ref, ...), custom_call_target="tpu_custom_call" | custom-call | flops 16777216 | bytes 5242880 | tf_op jit(solution)/shard_map/pallas_call | solution.py:463
  17.0 4.8 %shard_map.248.refs_6_.refs_2_ = f32[4,4096]{1,0:T(4,128)S(1)} custom-call(bf16[4,1024]{1,0:T(4,128)(2,1)S(1)} %get-tuple-element.82.silu_ref, bf16[1024,6144]{1,0:T(8,128)(2,1)} %refs_6_.7, f32[1,6144]{1,0:T(1,128)S(1)} %bitcast.24), custom_call_target="tpu_custom_call" | custom-call | flops 33554432 | bytes 8388608 | tf_op jit(solution)/shard_map/pallas_call | solution.py:490
  23.4 1.9 collective-permute-done.1.refs_9_
  26.1 1.5 collective-permute-start.5
  28.9 6.4 %shard_map.247 = (bf16[512,1024]{1,0:T(8,128)(2,1)}, bf16[16,512,128]{2,1,0:T(8,128)(2,1)S(1)}, bf16[512,128]{1,0:T(8,128)(2,1)S(1)}, bf16[128,1024]{1,0:T(8,128)(2,1)}, bf16[128,1024]{1,0:T(8,128)(2,1)}) custom-call(s32[1]{0:T(128)} %bitcast.refs_0_.me_ref, s32[1024,1]{1,0:T(8,128)S(1)} %get-tuple-element.73.refs_1_.keyclip_ref.refs_0_, ...), custom_call_target="tpu_custom_call" | custom-call | flops 2147483648 | bytes 6291456 | tf_op jit(solution)/shard_map/pallas_call | solution.py:581
  35.3 3.5 %collective-permute-start.7 = (bf16[128,1024]{1,0:T(8,128)(2,1)}, bf16[128,1024]{1,0:T(8,128)(2,1)S(1)}, u32[]{:S(2)}, u32[]{:S(2)}) collective-permute-start(bf16[128,1024]{1,0:T(8,128)(2,1)} %get-tuple-element.88.refs_13_.refs_15_), channel_id=1, source_target_pairs={{0,2},{1,3},{2,0},{3,1},{4,6},{5,7},{6,4},{7,5},{8,10},{9,11},{10,... | collective-permute-start | bytes 786440 | tf_op jit(solution)/shard_map/ppermute | solution.py:317
  38.8 1.1 collective-permute-start.8
  39.9 1.5 collective-permute-start.9
  41.5 7.6 %shard_map.249 = (bf16[512,1024]{1,0:T(8,128)(2,1)}, bf16[16,512,128]{2,1,0:T(8,128)(2,1)S(1)}, bf16[512,128]{1,0:T(8,128)(2,1)S(1)}) custom-call(s32[1]{0:T(128)} %bitcast.refs_0_.me_ref, s32[1024,1]{1,0:T(8,128)S(1)} %get-tuple-element.73.refs_1_.keyclip_ref.refs_0_, f32[4,2048]{1,0:T(4,128)S(1)} %get-tuple-element.76.refs_2_.refs_3_, ...), custom_call_target="tpu_custom_call" | custom-call | flops 2147483648 | bytes 6291456 | tf_op jit(solution)/shard_map/pallas_call | solution.py:581
  49.2 11.5 %shard_map.250 = (bf16[128,1024]{1,0:T(8,128)(2,1)}, bf16[1024,1024]{1,0:T(8,128)(2,1)S(1)}, bf16[1024,2048]{1,0:T(8,128)(2,1)S(1)}, bf16[2048,1024]{1,0:T(8,128)(2,1)S(1)}) custom-call(bf16[1024,256]{1,0:T(8,128)(2,1)} %get-tuple-element.75.keymark_ref.rowmark_ref, bf16[1024,256]{1,0:T(8,128)(2,1)} %get-tuple-element.75.keymark_ref.rowmark_ref, ...), custom_call_target="tpu_custom_call" | custom-call | flops 536870912 | bytes 1048576 | tf_op jit(solution)/shard_map/pallas_call | solution.py:668
  61.6 8.6 %shard_map.251 = (bf16[128,1024]{1,0:T(8,128)(2,1)}, bf16[128,1024]{1,0:T(8,128)(2,1)}, f32[128,1024]{1,0:T(8,128)}, bf16[128,1024]{1,0:T(8,128)(2,1)}, bf16[8,1...) custom-call(s32[1,4]{1,0:T(1,128)S(1)} %copy-done.11, s32[1024,1]{1,0:T(8,128)S(1)} %get-tuple-element.73.refs_1_.keyclip_ref.refs_0_, ...), custom_call_target="tpu_custom_call" | custom-call | flops 2684354560 | bytes 3145728 | tf_op jit(solution)/shard_map/pallas_call | solution.py:981
  70.1 2.4 %collective-permute-start.12 = (bf16[128,1024]{1,0:T(8,128)(2,1)}, bf16[128,1024]{1,0:T(8,128)(2,1)S(1)}, u32[]{:S(2)}, u32[]{:S(2)}) collective-permute-start(bf16[128,1024]{1,0:T(8,128)(2,1)} %get-tuple-element.97.refs_1_.refs_11_), channel_id=1, source_target_pairs={{0,2},{1,3},{2,0},{3,1},{4,6},{5,7},{6,4},{7,5},{8,10},{9,11},{10,... | collective-permute-start | bytes 786440 | tf_op jit(solution)/shard_map/ppermute | solution.py:317
  72.5 1.7 collective-permute-start.13
  74.2 3.5 %all-to-all-start = ((bf16[8,128,128]{2,1,0:T(8,128)(2,1)}), bf16[8,128,128]{2,1,0:T(8,128)(2,1)S(1)}, u32[]{:S(2)}, u32[]{:S(2)}) async-start(bf16[8,128,128]{2,1,0:T(8,128)(2,1)} %get-tuple-element.95), calls=%async_computation | async-start | bytes 524288 | tf_op jit(solution)/shard_map/all_to_all | solution.py:1495
  77.8 1.9 collective-permute-start.10
  79.7 8.4 %shard_map.252 = (f32[1024,2048]{1,0:T(8,128)}, bf16[128,1024]{1,0:T(8,128)(2,1)}) custom-call(s32[1]{0:T(128)} %bitcast.refs_0_.me_ref, s32[1024,1]{1,0:T(8,128)S(1)} %get-tuple-element.73.refs_1_.keyclip_ref.refs_0_, s32[1,1024]{1,0:T(1,128)S(1)} %get-tuple-element.74.refs_2_.rowclip_ref.refs_1_, ...), custom_call_target="tpu_custom_call", output_to_operand_aliasing={{1}: (8, {})} | custom-call | flops 536870912 | bytes 9437184 | tf_op jit(solution)/shard_map/pallas_call | solution.py:730
  88.1 1.0 broadcast_select_fusion
  89.9 1.5 collective-permute-start.14
  91.4 1.5 collective-permute-start.11
  92.9 2.4 %collective-permute-start.15 = (bf16[128,1024]{1,0:T(8,128)(2,1)S(1)}, bf16[128,1024]{1,0:T(8,128)(2,1)}, u32[]{:S(2)}, u32[]{:S(2)}) collective-permute-start(bf16[128,1024]{1,0:T(8,128)(2,1)S(1)} %copy-done.13), channel_id=1, source_target_pairs={{0,6},{1,7},{2,4},{3,5},{4,2},{5,3},{6,0},{7,1},{8,14},{9,15},{10,... | collective-permute-start | bytes 786440 | tf_op jit(solution)/shard_map/ppermute | solution.py:317
  95.3 2.7 %collective-permute-done.11 = f32[8,4096]{1,0:T(8,128)S(1)} collective-permute-done((f32[8,4096]{1,0:T(8,128)S(1)}, f32[8,4096]{1,0:T(8,128)S(1)}, u32[]{:S(2)}, u32[]{:S(2)}) %collective-permute-start.11) | collective-permute-done | bytes 131104 | tf_op jit(solution)/shard_map/ppermute | solution.py:317
  98.8 13.0 %shard_map.253 = (bf16[1024,384]{1,0:T(8,128)(2,1)}, bf16[8,128,384]{2,1,0:T(8,128)(2,1)}, f32[8,4096]{1,0:T(8,128)S(1)}) custom-call(s32[1]{0:T(128)} %bitcast.refs_0_.me_ref, f32[1024,2048]{1,0:T(8,128)} %get-tuple-element.94.p_ref, bf16[512,128]{1,0:T(8,128)(2,1)S(1)} %get-tuple-element.91.qa_ref, ...), custom_call_target="tpu_custom_call", output_to_operand_aliasing={{2}: (11, {})} | custom-call | flops 1073741824 | bytes 12582912 | tf_op jit(solution)/shard_map/pallas_call | solution.py:835
  111.8 3.8 %all-to-all-start.1 = ((bf16[8,128,384]{2,1,0:T(8,128)(2,1)}), bf16[8,128,384]{2,1,0:T(8,128)(2,1)S(1)}, u32[]{:S(2)}, u32[]{:S(2)}) async-start(bf16[8,128,384]{2,1,0:T(8,128)(2,1)} %get-tuple-element.98), calls=%async_computation.1 | async-start | bytes 1572864 | tf_op jit(solution)/shard_map/all_to_all | solution.py:1512
  116.5 9.7 %shard_map.254 = (f32[512,1920]{1,0:T(8,128)}, bf16[512,640]{1,0:T(8,128)(2,1)}, bf16[512,640]{1,0:T(8,128)(2,1)}, bf16[512,640]{1,0:T(8,128)(2,1)}) custom-call(s32[3]{0:T(128)S(1)} %pad_add_fusion.refs_0_, s32[1024,1]{1,0:T(8,128)S(1)} %get-tuple-element.73.refs_1_.keyclip_ref.refs_0_, f32[4,4096]{1,0:T(4,128)S(1)} %shard_map.248.refs_6_.refs_2_, ...), custom_call_target="tpu_custom_call" | custom-call | flops 3758096384 | bytes 10485760 | tf_op jit(solution)/shard_map/pallas_call | solution.py:1160
  126.9 1.7 collective-permute-done.16.refs_2_
  130.5 3.9 %shard_map.255 = (f32[8,32,896]{2,1,0:T(8,128)}, bf16[8,32,896]{2,1,0:T(8,128)(2,1)}, bf16[8,32,512]{2,1,0:T(8,128)(2,1)}, bf16[8,32,512]{2,1,0:T(8,128)(2,1)}, bf16[8,32,1024]{2,1,0:T(8,128)(2,1)}) custom-call(s32[3]{0:T(128)S(1)} %pad_add_fusion.refs_0_, f32[512,1920]{1,0:T(8,128)} %get-tuple-element.103.refs_1_, ...), custom_call_target="tpu_custom_call" | custom-call | bytes 8388608 | tf_op jit(solution)/shard_map/pallas_call | solution.py:1323
  134.9 1.7 collective-permute-start.20
  136.5 1.3 collective-permute-start.21
  137.8 6.9 %shard_map.256 = (bf16[128,1024]{1,0:T(8,128)(2,1)}, f32[8,2048]{1,0:T(8,128)S(1)}, f32[8,32,896]{2,1,0:T(8,128)}, f32[8,4096]{1,0:T(8,128)S(1)}) custom-call(s32[1024,1]{1,0:T(8,128)S(1)} %get-tuple-element.73.refs_1_.keyclip_ref.refs_0_, s32[1,1024]{1,0:T(1,128)S(1)} %get-tuple-element.74.refs_2_.rowclip_ref.refs_1_, ...), custom_call_target="tpu_custom_call", output_to_operand_aliasing={{2}: (7, {}), {3}: (8, {})} | custom-call | flops 805306368 | bytes 2097152 | tf_op jit(solution)/shard_map/pallas_call | solution.py:1033
  144.7 2.6 %collective-permute-start.23 = (f32[8,4096]{1,0:T(8,128)S(1)}, f32[8,4096]{1,0:T(8,128)S(1)}, u32[]{:S(2)}, u32[]{:S(2)}) collective-permute-start(f32[8,4096]{1,0:T(8,128)S(1)} %get-tuple-element.116), channel_id=1, source_target_pairs={{0,4},{1,5},{2,6},{3,7},{4,0},{5,1},{6,2},{7,3},{8,12},{9,13},{10,... | collective-permute-start | bytes 393224 | tf_op jit(solution)/shard_map/ppermute | solution.py:317
  147.3 1.5 collective-permute-start.22
  148.8 3.0 %collective-permute-done.22 = f32[8,2048]{1,0:T(8,128)S(1)} collective-permute-done((f32[8,2048]{1,0:T(8,128)S(1)}, f32[8,2048]{1,0:T(8,128)S(1)}, u32[]{:S(2)}, u32[]{:S(2)}) %collective-permute-start.22) | collective-permute-done | bytes 65568 | tf_op jit(solution)/shard_map/ppermute | solution.py:317
  151.8 1.4 collective-permute-done.23
  153.8 2.3 %shard_map.257 = (f32[8,2048]{1,0:T(8,128)S(1)}, f32[8,4096]{1,0:T(8,128)S(1)}, bf16[8,32,1664]{2,1,0:T(8,128)(2,1)}, bf16[64,1024]{1,0:T(8,128)(2,1)S(1)}) custom-call(f32[8,32,896]{2,1,0:T(8,128)} %get-tuple-element.110.refs_0_, bf16[8,32,896]{2,1,0:T(8,128)(2,1)S(1)} %collective-permute-done.19.refs_1_, ...), custom_call_target="tpu_custom_call", output_to_operand_aliasing={{0}: (5, {}), {1}: (6, {})} | custom-call | bytes 4194304 | tf_op jit(solution)/shard_map/pallas_call | solution.py:1359
  156.2 5.1 %all-to-all-start.2 = ((bf16[8,32,1664]{2,1,0:T(8,128)(2,1)}), bf16[8,32,1664]{2,1,0:T(8,128)(2,1)S(1)}, u32[]{:S(2)}, u32[]{:S(2)}) async-start(bf16[8,32,1664]{2,1,0:T(8,128)(2,1)} %get-tuple-element.117), calls=%async_computation.2 | async-start | bytes 1703936 | tf_op jit(solution)/shard_map/all_to_all | solution.py:1540
  161.8 1.2 collective-permute-start.27
  163.1 2.1 %collective-permute-start.24 = (f32[8,2048]{1,0:T(8,128)S(1)}, f32[8,2048]{1,0:T(8,128)S(1)}, u32[]{:S(2)}, u32[]{:S(2)}) collective-permute-start(f32[8,2048]{1,0:T(8,128)S(1)} %get-tuple-element.118), channel_id=1, source_target_pairs={{0,1},{1,0},{2,3},{3,2},{4,5},{5,4},{6,7},{7,6},{8,9},{9,8},{10,11... | collective-permute-start | bytes 196616 | tf_op jit(solution)/shard_map/ppermute | solution.py:317
  165.7 3.7 %collective-permute-done.27.refs_4_ = f32[8,4096]{1,0:T(8,128)S(1)} collective-permute-done((f32[8,4096]{1,0:T(8,128)S(1)}, f32[8,4096]{1,0:T(8,128)S(1)}, u32[]{:S(2)}, u32[]{:S(2)}) %collective-permute-start.27) | collective-permute-done | bytes 131104 | tf_op jit(solution)/shard_map/ppermute | solution.py:317
  171.0 7.0 %shard_map.258 = (f32[128,6144]{1,0:T(8,128)}, f32[1,6144]{1,0:T(1,128)}, f32[1024,64]{1,0:T(8,128)}) custom-call(s32[1]{0:T(128)} %bitcast.8.refs_0_, f32[8,4096]{1,0:T(8,128)S(1)} %get-tuple-element.119.refs_1_, f32[8,4096]{1,0:T(8,128)S(1)} %collective-permute-done.25.refs_2_, f32[8,4096]{1,0:T(8,128)S(1)} %collective-permute-done.26.refs_3_, ...), custom_call_target="tpu_custom_call" | custom-call | flops 32768 | bytes 1024 | tf_op jit(solution)/shard_map/pallas_call | solution.py:1262
  178.0 4.8 %all-to-all-done.2.refs_0_ = bf16[8,32,1664]{2,1,0:T(8,128)(2,1)S(1)} async-done(((bf16[8,32,1664]{2,1,0:T(8,128)(2,1)}), bf16[8,32,1664]{2,1,0:T(8,128)(2,1)S(1)}, u32[]{:S(2)}, u32[]{:S(2)}) %all-to-all-start.2) | async-done | bytes 852000 | tf_op jit(solution)/shard_map/all_to_all | solution.py:1540
  185.6 4.2 %collective-permute-done.28 = f32[8,2048]{1,0:T(8,128)S(1)} collective-permute-done((f32[8,2048]{1,0:T(8,128)S(1)}, f32[8,2048]{1,0:T(8,128)S(1)}, u32[]{:S(2)}, u32[]{:S(2)}) %collective-permute-start.28) | collective-permute-done | bytes 65568 | tf_op jit(solution)/shard_map/ppermute | solution.py:317
  189.9 1.6 collective-permute-start.30
  192.3 2.8 %collective-permute-done.30.refs_3_ = f32[8,2048]{1,0:T(8,128)S(1)} collective-permute-done((f32[8,2048]{1,0:T(8,128)S(1)}, f32[8,2048]{1,0:T(8,128)S(1)}, u32[]{:S(2)}, u32[]{:S(2)}) %collective-permute-start.30) | collective-permute-done | bytes 65568 | tf_op jit(solution)/shard_map/ppermute | solution.py:317
  195.9 4.8 %shard_map.260 = (f32[128,6144]{1,0:T(8,128)}, f32[1,6144]{1,0:T(1,128)}, f32[32,1024]{1,0:T(8,128)}) custom-call(s32[1]{0:T(128)} %bitcast.8.refs_0_, f32[8,2048]{1,0:T(8,128)S(1)} %add.102.refs_1_, f32[8,2048]{1,0:T(8,128)S(1)} %collective-permute-done.29.refs_2_, ...), custom_call_target="tpu_custom_call", output_to_operand_aliasing={{0}: (10, {}), {1}: (11, {})} | custom-call | flops 32768 | bytes 1024 | tf_op jit(solution)/shard_map/pallas_call | solution.py:1262
  201.3 2.8 %shard_map.261 = (f32[128,3072]{1,0:T(8,128)}, f32[128,1024]{1,0:T(8,128)}, f32[128,2048]{1,0:T(8,128)}, f32[256,1024]{1,0:T(8,128)}) custom-call(s32[3]{0:T(128)S(1)} %pad_add_fusion.refs_0_, bf16[192,1024]{1,0:T(8,128)(2,1)S(1)} %copy-done.4, bf16[192,1024]{1,0:T(8,128)(2,1)S(1)} %collective-permute-done.32.refs_2_, ...), custom_call_target="tpu_custom_call" | custom-call | bytes 6291456 | tf_op jit(solution)/shard_map/pallas_call | solution.py:1443
  (129 shorter events, 20.7 us)
Async XLA Ops:
  0.6 22.4 %collective-permute-start = (bf16[128,1024]{1,0:T(8,128)(2,1)}, bf16[128,1024]{1,0:T(8,128)(2,1)S(1)}, u32[]{:S(2)}, u32[]{:S(2)}) collective-permute-start(bf16[128,1024]{1,0:T(8,128)(2,1)} %refs_2_.5), channel_id=1, source_target_pairs={{0,2},{1,3},{2,0},{3,1},{4,6},{5,7},{6,4},{7,5},{8,10},{9,11},{10,... | collective-permute-start | bytes 786440 | tf_op jit(solution)/shard_map/ppermute | solution.py:317
  3.7 21.6 %collective-permute-start.1 = (bf16[128,1024]{1,0:T(8,128)(2,1)}, bf16[128,1024]{1,0:T(8,128)(2,1)S(1)}, u32[]{:S(2)}, u32[]{:S(2)}) collective-permute-start(bf16[128,1024]{1,0:T(8,128)(2,1)} %refs_2_.5), channel_id=1, source_target_pairs={{0,4},{1,5},{2,6},{3,7},{4,0},{5,1},{6,2},{7,3},{8,12},{9,13},{10,... | collective-permute-start | bytes 786440 | tf_op jit(solution)/shard_map/ppermute | solution.py:317
  6.3 21.3 %collective-permute-start.2 = (bf16[128,1024]{1,0:T(8,128)(2,1)}, bf16[128,1024]{1,0:T(8,128)(2,1)S(1)}, u32[]{:S(2)}, u32[]{:S(2)}) collective-permute-start(bf16[128,1024]{1,0:T(8,128)(2,1)} %refs_2_.5), channel_id=1, source_target_pairs={{0,6},{1,7},{2,4},{3,5},{4,2},{5,3},{6,0},{7,1},{8,14},{9,15},{10,... | collective-permute-start | bytes 786440 | tf_op jit(solution)/shard_map/ppermute | solution.py:317
  6.3 32.5 %collective-permute-start.3 = (bf16[128,1024]{1,0:T(8,128)(2,1)}, bf16[128,1024]{1,0:T(8,128)(2,1)}, u32[]{:S(2)}, u32[]{:S(2)}) collective-permute-start(bf16[128,1024]{1,0:T(8,128)(2,1)} %refs_2_.5), channel_id=1, source_target_pairs={{0,1},{1,0},{2,3},{3,2},{4,5},{5,4},{6,7},{7,6},{8,9},{9,8},{10,11... | collective-permute-start | bytes 786440 | tf_op jit(solution)/shard_map/ppermute | solution.py:317
  23.1 16.8 %collective-permute-start.4 = (bf16[128,1024]{1,0:T(8,128)(2,1)S(1)}, bf16[128,1024]{1,0:T(8,128)(2,1)}, u32[]{:S(2)}, u32[]{:S(2)}) collective-permute-start(bf16[128,1024]{1,0:T(8,128)(2,1)S(1)} %broadcast_add_fusion.2), channel_id=1, source_target_pairs={{0,1},{1,0},{2,3},{3,2},{4,5},{5,4},{6,7},{7,6},{8,9},{9,8},{10,11... | collective-permute-start | bytes 786440 | tf_op jit(solution)/shard_map/ppermute | solution.py:317
  26.1 15.3 %collective-permute-start.5 = (bf16[128,1024]{1,0:T(8,128)(2,1)}, bf16[128,1024]{1,0:T(8,128)(2,1)}, u32[]{:S(2)}, u32[]{:S(2)}) collective-permute-start(bf16[128,1024]{1,0:T(8,128)(2,1)} %broadcast_add_fusion.1), channel_id=1, source_target_pairs={{0,1},{1,0},{2,3},{3,2},{4,5},{5,4},{6,7},{7,6},{8,9},{9,8},{10,11... | collective-permute-start | bytes 786440 | tf_op jit(solution)/shard_map/ppermute | solution.py:317
  28.4 13.1 %collective-permute-start.6 = (bf16[128,1024]{1,0:T(8,128)(2,1)}, bf16[128,1024]{1,0:T(8,128)(2,1)}, u32[]{:S(2)}, u32[]{:S(2)}) collective-permute-start(bf16[128,1024]{1,0:T(8,128)(2,1)} %broadcast_add_fusion), channel_id=1, source_target_pairs={{0,1},{1,0},{2,3},{3,2},{4,5},{5,4},{6,7},{7,6},{8,9},{9,8},{10,11... | collective-permute-start | bytes 786440 | tf_op jit(solution)/shard_map/ppermute | solution.py:317
  35.3 13.8 %copy-start = (bf16[16,512,128]{2,1,0:T(8,128)(2,1)}, bf16[16,512,128]{2,1,0:T(8,128)(2,1)S(1)}, u32[]{:S(2)}) copy-start(bf16[16,512,128]{2,1,0:T(8,128)(2,1)S(1)} %get-tuple-element.81.ka_ref.va_ref) | copy-start | bytes 6291460
  35.3 25.4 %collective-permute-start.7 = (bf16[128,1024]{1,0:T(8,128)(2,1)}, bf16[128,1024]{1,0:T(8,128)(2,1)S(1)}, u32[]{:S(2)}, u32[]{:S(2)}) collective-permute-start(bf16[128,1024]{1,0:T(8,128)(2,1)} %get-tuple-element.88.refs_13_.refs_15_), channel_id=1, source_target_pairs={{0,2},{1,3},{2,0},{3,1},{4,6},{5,7},{6,4},{7,5},{8,10},{9,11},{10,... | collective-permute-start | bytes 786440 | tf_op jit(solution)/shard_map/ppermute | solution.py:317
  38.8 21.9 %collective-permute-start.8 = (bf16[128,1024]{1,0:T(8,128)(2,1)}, bf16[128,1024]{1,0:T(8,128)(2,1)S(1)}, u32[]{:S(2)}, u32[]{:S(2)}) collective-permute-start(bf16[128,1024]{1,0:T(8,128)(2,1)} %get-tuple-element.88.refs_13_.refs_15_), channel_id=1, source_target_pairs={{0,4},{1,5},{2,6},{3,7},{4,0},{5,1},{6,2},{7,3},{8,12},{9,13},{10,... | collective-permute-start | bytes 786440 | tf_op jit(solution)/shard_map/ppermute | solution.py:317
  39.9 20.9 %collective-permute-start.9 = (bf16[128,1024]{1,0:T(8,128)(2,1)}, bf16[128,1024]{1,0:T(8,128)(2,1)}, u32[]{:S(2)}, u32[]{:S(2)}) collective-permute-start(bf16[128,1024]{1,0:T(8,128)(2,1)} %get-tuple-element.88.refs_13_.refs_15_), channel_id=1, source_target_pairs={{0,6},{1,7},{2,4},{3,5},{4,2},{5,3},{6,0},{7,1},{8,14},{9,15},{10,... | collective-permute-start | bytes 786440 | tf_op jit(solution)/shard_map/ppermute | solution.py:317
  49.1 12.4 %copy-start.7 = (f32[2048]{0:T(1024)S(1)}, f32[2048]{0:T(1024)}, u32[]{:S(2)}) copy-start(f32[2048]{0:T(1024)} %param.26) | copy-start | bytes 24580
  49.1 12.4 %copy-start.8 = (f32[1024]{0:T(1024)S(1)}, f32[1024]{0:T(1024)}, u32[]{:S(2)}) copy-start(f32[1024]{0:T(1024)} %param.24) | copy-start | bytes 12292
  49.1 12.4 %copy-start.9 = (f32[1024]{0:T(1024)S(1)}, f32[1024]{0:T(1024)}, u32[]{:S(2)}) copy-start(f32[1024]{0:T(1024)} %param.28) | copy-start | bytes 12292
  70.1 19.0 %copy-start.18 = (bf16[128,1024]{1,0:T(8,128)(2,1)S(1)}, bf16[128,1024]{1,0:T(8,128)(2,1)}, u32[]{:S(2)}) copy-start(bf16[128,1024]{1,0:T(8,128)(2,1)} %get-tuple-element.84.refs_5_) | copy-start | bytes 786436
  70.1 27.9 %collective-permute-start.12 = (bf16[128,1024]{1,0:T(8,128)(2,1)}, bf16[128,1024]{1,0:T(8,128)(2,1)S(1)}, u32[]{:S(2)}, u32[]{:S(2)}) collective-permute-start(bf16[128,1024]{1,0:T(8,128)(2,1)} %get-tuple-element.97.refs_1_.refs_11_), channel_id=1, source_target_pairs={{0,2},{1,3},{2,0},{3,1},{4,6},{5,7},{6,4},{7,5},{8,10},{9,11},{10,... | collective-permute-start | bytes 786440 | tf_op jit(solution)/shard_map/ppermute | solution.py:317
  72.5 25.5 %collective-permute-start.13 = (bf16[128,1024]{1,0:T(8,128)(2,1)}, bf16[128,1024]{1,0:T(8,128)(2,1)S(1)}, u32[]{:S(2)}, u32[]{:S(2)}) collective-permute-start(bf16[128,1024]{1,0:T(8,128)(2,1)} %get-tuple-element.97.refs_1_.refs_11_), channel_id=1, source_target_pairs={{0,4},{1,5},{2,6},{3,7},{4,0},{5,1},{6,2},{7,3},{8,12},{9,13},{10,... | collective-permute-start | bytes 786440 | tf_op jit(solution)/shard_map/ppermute | solution.py:317
  74.2 18.7 %copy-start.13 = (bf16[128,1024]{1,0:T(8,128)(2,1)S(1)}, bf16[128,1024]{1,0:T(8,128)(2,1)}, u32[]{:S(2)}) copy-start(bf16[128,1024]{1,0:T(8,128)(2,1)} %get-tuple-element.97.refs_1_.refs_11_) | copy-start | bytes 786436
  74.2 23.8 %all-to-all-start = ((bf16[8,128,128]{2,1,0:T(8,128)(2,1)}), bf16[8,128,128]{2,1,0:T(8,128)(2,1)S(1)}, u32[]{:S(2)}, u32[]{:S(2)}) async-start(bf16[8,128,128]{2,1,0:T(8,128)(2,1)} %get-tuple-element.95), calls=%async_computation | async-start | bytes 524288 | tf_op jit(solution)/shard_map/all_to_all | solution.py:1495
  77.8 13.6 %collective-permute-start.10 = (f32[8,4096]{1,0:T(8,128)S(1)}, f32[8,4096]{1,0:T(8,128)S(1)}, u32[]{:S(2)}, u32[]{:S(2)}) collective-permute-start(f32[8,4096]{1,0:T(8,128)S(1)} %get-tuple-element.96), channel_id=1, source_target_pairs={{0,1},{1,0},{2,3},{3,2},{4,5},{5,4},{6,7},{7,6},{8,9},{9,8},{10,11... | collective-permute-start | bytes 393224 | tf_op jit(solution)/shard_map/ppermute | solution.py:317
  89.9 25.8 %collective-permute-start.14 = (bf16[128,1536]{1,0:T(8,128)(2,1)S(1)}, bf16[128,1536]{1,0:T(8,128)(2,1)S(1)}, u32[]{:S(2)}, u32[]{:S(2)}) collective-permute-start(bf16[128,1536]{1,0:T(8,128)(2,1)S(1)} %get-tuple-element.133), channel_id=1, source_target_pairs={{0,16},{8,24},{16,0},{24,8},{1,17},{9,25},{17,1},{25,9},{2,18},{10... | collective-permute-start | bytes 1179656 | tf_op jit(solution)/shard_map/ppermute | solution.py:317
  91.4 6.6 %collective-permute-start.11 = (f32[8,4096]{1,0:T(8,128)S(1)}, f32[8,4096]{1,0:T(8,128)S(1)}, u32[]{:S(2)}, u32[]{:S(2)}) collective-permute-start(f32[8,4096]{1,0:T(8,128)S(1)} %add.93), channel_id=1, source_target_pairs={{0,2},{1,3},{2,0},{3,1},{4,6},{5,7},{6,4},{7,5},{8,10},{9,11},{10,... | collective-permute-start | bytes 393224 | tf_op jit(solution)/shard_map/ppermute | solution.py:317
  92.9 22.8 %collective-permute-start.15 = (bf16[128,1024]{1,0:T(8,128)(2,1)S(1)}, bf16[128,1024]{1,0:T(8,128)(2,1)}, u32[]{:S(2)}, u32[]{:S(2)}) collective-permute-start(bf16[128,1024]{1,0:T(8,128)(2,1)S(1)} %copy-done.13), channel_id=1, source_target_pairs={{0,6},{1,7},{2,4},{3,5},{4,2},{5,3},{6,0},{7,1},{8,14},{9,15},{10,... | collective-permute-start | bytes 786440 | tf_op jit(solution)/shard_map/ppermute | solution.py:317
  111.8 26.0 %all-to-all-start.1 = ((bf16[8,128,384]{2,1,0:T(8,128)(2,1)}), bf16[8,128,384]{2,1,0:T(8,128)(2,1)S(1)}, u32[]{:S(2)}, u32[]{:S(2)}) async-start(bf16[8,128,384]{2,1,0:T(8,128)(2,1)} %get-tuple-element.98), calls=%async_computation.1 | async-start | bytes 1572864 | tf_op jit(solution)/shard_map/all_to_all | solution.py:1512
  126.2 2.4 %collective-permute-start.16 = (bf16[512,640]{1,0:T(8,128)(2,1)}, bf16[512,640]{1,0:T(8,128)(2,1)S(1)}, u32[]{:S(2)}, u32[]{:S(2)}) collective-permute-start(bf16[512,640]{1,0:T(8,128)(2,1)} %get-tuple-element.104), channel_id=1, source_target_pairs={{0,8},{8,0},{16,24},{24,16},{1,9},{9,1},{17,25},{25,17},{2,10},{10... | collective-permute-start | bytes 1966088 | tf_op jit(solution)/shard_map/ppermute | solution.py:317
  126.3 3.2 %collective-permute-start.17 = (bf16[512,640]{1,0:T(8,128)(2,1)}, bf16[512,640]{1,0:T(8,128)(2,1)S(1)}, u32[]{:S(2)}, u32[]{:S(2)}) collective-permute-start(bf16[512,640]{1,0:T(8,128)(2,1)} %get-tuple-element.105), channel_id=1, source_target_pairs={{0,8},{8,0},{16,24},{24,16},{1,9},{9,1},{17,25},{25,17},{2,10},{10... | collective-permute-start | bytes 1966088 | tf_op jit(solution)/shard_map/ppermute | solution.py:317
  126.8 3.7 %collective-permute-start.18 = (bf16[512,640]{1,0:T(8,128)(2,1)}, bf16[512,640]{1,0:T(8,128)(2,1)S(1)}, u32[]{:S(2)}, u32[]{:S(2)}) collective-permute-start(bf16[512,640]{1,0:T(8,128)(2,1)} %get-tuple-element.106), channel_id=1, source_target_pairs={{0,8},{8,0},{16,24},{24,16},{1,9},{9,1},{17,25},{25,17},{2,10},{10... | collective-permute-start | bytes 1966088 | tf_op jit(solution)/shard_map/ppermute | solution.py:317
  134.4 19.5 %collective-permute-start.19 = (bf16[8,32,896]{2,1,0:T(8,128)(2,1)}, bf16[8,32,896]{2,1,0:T(8,128)(2,1)S(1)}, u32[]{:S(2)}, u32[]{:S(2)}) collective-permute-start(bf16[8,32,896]{2,1,0:T(8,128)(2,1)} %get-tuple-element.111), channel_id=1, source_target_pairs={{0,16},{8,24},{16,0},{24,8},{1,17},{9,25},{17,1},{25,9},{2,18},{10... | collective-permute-start | bytes 1376264 | tf_op jit(solution)/shard_map/ppermute | solution.py:317
  134.9 18.3 %collective-permute-start.20 = (bf16[8,32,512]{2,1,0:T(8,128)(2,1)}, bf16[8,32,512]{2,1,0:T(8,128)(2,1)S(1)}, u32[]{:S(2)}, u32[]{:S(2)}) collective-permute-start(bf16[8,32,512]{2,1,0:T(8,128)(2,1)} %get-tuple-element.112), channel_id=1, source_target_pairs={{0,1},{1,0},{2,3},{3,2},{4,5},{5,4},{6,7},{7,6},{8,9},{9,8},{10,11... | collective-permute-start | bytes 786440 | tf_op jit(solution)/shard_map/ppermute | solution.py:317
  136.5 17.3 %collective-permute-start.21 = (bf16[8,32,512]{2,1,0:T(8,128)(2,1)}, bf16[8,32,512]{2,1,0:T(8,128)(2,1)S(1)}, u32[]{:S(2)}, u32[]{:S(2)}) collective-permute-start(bf16[8,32,512]{2,1,0:T(8,128)(2,1)} %get-tuple-element.113), channel_id=1, source_target_pairs={{0,17},{1,16},{2,19},{3,18},{4,21},{5,20},{6,23},{7,22},{8,25},{9,... | collective-permute-start | bytes 786440 | tf_op jit(solution)/shard_map/ppermute | solution.py:1535
  144.7 25.4 %copy-start.3 = (f32[32,1024]{1,0:T(8,128)S(1)}, f32[32,1024]{1,0:T(8,128)}, u32[]{:S(2)}) copy-start(f32[32,1024]{1,0:T(8,128)} %refs_3_.2) | copy-start | bytes 393220
  144.7 8.5 %collective-permute-start.23 = (f32[8,4096]{1,0:T(8,128)S(1)}, f32[8,4096]{1,0:T(8,128)S(1)}, u32[]{:S(2)}, u32[]{:S(2)}) collective-permute-start(f32[8,4096]{1,0:T(8,128)S(1)} %get-tuple-element.116), channel_id=1, source_target_pairs={{0,4},{1,5},{2,6},{3,7},{4,0},{5,1},{6,2},{7,3},{8,12},{9,13},{10,... | collective-permute-start | bytes 393224 | tf_op jit(solution)/shard_map/ppermute | solution.py:317
  147.3 4.4 %collective-permute-start.22 = (f32[8,2048]{1,0:T(8,128)S(1)}, f32[8,2048]{1,0:T(8,128)S(1)}, u32[]{:S(2)}, u32[]{:S(2)}) collective-permute-start(f32[8,2048]{1,0:T(8,128)S(1)} %get-tuple-element.115), channel_id=1, source_target_pairs={{0,2},{1,3},{2,0},{3,1},{4,6},{5,7},{6,4},{7,5},{8,10},{9,11},{10,... | collective-permute-start | bytes 196616 | tf_op jit(solution)/shard_map/ppermute | solution.py:317
  156.2 26.7 %all-to-all-start.2 = ((bf16[8,32,1664]{2,1,0:T(8,128)(2,1)}), bf16[8,32,1664]{2,1,0:T(8,128)(2,1)S(1)}, u32[]{:S(2)}, u32[]{:S(2)}) async-start(bf16[8,32,1664]{2,1,0:T(8,128)(2,1)} %get-tuple-element.117), calls=%async_computation.2 | async-start | bytes 1703936 | tf_op jit(solution)/shard_map/all_to_all | solution.py:1540
  161.2 8.3 %collective-permute-start.25 = (f32[8,4096]{1,0:T(8,128)S(1)}, f32[8,4096]{1,0:T(8,128)S(1)}, u32[]{:S(2)}, u32[]{:S(2)}) collective-permute-start(f32[8,4096]{1,0:T(8,128)S(1)} %get-tuple-element.119.refs_1_), channel_id=1, source_target_pairs={{0,8},{8,0},{16,24},{24,16},{1,9},{9,1},{17,25},{25,17},{2,10},{10... | collective-permute-start | bytes 393224 | tf_op jit(solution)/shard_map/ppermute | solution.py:317
  161.2 8.2 %collective-permute-start.26 = (f32[8,4096]{1,0:T(8,128)S(1)}, f32[8,4096]{1,0:T(8,128)S(1)}, u32[]{:S(2)}, u32[]{:S(2)}) collective-permute-start(f32[8,4096]{1,0:T(8,128)S(1)} %get-tuple-element.119.refs_1_), channel_id=1, source_target_pairs={{0,16},{8,24},{16,0},{24,8},{1,17},{9,25},{17,1},{25,9},{2,18},{10... | collective-permute-start | bytes 393224 | tf_op jit(solution)/shard_map/ppermute | solution.py:317
  161.8 7.6 %collective-permute-start.27 = (f32[8,4096]{1,0:T(8,128)S(1)}, f32[8,4096]{1,0:T(8,128)S(1)}, u32[]{:S(2)}, u32[]{:S(2)}) collective-permute-start(f32[8,4096]{1,0:T(8,128)S(1)} %get-tuple-element.119.refs_1_), channel_id=1, source_target_pairs={{0,24},{8,16},{16,8},{24,0},{1,25},{9,17},{17,9},{25,1},{2,26},{10... | collective-permute-start | bytes 393224 | tf_op jit(solution)/shard_map/ppermute | solution.py:317
  163.1 7.9 %collective-permute-start.24 = (f32[8,2048]{1,0:T(8,128)S(1)}, f32[8,2048]{1,0:T(8,128)S(1)}, u32[]{:S(2)}, u32[]{:S(2)}) collective-permute-start(f32[8,2048]{1,0:T(8,128)S(1)} %get-tuple-element.118), channel_id=1, source_target_pairs={{0,1},{1,0},{2,3},{3,2},{4,5},{5,4},{6,7},{7,6},{8,9},{9,8},{10,11... | collective-permute-start | bytes 196616 | tf_op jit(solution)/shard_map/ppermute | solution.py:317
  165.2 26.6 %collective-permute-start.36 = (bf16[64,1024]{1,0:T(8,128)(2,1)S(1)}, bf16[64,1024]{1,0:T(8,128)(2,1)S(1)}, u32[]{:S(2)}, u32[]{:S(2)}) collective-permute-start(bf16[64,1024]{1,0:T(8,128)(2,1)S(1)} %get-tuple-element.128.refs_5_), channel_id=1, source_target_pairs={{0,16},{8,24},{16,0},{24,8},{1,17},{9,25},{17,1},{25,9},{2,18},{10... | collective-permute-start | bytes 393224 | tf_op jit(solution)/shard_map/ppermute | solution.py:317
  183.7 11.5 %collective-permute-start.33 = (bf16[192,1024]{1,0:T(8,128)(2,1)}, bf16[192,1024]{1,0:T(8,128)(2,1)S(1)}, u32[]{:S(2)}, u32[]{:S(2)}) collective-permute-start(bf16[192,1024]{1,0:T(8,128)(2,1)} %get-tuple-element.127.refs_1_), channel_id=1, source_target_pairs={{0,16},{8,24},{16,0},{24,8},{1,17},{9,25},{17,1},{25,9},{2,18},{10... | collective-permute-start | bytes 1179656 | tf_op jit(solution)/shard_map/ppermute | solution.py:317
  184.3 5.5 %collective-permute-start.28 = (f32[8,2048]{1,0:T(8,128)S(1)}, f32[8,2048]{1,0:T(8,128)S(1)}, u32[]{:S(2)}, u32[]{:S(2)}) collective-permute-start(f32[8,2048]{1,0:T(8,128)S(1)} %get-tuple-element.121), channel_id=1, source_target_pairs={{0,4},{1,5},{2,6},{3,7},{4,0},{5,1},{6,2},{7,3},{8,12},{9,13},{10,... | collective-permute-start | bytes 196616 | tf_op jit(solution)/shard_map/ppermute | solution.py:317
  189.8 2.4 %collective-permute-start.29 = (f32[8,2048]{1,0:T(8,128)S(1)}, f32[8,2048]{1,0:T(8,128)S(1)}, u32[]{:S(2)}, u32[]{:S(2)}) collective-permute-start(f32[8,2048]{1,0:T(8,128)S(1)} %add.102.refs_1_), channel_id=1, source_target_pairs={{0,8},{8,0},{16,24},{24,16},{1,9},{9,1},{17,25},{25,17},{2,10},{10... | collective-permute-start | bytes 196616 | tf_op jit(solution)/shard_map/ppermute | solution.py:317
  189.9 5.3 %collective-permute-start.30 = (f32[8,2048]{1,0:T(8,128)S(1)}, f32[8,2048]{1,0:T(8,128)S(1)}, u32[]{:S(2)}, u32[]{:S(2)}) collective-permute-start(f32[8,2048]{1,0:T(8,128)S(1)} %add.102.refs_1_), channel_id=1, source_target_pairs={{0,16},{8,24},{16,0},{24,8},{1,17},{9,25},{17,1},{25,9},{2,18},{10... | collective-permute-start | bytes 196616 | tf_op jit(solution)/shard_map/ppermute | solution.py:317
  191.4 4.4 %collective-permute-start.31 = (f32[8,2048]{1,0:T(8,128)S(1)}, f32[8,2048]{1,0:T(8,128)S(1)}, u32[]{:S(2)}, u32[]{:S(2)}) collective-permute-start(f32[8,2048]{1,0:T(8,128)S(1)} %add.102.refs_1_), channel_id=1, source_target_pairs={{0,24},{8,16},{16,8},{24,0},{1,25},{9,17},{17,9},{25,1},{2,26},{10... | collective-permute-start | bytes 196616 | tf_op jit(solution)/shard_map/ppermute | solution.py:317
  191.7 9.5 %collective-permute-start.35 = (bf16[64,1024]{1,0:T(8,128)(2,1)S(1)}, bf16[64,1024]{1,0:T(8,128)(2,1)S(1)}, u32[]{:S(2)}, u32[]{:S(2)}) collective-permute-start(bf16[64,1024]{1,0:T(8,128)(2,1)S(1)} %get-tuple-element.128.refs_5_), channel_id=1, source_target_pairs={{0,8},{8,0},{16,24},{24,16},{1,9},{9,1},{17,25},{25,17},{2,10},{10... | collective-permute-start | bytes 393224 | tf_op jit(solution)/shard_map/ppermute | solution.py:317
  192.2 9.1 %collective-permute-start.37 = (bf16[64,1024]{1,0:T(8,128)(2,1)S(1)}, bf16[64,1024]{1,0:T(8,128)(2,1)S(1)}, u32[]{:S(2)}, u32[]{:S(2)}) collective-permute-start(bf16[64,1024]{1,0:T(8,128)(2,1)S(1)} %collective-permute-done.36.refs_7_), channel_id=1, source_target_pairs={{0,8},{8,0},{16,24},{24,16},{1,9},{9,1},{17,25},{25,17},{2,10},{10... | collective-permute-start | bytes 393224 | tf_op jit(solution)/shard_map/ppermute | solution.py:317
  195.2 6.1 %collective-permute-start.32 = (bf16[192,1024]{1,0:T(8,128)(2,1)}, bf16[192,1024]{1,0:T(8,128)(2,1)S(1)}, u32[]{:S(2)}, u32[]{:S(2)}) collective-permute-start(bf16[192,1024]{1,0:T(8,128)(2,1)} %get-tuple-element.127.refs_1_), channel_id=1, source_target_pairs={{0,8},{8,0},{16,24},{24,16},{1,9},{9,1},{17,25},{25,17},{2,10},{10... | collective-permute-start | bytes 1179656 | tf_op jit(solution)/shard_map/ppermute | solution.py:317
  195.2 6.1 %collective-permute-start.34 = (bf16[192,1024]{1,0:T(8,128)(2,1)S(1)}, bf16[192,1024]{1,0:T(8,128)(2,1)S(1)}, u32[]{:S(2)}, u32[]{:S(2)}) collective-permute-start(bf16[192,1024]{1,0:T(8,128)(2,1)S(1)} %collective-permute-done.33.refs_3_), channel_id=1, source_target_pairs={{0,8},{8,0},{16,24},{24,16},{1,9},{9,1},{17,25},{25,17},{2,10},{10... | collective-permute-start | bytes 1179656 | tf_op jit(solution)/shard_map/ppermute | solution.py:317
  (16 other events, 58.8 us)

commit v6 on v5

--- a/solution.py
+++ b/solution.py
@@ -902,7 +902,9 @@
         )
 
     def whole(self, value, row):
-        return dot_low((self.place == row).astype(F32).astype(BF), value)
+        total = jnp.sum(value.astype(F32), axis=0, keepdims=True)
+        place = lax.broadcasted_iota(jnp.int32, (8, value.shape[1]), 0)
+        return jnp.where(place == row, total, 0.0)
 
 
 def middle_kernel(
@@ -1230,7 +1232,7 @@
     width = w_mod.shape[0]
     all_columns = 6 * width
     rows, own = silu.shape
-    tile = 1024
+    tile = 2048
     skip = column // tile
     first = rest is None
     shapes = [

time: 205 us -> 205 us (level)
  no operation moved by 1% of the time
where the time goes in v6:
time: 205 us; the launch traced here: 204 us
  Pallas kernels  104 us (51%)
  starting transfers between devices  55.9 us (27%)
  waiting for transfers between devices  30.4 us (15%)
  local copies, waits for them, and re-layouts  7.6 us (4%)
  other arithmetic  4.33 us (2%)
    ppermute x37, starting transfers between devices, swapped_with(): return lax.ppermute(value, axis, [(i, i ^ offset) for i in range(size)])  42.3 us
    ppermute x37, waiting for transfers between devices, swapped_with(): return lax.ppermute(value, axis, [(i, i ^ offset) for i in range(size)])  24.3 us
    pallas_call x2, Pallas kernels, project(): pl.pallas_call(lambda *refs: project_kernel(clips, with_own, *refs), grid...  14 us
    pallas_call x1, Pallas kernels, attend_back(): pl.pallas_call(attend_back_kernel, grid_spec=grid_spec, out_shape=[shape_...  13 us
    pallas_call x1, Pallas kernels, attend(): pl.pallas_call(attend_kernel, grid=(width // LANES,), in_specs=[pl.BlockS...  11.5 us
    pallas_call x2, Pallas kernels, table_part(): pl.pallas_call(lambda *refs: table_kernel(first, clips, *refs), grid=(col...  11.2 us
    pallas_call x1, Pallas kernels, weights_part(): pl.pallas_call(lambda *refs: weights_kernel(clips, count, *refs), grid=(1...  9.74 us
    pallas_call x1, Pallas kernels, heads_probs(): pl.pallas_call(probs_kernel, grid_spec=grid_spec, out_shape=[shape_of((ro...  8.39 us
  transfers between devices with their start and end apart: 41, of which 15 were waited for; matrix products, arithmetic and copies ran while one was open for 3% of the time, Pallas kernels for 44%

profile of v6, /device:TPU:0, one launch (start us, length us, event | category | flops | bytes accessed | tf_op | source)
XLA Modules:
  0.0 204.0 jit_solution(8269974096270371253)
XLA Ops:
  0.6 3.1 %collective-permute-start = (bf16[128,1024]{1,0:T(8,128)(2,1)}, bf16[128,1024]{1,0:T(8,128)(2,1)S(1)}, u32[]{:S(2)}, u32[]{:S(2)}) collective-permute-start(bf16[128,1024]{1,0:T(8,128)(2,1)} %refs_2_.5), channel_id=1, source_target_pairs={{0,2},{1,3},{2,0},{3,1},{4,6},{5,7},{6,4},{7,5},{8,10},{9,11},{10,... | collective-permute-start | bytes 786440 | tf_op jit(solution)/shard_map/ppermute | solution.py:317
  3.7 2.6 %collective-permute-start.1 = (bf16[128,1024]{1,0:T(8,128)(2,1)}, bf16[128,1024]{1,0:T(8,128)(2,1)S(1)}, u32[]{:S(2)}, u32[]{:S(2)}) collective-permute-start(bf16[128,1024]{1,0:T(8,128)(2,1)} %refs_2_.5), channel_id=1, source_target_pairs={{0,4},{1,5},{2,6},{3,7},{4,0},{5,1},{6,2},{7,3},{8,12},{9,13},{10,... | collective-permute-start | bytes 786440 | tf_op jit(solution)/shard_map/ppermute | solution.py:317
  6.3 1.7 collective-permute-start.3
  11.0 5.9 %shard_map.246 = (f32[4,2048]{1,0:T(4,128)S(1)}, bf16[4,1024]{1,0:T(4,128)(2,1)S(1)}, s32[1024,1]{1,0:T(8,128)S(1)}, s32[1,1024]{1,0:T(1,128)S(1)}, f32[1024,128...) custom-call(s32[1]{0:T(128)} %bitcast.refs_0_.me_ref, ...), custom_call_target="tpu_custom_call" | custom-call | flops 16777216 | bytes 5242880 | tf_op jit(solution)/shard_map/pallas_call | solution.py:463
  17.0 4.8 %shard_map.248.refs_6_.refs_2_ = f32[4,4096]{1,0:T(4,128)S(1)} custom-call(bf16[4,1024]{1,0:T(4,128)(2,1)S(1)} %get-tuple-element.82.silu_ref, bf16[1024,6144]{1,0:T(8,128)(2,1)} %refs_6_.7, f32[1,6144]{1,0:T(1,128)S(1)} %bitcast.24), custom_call_target="tpu_custom_call" | custom-call | flops 33554432 | bytes 8388608 | tf_op jit(solution)/shard_map/pallas_call | solution.py:490
  23.4 1.9 collective-permute-done.1.refs_9_
  26.1 1.5 collective-permute-start.5
  28.9 6.4 %shard_map.247 = (bf16[512,1024]{1,0:T(8,128)(2,1)}, bf16[16,512,128]{2,1,0:T(8,128)(2,1)S(1)}, bf16[512,128]{1,0:T(8,128)(2,1)S(1)}, bf16[128,1024]{1,0:T(8,128)(2,1)}, bf16[128,1024]{1,0:T(8,128)(2,1)}) custom-call(s32[1]{0:T(128)} %bitcast.refs_0_.me_ref, s32[1024,1]{1,0:T(8,128)S(1)} %get-tuple-element.73.refs_1_.keyclip_ref.refs_0_, ...), custom_call_target="tpu_custom_call" | custom-call | flops 2147483648 | bytes 6291456 | tf_op jit(solution)/shard_map/pallas_call | solution.py:581
  35.3 3.5 %collective-permute-start.7 = (bf16[128,1024]{1,0:T(8,128)(2,1)}, bf16[128,1024]{1,0:T(8,128)(2,1)S(1)}, u32[]{:S(2)}, u32[]{:S(2)}) collective-permute-start(bf16[128,1024]{1,0:T(8,128)(2,1)} %get-tuple-element.88.refs_13_.refs_15_), channel_id=1, source_target_pairs={{0,2},{1,3},{2,0},{3,1},{4,6},{5,7},{6,4},{7,5},{8,10},{9,11},{10,... | collective-permute-start | bytes 786440 | tf_op jit(solution)/shard_map/ppermute | solution.py:317
  38.8 1.1 collective-permute-start.8
  39.9 1.5 collective-permute-start.9
  41.5 7.6 %shard_map.249 = (bf16[512,1024]{1,0:T(8,128)(2,1)}, bf16[16,512,128]{2,1,0:T(8,128)(2,1)S(1)}, bf16[512,128]{1,0:T(8,128)(2,1)S(1)}) custom-call(s32[1]{0:T(128)} %bitcast.refs_0_.me_ref, s32[1024,1]{1,0:T(8,128)S(1)} %get-tuple-element.73.refs_1_.keyclip_ref.refs_0_, f32[4,2048]{1,0:T(4,128)S(1)} %get-tuple-element.76.refs_2_.refs_3_, ...), custom_call_target="tpu_custom_call" | custom-call | flops 2147483648 | bytes 6291456 | tf_op jit(solution)/shard_map/pallas_call | solution.py:581
  49.2 11.5 %shard_map.250 = (bf16[128,1024]{1,0:T(8,128)(2,1)}, bf16[1024,1024]{1,0:T(8,128)(2,1)S(1)}, bf16[1024,2048]{1,0:T(8,128)(2,1)S(1)}, bf16[2048,1024]{1,0:T(8,128)(2,1)S(1)}) custom-call(bf16[1024,256]{1,0:T(8,128)(2,1)} %get-tuple-element.75.keymark_ref.rowmark_ref, bf16[1024,256]{1,0:T(8,128)(2,1)} %get-tuple-element.75.keymark_ref.rowmark_ref, ...), custom_call_target="tpu_custom_call" | custom-call | flops 536870912 | bytes 1048576 | tf_op jit(solution)/shard_map/pallas_call | solution.py:668
  61.6 8.4 %shard_map.251 = (bf16[128,1024]{1,0:T(8,128)(2,1)}, bf16[128,1024]{1,0:T(8,128)(2,1)}, f32[128,1024]{1,0:T(8,128)}, bf16[128,1024]{1,0:T(8,128)(2,1)}, bf16[8,1...) custom-call(s32[1,4]{1,0:T(1,128)S(1)} %copy-done.11, s32[1024,1]{1,0:T(8,128)S(1)} %get-tuple-element.73.refs_1_.keyclip_ref.refs_0_, ...), custom_call_target="tpu_custom_call" | custom-call | flops 2684354560 | bytes 3145728 | tf_op jit(solution)/shard_map/pallas_call | solution.py:983
  69.9 2.4 %collective-permute-start.12 = (bf16[128,1024]{1,0:T(8,128)(2,1)}, bf16[128,1024]{1,0:T(8,128)(2,1)S(1)}, u32[]{:S(2)}, u32[]{:S(2)}) collective-permute-start(bf16[128,1024]{1,0:T(8,128)(2,1)} %get-tuple-element.97.refs_1_.refs_11_), channel_id=1, source_target_pairs={{0,2},{1,3},{2,0},{3,1},{4,6},{5,7},{6,4},{7,5},{8,10},{9,11},{10,... | collective-permute-start | bytes 786440 | tf_op jit(solution)/shard_map/ppermute | solution.py:317
  72.4 1.7 collective-permute-start.13
  74.0 3.5 %all-to-all-start = ((bf16[8,128,128]{2,1,0:T(8,128)(2,1)}), bf16[8,128,128]{2,1,0:T(8,128)(2,1)S(1)}, u32[]{:S(2)}, u32[]{:S(2)}) async-start(bf16[8,128,128]{2,1,0:T(8,128)(2,1)} %get-tuple-element.95), calls=%async_computation | async-start | bytes 524288 | tf_op jit(solution)/shard_map/all_to_all | solution.py:1497
  77.6 1.9 collective-permute-start.10
  79.5 8.4 %shard_map.252 = (f32[1024,2048]{1,0:T(8,128)}, bf16[128,1024]{1,0:T(8,128)(2,1)}) custom-call(s32[1]{0:T(128)} %bitcast.refs_0_.me_ref, s32[1024,1]{1,0:T(8,128)S(1)} %get-tuple-element.73.refs_1_.keyclip_ref.refs_0_, s32[1,1024]{1,0:T(1,128)S(1)} %get-tuple-element.74.refs_2_.rowclip_ref.refs_1_, ...), custom_call_target="tpu_custom_call", output_to_operand_aliasing={{1}: (8, {})} | custom-call | flops 536870912 | bytes 9437184 | tf_op jit(solution)/shard_map/pallas_call | solution.py:730
  87.9 1.0 broadcast_select_fusion
  89.7 1.5 collective-permute-start.14
  91.2 1.5 collective-permute-start.11
  92.7 2.4 %collective-permute-start.15 = (bf16[128,1024]{1,0:T(8,128)(2,1)S(1)}, bf16[128,1024]{1,0:T(8,128)(2,1)}, u32[]{:S(2)}, u32[]{:S(2)}) collective-permute-start(bf16[128,1024]{1,0:T(8,128)(2,1)S(1)} %copy-done.13), channel_id=1, source_target_pairs={{0,6},{1,7},{2,4},{3,5},{4,2},{5,3},{6,0},{7,1},{8,14},{9,15},{10,... | collective-permute-start | bytes 786440 | tf_op jit(solution)/shard_map/ppermute | solution.py:317
  95.1 2.7 %collective-permute-done.11 = f32[8,4096]{1,0:T(8,128)S(1)} collective-permute-done((f32[8,4096]{1,0:T(8,128)S(1)}, f32[8,4096]{1,0:T(8,128)S(1)}, u32[]{:S(2)}, u32[]{:S(2)}) %collective-permute-start.11) | collective-permute-done | bytes 131104 | tf_op jit(solution)/shard_map/ppermute | solution.py:317
  98.6 13.0 %shard_map.253 = (bf16[1024,384]{1,0:T(8,128)(2,1)}, bf16[8,128,384]{2,1,0:T(8,128)(2,1)}, f32[8,4096]{1,0:T(8,128)S(1)}) custom-call(s32[1]{0:T(128)} %bitcast.refs_0_.me_ref, f32[1024,2048]{1,0:T(8,128)} %get-tuple-element.94.p_ref, bf16[512,128]{1,0:T(8,128)(2,1)S(1)} %get-tuple-element.91.qa_ref, ...), custom_call_target="tpu_custom_call", output_to_operand_aliasing={{2}: (11, {})} | custom-call | flops 1073741824 | bytes 12582912 | tf_op jit(solution)/shard_map/pallas_call | solution.py:835
  111.6 3.8 %all-to-all-start.1 = ((bf16[8,128,384]{2,1,0:T(8,128)(2,1)}), bf16[8,128,384]{2,1,0:T(8,128)(2,1)S(1)}, u32[]{:S(2)}, u32[]{:S(2)}) async-start(bf16[8,128,384]{2,1,0:T(8,128)(2,1)} %get-tuple-element.98), calls=%async_computation.1 | async-start | bytes 1572864 | tf_op jit(solution)/shard_map/all_to_all | solution.py:1514
  116.3 9.7 %shard_map.254 = (f32[512,1920]{1,0:T(8,128)}, bf16[512,640]{1,0:T(8,128)(2,1)}, bf16[512,640]{1,0:T(8,128)(2,1)}, bf16[512,640]{1,0:T(8,128)(2,1)}) custom-call(s32[3]{0:T(128)S(1)} %pad_add_fusion.refs_0_, s32[1024,1]{1,0:T(8,128)S(1)} %get-tuple-element.73.refs_1_.keyclip_ref.refs_0_, f32[4,4096]{1,0:T(4,128)S(1)} %shard_map.248.refs_6_.refs_2_, ...), custom_call_target="tpu_custom_call" | custom-call | flops 3758096384 | bytes 10485760 | tf_op jit(solution)/shard_map/pallas_call | solution.py:1162
  126.7 1.7 collective-permute-done.16.refs_2_
  130.3 3.9 %shard_map.255 = (f32[8,32,896]{2,1,0:T(8,128)}, bf16[8,32,896]{2,1,0:T(8,128)(2,1)}, bf16[8,32,512]{2,1,0:T(8,128)(2,1)}, bf16[8,32,512]{2,1,0:T(8,128)(2,1)}, bf16[8,32,1024]{2,1,0:T(8,128)(2,1)}) custom-call(s32[3]{0:T(128)S(1)} %pad_add_fusion.refs_0_, f32[512,1920]{1,0:T(8,128)} %get-tuple-element.103.refs_1_, ...), custom_call_target="tpu_custom_call" | custom-call | bytes 8388608 | tf_op jit(solution)/shard_map/pallas_call | solution.py:1325
  134.7 1.7 collective-permute-start.20
  136.3 1.3 collective-permute-start.21
  137.7 6.8 %shard_map.256 = (bf16[128,1024]{1,0:T(8,128)(2,1)}, f32[8,2048]{1,0:T(8,128)S(1)}, f32[8,32,896]{2,1,0:T(8,128)}, f32[8,4096]{1,0:T(8,128)S(1)}) custom-call(s32[1024,1]{1,0:T(8,128)S(1)} %get-tuple-element.73.refs_1_.keyclip_ref.refs_0_, s32[1,1024]{1,0:T(1,128)S(1)} %get-tuple-element.74.refs_2_.rowclip_ref.refs_1_, ...), custom_call_target="tpu_custom_call", output_to_operand_aliasing={{2}: (7, {}), {3}: (8, {})} | custom-call | flops 805306368 | bytes 2097152 | tf_op jit(solution)/shard_map/pallas_call | solution.py:1035
  144.5 2.6 %collective-permute-start.23 = (f32[8,4096]{1,0:T(8,128)S(1)}, f32[8,4096]{1,0:T(8,128)S(1)}, u32[]{:S(2)}, u32[]{:S(2)}) collective-permute-start(f32[8,4096]{1,0:T(8,128)S(1)} %get-tuple-element.116), channel_id=1, source_target_pairs={{0,4},{1,5},{2,6},{3,7},{4,0},{5,1},{6,2},{7,3},{8,12},{9,13},{10,... | collective-permute-start | bytes 393224 | tf_op jit(solution)/shard_map/ppermute | solution.py:317
  147.1 1.5 collective-permute-start.22
  148.6 3.0 %collective-permute-done.22 = f32[8,2048]{1,0:T(8,128)S(1)} collective-permute-done((f32[8,2048]{1,0:T(8,128)S(1)}, f32[8,2048]{1,0:T(8,128)S(1)}, u32[]{:S(2)}, u32[]{:S(2)}) %collective-permute-start.22) | collective-permute-done | bytes 65568 | tf_op jit(solution)/shard_map/ppermute | solution.py:317
  151.6 1.4 collective-permute-done.23
  153.6 2.3 %shard_map.257 = (f32[8,2048]{1,0:T(8,128)S(1)}, f32[8,4096]{1,0:T(8,128)S(1)}, bf16[8,32,1664]{2,1,0:T(8,128)(2,1)}, bf16[64,1024]{1,0:T(8,128)(2,1)S(1)}) custom-call(f32[8,32,896]{2,1,0:T(8,128)} %get-tuple-element.110.refs_0_, bf16[8,32,896]{2,1,0:T(8,128)(2,1)S(1)} %collective-permute-done.19.refs_1_, ...), custom_call_target="tpu_custom_call", output_to_operand_aliasing={{0}: (5, {}), {1}: (6, {})} | custom-call | bytes 4194304 | tf_op jit(solution)/shard_map/pallas_call | solution.py:1361
  156.0 5.0 %all-to-all-start.2 = ((bf16[8,32,1664]{2,1,0:T(8,128)(2,1)}), bf16[8,32,1664]{2,1,0:T(8,128)(2,1)S(1)}, u32[]{:S(2)}, u32[]{:S(2)}) async-start(bf16[8,32,1664]{2,1,0:T(8,128)(2,1)} %get-tuple-element.117), calls=%async_computation.2 | async-start | bytes 1703936 | tf_op jit(solution)/shard_map/all_to_all | solution.py:1542
  161.6 1.3 collective-permute-start.27
  162.9 2.1 %collective-permute-start.24 = (f32[8,2048]{1,0:T(8,128)S(1)}, f32[8,2048]{1,0:T(8,128)S(1)}, u32[]{:S(2)}, u32[]{:S(2)}) collective-permute-start(f32[8,2048]{1,0:T(8,128)S(1)} %get-tuple-element.118), channel_id=1, source_target_pairs={{0,1},{1,0},{2,3},{3,2},{4,5},{5,4},{6,7},{7,6},{8,9},{9,8},{10,11... | collective-permute-start | bytes 196616 | tf_op jit(solution)/shard_map/ppermute | solution.py:317
  165.5 3.7 %collective-permute-done.27.refs_4_ = f32[8,4096]{1,0:T(8,128)S(1)} collective-permute-done((f32[8,4096]{1,0:T(8,128)S(1)}, f32[8,4096]{1,0:T(8,128)S(1)}, u32[]{:S(2)}, u32[]{:S(2)}) %collective-permute-start.27) | collective-permute-done | bytes 131104 | tf_op jit(solution)/shard_map/ppermute | solution.py:317
  170.8 6.3 %shard_map.258 = (f32[128,6144]{1,0:T(8,128)}, f32[1,6144]{1,0:T(1,128)}, f32[1024,64]{1,0:T(8,128)}) custom-call(s32[1]{0:T(128)} %bitcast.8.refs_0_, f32[8,4096]{1,0:T(8,128)S(1)} %get-tuple-element.119.refs_1_, f32[8,4096]{1,0:T(8,128)S(1)} %collective-permute-done.25.refs_2_, f32[8,4096]{1,0:T(8,128)S(1)} %collective-permute-done.26.refs_3_, ...), custom_call_target="tpu_custom_call" | custom-call | flops 32768 | bytes 1024 | tf_op jit(solution)/shard_map/pallas_call | solution.py:1264
  177.1 5.5 %all-to-all-done.2.refs_0_ = bf16[8,32,1664]{2,1,0:T(8,128)(2,1)S(1)} async-done(((bf16[8,32,1664]{2,1,0:T(8,128)(2,1)}), bf16[8,32,1664]{2,1,0:T(8,128)(2,1)S(1)}, u32[]{:S(2)}, u32[]{:S(2)}) %all-to-all-start.2) | async-done | bytes 852000 | tf_op jit(solution)/shard_map/all_to_all | solution.py:1542
  185.3 4.2 %collective-permute-done.28 = f32[8,2048]{1,0:T(8,128)S(1)} collective-permute-done((f32[8,2048]{1,0:T(8,128)S(1)}, f32[8,2048]{1,0:T(8,128)S(1)}, u32[]{:S(2)}, u32[]{:S(2)}) %collective-permute-start.28) | collective-permute-done | bytes 65568 | tf_op jit(solution)/shard_map/ppermute | solution.py:317
  189.6 1.6 collective-permute-start.30
  192.1 2.9 %collective-permute-done.30.refs_3_ = f32[8,2048]{1,0:T(8,128)S(1)} collective-permute-done((f32[8,2048]{1,0:T(8,128)S(1)}, f32[8,2048]{1,0:T(8,128)S(1)}, u32[]{:S(2)}, u32[]{:S(2)}) %collective-permute-start.30) | collective-permute-done | bytes 65568 | tf_op jit(solution)/shard_map/ppermute | solution.py:317
  195.7 4.9 %shard_map.260 = (f32[128,6144]{1,0:T(8,128)}, f32[1,6144]{1,0:T(1,128)}, f32[32,1024]{1,0:T(8,128)}) custom-call(s32[1]{0:T(128)} %bitcast.8.refs_0_, f32[8,2048]{1,0:T(8,128)S(1)} %add.102.refs_1_, f32[8,2048]{1,0:T(8,128)S(1)} %collective-permute-done.29.refs_2_, ...), custom_call_target="tpu_custom_call", output_to_operand_aliasing={{0}: (10, {}), {1}: (11, {})} | custom-call | flops 32768 | bytes 1024 | tf_op jit(solution)/shard_map/pallas_call | solution.py:1264
  201.2 2.8 %shard_map.261 = (f32[128,3072]{1,0:T(8,128)}, f32[128,1024]{1,0:T(8,128)}, f32[128,2048]{1,0:T(8,128)}, f32[256,1024]{1,0:T(8,128)}) custom-call(s32[3]{0:T(128)S(1)} %pad_add_fusion.refs_0_, bf16[192,1024]{1,0:T(8,128)(2,1)S(1)} %copy-done.4, bf16[192,1024]{1,0:T(8,128)(2,1)S(1)} %collective-permute-done.32.refs_2_, ...), custom_call_target="tpu_custom_call" | custom-call | bytes 6291456 | tf_op jit(solution)/shard_map/pallas_call | solution.py:1445
  (129 shorter events, 20.7 us)
Async XLA Ops:
  0.6 22.4 %collective-permute-start = (bf16[128,1024]{1,0:T(8,128)(2,1)}, bf16[128,1024]{1,0:T(8,128)(2,1)S(1)}, u32[]{:S(2)}, u32[]{:S(2)}) collective-permute-start(bf16[128,1024]{1,0:T(8,128)(2,1)} %refs_2_.5), channel_id=1, source_target_pairs={{0,2},{1,3},{2,0},{3,1},{4,6},{5,7},{6,4},{7,5},{8,10},{9,11},{10,... | collective-permute-start | bytes 786440 | tf_op jit(solution)/shard_map/ppermute | solution.py:317
  3.7 21.6 %collective-permute-start.1 = (bf16[128,1024]{1,0:T(8,128)(2,1)}, bf16[128,1024]{1,0:T(8,128)(2,1)S(1)}, u32[]{:S(2)}, u32[]{:S(2)}) collective-permute-start(bf16[128,1024]{1,0:T(8,128)(2,1)} %refs_2_.5), channel_id=1, source_target_pairs={{0,4},{1,5},{2,6},{3,7},{4,0},{5,1},{6,2},{7,3},{8,12},{9,13},{10,... | collective-permute-start | bytes 786440 | tf_op jit(solution)/shard_map/ppermute | solution.py:317
  6.3 21.3 %collective-permute-start.2 = (bf16[128,1024]{1,0:T(8,128)(2,1)}, bf16[128,1024]{1,0:T(8,128)(2,1)S(1)}, u32[]{:S(2)}, u32[]{:S(2)}) collective-permute-start(bf16[128,1024]{1,0:T(8,128)(2,1)} %refs_2_.5), channel_id=1, source_target_pairs={{0,6},{1,7},{2,4},{3,5},{4,2},{5,3},{6,0},{7,1},{8,14},{9,15},{10,... | collective-permute-start | bytes 786440 | tf_op jit(solution)/shard_map/ppermute | solution.py:317
  6.3 32.5 %collective-permute-start.3 = (bf16[128,1024]{1,0:T(8,128)(2,1)}, bf16[128,1024]{1,0:T(8,128)(2,1)}, u32[]{:S(2)}, u32[]{:S(2)}) collective-permute-start(bf16[128,1024]{1,0:T(8,128)(2,1)} %refs_2_.5), channel_id=1, source_target_pairs={{0,1},{1,0},{2,3},{3,2},{4,5},{5,4},{6,7},{7,6},{8,9},{9,8},{10,11... | collective-permute-start | bytes 786440 | tf_op jit(solution)/shard_map/ppermute | solution.py:317
  23.1 16.8 %collective-permute-start.4 = (bf16[128,1024]{1,0:T(8,128)(2,1)S(1)}, bf16[128,1024]{1,0:T(8,128)(2,1)}, u32[]{:S(2)}, u32[]{:S(2)}) collective-permute-start(bf16[128,1024]{1,0:T(8,128)(2,1)S(1)} %broadcast_add_fusion.2), channel_id=1, source_target_pairs={{0,1},{1,0},{2,3},{3,2},{4,5},{5,4},{6,7},{7,6},{8,9},{9,8},{10,11... | collective-permute-start | bytes 786440 | tf_op jit(solution)/shard_map/ppermute | solution.py:317
  26.1 15.3 %collective-permute-start.5 = (bf16[128,1024]{1,0:T(8,128)(2,1)}, bf16[128,1024]{1,0:T(8,128)(2,1)}, u32[]{:S(2)}, u32[]{:S(2)}) collective-permute-start(bf16[128,1024]{1,0:T(8,128)(2,1)} %broadcast_add_fusion.1), channel_id=1, source_target_pairs={{0,1},{1,0},{2,3},{3,2},{4,5},{5,4},{6,7},{7,6},{8,9},{9,8},{10,11... | collective-permute-start | bytes 786440 | tf_op jit(solution)/shard_map/ppermute | solution.py:317
  28.4 13.1 %collective-permute-start.6 = (bf16[128,1024]{1,0:T(8,128)(2,1)}, bf16[128,1024]{1,0:T(8,128)(2,1)}, u32[]{:S(2)}, u32[]{:S(2)}) collective-permute-start(bf16[128,1024]{1,0:T(8,128)(2,1)} %broadcast_add_fusion), channel_id=1, source_target_pairs={{0,1},{1,0},{2,3},{3,2},{4,5},{5,4},{6,7},{7,6},{8,9},{9,8},{10,11... | collective-permute-start | bytes 786440 | tf_op jit(solution)/shard_map/ppermute | solution.py:317
  35.3 13.8 %copy-start = (bf16[16,512,128]{2,1,0:T(8,128)(2,1)}, bf16[16,512,128]{2,1,0:T(8,128)(2,1)S(1)}, u32[]{:S(2)}) copy-start(bf16[16,512,128]{2,1,0:T(8,128)(2,1)S(1)} %get-tuple-element.81.ka_ref.va_ref) | copy-start | bytes 6291460
  35.3 25.4 %collective-permute-start.7 = (bf16[128,1024]{1,0:T(8,128)(2,1)}, bf16[128,1024]{1,0:T(8,128)(2,1)S(1)}, u32[]{:S(2)}, u32[]{:S(2)}) collective-permute-start(bf16[128,1024]{1,0:T(8,128)(2,1)} %get-tuple-element.88.refs_13_.refs_15_), channel_id=1, source_target_pairs={{0,2},{1,3},{2,0},{3,1},{4,6},{5,7},{6,4},{7,5},{8,10},{9,11},{10,... | collective-permute-start | bytes 786440 | tf_op jit(solution)/shard_map/ppermute | solution.py:317
  38.8 21.9 %collective-permute-start.8 = (bf16[128,1024]{1,0:T(8,128)(2,1)}, bf16[128,1024]{1,0:T(8,128)(2,1)S(1)}, u32[]{:S(2)}, u32[]{:S(2)}) collective-permute-start(bf16[128,1024]{1,0:T(8,128)(2,1)} %get-tuple-element.88.refs_13_.refs_15_), channel_id=1, source_target_pairs={{0,4},{1,5},{2,6},{3,7},{4,0},{5,1},{6,2},{7,3},{8,12},{9,13},{10,... | collective-permute-start | bytes 786440 | tf_op jit(solution)/shard_map/ppermute | solution.py:317
  39.9 20.9 %collective-permute-start.9 = (bf16[128,1024]{1,0:T(8,128)(2,1)}, bf16[128,1024]{1,0:T(8,128)(2,1)}, u32[]{:S(2)}, u32[]{:S(2)}) collective-permute-start(bf16[128,1024]{1,0:T(8,128)(2,1)} %get-tuple-element.88.refs_13_.refs_15_), channel_id=1, source_target_pairs={{0,6},{1,7},{2,4},{3,5},{4,2},{5,3},{6,0},{7,1},{8,14},{9,15},{10,... | collective-permute-start | bytes 786440 | tf_op jit(solution)/shard_map/ppermute | solution.py:317
  49.1 12.4 %copy-start.7 = (f32[2048]{0:T(1024)S(1)}, f32[2048]{0:T(1024)}, u32[]{:S(2)}) copy-start(f32[2048]{0:T(1024)} %param.26) | copy-start | bytes 24580
  49.1 12.4 %copy-start.8 = (f32[1024]{0:T(1024)S(1)}, f32[1024]{0:T(1024)}, u32[]{:S(2)}) copy-start(f32[1024]{0:T(1024)} %param.24) | copy-start | bytes 12292
  49.1 12.4 %copy-start.9 = (f32[1024]{0:T(1024)S(1)}, f32[1024]{0:T(1024)}, u32[]{:S(2)}) copy-start(f32[1024]{0:T(1024)} %param.28) | copy-start | bytes 12292
  69.9 19.0 %copy-start.18 = (bf16[128,1024]{1,0:T(8,128)(2,1)S(1)}, bf16[128,1024]{1,0:T(8,128)(2,1)}, u32[]{:S(2)}) copy-start(bf16[128,1024]{1,0:T(8,128)(2,1)} %get-tuple-element.84.refs_5_) | copy-start | bytes 786436
  69.9 27.9 %collective-permute-start.12 = (bf16[128,1024]{1,0:T(8,128)(2,1)}, bf16[128,1024]{1,0:T(8,128)(2,1)S(1)}, u32[]{:S(2)}, u32[]{:S(2)}) collective-permute-start(bf16[128,1024]{1,0:T(8,128)(2,1)} %get-tuple-element.97.refs_1_.refs_11_), channel_id=1, source_target_pairs={{0,2},{1,3},{2,0},{3,1},{4,6},{5,7},{6,4},{7,5},{8,10},{9,11},{10,... | collective-permute-start | bytes 786440 | tf_op jit(solution)/shard_map/ppermute | solution.py:317
  72.4 25.5 %collective-permute-start.13 = (bf16[128,1024]{1,0:T(8,128)(2,1)}, bf16[128,1024]{1,0:T(8,128)(2,1)S(1)}, u32[]{:S(2)}, u32[]{:S(2)}) collective-permute-start(bf16[128,1024]{1,0:T(8,128)(2,1)} %get-tuple-element.97.refs_1_.refs_11_), channel_id=1, source_target_pairs={{0,4},{1,5},{2,6},{3,7},{4,0},{5,1},{6,2},{7,3},{8,12},{9,13},{10,... | collective-permute-start | bytes 786440 | tf_op jit(solution)/shard_map/ppermute | solution.py:317
  74.0 18.7 %copy-start.13 = (bf16[128,1024]{1,0:T(8,128)(2,1)S(1)}, bf16[128,1024]{1,0:T(8,128)(2,1)}, u32[]{:S(2)}) copy-start(bf16[128,1024]{1,0:T(8,128)(2,1)} %get-tuple-element.97.refs_1_.refs_11_) | copy-start | bytes 786436
  74.0 23.8 %all-to-all-start = ((bf16[8,128,128]{2,1,0:T(8,128)(2,1)}), bf16[8,128,128]{2,1,0:T(8,128)(2,1)S(1)}, u32[]{:S(2)}, u32[]{:S(2)}) async-start(bf16[8,128,128]{2,1,0:T(8,128)(2,1)} %get-tuple-element.95), calls=%async_computation | async-start | bytes 524288 | tf_op jit(solution)/shard_map/all_to_all | solution.py:1497
  77.6 13.6 %collective-permute-start.10 = (f32[8,4096]{1,0:T(8,128)S(1)}, f32[8,4096]{1,0:T(8,128)S(1)}, u32[]{:S(2)}, u32[]{:S(2)}) collective-permute-start(f32[8,4096]{1,0:T(8,128)S(1)} %get-tuple-element.96), channel_id=1, source_target_pairs={{0,1},{1,0},{2,3},{3,2},{4,5},{5,4},{6,7},{7,6},{8,9},{9,8},{10,11... | collective-permute-start | bytes 393224 | tf_op jit(solution)/shard_map/ppermute | solution.py:317
  89.7 25.8 %collective-permute-start.14 = (bf16[128,1536]{1,0:T(8,128)(2,1)S(1)}, bf16[128,1536]{1,0:T(8,128)(2,1)S(1)}, u32[]{:S(2)}, u32[]{:S(2)}) collective-permute-start(bf16[128,1536]{1,0:T(8,128)(2,1)S(1)} %get-tuple-element.133), channel_id=1, source_target_pairs={{0,16},{8,24},{16,0},{24,8},{1,17},{9,25},{17,1},{25,9},{2,18},{10... | collective-permute-start | bytes 1179656 | tf_op jit(solution)/shard_map/ppermute | solution.py:317
  91.2 6.6 %collective-permute-start.11 = (f32[8,4096]{1,0:T(8,128)S(1)}, f32[8,4096]{1,0:T(8,128)S(1)}, u32[]{:S(2)}, u32[]{:S(2)}) collective-permute-start(f32[8,4096]{1,0:T(8,128)S(1)} %add.93), channel_id=1, source_target_pairs={{0,2},{1,3},{2,0},{3,1},{4,6},{5,7},{6,4},{7,5},{8,10},{9,11},{10,... | collective-permute-start | bytes 393224 | tf_op jit(solution)/shard_map/ppermute | solution.py:317
  92.7 22.8 %collective-permute-start.15 = (bf16[128,1024]{1,0:T(8,128)(2,1)S(1)}, bf16[128,1024]{1,0:T(8,128)(2,1)}, u32[]{:S(2)}, u32[]{:S(2)}) collective-permute-start(bf16[128,1024]{1,0:T(8,128)(2,1)S(1)} %copy-done.13), channel_id=1, source_target_pairs={{0,6},{1,7},{2,4},{3,5},{4,2},{5,3},{6,0},{7,1},{8,14},{9,15},{10,... | collective-permute-start | bytes 786440 | tf_op jit(solution)/shard_map/ppermute | solution.py:317
  111.6 26.0 %all-to-all-start.1 = ((bf16[8,128,384]{2,1,0:T(8,128)(2,1)}), bf16[8,128,384]{2,1,0:T(8,128)(2,1)S(1)}, u32[]{:S(2)}, u32[]{:S(2)}) async-start(bf16[8,128,384]{2,1,0:T(8,128)(2,1)} %get-tuple-element.98), calls=%async_computation.1 | async-start | bytes 1572864 | tf_op jit(solution)/shard_map/all_to_all | solution.py:1514
  126.0 2.4 %collective-permute-start.16 = (bf16[512,640]{1,0:T(8,128)(2,1)}, bf16[512,640]{1,0:T(8,128)(2,1)S(1)}, u32[]{:S(2)}, u32[]{:S(2)}) collective-permute-start(bf16[512,640]{1,0:T(8,128)(2,1)} %get-tuple-element.104), channel_id=1, source_target_pairs={{0,8},{8,0},{16,24},{24,16},{1,9},{9,1},{17,25},{25,17},{2,10},{10... | collective-permute-start | bytes 1966088 | tf_op jit(solution)/shard_map/ppermute | solution.py:317
  126.1 3.2 %collective-permute-start.17 = (bf16[512,640]{1,0:T(8,128)(2,1)}, bf16[512,640]{1,0:T(8,128)(2,1)S(1)}, u32[]{:S(2)}, u32[]{:S(2)}) collective-permute-start(bf16[512,640]{1,0:T(8,128)(2,1)} %get-tuple-element.105), channel_id=1, source_target_pairs={{0,8},{8,0},{16,24},{24,16},{1,9},{9,1},{17,25},{25,17},{2,10},{10... | collective-permute-start | bytes 1966088 | tf_op jit(solution)/shard_map/ppermute | solution.py:317
  126.6 3.7 %collective-permute-start.18 = (bf16[512,640]{1,0:T(8,128)(2,1)}, bf16[512,640]{1,0:T(8,128)(2,1)S(1)}, u32[]{:S(2)}, u32[]{:S(2)}) collective-permute-start(bf16[512,640]{1,0:T(8,128)(2,1)} %get-tuple-element.106), channel_id=1, source_target_pairs={{0,8},{8,0},{16,24},{24,16},{1,9},{9,1},{17,25},{25,17},{2,10},{10... | collective-permute-start | bytes 1966088 | tf_op jit(solution)/shard_map/ppermute | solution.py:317
  134.2 19.5 %collective-permute-start.19 = (bf16[8,32,896]{2,1,0:T(8,128)(2,1)}, bf16[8,32,896]{2,1,0:T(8,128)(2,1)S(1)}, u32[]{:S(2)}, u32[]{:S(2)}) collective-permute-start(bf16[8,32,896]{2,1,0:T(8,128)(2,1)} %get-tuple-element.111), channel_id=1, source_target_pairs={{0,16},{8,24},{16,0},{24,8},{1,17},{9,25},{17,1},{25,9},{2,18},{10... | collective-permute-start | bytes 1376264 | tf_op jit(solution)/shard_map/ppermute | solution.py:317
  134.7 18.3 %collective-permute-start.20 = (bf16[8,32,512]{2,1,0:T(8,128)(2,1)}, bf16[8,32,512]{2,1,0:T(8,128)(2,1)S(1)}, u32[]{:S(2)}, u32[]{:S(2)}) collective-permute-start(bf16[8,32,512]{2,1,0:T(8,128)(2,1)} %get-tuple-element.112), channel_id=1, source_target_pairs={{0,1},{1,0},{2,3},{3,2},{4,5},{5,4},{6,7},{7,6},{8,9},{9,8},{10,11... | collective-permute-start | bytes 786440 | tf_op jit(solution)/shard_map/ppermute | solution.py:317
  136.3 17.3 %collective-permute-start.21 = (bf16[8,32,512]{2,1,0:T(8,128)(2,1)}, bf16[8,32,512]{2,1,0:T(8,128)(2,1)S(1)}, u32[]{:S(2)}, u32[]{:S(2)}) collective-permute-start(bf16[8,32,512]{2,1,0:T(8,128)(2,1)} %get-tuple-element.113), channel_id=1, source_target_pairs={{0,17},{1,16},{2,19},{3,18},{4,21},{5,20},{6,23},{7,22},{8,25},{9,... | collective-permute-start | bytes 786440 | tf_op jit(solution)/shard_map/ppermute | solution.py:1537
  144.5 25.4 %copy-start.3 = (f32[32,1024]{1,0:T(8,128)S(1)}, f32[32,1024]{1,0:T(8,128)}, u32[]{:S(2)}) copy-start(f32[32,1024]{1,0:T(8,128)} %refs_3_.2) | copy-start | bytes 393220
  144.5 8.5 %collective-permute-start.23 = (f32[8,4096]{1,0:T(8,128)S(1)}, f32[8,4096]{1,0:T(8,128)S(1)}, u32[]{:S(2)}, u32[]{:S(2)}) collective-permute-start(f32[8,4096]{1,0:T(8,128)S(1)} %get-tuple-element.116), channel_id=1, source_target_pairs={{0,4},{1,5},{2,6},{3,7},{4,0},{5,1},{6,2},{7,3},{8,12},{9,13},{10,... | collective-permute-start | bytes 393224 | tf_op jit(solution)/shard_map/ppermute | solution.py:317
  147.1 4.4 %collective-permute-start.22 = (f32[8,2048]{1,0:T(8,128)S(1)}, f32[8,2048]{1,0:T(8,128)S(1)}, u32[]{:S(2)}, u32[]{:S(2)}) collective-permute-start(f32[8,2048]{1,0:T(8,128)S(1)} %get-tuple-element.115), channel_id=1, source_target_pairs={{0,2},{1,3},{2,0},{3,1},{4,6},{5,7},{6,4},{7,5},{8,10},{9,11},{10,... | collective-permute-start | bytes 196616 | tf_op jit(solution)/shard_map/ppermute | solution.py:317
  156.0 26.7 %all-to-all-start.2 = ((bf16[8,32,1664]{2,1,0:T(8,128)(2,1)}), bf16[8,32,1664]{2,1,0:T(8,128)(2,1)S(1)}, u32[]{:S(2)}, u32[]{:S(2)}) async-start(bf16[8,32,1664]{2,1,0:T(8,128)(2,1)} %get-tuple-element.117), calls=%async_computation.2 | async-start | bytes 1703936 | tf_op jit(solution)/shard_map/all_to_all | solution.py:1542
  161.0 8.3 %collective-permute-start.25 = (f32[8,4096]{1,0:T(8,128)S(1)}, f32[8,4096]{1,0:T(8,128)S(1)}, u32[]{:S(2)}, u32[]{:S(2)}) collective-permute-start(f32[8,4096]{1,0:T(8,128)S(1)} %get-tuple-element.119.refs_1_), channel_id=1, source_target_pairs={{0,8},{8,0},{16,24},{24,16},{1,9},{9,1},{17,25},{25,17},{2,10},{10... | collective-permute-start | bytes 393224 | tf_op jit(solution)/shard_map/ppermute | solution.py:317
  161.0 8.2 %collective-permute-start.26 = (f32[8,4096]{1,0:T(8,128)S(1)}, f32[8,4096]{1,0:T(8,128)S(1)}, u32[]{:S(2)}, u32[]{:S(2)}) collective-permute-start(f32[8,4096]{1,0:T(8,128)S(1)} %get-tuple-element.119.refs_1_), channel_id=1, source_target_pairs={{0,16},{8,24},{16,0},{24,8},{1,17},{9,25},{17,1},{25,9},{2,18},{10... | collective-permute-start | bytes 393224 | tf_op jit(solution)/shard_map/ppermute | solution.py:317
  161.6 7.6 %collective-permute-start.27 = (f32[8,4096]{1,0:T(8,128)S(1)}, f32[8,4096]{1,0:T(8,128)S(1)}, u32[]{:S(2)}, u32[]{:S(2)}) collective-permute-start(f32[8,4096]{1,0:T(8,128)S(1)} %get-tuple-element.119.refs_1_), channel_id=1, source_target_pairs={{0,24},{8,16},{16,8},{24,0},{1,25},{9,17},{17,9},{25,1},{2,26},{10... | collective-permute-start | bytes 393224 | tf_op jit(solution)/shard_map/ppermute | solution.py:317
  162.9 7.9 %collective-permute-start.24 = (f32[8,2048]{1,0:T(8,128)S(1)}, f32[8,2048]{1,0:T(8,128)S(1)}, u32[]{:S(2)}, u32[]{:S(2)}) collective-permute-start(f32[8,2048]{1,0:T(8,128)S(1)} %get-tuple-element.118), channel_id=1, source_target_pairs={{0,1},{1,0},{2,3},{3,2},{4,5},{5,4},{6,7},{7,6},{8,9},{9,8},{10,11... | collective-permute-start | bytes 196616 | tf_op jit(solution)/shard_map/ppermute | solution.py:317
  165.0 26.6 %collective-permute-start.36 = (bf16[64,1024]{1,0:T(8,128)(2,1)S(1)}, bf16[64,1024]{1,0:T(8,128)(2,1)S(1)}, u32[]{:S(2)}, u32[]{:S(2)}) collective-permute-start(bf16[64,1024]{1,0:T(8,128)(2,1)S(1)} %get-tuple-element.128.refs_5_), channel_id=1, source_target_pairs={{0,16},{8,24},{16,0},{24,8},{1,17},{9,25},{17,1},{25,9},{2,18},{10... | collective-permute-start | bytes 393224 | tf_op jit(solution)/shard_map/ppermute | solution.py:317
  183.5 11.5 %collective-permute-start.33 = (bf16[192,1024]{1,0:T(8,128)(2,1)}, bf16[192,1024]{1,0:T(8,128)(2,1)S(1)}, u32[]{:S(2)}, u32[]{:S(2)}) collective-permute-start(bf16[192,1024]{1,0:T(8,128)(2,1)} %get-tuple-element.127.refs_1_), channel_id=1, source_target_pairs={{0,16},{8,24},{16,0},{24,8},{1,17},{9,25},{17,1},{25,9},{2,18},{10... | collective-permute-start | bytes 1179656 | tf_op jit(solution)/shard_map/ppermute | solution.py:317
  184.1 5.5 %collective-permute-start.28 = (f32[8,2048]{1,0:T(8,128)S(1)}, f32[8,2048]{1,0:T(8,128)S(1)}, u32[]{:S(2)}, u32[]{:S(2)}) collective-permute-start(f32[8,2048]{1,0:T(8,128)S(1)} %get-tuple-element.121), channel_id=1, source_target_pairs={{0,4},{1,5},{2,6},{3,7},{4,0},{5,1},{6,2},{7,3},{8,12},{9,13},{10,... | collective-permute-start | bytes 196616 | tf_op jit(solution)/shard_map/ppermute | solution.py:317
  189.6 2.4 %collective-permute-start.29 = (f32[8,2048]{1,0:T(8,128)S(1)}, f32[8,2048]{1,0:T(8,128)S(1)}, u32[]{:S(2)}, u32[]{:S(2)}) collective-permute-start(f32[8,2048]{1,0:T(8,128)S(1)} %add.102.refs_1_), channel_id=1, source_target_pairs={{0,8},{8,0},{16,24},{24,16},{1,9},{9,1},{17,25},{25,17},{2,10},{10... | collective-permute-start | bytes 196616 | tf_op jit(solution)/shard_map/ppermute | solution.py:317
  189.6 5.3 %collective-permute-start.30 = (f32[8,2048]{1,0:T(8,128)S(1)}, f32[8,2048]{1,0:T(8,128)S(1)}, u32[]{:S(2)}, u32[]{:S(2)}) collective-permute-start(f32[8,2048]{1,0:T(8,128)S(1)} %add.102.refs_1_), channel_id=1, source_target_pairs={{0,16},{8,24},{16,0},{24,8},{1,17},{9,25},{17,1},{25,9},{2,18},{10... | collective-permute-start | bytes 196616 | tf_op jit(solution)/shard_map/ppermute | solution.py:317
  191.2 4.4 %collective-permute-start.31 = (f32[8,2048]{1,0:T(8,128)S(1)}, f32[8,2048]{1,0:T(8,128)S(1)}, u32[]{:S(2)}, u32[]{:S(2)}) collective-permute-start(f32[8,2048]{1,0:T(8,128)S(1)} %add.102.refs_1_), channel_id=1, source_target_pairs={{0,24},{8,16},{16,8},{24,0},{1,25},{9,17},{17,9},{25,1},{2,26},{10... | collective-permute-start | bytes 196616 | tf_op jit(solution)/shard_map/ppermute | solution.py:317
  191.5 9.7 %collective-permute-start.35 = (bf16[64,1024]{1,0:T(8,128)(2,1)S(1)}, bf16[64,1024]{1,0:T(8,128)(2,1)S(1)}, u32[]{:S(2)}, u32[]{:S(2)}) collective-permute-start(bf16[64,1024]{1,0:T(8,128)(2,1)S(1)} %get-tuple-element.128.refs_5_), channel_id=1, source_target_pairs={{0,8},{8,0},{16,24},{24,16},{1,9},{9,1},{17,25},{25,17},{2,10},{10... | collective-permute-start | bytes 393224 | tf_op jit(solution)/shard_map/ppermute | solution.py:317
  191.9 9.3 %collective-permute-start.37 = (bf16[64,1024]{1,0:T(8,128)(2,1)S(1)}, bf16[64,1024]{1,0:T(8,128)(2,1)S(1)}, u32[]{:S(2)}, u32[]{:S(2)}) collective-permute-start(bf16[64,1024]{1,0:T(8,128)(2,1)S(1)} %collective-permute-done.36.refs_7_), channel_id=1, source_target_pairs={{0,8},{8,0},{16,24},{24,16},{1,9},{9,1},{17,25},{25,17},{2,10},{10... | collective-permute-start | bytes 393224 | tf_op jit(solution)/shard_map/ppermute | solution.py:317
  195.0 6.3 %collective-permute-start.32 = (bf16[192,1024]{1,0:T(8,128)(2,1)}, bf16[192,1024]{1,0:T(8,128)(2,1)S(1)}, u32[]{:S(2)}, u32[]{:S(2)}) collective-permute-start(bf16[192,1024]{1,0:T(8,128)(2,1)} %get-tuple-element.127.refs_1_), channel_id=1, source_target_pairs={{0,8},{8,0},{16,24},{24,16},{1,9},{9,1},{17,25},{25,17},{2,10},{10... | collective-permute-start | bytes 1179656 | tf_op jit(solution)/shard_map/ppermute | solution.py:317
  195.0 6.3 %collective-permute-start.34 = (bf16[192,1024]{1,0:T(8,128)(2,1)S(1)}, bf16[192,1024]{1,0:T(8,128)(2,1)S(1)}, u32[]{:S(2)}, u32[]{:S(2)}) collective-permute-start(bf16[192,1024]{1,0:T(8,128)(2,1)S(1)} %collective-permute-done.33.refs_3_), channel_id=1, source_target_pairs={{0,8},{8,0},{16,24},{24,16},{1,9},{9,1},{17,25},{25,17},{2,10},{10... | collective-permute-start | bytes 1179656 | tf_op jit(solution)/shard_map/ppermute | solution.py:317
  (16 other events, 59.0 us)

commit v7 on v6

--- a/solution.py
+++ b/solution.py
@@ -323,9 +323,8 @@
 
 def gathered_blocks(value, count, zero):
     evens = even_blocks(value, count)
-    return evens, [swapped_with(e, "blk", 1) for e in evens[:1]] + [
-        swapped_with(e + zero, "blk", 1) for e in evens[1:]
-    ]
+    waiting = [e if i in (0, count // 2 - 1) else e + zero for i, e in enumerate(evens)]
+    return evens, [swapped_with(e, "blk", 1) for e in waiting]
 
 
 def offset_of(index, count):

time: 205 us -> 205 us (level)
    unnamed x46 -> x44, local copies, waits for them, and re-layouts: 5.31 us -> 5.31 us
where the time goes in v7:
time: 205 us; the launch traced here: 204 us
  Pallas kernels  104 us (51%)
  starting transfers between devices  56.1 us (27%)
  waiting for transfers between devices  31.1 us (15%)
  local copies, waits for them, and re-layouts  7.61 us (4%)
  other arithmetic  3.57 us (2%)
    ppermute x37, starting transfers between devices, swapped_with(): return lax.ppermute(value, axis, [(i, i ^ offset) for i in range(size)])  42.4 us
    ppermute x37, waiting for transfers between devices, swapped_with(): return lax.ppermute(value, axis, [(i, i ^ offset) for i in range(size)])  24.9 us
    pallas_call x2, Pallas kernels, project(): pl.pallas_call(lambda *refs: project_kernel(clips, with_own, *refs), grid...  14 us
    pallas_call x1, Pallas kernels, attend_back(): pl.pallas_call(attend_back_kernel, grid_spec=grid_spec, out_shape=[shape_...  13 us
    pallas_call x1, Pallas kernels, attend(): pl.pallas_call(attend_kernel, grid=(width // LANES,), in_specs=[pl.BlockS...  11.5 us
    pallas_call x2, Pallas kernels, table_part(): pl.pallas_call(lambda *refs: table_kernel(first, clips, *refs), grid=(col...  11.2 us
    pallas_call x1, Pallas kernels, weights_part(): pl.pallas_call(lambda *refs: weights_kernel(clips, count, *refs), grid=(1...  9.73 us
    pallas_call x1, Pallas kernels, middle_part(): pl.pallas_call(lambda *refs: middle_kernel(clips, *refs), grid=(1,), in_s...  8.37 us
  transfers between devices with their start and end apart: 41, of which 15 were waited for; matrix products, arithmetic and copies ran while one was open for 3% of the time, Pallas kernels for 44%

profile of v7, /device:TPU:0, one launch (start us, length us, event | category | flops | bytes accessed | tf_op | source)
XLA Modules:
  0.0 204.0 jit_solution(16835788106223395939)
XLA Ops:
  0.6 3.1 %collective-permute-start = (bf16[128,1024]{1,0:T(8,128)(2,1)}, bf16[128,1024]{1,0:T(8,128)(2,1)S(1)}, u32[]{:S(2)}, u32[]{:S(2)}) collective-permute-start(bf16[128,1024]{1,0:T(8,128)(2,1)} %refs_2_.5), channel_id=1, source_target_pairs={{0,2},{1,3},{2,0},{3,1},{4,6},{5,7},{6,4},{7,5},{8,10},{9,11},{10,... | collective-permute-start | bytes 786440 | tf_op jit(solution)/shard_map/ppermute | solution.py:317
  3.7 2.6 %collective-permute-start.1 = (bf16[128,1024]{1,0:T(8,128)(2,1)}, bf16[128,1024]{1,0:T(8,128)(2,1)S(1)}, u32[]{:S(2)}, u32[]{:S(2)}) collective-permute-start(bf16[128,1024]{1,0:T(8,128)(2,1)} %refs_2_.5), channel_id=1, source_target_pairs={{0,4},{1,5},{2,6},{3,7},{4,0},{5,1},{6,2},{7,3},{8,12},{9,13},{10,... | collective-permute-start | bytes 786440 | tf_op jit(solution)/shard_map/ppermute | solution.py:317
  6.3 1.7 collective-permute-start.3
  11.0 5.9 %shard_map.246 = (f32[4,2048]{1,0:T(4,128)S(1)}, bf16[4,1024]{1,0:T(4,128)(2,1)S(1)}, s32[1024,1]{1,0:T(8,128)S(1)}, s32[1,1024]{1,0:T(1,128)S(1)}, f32[1024,128...) custom-call(s32[1]{0:T(128)} %bitcast.refs_0_.me_ref, ...), custom_call_target="tpu_custom_call" | custom-call | flops 16777216 | bytes 5242880 | tf_op jit(solution)/shard_map/pallas_call | solution.py:462
  17.0 4.8 %shard_map.248.refs_6_.refs_2_ = f32[4,4096]{1,0:T(4,128)S(1)} custom-call(bf16[4,1024]{1,0:T(4,128)(2,1)S(1)} %get-tuple-element.82.silu_ref, bf16[1024,6144]{1,0:T(8,128)(2,1)} %refs_6_.7, f32[1,6144]{1,0:T(1,128)S(1)} %bitcast.24), custom_call_target="tpu_custom_call" | custom-call | flops 33554432 | bytes 8388608 | tf_op jit(solution)/shard_map/pallas_call | solution.py:489
  23.4 1.9 collective-permute-done.1.refs_9_
  26.1 1.5 collective-permute-start.5
  28.1 6.4 %shard_map.247 = (bf16[512,1024]{1,0:T(8,128)(2,1)}, bf16[16,512,128]{2,1,0:T(8,128)(2,1)S(1)}, bf16[512,128]{1,0:T(8,128)(2,1)S(1)}, bf16[128,1024]{1,0:T(8,128)(2,1)}, bf16[128,1024]{1,0:T(8,128)(2,1)}) custom-call(s32[1]{0:T(128)} %bitcast.refs_0_.me_ref, s32[1024,1]{1,0:T(8,128)S(1)} %get-tuple-element.73.refs_1_.keyclip_ref.refs_0_, ...), custom_call_target="tpu_custom_call" | custom-call | flops 2147483648 | bytes 6291456 | tf_op jit(solution)/shard_map/pallas_call | solution.py:580
  34.5 3.6 %collective-permute-start.7 = (bf16[128,1024]{1,0:T(8,128)(2,1)}, bf16[128,1024]{1,0:T(8,128)(2,1)S(1)}, u32[]{:S(2)}, u32[]{:S(2)}) collective-permute-start(bf16[128,1024]{1,0:T(8,128)(2,1)} %get-tuple-element.88.refs_13_.refs_15_), channel_id=1, source_target_pairs={{0,2},{1,3},{2,0},{3,1},{4,6},{5,7},{6,4},{7,5},{8,10},{9,11},{10,... | collective-permute-start | bytes 786440 | tf_op jit(solution)/shard_map/ppermute | solution.py:317
  38.1 1.1 collective-permute-start.8
  39.2 1.5 collective-permute-start.9
  41.5 7.6 %shard_map.249 = (bf16[512,1024]{1,0:T(8,128)(2,1)}, bf16[16,512,128]{2,1,0:T(8,128)(2,1)S(1)}, bf16[512,128]{1,0:T(8,128)(2,1)S(1)}) custom-call(s32[1]{0:T(128)} %bitcast.refs_0_.me_ref, s32[1024,1]{1,0:T(8,128)S(1)} %get-tuple-element.73.refs_1_.keyclip_ref.refs_0_, f32[4,2048]{1,0:T(4,128)S(1)} %get-tuple-element.76.refs_2_.refs_3_, ...), custom_call_target="tpu_custom_call" | custom-call | flops 2147483648 | bytes 6291456 | tf_op jit(solution)/shard_map/pallas_call | solution.py:580
  49.2 11.5 %shard_map.250 = (bf16[128,1024]{1,0:T(8,128)(2,1)}, bf16[1024,1024]{1,0:T(8,128)(2,1)S(1)}, bf16[1024,2048]{1,0:T(8,128)(2,1)S(1)}, bf16[2048,1024]{1,0:T(8,128)(2,1)S(1)}) custom-call(bf16[1024,256]{1,0:T(8,128)(2,1)} %get-tuple-element.75.keymark_ref.rowmark_ref, bf16[1024,256]{1,0:T(8,128)(2,1)} %get-tuple-element.75.keymark_ref.rowmark_ref, ...), custom_call_target="tpu_custom_call" | custom-call | flops 536870912 | bytes 1048576 | tf_op jit(solution)/shard_map/pallas_call | solution.py:667
  61.6 8.4 %shard_map.251 = (bf16[128,1024]{1,0:T(8,128)(2,1)}, bf16[128,1024]{1,0:T(8,128)(2,1)}, f32[128,1024]{1,0:T(8,128)}, bf16[128,1024]{1,0:T(8,128)(2,1)}, bf16[8,1...) custom-call(s32[1,4]{1,0:T(1,128)S(1)} %copy-done.11, s32[1024,1]{1,0:T(8,128)S(1)} %get-tuple-element.73.refs_1_.keyclip_ref.refs_0_, ...), custom_call_target="tpu_custom_call" | custom-call | flops 2684354560 | bytes 3145728 | tf_op jit(solution)/shard_map/pallas_call | solution.py:982
  69.9 1.6 collective-permute-start.12
  71.6 2.5 %collective-permute-start.13 = (bf16[128,1024]{1,0:T(8,128)(2,1)}, bf16[128,1024]{1,0:T(8,128)(2,1)S(1)}, u32[]{:S(2)}, u32[]{:S(2)}) collective-permute-start(bf16[128,1024]{1,0:T(8,128)(2,1)} %get-tuple-element.97.refs_1_.refs_11_), channel_id=1, source_target_pairs={{0,4},{1,5},{2,6},{3,7},{4,0},{5,1},{6,2},{7,3},{8,12},{9,13},{10,... | collective-permute-start | bytes 786440 | tf_op jit(solution)/shard_map/ppermute | solution.py:317
  74.0 3.5 %all-to-all-start = ((bf16[8,128,128]{2,1,0:T(8,128)(2,1)}), bf16[8,128,128]{2,1,0:T(8,128)(2,1)S(1)}, u32[]{:S(2)}, u32[]{:S(2)}) async-start(bf16[8,128,128]{2,1,0:T(8,128)(2,1)} %get-tuple-element.95), calls=%async_computation | async-start | bytes 524288 | tf_op jit(solution)/shard_map/all_to_all | solution.py:1496
  77.6 1.9 collective-permute-start.10
  79.5 8.4 %shard_map.252 = (f32[1024,2048]{1,0:T(8,128)}, bf16[128,1024]{1,0:T(8,128)(2,1)}) custom-call(s32[1]{0:T(128)} %bitcast.refs_0_.me_ref, s32[1024,1]{1,0:T(8,128)S(1)} %get-tuple-element.73.refs_1_.keyclip_ref.refs_0_, s32[1,1024]{1,0:T(1,128)S(1)} %get-tuple-element.74.refs_2_.rowclip_ref.refs_1_, ...), custom_call_target="tpu_custom_call", output_to_operand_aliasing={{1}: (8, {})} | custom-call | flops 536870912 | bytes 9437184 | tf_op jit(solution)/shard_map/pallas_call | solution.py:729
  87.9 1.0 broadcast_select_fusion
  89.7 1.5 collective-permute-start.14
  91.2 1.5 collective-permute-start.11
  92.8 2.4 %collective-permute-start.15 = (bf16[128,1024]{1,0:T(8,128)(2,1)S(1)}, bf16[128,1024]{1,0:T(8,128)(2,1)}, u32[]{:S(2)}, u32[]{:S(2)}) collective-permute-start(bf16[128,1024]{1,0:T(8,128)(2,1)S(1)} %copy-done.13), channel_id=1, source_target_pairs={{0,6},{1,7},{2,4},{3,5},{4,2},{5,3},{6,0},{7,1},{8,14},{9,15},{10,... | collective-permute-start | bytes 786440 | tf_op jit(solution)/shard_map/ppermute | solution.py:317
  95.1 2.7 %collective-permute-done.11 = f32[8,4096]{1,0:T(8,128)S(1)} collective-permute-done((f32[8,4096]{1,0:T(8,128)S(1)}, f32[8,4096]{1,0:T(8,128)S(1)}, u32[]{:S(2)}, u32[]{:S(2)}) %collective-permute-start.11) | collective-permute-done | bytes 131104 | tf_op jit(solution)/shard_map/ppermute | solution.py:317
  98.6 13.0 %shard_map.253 = (bf16[1024,384]{1,0:T(8,128)(2,1)}, bf16[8,128,384]{2,1,0:T(8,128)(2,1)}, f32[8,4096]{1,0:T(8,128)S(1)}) custom-call(s32[1]{0:T(128)} %bitcast.refs_0_.me_ref, f32[1024,2048]{1,0:T(8,128)} %get-tuple-element.94.p_ref, bf16[512,128]{1,0:T(8,128)(2,1)S(1)} %get-tuple-element.91.qa_ref, ...), custom_call_target="tpu_custom_call", output_to_operand_aliasing={{2}: (11, {})} | custom-call | flops 1073741824 | bytes 12582912 | tf_op jit(solution)/shard_map/pallas_call | solution.py:834
  111.6 3.8 %all-to-all-start.1 = ((bf16[8,128,384]{2,1,0:T(8,128)(2,1)}), bf16[8,128,384]{2,1,0:T(8,128)(2,1)S(1)}, u32[]{:S(2)}, u32[]{:S(2)}) async-start(bf16[8,128,384]{2,1,0:T(8,128)(2,1)} %get-tuple-element.98), calls=%async_computation.1 | async-start | bytes 1572864 | tf_op jit(solution)/shard_map/all_to_all | solution.py:1513
  116.3 9.7 %shard_map.254 = (f32[512,1920]{1,0:T(8,128)}, bf16[512,640]{1,0:T(8,128)(2,1)}, bf16[512,640]{1,0:T(8,128)(2,1)}, bf16[512,640]{1,0:T(8,128)(2,1)}) custom-call(s32[3]{0:T(128)S(1)} %pad_add_fusion.refs_0_, s32[1024,1]{1,0:T(8,128)S(1)} %get-tuple-element.73.refs_1_.keyclip_ref.refs_0_, f32[4,4096]{1,0:T(4,128)S(1)} %shard_map.248.refs_6_.refs_2_, ...), custom_call_target="tpu_custom_call" | custom-call | flops 3758096384 | bytes 10485760 | tf_op jit(solution)/shard_map/pallas_call | solution.py:1161
  126.7 1.7 collective-permute-done.16.refs_2_
  130.3 3.9 %shard_map.255 = (f32[8,32,896]{2,1,0:T(8,128)}, bf16[8,32,896]{2,1,0:T(8,128)(2,1)}, bf16[8,32,512]{2,1,0:T(8,128)(2,1)}, bf16[8,32,512]{2,1,0:T(8,128)(2,1)}, bf16[8,32,1024]{2,1,0:T(8,128)(2,1)}) custom-call(s32[3]{0:T(128)S(1)} %pad_add_fusion.refs_0_, f32[512,1920]{1,0:T(8,128)} %get-tuple-element.103.refs_1_, ...), custom_call_target="tpu_custom_call" | custom-call | bytes 8388608 | tf_op jit(solution)/shard_map/pallas_call | solution.py:1324
  134.7 1.7 collective-permute-start.20
  136.3 1.3 collective-permute-start.21
  137.6 6.8 %shard_map.256 = (bf16[128,1024]{1,0:T(8,128)(2,1)}, f32[8,2048]{1,0:T(8,128)S(1)}, f32[8,32,896]{2,1,0:T(8,128)}, f32[8,4096]{1,0:T(8,128)S(1)}) custom-call(s32[1024,1]{1,0:T(8,128)S(1)} %get-tuple-element.73.refs_1_.keyclip_ref.refs_0_, s32[1,1024]{1,0:T(1,128)S(1)} %get-tuple-element.74.refs_2_.rowclip_ref.refs_1_, ...), custom_call_target="tpu_custom_call", output_to_operand_aliasing={{2}: (7, {}), {3}: (8, {})} | custom-call | flops 805306368 | bytes 2097152 | tf_op jit(solution)/shard_map/pallas_call | solution.py:1034
  144.5 2.6 %collective-permute-start.23 = (f32[8,4096]{1,0:T(8,128)S(1)}, f32[8,4096]{1,0:T(8,128)S(1)}, u32[]{:S(2)}, u32[]{:S(2)}) collective-permute-start(f32[8,4096]{1,0:T(8,128)S(1)} %get-tuple-element.116), channel_id=1, source_target_pairs={{0,4},{1,5},{2,6},{3,7},{4,0},{5,1},{6,2},{7,3},{8,12},{9,13},{10,... | collective-permute-start | bytes 393224 | tf_op jit(solution)/shard_map/ppermute | solution.py:317
  147.1 1.5 collective-permute-start.22
  148.6 2.9 %collective-permute-done.22 = f32[8,2048]{1,0:T(8,128)S(1)} collective-permute-done((f32[8,2048]{1,0:T(8,128)S(1)}, f32[8,2048]{1,0:T(8,128)S(1)}, u32[]{:S(2)}, u32[]{:S(2)}) %collective-permute-start.22) | collective-permute-done | bytes 65568 | tf_op jit(solution)/shard_map/ppermute | solution.py:317
  151.6 1.4 collective-permute-done.23
  153.6 2.3 %shard_map.257 = (f32[8,2048]{1,0:T(8,128)S(1)}, f32[8,4096]{1,0:T(8,128)S(1)}, bf16[8,32,1664]{2,1,0:T(8,128)(2,1)}, bf16[64,1024]{1,0:T(8,128)(2,1)S(1)}) custom-call(f32[8,32,896]{2,1,0:T(8,128)} %get-tuple-element.110.refs_0_, bf16[8,32,896]{2,1,0:T(8,128)(2,1)S(1)} %collective-permute-done.19.refs_1_, ...), custom_call_target="tpu_custom_call", output_to_operand_aliasing={{0}: (5, {}), {1}: (6, {})} | custom-call | bytes 4194304 | tf_op jit(solution)/shard_map/pallas_call | solution.py:1360
  155.9 5.0 %all-to-all-start.2 = ((bf16[8,32,1664]{2,1,0:T(8,128)(2,1)}), bf16[8,32,1664]{2,1,0:T(8,128)(2,1)S(1)}, u32[]{:S(2)}, u32[]{:S(2)}) async-start(bf16[8,32,1664]{2,1,0:T(8,128)(2,1)} %get-tuple-element.117), calls=%async_computation.2 | async-start | bytes 1703936 | tf_op jit(solution)/shard_map/all_to_all | solution.py:1541
  161.6 1.3 collective-permute-start.27
  162.9 2.1 %collective-permute-start.24 = (f32[8,2048]{1,0:T(8,128)S(1)}, f32[8,2048]{1,0:T(8,128)S(1)}, u32[]{:S(2)}, u32[]{:S(2)}) collective-permute-start(f32[8,2048]{1,0:T(8,128)S(1)} %get-tuple-element.118), channel_id=1, source_target_pairs={{0,1},{1,0},{2,3},{3,2},{4,5},{5,4},{6,7},{7,6},{8,9},{9,8},{10,11... | collective-permute-start | bytes 196616 | tf_op jit(solution)/shard_map/ppermute | solution.py:317
  165.5 3.8 %collective-permute-done.27.refs_4_ = f32[8,4096]{1,0:T(8,128)S(1)} collective-permute-done((f32[8,4096]{1,0:T(8,128)S(1)}, f32[8,4096]{1,0:T(8,128)S(1)}, u32[]{:S(2)}, u32[]{:S(2)}) %collective-permute-start.27) | collective-permute-done | bytes 131104 | tf_op jit(solution)/shard_map/ppermute | solution.py:317
  170.8 6.3 %shard_map.258 = (f32[128,6144]{1,0:T(8,128)}, f32[1,6144]{1,0:T(1,128)}, f32[1024,64]{1,0:T(8,128)}) custom-call(s32[1]{0:T(128)} %bitcast.8.refs_0_, f32[8,4096]{1,0:T(8,128)S(1)} %get-tuple-element.119.refs_1_, f32[8,4096]{1,0:T(8,128)S(1)} %collective-permute-done.25.refs_2_, f32[8,4096]{1,0:T(8,128)S(1)} %collective-permute-done.26.refs_3_, ...), custom_call_target="tpu_custom_call" | custom-call | flops 32768 | bytes 1024 | tf_op jit(solution)/shard_map/pallas_call | solution.py:1263
  177.1 5.5 %all-to-all-done.2.refs_0_ = bf16[8,32,1664]{2,1,0:T(8,128)(2,1)S(1)} async-done(((bf16[8,32,1664]{2,1,0:T(8,128)(2,1)}), bf16[8,32,1664]{2,1,0:T(8,128)(2,1)S(1)}, u32[]{:S(2)}, u32[]{:S(2)}) %all-to-all-start.2) | async-done | bytes 852000 | tf_op jit(solution)/shard_map/all_to_all | solution.py:1541
  185.3 4.2 %collective-permute-done.28 = f32[8,2048]{1,0:T(8,128)S(1)} collective-permute-done((f32[8,2048]{1,0:T(8,128)S(1)}, f32[8,2048]{1,0:T(8,128)S(1)}, u32[]{:S(2)}, u32[]{:S(2)}) %collective-permute-start.28) | collective-permute-done | bytes 65568 | tf_op jit(solution)/shard_map/ppermute | solution.py:317
  189.6 1.6 collective-permute-start.30
  192.1 2.9 %collective-permute-done.30.refs_3_ = f32[8,2048]{1,0:T(8,128)S(1)} collective-permute-done((f32[8,2048]{1,0:T(8,128)S(1)}, f32[8,2048]{1,0:T(8,128)S(1)}, u32[]{:S(2)}, u32[]{:S(2)}) %collective-permute-start.30) | collective-permute-done | bytes 65568 | tf_op jit(solution)/shard_map/ppermute | solution.py:317
  195.7 4.9 %shard_map.260 = (f32[128,6144]{1,0:T(8,128)}, f32[1,6144]{1,0:T(1,128)}, f32[32,1024]{1,0:T(8,128)}) custom-call(s32[1]{0:T(128)} %bitcast.8.refs_0_, f32[8,2048]{1,0:T(8,128)S(1)} %add.97.refs_1_, f32[8,2048]{1,0:T(8,128)S(1)} %collective-permute-done.29.refs_2_, ...), custom_call_target="tpu_custom_call", output_to_operand_aliasing={{0}: (10, {}), {1}: (11, {})} | custom-call | flops 32768 | bytes 1024 | tf_op jit(solution)/shard_map/pallas_call | solution.py:1263
  201.2 2.8 %shard_map.261 = (f32[128,3072]{1,0:T(8,128)}, f32[128,1024]{1,0:T(8,128)}, f32[128,2048]{1,0:T(8,128)}, f32[256,1024]{1,0:T(8,128)}) custom-call(s32[3]{0:T(128)S(1)} %pad_add_fusion.refs_0_, bf16[192,1024]{1,0:T(8,128)(2,1)S(1)} %copy-done.4, bf16[192,1024]{1,0:T(8,128)(2,1)S(1)} %collective-permute-done.32.refs_2_, ...), custom_call_target="tpu_custom_call" | custom-call | bytes 6291456 | tf_op jit(solution)/shard_map/pallas_call | solution.py:1444
  (126 shorter events, 20.6 us)
Async XLA Ops:
  0.6 22.4 %collective-permute-start = (bf16[128,1024]{1,0:T(8,128)(2,1)}, bf16[128,1024]{1,0:T(8,128)(2,1)S(1)}, u32[]{:S(2)}, u32[]{:S(2)}) collective-permute-start(bf16[128,1024]{1,0:T(8,128)(2,1)} %refs_2_.5), channel_id=1, source_target_pairs={{0,2},{1,3},{2,0},{3,1},{4,6},{5,7},{6,4},{7,5},{8,10},{9,11},{10,... | collective-permute-start | bytes 786440 | tf_op jit(solution)/shard_map/ppermute | solution.py:317
  3.7 21.6 %collective-permute-start.1 = (bf16[128,1024]{1,0:T(8,128)(2,1)}, bf16[128,1024]{1,0:T(8,128)(2,1)S(1)}, u32[]{:S(2)}, u32[]{:S(2)}) collective-permute-start(bf16[128,1024]{1,0:T(8,128)(2,1)} %refs_2_.5), channel_id=1, source_target_pairs={{0,4},{1,5},{2,6},{3,7},{4,0},{5,1},{6,2},{7,3},{8,12},{9,13},{10,... | collective-permute-start | bytes 786440 | tf_op jit(solution)/shard_map/ppermute | solution.py:317
  6.3 21.3 %collective-permute-start.2 = (bf16[128,1024]{1,0:T(8,128)(2,1)}, bf16[128,1024]{1,0:T(8,128)(2,1)}, u32[]{:S(2)}, u32[]{:S(2)}) collective-permute-start(bf16[128,1024]{1,0:T(8,128)(2,1)} %refs_2_.5), channel_id=1, source_target_pairs={{0,6},{1,7},{2,4},{3,5},{4,2},{5,3},{6,0},{7,1},{8,14},{9,15},{10,... | collective-permute-start | bytes 786440 | tf_op jit(solution)/shard_map/ppermute | solution.py:317
  6.3 31.8 %collective-permute-start.3 = (bf16[128,1024]{1,0:T(8,128)(2,1)}, bf16[128,1024]{1,0:T(8,128)(2,1)}, u32[]{:S(2)}, u32[]{:S(2)}) collective-permute-start(bf16[128,1024]{1,0:T(8,128)(2,1)} %refs_2_.5), channel_id=1, source_target_pairs={{0,1},{1,0},{2,3},{3,2},{4,5},{5,4},{6,7},{7,6},{8,9},{9,8},{10,11... | collective-permute-start | bytes 786440 | tf_op jit(solution)/shard_map/ppermute | solution.py:317
  23.1 16.1 %collective-permute-start.4 = (bf16[128,1024]{1,0:T(8,128)(2,1)S(1)}, bf16[128,1024]{1,0:T(8,128)(2,1)}, u32[]{:S(2)}, u32[]{:S(2)}) collective-permute-start(bf16[128,1024]{1,0:T(8,128)(2,1)S(1)} %broadcast_add_fusion.1), channel_id=1, source_target_pairs={{0,1},{1,0},{2,3},{3,2},{4,5},{5,4},{6,7},{7,6},{8,9},{9,8},{10,11... | collective-permute-start | bytes 786440 | tf_op jit(solution)/shard_map/ppermute | solution.py:317
  26.1 14.5 %collective-permute-start.5 = (bf16[128,1024]{1,0:T(8,128)(2,1)}, bf16[128,1024]{1,0:T(8,128)(2,1)}, u32[]{:S(2)}, u32[]{:S(2)}) collective-permute-start(bf16[128,1024]{1,0:T(8,128)(2,1)} %broadcast_add_fusion), channel_id=1, source_target_pairs={{0,1},{1,0},{2,3},{3,2},{4,5},{5,4},{6,7},{7,6},{8,9},{9,8},{10,11... | collective-permute-start | bytes 786440 | tf_op jit(solution)/shard_map/ppermute | solution.py:317
  27.6 13.8 %collective-permute-start.6 = (bf16[128,1024]{1,0:T(8,128)(2,1)}, bf16[128,1024]{1,0:T(8,128)(2,1)}, u32[]{:S(2)}, u32[]{:S(2)}) collective-permute-start(bf16[128,1024]{1,0:T(8,128)(2,1)} %collective-permute-done.2.refs_10_), channel_id=1, source_target_pairs={{0,1},{1,0},{2,3},{3,2},{4,5},{5,4},{6,7},{7,6},{8,9},{9,8},{10,11... | collective-permute-start | bytes 786440 | tf_op jit(solution)/shard_map/ppermute | solution.py:317
  34.5 14.6 %copy-start = (bf16[16,512,128]{2,1,0:T(8,128)(2,1)}, bf16[16,512,128]{2,1,0:T(8,128)(2,1)S(1)}, u32[]{:S(2)}) copy-start(bf16[16,512,128]{2,1,0:T(8,128)(2,1)S(1)} %get-tuple-element.81.ka_ref.va_ref) | copy-start | bytes 6291460
  34.5 26.2 %collective-permute-start.7 = (bf16[128,1024]{1,0:T(8,128)(2,1)}, bf16[128,1024]{1,0:T(8,128)(2,1)S(1)}, u32[]{:S(2)}, u32[]{:S(2)}) collective-permute-start(bf16[128,1024]{1,0:T(8,128)(2,1)} %get-tuple-element.88.refs_13_.refs_15_), channel_id=1, source_target_pairs={{0,2},{1,3},{2,0},{3,1},{4,6},{5,7},{6,4},{7,5},{8,10},{9,11},{10,... | collective-permute-start | bytes 786440 | tf_op jit(solution)/shard_map/ppermute | solution.py:317
  38.1 22.6 %collective-permute-start.8 = (bf16[128,1024]{1,0:T(8,128)(2,1)}, bf16[128,1024]{1,0:T(8,128)(2,1)S(1)}, u32[]{:S(2)}, u32[]{:S(2)}) collective-permute-start(bf16[128,1024]{1,0:T(8,128)(2,1)} %get-tuple-element.88.refs_13_.refs_15_), channel_id=1, source_target_pairs={{0,4},{1,5},{2,6},{3,7},{4,0},{5,1},{6,2},{7,3},{8,12},{9,13},{10,... | collective-permute-start | bytes 786440 | tf_op jit(solution)/shard_map/ppermute | solution.py:317
  39.2 21.6 %collective-permute-start.9 = (bf16[128,1024]{1,0:T(8,128)(2,1)}, bf16[128,1024]{1,0:T(8,128)(2,1)}, u32[]{:S(2)}, u32[]{:S(2)}) collective-permute-start(bf16[128,1024]{1,0:T(8,128)(2,1)} %get-tuple-element.88.refs_13_.refs_15_), channel_id=1, source_target_pairs={{0,6},{1,7},{2,4},{3,5},{4,2},{5,3},{6,0},{7,1},{8,14},{9,15},{10,... | collective-permute-start | bytes 786440 | tf_op jit(solution)/shard_map/ppermute | solution.py:317
  49.1 12.4 %copy-start.7 = (f32[2048]{0:T(1024)S(1)}, f32[2048]{0:T(1024)}, u32[]{:S(2)}) copy-start(f32[2048]{0:T(1024)} %param.26) | copy-start | bytes 24580
  49.1 12.4 %copy-start.8 = (f32[1024]{0:T(1024)S(1)}, f32[1024]{0:T(1024)}, u32[]{:S(2)}) copy-start(f32[1024]{0:T(1024)} %param.24) | copy-start | bytes 12292
  49.1 12.4 %copy-start.9 = (f32[1024]{0:T(1024)S(1)}, f32[1024]{0:T(1024)}, u32[]{:S(2)}) copy-start(f32[1024]{0:T(1024)} %param.28) | copy-start | bytes 12292
  69.9 18.9 %copy-start.18 = (bf16[128,1024]{1,0:T(8,128)(2,1)S(1)}, bf16[128,1024]{1,0:T(8,128)(2,1)}, u32[]{:S(2)}) copy-start(bf16[128,1024]{1,0:T(8,128)(2,1)} %get-tuple-element.84.refs_5_) | copy-start | bytes 786436
  69.9 27.9 %collective-permute-start.12 = (bf16[128,1024]{1,0:T(8,128)(2,1)}, bf16[128,1024]{1,0:T(8,128)(2,1)S(1)}, u32[]{:S(2)}, u32[]{:S(2)}) collective-permute-start(bf16[128,1024]{1,0:T(8,128)(2,1)} %get-tuple-element.97.refs_1_.refs_11_), channel_id=1, source_target_pairs={{0,2},{1,3},{2,0},{3,1},{4,6},{5,7},{6,4},{7,5},{8,10},{9,11},{10,... | collective-permute-start | bytes 786440 | tf_op jit(solution)/shard_map/ppermute | solution.py:317
  71.6 26.3 %collective-permute-start.13 = (bf16[128,1024]{1,0:T(8,128)(2,1)}, bf16[128,1024]{1,0:T(8,128)(2,1)S(1)}, u32[]{:S(2)}, u32[]{:S(2)}) collective-permute-start(bf16[128,1024]{1,0:T(8,128)(2,1)} %get-tuple-element.97.refs_1_.refs_11_), channel_id=1, source_target_pairs={{0,4},{1,5},{2,6},{3,7},{4,0},{5,1},{6,2},{7,3},{8,12},{9,13},{10,... | collective-permute-start | bytes 786440 | tf_op jit(solution)/shard_map/ppermute | solution.py:317
  74.0 18.7 %copy-start.13 = (bf16[128,1024]{1,0:T(8,128)(2,1)S(1)}, bf16[128,1024]{1,0:T(8,128)(2,1)}, u32[]{:S(2)}) copy-start(bf16[128,1024]{1,0:T(8,128)(2,1)} %get-tuple-element.97.refs_1_.refs_11_) | copy-start | bytes 786436
  74.0 23.8 %all-to-all-start = ((bf16[8,128,128]{2,1,0:T(8,128)(2,1)}), bf16[8,128,128]{2,1,0:T(8,128)(2,1)S(1)}, u32[]{:S(2)}, u32[]{:S(2)}) async-start(bf16[8,128,128]{2,1,0:T(8,128)(2,1)} %get-tuple-element.95), calls=%async_computation | async-start | bytes 524288 | tf_op jit(solution)/shard_map/all_to_all | solution.py:1496
  77.6 13.6 %collective-permute-start.10 = (f32[8,4096]{1,0:T(8,128)S(1)}, f32[8,4096]{1,0:T(8,128)S(1)}, u32[]{:S(2)}, u32[]{:S(2)}) collective-permute-start(f32[8,4096]{1,0:T(8,128)S(1)} %get-tuple-element.96), channel_id=1, source_target_pairs={{0,1},{1,0},{2,3},{3,2},{4,5},{5,4},{6,7},{7,6},{8,9},{9,8},{10,11... | collective-permute-start | bytes 393224 | tf_op jit(solution)/shard_map/ppermute | solution.py:317
  89.7 25.8 %collective-permute-start.14 = (bf16[128,1536]{1,0:T(8,128)(2,1)S(1)}, bf16[128,1536]{1,0:T(8,128)(2,1)S(1)}, u32[]{:S(2)}, u32[]{:S(2)}) collective-permute-start(bf16[128,1536]{1,0:T(8,128)(2,1)S(1)} %get-tuple-element.133), channel_id=1, source_target_pairs={{0,16},{8,24},{16,0},{24,8},{1,17},{9,25},{17,1},{25,9},{2,18},{10... | collective-permute-start | bytes 1179656 | tf_op jit(solution)/shard_map/ppermute | solution.py:317
  91.2 6.6 %collective-permute-start.11 = (f32[8,4096]{1,0:T(8,128)S(1)}, f32[8,4096]{1,0:T(8,128)S(1)}, u32[]{:S(2)}, u32[]{:S(2)}) collective-permute-start(f32[8,4096]{1,0:T(8,128)S(1)} %add.88), channel_id=1, source_target_pairs={{0,2},{1,3},{2,0},{3,1},{4,6},{5,7},{6,4},{7,5},{8,10},{9,11},{10,... | collective-permute-start | bytes 393224 | tf_op jit(solution)/shard_map/ppermute | solution.py:317
  92.8 22.8 %collective-permute-start.15 = (bf16[128,1024]{1,0:T(8,128)(2,1)S(1)}, bf16[128,1024]{1,0:T(8,128)(2,1)}, u32[]{:S(2)}, u32[]{:S(2)}) collective-permute-start(bf16[128,1024]{1,0:T(8,128)(2,1)S(1)} %copy-done.13), channel_id=1, source_target_pairs={{0,6},{1,7},{2,4},{3,5},{4,2},{5,3},{6,0},{7,1},{8,14},{9,15},{10,... | collective-permute-start | bytes 786440 | tf_op jit(solution)/shard_map/ppermute | solution.py:317
  111.6 26.0 %all-to-all-start.1 = ((bf16[8,128,384]{2,1,0:T(8,128)(2,1)}), bf16[8,128,384]{2,1,0:T(8,128)(2,1)S(1)}, u32[]{:S(2)}, u32[]{:S(2)}) async-start(bf16[8,128,384]{2,1,0:T(8,128)(2,1)} %get-tuple-element.98), calls=%async_computation.1 | async-start | bytes 1572864 | tf_op jit(solution)/shard_map/all_to_all | solution.py:1513
  126.0 2.4 %collective-permute-start.16 = (bf16[512,640]{1,0:T(8,128)(2,1)}, bf16[512,640]{1,0:T(8,128)(2,1)S(1)}, u32[]{:S(2)}, u32[]{:S(2)}) collective-permute-start(bf16[512,640]{1,0:T(8,128)(2,1)} %get-tuple-element.104), channel_id=1, source_target_pairs={{0,8},{8,0},{16,24},{24,16},{1,9},{9,1},{17,25},{25,17},{2,10},{10... | collective-permute-start | bytes 1966088 | tf_op jit(solution)/shard_map/ppermute | solution.py:317
  126.1 3.2 %collective-permute-start.17 = (bf16[512,640]{1,0:T(8,128)(2,1)}, bf16[512,640]{1,0:T(8,128)(2,1)S(1)}, u32[]{:S(2)}, u32[]{:S(2)}) collective-permute-start(bf16[512,640]{1,0:T(8,128)(2,1)} %get-tuple-element.105), channel_id=1, source_target_pairs={{0,8},{8,0},{16,24},{24,16},{1,9},{9,1},{17,25},{25,17},{2,10},{10... | collective-permute-start | bytes 1966088 | tf_op jit(solution)/shard_map/ppermute | solution.py:317
  126.6 3.7 %collective-permute-start.18 = (bf16[512,640]{1,0:T(8,128)(2,1)}, bf16[512,640]{1,0:T(8,128)(2,1)S(1)}, u32[]{:S(2)}, u32[]{:S(2)}) collective-permute-start(bf16[512,640]{1,0:T(8,128)(2,1)} %get-tuple-element.106), channel_id=1, source_target_pairs={{0,8},{8,0},{16,24},{24,16},{1,9},{9,1},{17,25},{25,17},{2,10},{10... | collective-permute-start | bytes 1966088 | tf_op jit(solution)/shard_map/ppermute | solution.py:317
  134.1 19.5 %collective-permute-start.19 = (bf16[8,32,896]{2,1,0:T(8,128)(2,1)}, bf16[8,32,896]{2,1,0:T(8,128)(2,1)S(1)}, u32[]{:S(2)}, u32[]{:S(2)}) collective-permute-start(bf16[8,32,896]{2,1,0:T(8,128)(2,1)} %get-tuple-element.111), channel_id=1, source_target_pairs={{0,16},{8,24},{16,0},{24,8},{1,17},{9,25},{17,1},{25,9},{2,18},{10... | collective-permute-start | bytes 1376264 | tf_op jit(solution)/shard_map/ppermute | solution.py:317
  134.7 18.3 %collective-permute-start.20 = (bf16[8,32,512]{2,1,0:T(8,128)(2,1)}, bf16[8,32,512]{2,1,0:T(8,128)(2,1)S(1)}, u32[]{:S(2)}, u32[]{:S(2)}) collective-permute-start(bf16[8,32,512]{2,1,0:T(8,128)(2,1)} %get-tuple-element.112), channel_id=1, source_target_pairs={{0,1},{1,0},{2,3},{3,2},{4,5},{5,4},{6,7},{7,6},{8,9},{9,8},{10,11... | collective-permute-start | bytes 786440 | tf_op jit(solution)/shard_map/ppermute | solution.py:317
  136.3 17.3 %collective-permute-start.21 = (bf16[8,32,512]{2,1,0:T(8,128)(2,1)}, bf16[8,32,512]{2,1,0:T(8,128)(2,1)S(1)}, u32[]{:S(2)}, u32[]{:S(2)}) collective-permute-start(bf16[8,32,512]{2,1,0:T(8,128)(2,1)} %get-tuple-element.113), channel_id=1, source_target_pairs={{0,17},{1,16},{2,19},{3,18},{4,21},{5,20},{6,23},{7,22},{8,25},{9,... | collective-permute-start | bytes 786440 | tf_op jit(solution)/shard_map/ppermute | solution.py:1536
  144.5 25.5 %copy-start.3 = (f32[32,1024]{1,0:T(8,128)S(1)}, f32[32,1024]{1,0:T(8,128)}, u32[]{:S(2)}) copy-start(f32[32,1024]{1,0:T(8,128)} %refs_3_.2) | copy-start | bytes 393220
  144.5 8.5 %collective-permute-start.23 = (f32[8,4096]{1,0:T(8,128)S(1)}, f32[8,4096]{1,0:T(8,128)S(1)}, u32[]{:S(2)}, u32[]{:S(2)}) collective-permute-start(f32[8,4096]{1,0:T(8,128)S(1)} %get-tuple-element.116), channel_id=1, source_target_pairs={{0,4},{1,5},{2,6},{3,7},{4,0},{5,1},{6,2},{7,3},{8,12},{9,13},{10,... | collective-permute-start | bytes 393224 | tf_op jit(solution)/shard_map/ppermute | solution.py:317
  147.1 4.4 %collective-permute-start.22 = (f32[8,2048]{1,0:T(8,128)S(1)}, f32[8,2048]{1,0:T(8,128)S(1)}, u32[]{:S(2)}, u32[]{:S(2)}) collective-permute-start(f32[8,2048]{1,0:T(8,128)S(1)} %get-tuple-element.115), channel_id=1, source_target_pairs={{0,2},{1,3},{2,0},{3,1},{4,6},{5,7},{6,4},{7,5},{8,10},{9,11},{10,... | collective-permute-start | bytes 196616 | tf_op jit(solution)/shard_map/ppermute | solution.py:317
  155.9 26.7 %all-to-all-start.2 = ((bf16[8,32,1664]{2,1,0:T(8,128)(2,1)}), bf16[8,32,1664]{2,1,0:T(8,128)(2,1)S(1)}, u32[]{:S(2)}, u32[]{:S(2)}) async-start(bf16[8,32,1664]{2,1,0:T(8,128)(2,1)} %get-tuple-element.117), calls=%async_computation.2 | async-start | bytes 1703936 | tf_op jit(solution)/shard_map/all_to_all | solution.py:1541
  161.0 8.3 %collective-permute-start.25 = (f32[8,4096]{1,0:T(8,128)S(1)}, f32[8,4096]{1,0:T(8,128)S(1)}, u32[]{:S(2)}, u32[]{:S(2)}) collective-permute-start(f32[8,4096]{1,0:T(8,128)S(1)} %get-tuple-element.119.refs_1_), channel_id=1, source_target_pairs={{0,8},{8,0},{16,24},{24,16},{1,9},{9,1},{17,25},{25,17},{2,10},{10... | collective-permute-start | bytes 393224 | tf_op jit(solution)/shard_map/ppermute | solution.py:317
  161.0 8.2 %collective-permute-start.26 = (f32[8,4096]{1,0:T(8,128)S(1)}, f32[8,4096]{1,0:T(8,128)S(1)}, u32[]{:S(2)}, u32[]{:S(2)}) collective-permute-start(f32[8,4096]{1,0:T(8,128)S(1)} %get-tuple-element.119.refs_1_), channel_id=1, source_target_pairs={{0,16},{8,24},{16,0},{24,8},{1,17},{9,25},{17,1},{25,9},{2,18},{10... | collective-permute-start | bytes 393224 | tf_op jit(solution)/shard_map/ppermute | solution.py:317
  161.6 7.7 %collective-permute-start.27 = (f32[8,4096]{1,0:T(8,128)S(1)}, f32[8,4096]{1,0:T(8,128)S(1)}, u32[]{:S(2)}, u32[]{:S(2)}) collective-permute-start(f32[8,4096]{1,0:T(8,128)S(1)} %get-tuple-element.119.refs_1_), channel_id=1, source_target_pairs={{0,24},{8,16},{16,8},{24,0},{1,25},{9,17},{17,9},{25,1},{2,26},{10... | collective-permute-start | bytes 393224 | tf_op jit(solution)/shard_map/ppermute | solution.py:317
  162.9 7.9 %collective-permute-start.24 = (f32[8,2048]{1,0:T(8,128)S(1)}, f32[8,2048]{1,0:T(8,128)S(1)}, u32[]{:S(2)}, u32[]{:S(2)}) collective-permute-start(f32[8,2048]{1,0:T(8,128)S(1)} %get-tuple-element.118), channel_id=1, source_target_pairs={{0,1},{1,0},{2,3},{3,2},{4,5},{5,4},{6,7},{7,6},{8,9},{9,8},{10,11... | collective-permute-start | bytes 196616 | tf_op jit(solution)/shard_map/ppermute | solution.py:317
  165.0 26.5 %collective-permute-start.36 = (bf16[64,1024]{1,0:T(8,128)(2,1)S(1)}, bf16[64,1024]{1,0:T(8,128)(2,1)S(1)}, u32[]{:S(2)}, u32[]{:S(2)}) collective-permute-start(bf16[64,1024]{1,0:T(8,128)(2,1)S(1)} %get-tuple-element.128.refs_5_), channel_id=1, source_target_pairs={{0,16},{8,24},{16,0},{24,8},{1,17},{9,25},{17,1},{25,9},{2,18},{10... | collective-permute-start | bytes 393224 | tf_op jit(solution)/shard_map/ppermute | solution.py:317
  183.5 11.5 %collective-permute-start.33 = (bf16[192,1024]{1,0:T(8,128)(2,1)}, bf16[192,1024]{1,0:T(8,128)(2,1)S(1)}, u32[]{:S(2)}, u32[]{:S(2)}) collective-permute-start(bf16[192,1024]{1,0:T(8,128)(2,1)} %get-tuple-element.127.refs_1_), channel_id=1, source_target_pairs={{0,16},{8,24},{16,0},{24,8},{1,17},{9,25},{17,1},{25,9},{2,18},{10... | collective-permute-start | bytes 1179656 | tf_op jit(solution)/shard_map/ppermute | solution.py:317
  184.1 5.5 %collective-permute-start.28 = (f32[8,2048]{1,0:T(8,128)S(1)}, f32[8,2048]{1,0:T(8,128)S(1)}, u32[]{:S(2)}, u32[]{:S(2)}) collective-permute-start(f32[8,2048]{1,0:T(8,128)S(1)} %get-tuple-element.121), channel_id=1, source_target_pairs={{0,4},{1,5},{2,6},{3,7},{4,0},{5,1},{6,2},{7,3},{8,12},{9,13},{10,... | collective-permute-start | bytes 196616 | tf_op jit(solution)/shard_map/ppermute | solution.py:317
  189.6 2.4 %collective-permute-start.29 = (f32[8,2048]{1,0:T(8,128)S(1)}, f32[8,2048]{1,0:T(8,128)S(1)}, u32[]{:S(2)}, u32[]{:S(2)}) collective-permute-start(f32[8,2048]{1,0:T(8,128)S(1)} %add.97.refs_1_), channel_id=1, source_target_pairs={{0,8},{8,0},{16,24},{24,16},{1,9},{9,1},{17,25},{25,17},{2,10},{10... | collective-permute-start | bytes 196616 | tf_op jit(solution)/shard_map/ppermute | solution.py:317
  189.6 5.3 %collective-permute-start.30 = (f32[8,2048]{1,0:T(8,128)S(1)}, f32[8,2048]{1,0:T(8,128)S(1)}, u32[]{:S(2)}, u32[]{:S(2)}) collective-permute-start(f32[8,2048]{1,0:T(8,128)S(1)} %add.97.refs_1_), channel_id=1, source_target_pairs={{0,16},{8,24},{16,0},{24,8},{1,17},{9,25},{17,1},{25,9},{2,18},{10... | collective-permute-start | bytes 196616 | tf_op jit(solution)/shard_map/ppermute | solution.py:317
  191.2 4.4 %collective-permute-start.31 = (f32[8,2048]{1,0:T(8,128)S(1)}, f32[8,2048]{1,0:T(8,128)S(1)}, u32[]{:S(2)}, u32[]{:S(2)}) collective-permute-start(f32[8,2048]{1,0:T(8,128)S(1)} %add.97.refs_1_), channel_id=1, source_target_pairs={{0,24},{8,16},{16,8},{24,0},{1,25},{9,17},{17,9},{25,1},{2,26},{10... | collective-permute-start | bytes 196616 | tf_op jit(solution)/shard_map/ppermute | solution.py:317
  191.5 9.7 %collective-permute-start.35 = (bf16[64,1024]{1,0:T(8,128)(2,1)S(1)}, bf16[64,1024]{1,0:T(8,128)(2,1)S(1)}, u32[]{:S(2)}, u32[]{:S(2)}) collective-permute-start(bf16[64,1024]{1,0:T(8,128)(2,1)S(1)} %get-tuple-element.128.refs_5_), channel_id=1, source_target_pairs={{0,8},{8,0},{16,24},{24,16},{1,9},{9,1},{17,25},{25,17},{2,10},{10... | collective-permute-start | bytes 393224 | tf_op jit(solution)/shard_map/ppermute | solution.py:317
  191.9 9.3 %collective-permute-start.37 = (bf16[64,1024]{1,0:T(8,128)(2,1)S(1)}, bf16[64,1024]{1,0:T(8,128)(2,1)S(1)}, u32[]{:S(2)}, u32[]{:S(2)}) collective-permute-start(bf16[64,1024]{1,0:T(8,128)(2,1)S(1)} %collective-permute-done.36.refs_7_), channel_id=1, source_target_pairs={{0,8},{8,0},{16,24},{24,16},{1,9},{9,1},{17,25},{25,17},{2,10},{10... | collective-permute-start | bytes 393224 | tf_op jit(solution)/shard_map/ppermute | solution.py:317
  195.0 6.3 %collective-permute-start.32 = (bf16[192,1024]{1,0:T(8,128)(2,1)}, bf16[192,1024]{1,0:T(8,128)(2,1)S(1)}, u32[]{:S(2)}, u32[]{:S(2)}) collective-permute-start(bf16[192,1024]{1,0:T(8,128)(2,1)} %get-tuple-element.127.refs_1_), channel_id=1, source_target_pairs={{0,8},{8,0},{16,24},{24,16},{1,9},{9,1},{17,25},{25,17},{2,10},{10... | collective-permute-start | bytes 1179656 | tf_op jit(solution)/shard_map/ppermute | solution.py:317
  195.0 6.3 %collective-permute-start.34 = (bf16[192,1024]{1,0:T(8,128)(2,1)S(1)}, bf16[192,1024]{1,0:T(8,128)(2,1)S(1)}, u32[]{:S(2)}, u32[]{:S(2)}) collective-permute-start(bf16[192,1024]{1,0:T(8,128)(2,1)S(1)} %collective-permute-done.33.refs_3_), channel_id=1, source_target_pairs={{0,8},{8,0},{16,24},{24,16},{1,9},{9,1},{17,25},{25,17},{2,10},{10... | collective-permute-start | bytes 1179656 | tf_op jit(solution)/shard_map/ppermute | solution.py:317
  (15 other events, 55.4 us)
